TPU v7x, 32 devices: a whole 2x2x4 slice. The times are simulated.
32 devices in a mesh: section: 2 (over core), fsdp: 4 (over y, x), rep: 4 (over z).
Axes of the slice: x: 2, y: 2, z: 4, core: 2. Of those that a mesh axis runs over, the one named last changes fastest.
Arguments:
- inputs: bfloat16 [64, 256, 384], P(('fsdp', 'rep')), may hold values from -6 to 6
- conditioning: bfloat16 [64, 384], P(('fsdp', 'rep')), may hold values from -6 to 6
- cotangent: bfloat16 [64, 256, 384], P(('fsdp', 'rep')), may hold values from -6 to 6
- micro_sizes: int32 [16, 2], P(('fsdp', 'rep')), may hold values from 1 to 2, as said below
- relative_bias_index: int32 [256, 256], replicated, may hold values from 0 to 960
- w_ada: bfloat16 [2, 384, 2304], P('section', 'fsdp'), may hold values from -0.3125 to 0.3125
- w_qkv: bfloat16 [2, 384, 1152], P('section', 'fsdp'), may hold values from -0.3125 to 0.3125
- w_proj: bfloat16 [2, 384, 384], P('section', 'fsdp'), may hold values from -1.25 to 1.25
- w_fc1: bfloat16 [2, 384, 1536], P('section', 'fsdp'), may hold values from -0.3125 to 0.3125
- w_fc2: bfloat16 [2, 1536, 384], P('section', 'fsdp'), may hold values from -0.15625 to 0.15625
- b_ada: bfloat16 [2, 2304], P('section', 'fsdp'), may hold values from -3 to 3
- b_qv: bfloat16 [2, 768], P('section', 'fsdp'), may hold values from -3 to 3
- b_proj: bfloat16 [2, 384], P('section', 'fsdp'), may hold values from -3 to 3
- b_fc1: bfloat16 [2, 1536], P('section', 'fsdp'), may hold values from -3 to 3
- b_fc2: bfloat16 [2, 384], P('section', 'fsdp'), may hold values from -3 to 3
- bias_table: bfloat16 [2, 6, 961], P('section'), may hold values from -5 to 5
Outputs:
- activations: bfloat16 [2, 64, 256, 384], P('section', ('fsdp', 'rep'))
- input_grads: float32 [2, 64, 256, 384], P('section', ('fsdp', 'rep'))
- cond_grad: float32 [64, 384], P(('fsdp', 'rep'))
- g_w_ada: float32 [2, 384, 2304], P('section', 'fsdp')
- g_w_qkv: float32 [2, 384, 1152], P('section', 'fsdp')
- g_w_proj: float32 [2, 384, 384], P('section', 'fsdp')
- g_w_fc1: float32 [2, 384, 1536], P('section', 'fsdp')
- g_w_fc2: float32 [2, 1536, 384], P('section', 'fsdp')
- g_b_ada: float32 [2, 2304], P('section', 'fsdp')
- g_b_qv: float32 [2, 768], P('section', 'fsdp')
- g_b_proj: float32 [2, 384], P('section', 'fsdp')
- g_b_fc1: float32 [2, 1536], P('section', 'fsdp')
- g_b_fc2: float32 [2, 384], P('section', 'fsdp')
- g_table: float32 [2, 6, 961], P('section')
Inputs may be any that keep to these rules, and one draw needn't show every extreme that they name: Only the first micro_sizes[g, m] of the 2 slots of micro-batch m of group g hold live samples; some micro-batch is full in every draw.
All inputs are finite; a program needn't handle non-finite values.
Results may differ from a plain program's by a relative error of at most 0.035.
Values may be sent and summed in bfloat16 or wider, within the bound.
No kernel may reach another device: no remote copies, remote signals or barrier semaphores. Data moves between devices by JAX's collectives and lax.ppermute only.
A program may use at most 128 MiB of HBM per device.

v0:
```python
import math

import jax
import jax.numpy as jnp
from jax import lax
from jax.sharding import PartitionSpec as P

EPSILON = 1e-06
PRECISE = lax.Precision.HIGHEST


def for_sending(x):
    return jax.tree.map(lambda a: a.astype(jnp.bfloat16) if a.dtype == jnp.float32 else a, x)


def from_behind(value, axis, steps):
    count = lax.axis_size(axis)
    first, last = (max(0, -steps), min(count, count - steps))
    return lax.ppermute(value, axis, [(source, source + steps) for source in range(first, last)])


def norm_rows(v):
    centre = v - jnp.mean(v, axis=-1, keepdims=True)
    spread = jnp.mean(centre * centre, axis=-1, keepdims=True)
    return centre * lax.rsqrt(spread + EPSILON)


def modulate(v, scale_part, shift_part):
    return norm_rows(v) * (1.0 + scale_part) + shift_part


def gelu_tanh(v):
    return 0.5 * v * (1.0 + jnp.tanh(0.7978845608028654 * (v + 0.044715 * v * v * v)))


def outer_sum(left, right):
    return lax.dot_general(
        left, right, (((0,), (0,)), ((), ())), preferred_element_type=jnp.float32
    )


def through(left, right):
    return lax.dot_general(
        left, right, (((1,), (1,)), ((), ())), preferred_element_type=jnp.float32
    )


def column_sums(values):
    return jnp.sum(values.astype(jnp.float32), axis=0)


def index_blocks(relative_bias_index):
    length = relative_bias_index.shape[0]
    block_rows = math.gcd(length, max(1, 4096 // length))
    block_count = length // block_rows
    return relative_bias_index.reshape(block_count, block_rows * length)


def table_lookup(table_one, relative_bias_index):
    length = relative_bias_index.shape[0]
    head_count, rel_count = table_one.shape
    blocks = index_blocks(relative_bias_index)
    entries = jnp.arange(rel_count, dtype=jnp.int32)

    def lookup_block(index_row):
        selector = (entries[:, None] == index_row[None, :]).astype(jnp.float32)
        return jnp.dot(table_one, selector, precision=PRECISE)

    looked = lax.map(lookup_block, blocks)
    return jnp.transpose(looked, (1, 0, 2)).reshape(head_count, length, length)


def table_gradient(score_total, relative_bias_index, rel_count):
    head_count = score_total.shape[0]
    blocks = index_blocks(relative_bias_index)
    block_count, block_width = blocks.shape
    score_blocks = jnp.transpose(
        score_total.reshape(head_count, block_count, block_width), (1, 0, 2)
    )
    entries = jnp.arange(rel_count, dtype=jnp.int32)

    def add_block(total, block_data):
        index_row, score_row = block_data
        selector = (index_row[:, None] == entries[None, :]).astype(jnp.float32)
        return (total + jnp.dot(score_row, selector, precision=PRECISE), None)

    start = jnp.zeros((head_count, rel_count), jnp.float32)
    total, unused = lax.scan(add_block, start, (blocks, score_blocks))
    return total


def layer_weights(shards):
    gathered = jax.tree.map(
        lambda part, own: part.astype(own.dtype),
        lax.all_gather(for_sending(shards), "fsdp", axis=1, tiled=True),
        shards,
    )
    return tuple((p[0] for p in gathered))


def forward(layer_input_rows, cond_block, weights, bias_heads):
    w_ada, w_qkv, w_proj, w_fc1, w_fc2, b_ada, b_qv, b_proj, b_fc1, b_fc2 = weights
    batch_size, length, model_width = layer_input_rows.shape
    head_count = bias_heads.shape[0]
    head_dim = model_width // head_count
    row_count = batch_size * length
    score_scale = head_dim ** (-0.5)
    cond_act = jax.nn.silu(cond_block).astype(jnp.bfloat16)
    modulation = jnp.dot(cond_act, w_ada, preferred_element_type=jnp.float32) + b_ada.astype(
        jnp.float32
    )
    pieces = [modulation[:, None, i * model_width : (i + 1) * model_width] for i in range(6)]
    normed_one = (
        modulate(layer_input_rows, pieces[1], pieces[0])
        .astype(jnp.bfloat16)
        .reshape(row_count, model_width)
    )
    projected = jnp.dot(normed_one, w_qkv, preferred_element_type=jnp.float32)
    bias_float = b_qv.astype(jnp.float32)
    head_shape = (batch_size, length, head_count, head_dim)
    queries = (
        (projected[:, :model_width] + bias_float[:model_width])
        .astype(jnp.bfloat16)
        .reshape(head_shape)
    )
    key_heads = projected[:, model_width : 2 * model_width].astype(jnp.bfloat16).reshape(head_shape)
    value_heads = (
        (projected[:, 2 * model_width :] + bias_float[model_width:])
        .astype(jnp.bfloat16)
        .reshape(head_shape)
    )
    scores = (
        jnp.einsum("bqhe,bkhe->bhqk", queries, key_heads, preferred_element_type=jnp.float32)
        * score_scale
    )
    scores = scores + bias_heads[None]
    probs = jax.nn.softmax(scores, axis=-1)
    probs_low = probs.astype(jnp.bfloat16)
    attended = jnp.einsum(
        "bhqk,bkhe->bqhe", probs_low, value_heads, preferred_element_type=jnp.float32
    )
    attended = attended.reshape(row_count, model_width).astype(jnp.bfloat16)
    branch = jnp.dot(attended, w_proj, preferred_element_type=jnp.float32) + b_proj.astype(
        jnp.float32
    )
    branch = branch.reshape(batch_size, length, model_width)
    middle = layer_input_rows + pieces[2] * branch
    normed_two = (
        modulate(middle, pieces[4], pieces[3]).astype(jnp.bfloat16).reshape(row_count, model_width)
    )
    hidden_pre = jnp.dot(normed_two, w_fc1, preferred_element_type=jnp.float32) + b_fc1.astype(
        jnp.float32
    )
    hidden_act = gelu_tanh(hidden_pre).astype(jnp.bfloat16)
    out_branch = jnp.dot(hidden_act, w_fc2, preferred_element_type=jnp.float32) + b_fc2.astype(
        jnp.float32
    )
    out_branch = out_branch.reshape(batch_size, length, model_width)
    layer_out = middle + pieces[5] * out_branch
    saved = (
        cond_act,
        pieces,
        normed_one,
        queries,
        key_heads,
        value_heads,
        probs,
        probs_low,
        attended,
        branch,
        middle,
        normed_two,
        hidden_pre,
        hidden_act,
        out_branch,
    )
    return (layer_out, saved)


def backward(
    layer_input_rows, cond_block, weights, bias_heads, relative_bias_index, rel_count, grad_out
):
    w_ada, w_qkv, w_proj, w_fc1, w_fc2 = weights[:5]
    layer_out, saved = forward(layer_input_rows, cond_block, weights, bias_heads)
    (
        cond_act,
        pieces,
        normed_one,
        queries,
        key_heads,
        value_heads,
        probs,
        probs_low,
        attended,
        branch,
        middle,
        normed_two,
        hidden_pre,
        hidden_act,
        out_branch,
    ) = saved
    batch_size, length, model_width = layer_input_rows.shape
    head_count = bias_heads.shape[0]
    head_dim = model_width // head_count
    row_count = batch_size * length
    score_scale = head_dim ** (-0.5)
    grad_gate_two = jnp.sum(grad_out * out_branch, axis=1)
    grad_outb = (grad_out * pieces[5]).astype(jnp.bfloat16).reshape(row_count, model_width)
    g_fc2 = outer_sum(hidden_act, grad_outb)
    g_bfc2 = column_sums(grad_outb)
    grad_act = through(grad_outb, w_fc2)
    grad_pre = jax.vjp(gelu_tanh, hidden_pre)[1](grad_act)[0].astype(jnp.bfloat16)
    g_fc1 = outer_sum(normed_two, grad_pre)
    g_bfc1 = column_sums(grad_pre)
    grad_normed_two = through(grad_pre, w_fc1).reshape(batch_size, length, model_width)
    grad_middle, grad_scale_two, grad_shift_two = jax.vjp(modulate, middle, pieces[4], pieces[3])[
        1
    ](grad_normed_two)
    grad_middle = grad_middle + grad_out
    grad_gate_one = jnp.sum(grad_middle * branch, axis=1)
    grad_branch = (grad_middle * pieces[2]).astype(jnp.bfloat16).reshape(row_count, model_width)
    g_proj = outer_sum(attended, grad_branch)
    g_bproj = column_sums(grad_branch)
    grad_att = (
        through(grad_branch, w_proj)
        .astype(jnp.bfloat16)
        .reshape(batch_size, length, head_count, head_dim)
    )
    grad_probs = jnp.einsum(
        "bqhe,bkhe->bhqk", grad_att, value_heads, preferred_element_type=jnp.float32
    )
    grad_values = jnp.einsum(
        "bhqk,bqhe->bkhe", probs_low, grad_att, preferred_element_type=jnp.float32
    )
    grad_values = grad_values.astype(jnp.bfloat16).reshape(row_count, model_width)
    grad_scores = probs * (grad_probs - jnp.sum(grad_probs * probs, axis=-1, keepdims=True))
    grad_scores = grad_scores.astype(jnp.bfloat16)
    grad_queries = jnp.einsum(
        "bhqk,bkhe->bqhe", grad_scores, key_heads, preferred_element_type=jnp.float32
    )
    grad_queries = (grad_queries * score_scale).astype(jnp.bfloat16).reshape(row_count, model_width)
    grad_keys = jnp.einsum(
        "bhqk,bqhe->bkhe", grad_scores, queries, preferred_element_type=jnp.float32
    )
    grad_keys = (grad_keys * score_scale).astype(jnp.bfloat16).reshape(row_count, model_width)
    score_total = jnp.sum(grad_scores.astype(jnp.float32), axis=0).reshape(
        head_count, length * length
    )
    g_table = table_gradient(score_total, relative_bias_index, rel_count)
    grad_qkv = jnp.concatenate([grad_queries, grad_keys, grad_values], axis=1)
    g_qkv = outer_sum(normed_one, grad_qkv)
    g_bqv = jnp.concatenate([column_sums(grad_queries), column_sums(grad_values)])
    grad_normed_one = through(grad_qkv, w_qkv).reshape(batch_size, length, model_width)
    grad_in, grad_scale_one, grad_shift_one = jax.vjp(
        modulate, layer_input_rows, pieces[1], pieces[0]
    )[1](grad_normed_one)
    grad_in = grad_in + grad_middle
    grad_mod = jnp.concatenate(
        [
            grad_shift_one[:, 0],
            grad_scale_one[:, 0],
            grad_gate_one,
            grad_shift_two[:, 0],
            grad_scale_two[:, 0],
            grad_gate_two,
        ],
        axis=1,
    )
    grad_mod = grad_mod.astype(jnp.bfloat16)
    g_ada = outer_sum(cond_act, grad_mod)
    g_bada = column_sums(grad_mod)
    grad_silu = through(grad_mod, w_ada)
    grad_cond = jax.vjp(jax.nn.silu, cond_block)[1](grad_silu)[0]
    layer_grads = (
        g_ada,
        g_qkv,
        g_proj,
        g_fc1,
        g_fc2,
        g_bada,
        g_bqv,
        g_bproj,
        g_bfc1,
        g_bfc2,
        g_table,
    )
    return (grad_in, grad_cond, layer_grads)


def add_tuples(first_tuple, second_tuple):
    if first_tuple is None:
        return second_tuple
    return tuple((a + b for a, b in zip(first_tuple, second_tuple)))


def per_device(
    inputs,
    conditioning,
    cotangent,
    micro_sizes,
    relative_bias_index,
    w_ada,
    w_qkv,
    w_proj,
    w_fc1,
    w_fc2,
    b_ada,
    b_qv,
    b_proj,
    b_fc1,
    b_fc2,
    bias_table,
):
    section_index = lax.axis_index("section")
    is_first = section_index == 0
    micro_count = micro_sizes.shape[1]
    sample_count, length, model_width = inputs.shape
    capacity = sample_count // micro_count
    shards = (w_ada, w_qkv, w_proj, w_fc1, w_fc2, b_ada, b_qv, b_proj, b_fc1, b_fc2)
    table_one = bias_table[0].astype(jnp.float32)
    rel_count = table_one.shape[1]
    bias_heads = table_lookup(table_one, relative_bias_index)
    slot_index = jnp.arange(sample_count)
    slot_micro = slot_index // capacity
    slot_sizes = jnp.sum(
        jnp.where(
            slot_micro[:, None] == jnp.arange(micro_count)[None, :], micro_sizes[0][None, :], 0
        ),
        axis=1,
    )
    live_mask = (
        (slot_index % capacity < slot_sizes).astype(jnp.float32).reshape(micro_count, capacity)
    )
    input_blocks = inputs.reshape(micro_count, capacity, length, model_width)
    cond_blocks = conditioning.astype(jnp.float32).reshape(micro_count, capacity, model_width)
    grad_blocks = cotangent.reshape(micro_count, capacity, length, model_width)
    received = jnp.zeros((capacity, length, model_width), jnp.bfloat16)
    section_inputs = []
    forward_outs = []
    for moment in range(micro_count + 1):
        weights = layer_weights(shards)
        latest = min(moment, micro_count - 1)
        former = max(moment - 1, 0)
        own_input = input_blocks[latest].astype(jnp.float32)
        layer_input_rows = jnp.where(is_first, own_input, received.astype(jnp.float32))
        cond_here = jnp.where(is_first, cond_blocks[latest], cond_blocks[former])
        layer_out, unused = forward(layer_input_rows, cond_here, weights, bias_heads)
        section_inputs.append(layer_input_rows)
        forward_outs.append(layer_out)
        if moment < micro_count:
            received = from_behind(layer_out.astype(jnp.bfloat16), "section", 1)
    kept_inputs = [
        jnp.where(is_first, section_inputs[m], section_inputs[m + 1]) for m in range(micro_count)
    ]
    act_blocks = [
        jnp.where(is_first, forward_outs[m], forward_outs[m + 1]) for m in range(micro_count)
    ]
    back_received = jnp.zeros((capacity, length, model_width), jnp.bfloat16)
    grad_total = None
    input_parts = []
    cond_parts = []
    for moment in range(micro_count + 1):
        weights = layer_weights(shards)
        latest = min(moment, micro_count - 1)
        former = max(moment - 1, 0)
        layer_input_rows = jnp.where(is_first, kept_inputs[former], kept_inputs[latest])
        cond_here = jnp.where(is_first, cond_blocks[former], cond_blocks[latest])
        valid_last = 1.0 if moment < micro_count else 0.0
        grad_here = (
            grad_blocks[latest].astype(jnp.float32) * live_mask[latest][:, None, None] * valid_last
        )
        grad_out = jnp.where(is_first, back_received.astype(jnp.float32), grad_here)
        grad_in, grad_cond, layer_grads = backward(
            layer_input_rows,
            cond_here,
            weights,
            bias_heads,
            relative_bias_index,
            rel_count,
            grad_out,
        )
        grad_total = add_tuples(grad_total, layer_grads)
        grad_low = grad_in.astype(jnp.bfloat16)
        input_parts.append(jnp.where(is_first, grad_in, grad_low.astype(jnp.float32)))
        cond_parts.append(grad_cond)
        if moment < micro_count:
            back_received = from_behind(grad_low, "section", -1)
    input_grads = jnp.concatenate(
        [jnp.where(is_first, input_parts[m + 1], input_parts[m]) for m in range(micro_count)],
        axis=0,
    )[None]
    cond_local = jnp.concatenate(
        [jnp.where(is_first, cond_parts[m + 1], cond_parts[m]) for m in range(micro_count)], axis=0
    )
    cond_grad = lax.psum(cond_local, "section")
    activations = jnp.concatenate(act_blocks, axis=0).astype(jnp.bfloat16)[None]
    full_grads = tuple((g[None] for g in grad_total[:10]))
    shard_grads = jax.tree.map(
        lambda part: part.astype(jnp.float32),
        lax.psum_scatter(for_sending(full_grads), "fsdp", scatter_dimension=1, tiled=True),
    )
    table_local = grad_total[10]
    shard_grads = jax.tree.map(
        lambda part: part.astype(jnp.float32), lax.psum(for_sending(shard_grads), "rep")
    )
    table_grad = lax.psum(table_local[None], ("fsdp", "rep"))
    return (
        activations,
        input_grads,
        cond_grad,
        shard_grads[0],
        shard_grads[1],
        shard_grads[2],
        shard_grads[3],
        shard_grads[4],
        shard_grads[5],
        shard_grads[6],
        shard_grads[7],
        shard_grads[8],
        shard_grads[9],
        table_grad,
    )


def solution(mesh):
    placed = (
        P(("fsdp", "rep"), None, None),
        P(("fsdp", "rep"), None),
        P(("fsdp", "rep"), None, None),
        P(("fsdp", "rep"), None),
        P(),
        P("section", "fsdp", None),
        P("section", "fsdp", None),
        P("section", "fsdp", None),
        P("section", "fsdp", None),
        P("section", "fsdp", None),
        P("section", "fsdp"),
        P("section", "fsdp"),
        P("section", "fsdp"),
        P("section", "fsdp"),
        P("section", "fsdp"),
        P("section", None, None),
    )
    return jax.shard_map(
        per_device,
        mesh=mesh,
        in_specs=placed,
        out_specs=(
            P("section", ("fsdp", "rep"), None, None),
            P("section", ("fsdp", "rep"), None, None),
            P(("fsdp", "rep"), None),
            P("section", "fsdp", None),
            P("section", "fsdp", None),
            P("section", "fsdp", None),
            P("section", "fsdp", None),
            P("section", "fsdp", None),
            P("section", "fsdp"),
            P("section", "fsdp"),
            P("section", "fsdp"),
            P("section", "fsdp"),
            P("section", "fsdp"),
            P("section", None, None),
        ),
        check_vma=False,
    )
```

profile of v0, /device:TPU:0, one launch (start us, length us, event | category | flops | bytes accessed | tf_op | source)
XLA Modules:
  0.0 1031.4 jit_solution(6121093093613506303)
XLA Ops:
  16.8 18.2 %all-reduce.6 = (bf16[2304]{0:T(1024)(128)(2,1)S(1)}, bf16[768]{0:T(1024)(128)(2,1)S(1)}, bf16[384]{0:T(512)(128)(2,1)S(1)}, bf16[384]{0:T(512)(128)(2,1)}) all-reduce(bf16[2304]{0:T(1024)(128)(2,1)S(1)} %dynamic-update-slice, bf16[768]{0:T(1024)(128)(2,1)S(1)} %dynamic-update-slice.1, ...), channel_id=1, replica_groups=mesh['section'=2,'fsdp'=4,'rep'=4] {'fsdp'}, use_global_device_ids=true, to_apply=%add | all-reduce | flops 3840 | bytes 15360
  39.3 13.2 %all_gather.22 = bf16[1,384,1152]{2,1,0:T(8,128)(2,1)S(1)} all-gather(bf16[1,96,1152]{2,1,0:T(8,128)(2,1)} %param.30), channel_id=1, replica_groups=mesh['section'=2,'fsdp'=4,'rep'=4] {'fsdp'}, dimensions={1}, use_global_device_ids=true | all-gather | bytes 1105920 | tf_op jit(solution)/shard_map/all_gather | solution.py:95
  53.1 91.6 %while.44 = (s32[]{:T(128)}, f32[16,6,4096]{2,1,0:T(8,128)}, s32[16,4096]{1,0:T(8,128)S(1)}, f32[6,961]{1,0:T(8,128)S(1)}, s32[]{:T(128)}) while((s32[]{:T(128)}, f32[16,6,4096]{2,1,0:T(8,128)}, s32[16,4096]{1,0:T(8,128)S(1)}, f32[6,961]{1,0:T(8,128)S(1)}, s32[]{:T(128)}) %tuple.199), condition=%wide.region_3.4_spmd.clone, body=%wide.region_2.3_spmd.clone.sunk | while | flops 287346688 | bytes 203365 | solution.py:69
  64.6 5.7 fusion.424
  93.2 5.7 fusion.424
  104.7 5.7 fusion.424
  110.4 5.7 fusion.424
  139.0 5.7 fusion.424
  151.3 9.3 all_gather.24
  161.9 7.9 all_gather.27
  386.3 154.0 %while.45 = (s32[]{:T(128)}, f32[6,961]{1,0:T(8,128)}, f32[16,6,4096]{2,0,1:T(8,128)}, s32[16,4096]{1,0:T(8,128)}, s32[]{:T(128)}, /*index=5*/s32[]{:T(128)}) while((s32[]{:T(128)}, f32[6,961]{1,0:T(8,128)}, f32[16,6,4096]{2,0,1:T(8,128)}, s32[16,4096]{1,0:T(8,128)}, s32[]{:T(128)}, /*index=5*/s32[]{:T(128)}) %tuple.243), condition=%wide.region_113.114_spmd.clone, body=%wide.region_112.113_spmd.clone.sunk | while | flops 287358208 | bytes 390287 | solution.py:88
  389.2 6.8 fusion.425
  398.8 6.8 fusion.425
  408.4 6.8 fusion.425
  418.0 6.8 fusion.425
  427.6 6.8 fusion.425
  437.2 6.8 fusion.425
  446.8 6.8 fusion.425
  456.4 6.8 fusion.425
  466.1 6.8 fusion.425
  475.7 6.8 fusion.425
  485.3 6.8 fusion.425
  494.9 6.8 fusion.425
  504.5 6.8 fusion.425
  514.1 6.8 fusion.425
  523.7 6.8 fusion.425
  533.3 6.8 fusion.425
  642.5 5.7 convolution_add_fusion.15
  664.3 119.6 %while.46 = (s32[]{:T(128)}, f32[6,961]{1,0:T(8,128)S(1)}, f32[16,6,4096]{2,0,1:T(8,128)}, s32[16,4096]{1,0:T(8,128)}, s32[]{:T(128)}, /*index=5*/s32[]{:T(128)}) while((s32[]{:T(128)}, f32[6,961]{1,0:T(8,128)S(1)}, f32[16,6,4096]{2,0,1:T(8,128)}, s32[16,4096]{1,0:T(8,128)}, s32[]{:T(128)}, /*index=5*/s32[]{:T(128)}) %tuple.247), condition=%wide.region_116.117_spmd.clone, body=%wide.region_115.116_spmd.clone.sunk | while | flops 287358208 | bytes 390287 | solution.py:88
  794.7 119.6 %while.47 = (s32[]{:T(128)}, f32[6,961]{1,0:T(8,128)S(1)}, f32[16,6,4096]{2,0,1:T(8,128)}, s32[16,4096]{1,0:T(8,128)}, s32[]{:T(128)}, /*index=5*/s32[]{:T(128)}) while((s32[]{:T(128)}, f32[6,961]{1,0:T(8,128)S(1)}, f32[16,6,4096]{2,0,1:T(8,128)}, s32[16,4096]{1,0:T(8,128)}, s32[]{:T(128)}, /*index=5*/s32[]{:T(128)}) %tuple.246), condition=%wide.region_119.120_spmd.clone, body=%wide.region_118.119_spmd.clone.sunk | while | flops 287358208 | bytes 390287 | solution.py:88
  920.9 78.4 %psum.95 = f32[1,6,961]{2,0,1:T(1,128)} all-reduce(f32[1,6,961]{2,0,1:T(1,128)S(1)} %broadcast_in_dim.67), channel_id=1, replica_groups=mesh['section'=2,'fsdp'=4,'rep'=4] {'fsdp','rep'}, use_global_device_ids=true, to_apply=%region_120.121 | all-reduce | flops 5766 | bytes 46128 | tf_op jit(solution)/shard_map/psum | solution.py:406
  1005.1 8.5 all-reduce.4
  (1090 shorter events, 731.9 us)
Async XLA Ops:
  7.2 165.2 %all-gather.4.cloned.1.call-start = ((), (), s32[]{:S(2)}) async-start(), calls=%async_computation.10 | async-start | bytes 2211840 | tf_op jit(solution)/shard_map/all_gather | solution.py:95
  7.9 194.4 %all-gather.8.cloned.1.call-start = ((), (), s32[]{:S(2)}) async-start(), calls=%async_computation.12 | async-start | bytes 1474560 | tf_op jit(solution)/shard_map/all_gather | solution.py:95
  8.7 193.7 %all-gather.6.cloned.1.call-start = ((), (), s32[]{:S(2)}) async-start(), calls=%async_computation.11 | async-start | bytes 1474560 | tf_op jit(solution)/shard_map/all_gather | solution.py:95
  9.4 904.9 %reduce-scatter.25.cloned.1.call-start = ((), (), s32[]{:S(2)}) async-start(), calls=%async_computation.15 | async-start | bytes 368640 | tf_op jit(solution)/shard_map/reduce_scatter | solution.py:400
  36.3 178.3 %copy-start.113 = (f32[4,384]{1,0:T(4,128)}, f32[4,384]{1,0:T(4,128)S(1)}, u32[]{:S(2)}) copy-start(f32[4,384]{1,0:T(4,128)S(1)} %convert_element_type.648) | copy-start | bytes 18436
  210.1 5.4 collective-permute-start
  247.7 2.6 collective-permute-start.1
  363.6 196.1 %collective-permute-start.2 = (bf16[2,256,384]{2,1,0:T(8,128)(2,1)}, bf16[2,256,384]{2,1,0:T(8,128)(2,1)}, u32[]{:S(2)}, u32[]{:S(2)}) collective-permute-start(bf16[2,256,384]{2,1,0:T(8,128)(2,1)} %get-tuple-element.350), channel_id=1, source_target_pairs={{16,0},{17,1},{18,2},{19,3},{20,4},{21,5},{22,6},{23,7},{24,8},{25... | collective-permute-start | bytes 1179656 | tf_op jit(solution)/shard_map/ppermute | solution.py:19
  386.3 154.0 %copy-start.11 = (f32[2,256,384]{2,1,0:T(8,128)S(1)}, f32[2,256,384]{2,1,0:T(8,128)}, u32[]{:S(2)}) copy-start(f32[2,256,384]{2,1,0:T(8,128)} %get-tuple-element.316) | copy-start | bytes 2359300
  590.0 6.3 collective-permute-start.3
  616.6 297.8 %reduce-scatter.23.cloned.1.call-start = ((), (), s32[]{:S(2)}) async-start(), calls=%async_computation.14 | async-start | bytes 1105920 | tf_op jit(solution)/shard_map/reduce_scatter | solution.py:400
  626.2 288.2 %reduce-scatter.27.cloned.1.call-start = ((), (), s32[]{:S(2)}) async-start(), calls=%async_computation.16 | async-start | bytes 1474560 | tf_op jit(solution)/shard_map/reduce_scatter | solution.py:400
  637.4 277.0 %reduce-scatter.29.cloned.1.call-start = ((), (), s32[]{:S(2)}) async-start(), calls=%async_computation.17 | async-start | bytes 1474560 | tf_op jit(solution)/shard_map/reduce_scatter | solution.py:400
  657.8 256.6 %reduce-scatter.21.cloned.1.call-start = ((), (), s32[]{:S(2)}) async-start(), calls=%async_computation.13 | async-start | bytes 2211840 | tf_op jit(solution)/shard_map/reduce_scatter | solution.py:400
  663.9 336.7 %reduce-scatter.35.cloned.1.call-start = ((), (), s32[]{:S(2)}) async-start(), calls=%async_computation.20 | async-start | bytes 122880
  664.2 119.8 %copy-start.203 = (f32[6,64]{1,0:T(8,128)S(1)}, f32[6,64]{1,0:T(8,128)}, u32[]{:S(2)}) copy-start(f32[6,64]{1,0:T(8,128)} %get-tuple-element.433) | copy-start | bytes 4612
  664.2 119.9 %copy-start.216 = (f32[384]{0:T(512)S(1)}, f32[384]{0:T(512)}, u32[]{:S(2)}) copy-start(f32[384]{0:T(512)} %get-tuple-element.304) | copy-start | bytes 4612
  664.2 119.9 %copy-start.218 = (f32[384]{0:T(512)S(1)}, f32[384]{0:T(512)}, u32[]{:S(2)}) copy-start(f32[384]{0:T(512)} %get-tuple-element.310) | copy-start | bytes 4612
  664.2 119.9 %copy-start.231 = (f32[384]{0:T(512)S(1)}, f32[384]{0:T(512)}, u32[]{:S(2)}) copy-start(f32[384]{0:T(512)} %get-tuple-element.307) | copy-start | bytes 4612
  664.2 120.7 %copy-start.215 = (f32[384]{0:T(512)S(1)}, f32[384]{0:T(512)}, u32[]{:S(2)}) copy-start(f32[384]{0:T(512)} %get-tuple-element.298) | copy-start | bytes 4612
  664.2 120.7 %copy-start.217 = (f32[384]{0:T(512)S(1)}, f32[384]{0:T(512)}, u32[]{:S(2)}) copy-start(f32[384]{0:T(512)} %get-tuple-element.346) | copy-start | bytes 4612
  664.2 120.7 %copy-start.230 = (f32[384]{0:T(512)S(1)}, f32[384]{0:T(512)}, u32[]{:S(2)}) copy-start(f32[384]{0:T(512)} %get-tuple-element.300) | copy-start | bytes 4612
  664.3 121.5 %copy-start.225 = (f32[1536]{0:T(1024)S(1)}, f32[1536]{0:T(1024)}, u32[]{:S(2)}) copy-start(f32[1536]{0:T(1024)} %get-tuple-element.441) | copy-start | bytes 18436
  664.3 121.5 %copy-start.226 = (f32[1536]{0:T(1024)S(1)}, f32[1536]{0:T(1024)}, u32[]{:S(2)}) copy-start(f32[1536]{0:T(1024)} %get-tuple-element.443) | copy-start | bytes 18436
  664.3 121.4 %copy-start.227 = (f32[1536]{0:T(1024)S(1)}, f32[1536]{0:T(1024)}, u32[]{:S(2)}) copy-start(f32[1536]{0:T(1024)} %get-tuple-element.439) | copy-start | bytes 18436
  664.3 122.6 %copy-start.247 = (f32[6,64]{1,0:T(8,128)S(1)}, f32[6,64]{1,0:T(8,128)}, u32[]{:S(2)}) copy-start(f32[6,64]{1,0:T(8,128)} %get-tuple-element.427) | copy-start | bytes 4612
  786.8 214.6 %reduce-scatter.39.cloned.1.call-start = ((), (), s32[]{:S(2)}) async-start(), calls=%async_computation.22 | async-start | bytes 122880
  787.4 214.8 %reduce-scatter.33.cloned.1.call-start = ((), (), s32[]{:S(2)}) async-start(), calls=%async_computation.19 | async-start | bytes 245760
  788.3 214.7 %reduce-scatter.37.cloned.1.call-start = ((), (), s32[]{:S(2)}) async-start(), calls=%async_computation.21 | async-start | bytes 491520
  788.9 215.2 %reduce-scatter.31.cloned.1.call-start = ((), (), s32[]{:S(2)}) async-start(), calls=%async_computation.18 | async-start | bytes 737280
  794.3 222.0 %all-reduce.9.cloned.1.call-start = ((), (), s32[]{:S(2)}) async-start(), calls=%async_computation.23 | async-start | bytes 2654208 | tf_op jit(solution)/shard_map/psum | solution.py:404
  794.7 119.8 %copy-start.1 = (bf16[1,384,2304]{2,1,0:T(8,128)(2,1)S(1)}, bf16[1,384,2304]{2,1,0:T(8,128)(2,1)}, u32[]{:S(2)}) copy-start(bf16[1,384,2304]{2,1,0:T(8,128)(2,1)} %all-gather.4.cloned.1.call-done) | copy-start | bytes 5308420
  (246 other events, 1314.6 us)
Sparse Core Ops, SparseCore 0:
  9.9 38.5 all-gather.3
  50.3 28.1 all-gather.7
  80.3 27.7 all-gather.5
  616.7 25.6 reduce-scatter.24
  645.7 26.6 reduce-scatter.22
  675.2 28.5 reduce-scatter.26
  706.7 28.5 reduce-scatter.28
  738.3 32.4 reduce-scatter.20
  786.9 25.1 reduce-scatter.34
  814.9 23.8 reduce-scatter.38
  842.1 24.0 reduce-scatter.32
  869.4 24.4 reduce-scatter.36
  897.3 25.2 reduce-scatter.30
  925.3 64.7 all-reduce.8
where the time goes:
time: 1040 us; the launch traced here: 1030 us
  matrix products  499 us (48%)
  local copies, waits for them, and re-layouts  258 us (25%)
  blocking collectives  140 us (13%)
  other arithmetic  104 us (10%)
  between operations  19.6 us (2%)
    dot_general x48, matrix products, add_block(): return (total + jnp.dot(score_row, selector, precision=PRECISE), None)  280 us
    dot_general x16, matrix products, lookup_block(): return jnp.dot(table_one, selector, precision=PRECISE)  91.3 us
    psum x1, blocking collectives, per_device(): table_grad = lax.psum(table_local[None], ('fsdp', 'rep'))  78.4 us
    dynamic_slice x48, local copies, waits for them, and re-layouts, table_gradient(): total, unused = lax.scan(add_block, start, (blocks, score_blocks))  68.6 us
    dynamic_slice x64, local copies, waits for them, and re-layouts, table_lookup(): looked = lax.map(lookup_block, blocks)  44.7 us
    unnamed x573, local copies, waits for them, and re-layouts  38.4 us
    all_gather x3, blocking collectives, layer_weights(): lax.all_gather(for_sending(shards), 'fsdp', axis=1, tiled=True)  30.4 us
    dot_general x15, matrix products, outer_sum(): lax.dot_general(left, right, (((0,), (0,)), ((), ())), preferred_element_...  28.6 us
  transfers between devices with their start and end apart: 18, of which 1 were waited for; matrix products, arithmetic and copies ran while one was open for 62% of the time, Pallas kernels for 0%

commit v1 on v0

v1 whole, which is shorter than its diff:
```python
import functools

import jax
import jax.numpy as jnp
from jax import lax
from jax.experimental import pallas as pl
from jax.experimental.pallas import tpu as pltpu
from jax.sharding import PartitionSpec as P

EPSILON = 1e-06
F32 = jnp.float32
BF16 = jnp.bfloat16
VMEM_BYTES = 58 * 1024 * 1024
LOW = 32


def dot(a, b):
    return jnp.dot(a, b, preferred_element_type=F32)


def dot_rows(a, b):
    return lax.dot_general(a, b, (((1,), (1,)), ((), ())), preferred_element_type=F32)


def dot_cols(a, b):
    return lax.dot_general(a, b, (((0,), (0,)), ((), ())), preferred_element_type=F32)


def norm_parts(v):
    centre = v - jnp.mean(v, axis=-1, keepdims=True)
    inverse = lax.rsqrt(jnp.mean(centre * centre, axis=-1, keepdims=True) + EPSILON)
    return centre * inverse, inverse


def norm_back(d_normed, scale, normed, inverse):
    d = d_normed * (1.0 + scale)
    return inverse * (
        d
        - jnp.mean(d, axis=-1, keepdims=True)
        - normed * jnp.mean(d * normed, axis=-1, keepdims=True)
    )


def col_sum(v):
    return jnp.sum(v, axis=0, keepdims=True)


def half_masks(width):
    lane = lax.broadcasted_iota(jnp.int32, (1, width), 1)
    first = jnp.where(lane < width // 2, 1.0, 0.0)
    return first.astype(BF16), (1.0 - first).astype(BF16)


def attention_copies(pack, w_qkv, w_proj, sems, first_sem, shard, pieces):
    model = w_proj.shape[0]
    q = model // pieces
    copies = []
    for p in range(pieces):
        off = pl.multiple_of((shard ^ p) * q, 16) if pieces > 1 else 0
        for c in range(4):
            source = pack.at[pl.ds((4 * p + c) * q, q), :]
            if c < 3:
                target = w_qkv.at[pl.ds(off, q), pl.ds(c * model, model)]
            else:
                target = w_proj.at[pl.ds(off, q), :]
            copies.append(
                pltpu.make_async_copy(source, target, sems.at[first_sem + len(copies)])
            )
    return copies


def mlp_copies(pack, w_fc1, w_fc2, sems, first_sem, shard, pieces):
    model = w_fc1.shape[0]
    q = model // pieces
    copies = []
    for p in range(pieces):
        off = pl.multiple_of((shard ^ p) * q, 16) if pieces > 1 else 0
        for c in range(4):
            copies.append(
                pltpu.make_async_copy(
                    pack.at[pl.ds((8 * p + c) * q, q), :],
                    w_fc1.at[pl.ds(off, q), pl.ds(c * model, model)],
                    sems.at[first_sem + len(copies)],
                )
            )
        copies.append(
            pltpu.make_async_copy(
                pack.at[pl.ds((8 * p + 4) * q, 4 * q), :],
                w_fc2.at[pl.ds(off * 4, 4 * q), :],
                sems.at[first_sem + len(copies)],
            )
        )
    return copies


def start_from(section, layer, own_copies, other_copies):
    @pl.when(section == layer)
    def _():
        for copy in own_copies:
            copy.start()

    @pl.when(section != layer)
    def _():
        for copy in other_copies:
            copy.start()


def wait_all(copies):
    for copy in copies:
        copy.wait()


def pack_attention(out_ref, g_qkv, g_proj, shard, pieces):
    model = g_proj.shape[0]
    q = model // pieces
    for p in range(pieces):
        off = pl.multiple_of((shard ^ p) * q, 16) if pieces > 1 else 0
        for c in range(3):
            out_ref[(4 * p + c) * q : (4 * p + c + 1) * q, :] = g_qkv[
                pl.ds(off, q), c * model : (c + 1) * model
            ]
        out_ref[(4 * p + 3) * q : (4 * p + 4) * q, :] = g_proj[pl.ds(off, q), :]


def pack_mlp(out_ref, g_fc1, g_fc2, shard, pieces):
    model = g_fc1.shape[0]
    q = model // pieces
    for p in range(pieces):
        off = pl.multiple_of((shard ^ p) * q, 16) if pieces > 1 else 0
        for c in range(4):
            out_ref[(8 * p + c) * q : (8 * p + c + 1) * q, :] = g_fc1[
                pl.ds(off, q), c * model : (c + 1) * model
            ]
        out_ref[(8 * p + 4) * q : (8 * p + 8) * q, :] = g_fc2[
            pl.ds(pl.multiple_of(off * 4, 16), 4 * q), :
        ]


def attention_forward(b, length, h, mod, bias, w_qkv, w_proj, b_qkv, b_proj, qkv, probs, att, branch, middle):
    model = w_proj.shape[0]
    heads = bias.shape[0]
    pair = 2 * model // heads
    rows = pl.ds(pl.multiple_of(b * length, length), length)
    masks = half_masks(pair)
    x = h[rows, :].astype(F32)
    normed, _ = norm_parts(x)
    normed_low = (normed * (1.0 + mod[b, 1:2, :]) + mod[b, 0:1, :]).astype(BF16)
    qkv[rows, :] = (dot(normed_low, w_qkv[...]) + b_qkv[...]).astype(BF16)
    for j in range(heads // 2):
        q_pair = qkv[rows, j * pair : (j + 1) * pair] * BF16((pair // 2) ** (-0.5))
        k_pair = qkv[rows, model + j * pair : model + (j + 1) * pair]
        v_pair = qkv[rows, 2 * model + j * pair : 2 * model + (j + 1) * pair]
        total = None
        for e in range(2):
            scores = dot_rows(q_pair * masks[e], k_pair) + bias[2 * j + e].astype(F32)
            raised = jnp.exp(scores - jnp.max(scores, axis=-1, keepdims=True))
            p = (raised * (1.0 / jnp.sum(raised, axis=-1, keepdims=True))).astype(BF16)
            probs[b, 2 * j + e] = p
            part = dot(p, v_pair * masks[e])
            total = part if total is None else total + part
        att[rows, j * pair : (j + 1) * pair] = total.astype(BF16)
    out = dot(att[rows, :], w_proj[...]) + b_proj[...]
    branch[rows, :] = out
    middle[rows, :] = x + mod[b, 2:3, :] * out


def mlp_forward(b, length, middle, mod, w_fc1, w_fc2, b_fc1, b_fc2, act, slope, out_branch, layer_out):
    model = w_fc1.shape[0]
    rows = pl.ds(pl.multiple_of(b * length, length), length)
    mid = middle[rows, :]
    normed, _ = norm_parts(mid)
    normed_low = (normed * (1.0 + mod[b, 4:5, :]) + mod[b, 3:4, :]).astype(BF16)
    total = b_fc2[...]
    for c in range(w_fc1.shape[1] // model):
        cols = slice(c * model, (c + 1) * model)
        v = dot(normed_low, w_fc1[:, cols]) + b_fc1[:, cols]
        square = v * v
        t = jnp.tanh(0.7978845608028654 * v * (1.0 + 0.044715 * square))
        half = 0.5 * (1.0 + t)
        a = (v * half).astype(BF16)
        act[rows, cols] = a
        slope[rows, cols] = (
            half
            + 0.5 * v * (1.0 - t * t) * (0.7978845608028654 + (3 * 0.044715 * 0.7978845608028654) * square)
        ).astype(BF16)
        total = total + dot(a, w_fc2[cols, :])
    out_branch[rows, :] = total
    layer_out[rows, :] = (mid + mod[b, 5:6, :] * total).astype(layer_out.dtype)


def mlp_backward(b, length, grad, middle, mod, w_fc1, w_fc2, act, slope, out_branch, d_middle, small, normed_low, d_pre, d_ob):
    model = w_fc1.shape[0]
    rows = pl.ds(pl.multiple_of(b * length, length), length)
    g = grad[rows, :].astype(F32)
    small[b, 2:3, :] = col_sum(g * out_branch[rows, :])
    d_out = g * mod[b, 5:6, :]
    d_out_low = d_out.astype(BF16)
    d_ob[rows, :] = d_out_low
    small[b, 3:4, :] = col_sum(d_out_low.astype(F32))
    normed, inverse = norm_parts(middle[rows, :])
    normed_low[rows, :] = (normed * (1.0 + mod[b, 4:5, :]) + mod[b, 3:4, :]).astype(BF16)
    d_normed = None
    for c in range(w_fc1.shape[1] // model):
        cols = slice(c * model, (c + 1) * model)
        d_act = dot_rows(d_out_low, w_fc2[cols, :])
        d_low = (d_act * slope[rows, cols].astype(F32)).astype(BF16)
        d_pre[rows, cols] = d_low
        small[b, 4 + c : 5 + c, :] = col_sum(d_low.astype(F32))
        part = dot_rows(d_low, w_fc1[:, cols])
        d_normed = part if d_normed is None else d_normed + part
    small[b, 0:1, :] = col_sum(d_normed)
    small[b, 1:2, :] = col_sum(d_normed * normed)
    d_middle[rows, :] = norm_back(d_normed, mod[b, 4:5, :], normed, inverse) + g


def mlp_weight_grads(normed_low, d_pre, act, d_ob, g_fc1, g_fc2):
    model = g_fc1.shape[0]
    for c in range(g_fc1.shape[1] // model):
        cols = slice(c * model, (c + 1) * model)
        g_fc1[:, cols] = dot_cols(normed_low[...], d_pre[:, cols]).astype(BF16)
        g_fc2[cols, :] = dot_cols(act[:, cols], d_ob[...]).astype(BF16)


def attention_backward(b, length, h, mod, w_qkv, w_proj, qkv, probs, att, branch, d_middle, d_in, small, score_sum, normed_low, d_qkv, d_br):
    model = w_proj.shape[0]
    heads = probs.shape[1]
    pair = 2 * model // heads
    scale = F32((pair // 2) ** (-0.5))
    rows = pl.ds(pl.multiple_of(b * length, length), length)
    masks = half_masks(pair)
    d_mid = d_middle[rows, :]
    small[b, 2:3, :] = col_sum(d_mid * branch[rows, :])
    d_branch = (d_mid * mod[b, 2:3, :]).astype(BF16)
    d_br[rows, :] = d_branch
    small[b, 5:6, :] = col_sum(d_branch.astype(F32))
    d_att = dot_rows(d_branch, w_proj[...]).astype(BF16)
    for j in range(heads // 2):
        q_pair = qkv[rows, j * pair : (j + 1) * pair]
        k_pair = qkv[rows, model + j * pair : model + (j + 1) * pair]
        v_pair = qkv[rows, 2 * model + j * pair : 2 * model + (j + 1) * pair]
        d_pair = d_att[:, j * pair : (j + 1) * pair]
        d_q = d_k = d_v = None
        for e in range(2):
            p_low = probs[b, 2 * j + e]
            p = p_low.astype(F32)
            d_here = d_pair * masks[e]
            d_p = dot_rows(d_here, v_pair)
            d_s = (p * (d_p - jnp.sum(d_p * p, axis=-1, keepdims=True))).astype(BF16)
            score_sum[2 * j + e] += d_s.astype(F32)
            v_part = dot_cols(p_low, d_here)
            q_part = dot(d_s, k_pair * masks[e])
            k_part = dot_cols(d_s, q_pair * masks[e])
            d_v = v_part if d_v is None else d_v + v_part
            d_q = q_part if d_q is None else d_q + q_part
            d_k = k_part if d_k is None else d_k + k_part
        d_qkv[rows, j * pair : (j + 1) * pair] = (d_q * scale).astype(BF16)
        d_qkv[rows, model + j * pair : model + (j + 1) * pair] = (d_k * scale).astype(BF16)
        d_qkv[rows, 2 * model + j * pair : 2 * model + (j + 1) * pair] = d_v.astype(BF16)
    small[b, 3:4, :] = col_sum(d_qkv[rows, :model].astype(F32))
    small[b, 4:5, :] = col_sum(d_qkv[rows, 2 * model :].astype(F32))
    small[b, 6:8, :] = jnp.zeros((2, model), F32)
    d_normed = dot_rows(d_qkv[rows, :], w_qkv[...])
    normed, inverse = norm_parts(h[rows, :].astype(F32))
    normed_low[rows, :] = (normed * (1.0 + mod[b, 1:2, :]) + mod[b, 0:1, :]).astype(BF16)
    small[b, 0:1, :] = col_sum(d_normed)
    small[b, 1:2, :] = col_sum(d_normed * normed)
    d_in[rows, :] = (norm_back(d_normed, mod[b, 1:2, :], normed, inverse) + d_mid).astype(d_in.dtype)


def attention_weight_grads(normed_low, d_qkv, att, d_br, g_qkv, g_proj):
    model = g_proj.shape[0]
    for c in range(3):
        cols = slice(c * model, (c + 1) * model)
        g_qkv[:, cols] = dot_cols(normed_low[...], d_qkv[:, cols]).astype(BF16)
    g_proj[...] = dot_cols(att[...], d_br[...]).astype(BF16)


def each_sample(count, body):
    def step(b, carry):
        body(b)
        return carry

    lax.fori_loop(0, count, step, 0)


def forward_attention_kernel(layer, pieces, length, pos, h, mod, bias, own, other, b_qkv, b_proj,
                             qkv, probs, att, branch, middle, w_qkv, w_proj, sems):
    section, shard = pos[0], pos[1]
    mine = attention_copies(own, w_qkv, w_proj, sems, 0, shard, pieces)
    theirs = attention_copies(other, w_qkv, w_proj, sems, 0, shard, pieces)
    start_from(section, layer, mine, theirs)
    wait_all(mine)
    each_sample(
        h.shape[0] // length,
        lambda b: attention_forward(b, length, h, mod, bias, w_qkv, w_proj, b_qkv, b_proj, qkv, probs, att, branch, middle),
    )


def forward_mlp_kernel(layer, pieces, length, pos, middle, mod, own, other, b_fc1, b_fc2,
                       act, slope, out_branch, layer_out, w_fc1, w_fc2, sems):
    section, shard = pos[0], pos[1]
    mine = mlp_copies(own, w_fc1, w_fc2, sems, 0, shard, pieces)
    theirs = mlp_copies(other, w_fc1, w_fc2, sems, 0, shard, pieces)
    start_from(section, layer, mine, theirs)
    wait_all(mine)
    each_sample(
        middle.shape[0] // length,
        lambda b: mlp_forward(b, length, middle, mod, w_fc1, w_fc2, b_fc1, b_fc2, act, slope, out_branch, layer_out),
    )


def both_kernel(layer, pieces, length, pos, h, grad, mod, bias, own_a, other_a, own_m, other_m,
                b_qkv, b_proj, b_fc1, b_fc2,
                layer_out, d_in, small_a, small_m, scores, pack_a, pack_m,
                w_qkv, w_proj, w_fc1, w_fc2, qkv, probs, att, branch, middle, act, slope, out_branch,
                d_middle, normed_low, d_pre, d_ob, d_qkv, score_sum, g_qkv, g_proj, g_fc1, g_fc2, sems):
    section, shard = pos[0], pos[1]
    mine_a = attention_copies(own_a, w_qkv, w_proj, sems, 0, shard, pieces)
    theirs_a = attention_copies(other_a, w_qkv, w_proj, sems, 0, shard, pieces)
    mine_m = mlp_copies(own_m, w_fc1, w_fc2, sems, len(mine_a), shard, pieces)
    theirs_m = mlp_copies(other_m, w_fc1, w_fc2, sems, len(mine_a), shard, pieces)
    start_from(section, layer, mine_a + mine_m, theirs_a + theirs_m)
    wait_all(mine_a)
    samples = h.shape[0] // length
    each_sample(
        samples,
        lambda b: attention_forward(b, length, h, mod, bias, w_qkv, w_proj, b_qkv, b_proj, qkv, probs, att, branch, middle),
    )
    wait_all(mine_m)

    def mlp(b):
        mlp_forward(b, length, middle, mod, w_fc1, w_fc2, b_fc1, b_fc2, act, slope, out_branch, layer_out)
        mlp_backward(b, length, grad, middle, mod, w_fc1, w_fc2, act, slope, out_branch, d_middle, small_m, normed_low, d_pre, d_ob)

    each_sample(samples, mlp)
    mlp_weight_grads(normed_low, d_pre, act, d_ob, g_fc1, g_fc2)
    pack_mlp(pack_m, g_fc1, g_fc2, shard, pieces)
    score_sum[...] = jnp.zeros_like(score_sum)
    each_sample(
        samples,
        lambda b: attention_backward(b, length, h, mod, w_qkv, w_proj, qkv, probs, att, branch, d_middle, d_in, small_a, score_sum, normed_low, d_qkv, d_ob),
    )
    scores[...] = score_sum[...].astype(BF16)
    attention_weight_grads(normed_low, d_qkv, att, d_ob, g_qkv, g_proj)
    pack_attention(pack_a, g_qkv, g_proj, shard, pieces)


def backward_mlp_kernel(layer, pieces, length, pos, grad, middle, mod, own, other, act, slope, out_branch,
                        d_middle, small, pack, w_fc1, w_fc2, normed_low, d_pre, d_ob, g_fc1, g_fc2, sems):
    section, shard = pos[0], pos[1]
    mine = mlp_copies(own, w_fc1, w_fc2, sems, 0, shard, pieces)
    theirs = mlp_copies(other, w_fc1, w_fc2, sems, 0, shard, pieces)
    start_from(section, layer, mine, theirs)
    wait_all(mine)
    each_sample(
        middle.shape[0] // length,
        lambda b: mlp_backward(b, length, grad, middle, mod, w_fc1, w_fc2, act, slope, out_branch, d_middle, small, normed_low, d_pre, d_ob),
    )
    mlp_weight_grads(normed_low, d_pre, act, d_ob, g_fc1, g_fc2)
    pack_mlp(pack, g_fc1, g_fc2, shard, pieces)


def backward_attention_kernel(layer, pieces, length, pos, h, mod, own, other, qkv, probs, att, branch, d_middle,
                              d_in, small, scores, pack, w_qkv, w_proj, normed_low, d_qkv, d_br, score_sum, g_qkv, g_proj, sems):
    section, shard = pos[0], pos[1]
    mine = attention_copies(own, w_qkv, w_proj, sems, 0, shard, pieces)
    theirs = attention_copies(other, w_qkv, w_proj, sems, 0, shard, pieces)
    start_from(section, layer, mine, theirs)
    score_sum[...] = jnp.zeros_like(score_sum)
    wait_all(mine)
    each_sample(
        h.shape[0] // length,
        lambda b: attention_backward(b, length, h, mod, w_qkv, w_proj, qkv, probs, att, branch, d_middle, d_in, small, score_sum, normed_low, d_qkv, d_br),
    )
    scores[...] = score_sum[...].astype(BF16)
    attention_weight_grads(normed_low, d_qkv, att, d_br, g_qkv, g_proj)
    pack_attention(pack, g_qkv, g_proj, shard, pieces)


def call(kernel, pos, operands, in_hbm, outs, scratch, sems=0):
    specs = [pl.BlockSpec(memory_space=pltpu.SMEM)]
    for i in range(len(operands)):
        specs.append(pl.BlockSpec(memory_space=pl.ANY if i in in_hbm else pltpu.VMEM))
    shapes = [pltpu.VMEM(shape, dtype) for shape, dtype in scratch]
    if sems:
        shapes.append(pltpu.SemaphoreType.DMA((sems,)))
    return pl.pallas_call(
        kernel,
        out_shape=[jax.ShapeDtypeStruct(shape, dtype) for shape, dtype in outs],
        in_specs=specs,
        out_specs=[pl.BlockSpec(memory_space=pltpu.VMEM) for _ in outs],
        scratch_shapes=shapes,
        compiler_params=pltpu.CompilerParams(vmem_limit_bytes=VMEM_BYTES),
    )(pos, *operands)


def forward_attention(layer, pieces, pos, h, mod, bias, own, other, b_qkv, b_proj):
    samples, length, model = mod.shape[0], bias.shape[1], h.shape[1]
    rows, heads = h.shape[0], bias.shape[0]
    return call(
        functools.partial(forward_attention_kernel, layer, pieces, length),
        pos, (h, mod, bias, own, other, b_qkv, b_proj), (3, 4),
        [((rows, 3 * model), BF16), ((samples, heads, length, length), BF16), ((rows, model), BF16),
         ((rows, model), F32), ((rows, model), F32)],
        [((model, 3 * model), BF16), ((model, model), BF16)], 4 * pieces,
    )


def forward_mlp(layer, pieces, length, pos, middle, mod, own, other, b_fc1, b_fc2):
    rows, model = middle.shape
    hidden = b_fc1.shape[1]
    return call(
        functools.partial(forward_mlp_kernel, layer, pieces, length),
        pos, (middle, mod, own, other, b_fc1, b_fc2), (2, 3),
        [((rows, hidden), BF16), ((rows, hidden), BF16), ((rows, model), F32), ((rows, model), BF16)],
        [((model, hidden), BF16), ((hidden, model), BF16)], 5 * pieces,
    )


def both_ways(layer, pieces, pos, h, grad, mod, bias, own_a, other_a, own_m, other_m, b_qkv, b_proj, b_fc1, b_fc2):
    samples, length = mod.shape[0], bias.shape[1]
    rows, model = h.shape
    hidden, heads = b_fc1.shape[1], bias.shape[0]
    return call(
        functools.partial(both_kernel, layer, pieces, length),
        pos, (h, grad, mod, bias, own_a, other_a, own_m, other_m, b_qkv, b_proj, b_fc1, b_fc2), (4, 5, 6, 7),
        [((rows, model), BF16), ((rows, model), BF16), ((samples, 8, model), F32), ((samples, 8, model), F32),
         ((heads, length, length), BF16), ((4 * model, model), BF16), ((8 * model, model), BF16)],
        [((model, 3 * model), BF16), ((model, model), BF16), ((model, hidden), BF16), ((hidden, model), BF16),
         ((rows, 3 * model), BF16), ((samples, heads, length, length), BF16), ((rows, model), BF16),
         ((rows, model), F32), ((rows, model), F32), ((rows, hidden), BF16), ((rows, hidden), BF16), ((rows, model), F32),
         ((rows, model), F32), ((rows, model), BF16), ((rows, hidden), BF16), ((rows, model), BF16),
         ((rows, 3 * model), BF16), ((heads, length, length), F32),
         ((model, 3 * model), BF16), ((model, model), BF16), ((model, hidden), BF16), ((hidden, model), BF16)],
        9 * pieces,
    )


def backward_mlp(layer, pieces, length, pos, grad, middle, mod, own, other, act, slope, out_branch):
    rows, model = middle.shape
    hidden, samples = act.shape[1], mod.shape[0]
    return call(
        functools.partial(backward_mlp_kernel, layer, pieces, length),
        pos, (grad, middle, mod, own, other, act, slope, out_branch), (3, 4),
        [((rows, model), F32), ((samples, 8, model), F32), ((8 * model, model), BF16)],
        [((model, hidden), BF16), ((hidden, model), BF16), ((rows, model), BF16), ((rows, hidden), BF16),
         ((rows, model), BF16), ((model, hidden), BF16), ((hidden, model), BF16)],
        5 * pieces,
    )


def backward_attention(layer, pieces, pos, h, mod, own, other, qkv, probs, att, branch, d_middle):
    rows, model = h.shape
    samples, heads, length = probs.shape[:3]
    return call(
        functools.partial(backward_attention_kernel, layer, pieces, length),
        pos, (h, mod, own, other, qkv, probs, att, branch, d_middle), (2, 3),
        [((rows, model), F32), ((samples, 8, model), F32), ((heads, length, length), BF16), ((4 * model, model), BF16)],
        [((model, 3 * model), BF16), ((model, model), BF16), ((rows, model), BF16), ((rows, 3 * model), BF16),
         ((rows, model), BF16), ((heads, length, length), F32), ((model, 3 * model), BF16), ((model, model), BF16)],
        4 * pieces,
    )


def lookup_kernel(table, index, out, work):
    heads, length = out.shape[0], out.shape[1]
    high_count = table.shape[0] // 8
    values = table[...]
    low_id = lax.broadcasted_iota(jnp.int32, (LOW, length), 0)

    def step(i, carry):
        block = index[pl.ds(pl.multiple_of(i * 8, 8), 8), :]
        for r in range(8):
            entry = block[r : r + 1, :]
            picks = jnp.where(low_id == (entry & (LOW - 1)), 1.0, 0.0).astype(BF16)
            found = dot(values, picks).reshape(high_count, 8, length)
            high = jnp.broadcast_to(entry >> 5, (8, length))
            bit = high_count // 2
            while bit:
                chosen = (high & bit) != 0
                found = jnp.where(chosen[None], found[bit : 2 * bit], found[:bit])
                bit //= 2
            for head in range(heads):
                work[head, pl.ds(i * 8 + r, 1), :] = found[0, head : head + 1, :]
        return carry

    lax.fori_loop(0, length // 8, step, 0)
    out[...] = work[...].astype(BF16)


def lookup(table, index):
    heads, entries = table.shape
    high_count = LOW
    padded = jnp.pad(table, ((0, 8 - heads), (0, high_count * LOW - entries)))
    rows = jnp.transpose(padded.reshape(8, high_count, LOW), (1, 0, 2)).reshape(high_count * 8, LOW)
    length = index.shape[0]
    return pl.pallas_call(
        lookup_kernel,
        out_shape=jax.ShapeDtypeStruct((heads, length, length), BF16),
        scratch_shapes=[pltpu.VMEM((heads, length, length), F32)],
        compiler_params=pltpu.CompilerParams(vmem_limit_bytes=VMEM_BYTES),
    )(rows, index)


def table_kernel(scores, index, out):
    heads, length = scores.shape[0], scores.shape[1]
    out[...] = jnp.zeros_like(out)
    ids = lax.broadcasted_iota(jnp.int32, (LOW, length), 0)

    def step(i, carry):
        rows = pl.ds(pl.multiple_of(i * 16, 16), 16)
        entries = index[rows, :]
        block = [scores[head, rows, :].astype(F32) for head in range(heads)]
        total = None
        for r in range(16):
            entry = entries[r : r + 1, :]
            low = jnp.where(ids == (entry & (LOW - 1)), 1.0, 0.0).astype(BF16)
            high = ids == (entry >> 5)
            left = jnp.concatenate(
                [jnp.where(high, block[head][r : r + 1, :], 0.0) for head in range(heads)], axis=0
            ).astype(BF16)
            part = dot_rows(left, low)
            total = part if total is None else total + part
        out[...] += total
        return carry

    lax.fori_loop(0, length // 16, step, 0)


def table_gradient(scores, index):
    heads = scores.shape[0]
    return pl.pallas_call(
        table_kernel,
        out_shape=jax.ShapeDtypeStruct((heads * LOW, LOW), F32),
        compiler_params=pltpu.CompilerParams(vmem_limit_bytes=VMEM_BYTES),
    )(scores, index)


def swap_section(value):
    return lax.ppermute(value, "section", [(0, 1), (1, 0)])


def pairs_of(count, step):
    return [(i, i ^ step) for i in range(count)]


def by_rank(pieces, rank):
    stack = jnp.stack(pieces)
    count = len(pieces)
    bit = 1
    while bit < count:
        moved = jnp.stack([stack[i ^ bit] for i in range(count)])
        stack = jnp.where((rank & bit) != 0, moved, stack)
        bit *= 2
    return stack


def one_section_pairs(layer, count, step):
    return [(layer * count + i, layer * count + (i ^ step)) for i in range(count)]


def reduce_grads(pack, layer, shards, rank):
    other = lax.ppermute(pack, "section", [(1 - layer, layer)])
    size = pack.shape[0] // shards
    sums = [
        pack[p * size : (p + 1) * size].astype(F32) + other[p * size : (p + 1) * size].astype(F32)
        for p in range(shards)
    ]
    total = sums[0]
    got = [
        lax.ppermute(sums[p].astype(BF16), ("section", "fsdp"), one_section_pairs(layer, shards, p))
        for p in range(1, shards)
    ]
    for piece in got:
        total = total + piece.astype(F32)
    replicas = lax.axis_size("rep")
    parts = total.reshape(replicas, size // replicas, -1)
    low_parts = parts.astype(BF16)
    mine = lax.dynamic_index_in_dim(parts, rank, 0, keepdims=False)
    names = ("section", "rep")
    got = [
        lax.ppermute(
            lax.dynamic_index_in_dim(low_parts, rank ^ j, 0, keepdims=False),
            names, one_section_pairs(layer, replicas, j),
        )
        for j in range(1, replicas)
    ]
    for piece in got:
        mine = mine + piece.astype(F32)
    mine = mine.astype(BF16)
    quarters = [mine] + [
        lax.ppermute(mine, names, one_section_pairs(layer, replicas, j)) for j in range(1, replicas)
    ]
    return by_rank(quarters, rank).reshape(size, -1)


def unpack_attention(pack):
    q = pack.shape[0] // 4
    return jnp.concatenate([pack[c * q : (c + 1) * q] for c in range(3)], axis=1), pack[3 * q :]


def unpack_mlp(pack):
    q = pack.shape[0] // 8
    return jnp.concatenate([pack[c * q : (c + 1) * q] for c in range(4)], axis=1), pack[4 * q :]


def pack_attention_shard(w_qkv, w_proj):
    model = w_proj.shape[1]
    return jnp.concatenate([w_qkv[:, c * model : (c + 1) * model] for c in range(3)] + [w_proj], axis=0)


def pack_mlp_shard(w_fc1, w_fc2):
    model = w_fc2.shape[1]
    return jnp.concatenate([w_fc1[:, c * model : (c + 1) * model] for c in range(4)] + [w_fc2], axis=0)


def per_device(inputs, conditioning, cotangent, micro_sizes, relative_bias_index,
               w_ada, w_qkv, w_proj, w_fc1, w_fc2, b_ada, b_qv, b_proj, b_fc1, b_fc2, bias_table):
    section = lax.axis_index("section")
    shard = lax.axis_index("fsdp")
    rank = lax.axis_index("rep")
    shards, replicas = lax.axis_size("fsdp"), lax.axis_size("rep")
    direct = shards == 4 and replicas == 4
    pieces = shards if direct else 1
    is_first = section == 0
    samples, length, model = inputs.shape
    heads, entries = bias_table.shape[1:]
    half = samples // 2
    pos = jnp.stack([section, shard]).astype(jnp.int32)

    def mine(first, second):
        return jnp.where(is_first, first, second)

    def own_samples(array):
        return lax.dynamic_slice_in_dim(array, section * half, half, 0)

    def in_order(own, other):
        return jnp.where(is_first, jnp.concatenate([own, other]), jnp.concatenate([other, own]))

    row = jnp.concatenate([conditioning.reshape(-1), b_ada[0], b_qv[0], b_proj[0], b_fc1[0], b_fc2[0]])
    pack_a = pack_attention_shard(w_qkv[0], w_proj[0])
    pack_m = pack_mlp_shard(w_fc1[0], w_fc2[0])
    cond_size = conditioning.size
    if direct:
        rows = [row] + [lax.ppermute(row, "fsdp", pairs_of(shards, p)) for p in range(1, shards)]
        all_a = [pack_a] + [lax.ppermute(pack_a, "fsdp", pairs_of(shards, p)) for p in range(1, shards)]
        cond_pieces = jnp.stack([r[:cond_size].reshape(samples, model) for r in rows])
        acts = jax.nn.silu(cond_pieces.astype(F32)).astype(BF16)
        width = model // shards
        acts = lax.dynamic_slice_in_dim(acts, shard * width, width, 2)
        partial = lax.dot_general(acts, w_ada[0], (((2,), (0,)), ((), ())), preferred_element_type=F32)
        modulation = partial[0]
        for p in range(1, shards):
            modulation = modulation + lax.ppermute(partial[p], "fsdp", pairs_of(shards, p))
        all_m = [pack_m] + [lax.ppermute(pack_m, "fsdp", pairs_of(shards, p)) for p in range(1, shards)]
        own_a = jnp.concatenate(all_a)
        own_m = jnp.concatenate(all_m)
        bias_rows = by_rank([r[cond_size:] for r in rows], shard)
        w_ada_all = lax.all_gather(w_ada[0], "fsdp", axis=0, tiled=True)
    else:
        bias_rows = lax.all_gather(row[cond_size:], "fsdp", axis=0)
        gathered_a = lax.all_gather(pack_a, "fsdp", axis=0)
        gathered_m = lax.all_gather(pack_m, "fsdp", axis=0)
        q = model // shards
        own_a = jnp.transpose(gathered_a.reshape(shards, 4, q, model), (1, 0, 2, 3)).reshape(4 * model, model)
        fc1 = jnp.transpose(gathered_m[:, : 4 * q].reshape(shards, 4, q, model), (1, 0, 2, 3))
        own_m = jnp.concatenate([fc1.reshape(4 * model, model), gathered_m[:, 4 * q :].reshape(4 * model, model)])
        w_ada_all = lax.all_gather(w_ada[0], "fsdp", axis=0, tiled=True)
        acts = jax.nn.silu(conditioning.astype(F32)).astype(BF16)
        modulation = dot(acts, w_ada_all)
    cuts = [b_ada.shape[1], b_qv.shape[1], b_proj.shape[1], b_fc1.shape[1], b_fc2.shape[1]]
    biases, at = [], 0
    for cut in cuts:
        biases.append(bias_rows[:, at : at + cut].reshape(1, -1).astype(F32))
        at += cut
    modulation = modulation + biases[0]
    bias_line = jnp.concatenate(biases[1:], axis=1)
    other_line = swap_section(bias_line)
    other_samples = lax.dynamic_slice_in_dim(modulation, (1 - section) * half, half, 0)
    other_mod = swap_section(other_samples)
    own_mod = own_samples(modulation)
    other_a = swap_section(own_a)
    other_m = swap_section(own_m)
    bias_own = lookup(bias_table[0], relative_bias_index)
    bias_other = swap_section(bias_own)

    def layer_values(layer):
        pick = (lambda a, b: mine(a, b)) if layer == 0 else (lambda a, b: mine(b, a))
        line = pick(bias_line, other_line)
        mod = pick(own_mod, other_mod).reshape(half, 6, model)
        b_qkv = jnp.concatenate([line[:, :model], jnp.zeros((1, model), F32), line[:, model : 2 * model]], axis=1)
        at = 2 * model
        hidden = w_fc1.shape[2]
        return (
            mod, pick(bias_own, bias_other), b_qkv, line[:, at : at + model],
            line[:, at + model : at + model + hidden], line[:, at + model + hidden :],
        )

    mod0, bias0, b_qkv0, b_proj0, b_fc10, b_fc20 = layer_values(0)
    mod1, bias1, b_qkv1, b_proj1, b_fc11, b_fc21 = layer_values(1)

    live = (jnp.arange(half)[:, None, None] < lax.dynamic_index_in_dim(micro_sizes[0], section, 0)).astype(BF16)
    h0 = own_samples(inputs).reshape(half * length, model)
    grad1 = (own_samples(cotangent) * live).reshape(half * length, model)

    qkv, probs, att, branch, middle = forward_attention(0, pieces, pos, h0, mod0, bias0, own_a, other_a, b_qkv0, b_proj0)
    act, slope, out_branch, h1 = forward_mlp(0, pieces, length, pos, middle, mod0, own_m, other_m, b_fc10, b_fc20)
    out1, d_h1, small_a1, small_m1, scores1, grads_a1, grads_m1 = both_ways(
        1, pieces, pos, h1, grad1, mod1, bias1, own_a, other_a, own_m, other_m, b_qkv1, b_proj1, b_fc11, b_fc21
    )
    d_middle, small_m0, grads_m0 = backward_mlp(0, pieces, length, pos, d_h1, middle, mod0, own_m, other_m, act, slope, out_branch)
    d_h0, small_a0, scores0, grads_a0 = backward_attention(0, pieces, pos, h0, mod0, own_a, other_a, qkv, probs, att, branch, d_middle)

    if direct:
        done1 = reduce_grads(jnp.concatenate([
            x for p in range(pieces)
            for x in (grads_a1[p * model : (p + 1) * model], grads_m1[2 * p * model : 2 * (p + 1) * model])
        ]), 1, shards, rank)
        done_a0 = reduce_grads(grads_a0, 0, shards, rank)
        done_m0 = reduce_grads(grads_m0, 0, shards, rank)
        total_a = mine(done_a0, done1[:model])
        total_m = mine(done_m0, done1[model:])
        g_qkv, g_proj = unpack_attention(total_a.astype(F32))
        g_fc1, g_fc2 = unpack_mlp(total_m.astype(F32))
    else:
        def whole(pack0, pack1):
            return (mine(pack0, pack1).astype(F32) + swap_section(mine(pack1, pack0)).astype(F32)).astype(BF16)

        grads = unpack_attention(whole(grads_a0, grads_a1)) + unpack_mlp(whole(grads_m0, grads_m1))
        grads = [lax.psum_scatter(g, "fsdp", scatter_dimension=0, tiled=True) for g in grads]
        g_qkv, g_proj, g_fc1, g_fc2 = [g.astype(F32) for g in lax.psum(tuple(grads), "rep")]

    other_out = swap_section(mine(out1, h1))
    activations = in_order(mine(h1, out1).reshape(half, length, model), other_out.reshape(half, length, model))
    other_in = swap_section(mine(d_h1, d_h0.astype(BF16)))
    input_grads = in_order(
        mine(d_h0, d_h1.astype(F32)).reshape(half, length, model),
        other_in.astype(F32).reshape(half, length, model),
    )

    tables = [table_gradient(scores, relative_bias_index) for scores in (scores0, scores1)]
    smalls = [
        jnp.concatenate([small_a0[:, :3], small_m0, small_a0[:, 3:]], axis=1),
        jnp.concatenate([small_a1[:, :3], small_m1, small_a1[:, 3:]], axis=1),
    ]
    small = in_order(mine(smalls[0], smalls[1]), swap_section(mine(smalls[1], smalls[0])))
    table = mine(tables[0], tables[1]) + swap_section(mine(tables[1], tables[0]))
    low = small[:, :6].astype(BF16)
    w_rows = w_ada_all.reshape(model, 6, model)
    d_act = sum(dot_rows(low[:, i], w_rows[:, i]) for i in range(6))
    cond = conditioning.astype(F32)
    gate = jax.nn.sigmoid(cond)
    cond_part = d_act * (gate * (1.0 + cond * (1.0 - gate)))
    cond_grad = cond_part + swap_section(cond_part)

    bias_sum = jnp.sum(small[:, 6:], axis=0).astype(BF16)
    packed = jnp.concatenate([
        low.reshape(-1, model), bias_sum, table.astype(BF16).reshape(-1, model)
    ], axis=0)
    every = lax.all_gather(packed, ("fsdp", "rep"), axis=0)
    groups = shards * replicas
    mod_rows = samples * 6
    d_mod = every[:, :mod_rows].reshape(groups * samples, 6 * model)
    cond_all = lax.all_gather(conditioning, ("fsdp", "rep"), axis=0, tiled=True)
    width = model // shards
    act_all = jax.nn.silu(cond_all.astype(F32)).astype(BF16)
    act_cols = lax.dynamic_slice_in_dim(act_all, shard * width, width, 1)
    g_ada = dot_cols(act_cols, d_mod)
    summed = jnp.sum(every[:, mod_rows:].astype(F32), axis=0)
    g_b_ada = jnp.sum(d_mod.astype(F32), axis=0)
    g_b_fc2, g_b_fc1 = summed[0], summed[1:5].reshape(-1)
    g_b_qv, g_b_proj = summed[5:7].reshape(-1), summed[7]
    g_table = summed[10:].reshape(heads, LOW * LOW)[:, :entries]

    def own_part(vector):
        size = vector.shape[0] // shards
        return lax.dynamic_slice_in_dim(vector, shard * size, size, 0)[None]

    return (
        activations[None], input_grads[None], cond_grad,
        g_ada[None], g_qkv[None], g_proj[None], g_fc1[None], g_fc2[None],
        own_part(g_b_ada), own_part(g_b_qv), own_part(g_b_proj), own_part(g_b_fc1), own_part(g_b_fc2),
        g_table[None],
    )


def solution(mesh):
    batch = ("fsdp", "rep")
    matrix = P("section", "fsdp", None)
    vector = P("section", "fsdp")
    return jax.shard_map(
        per_device,
        mesh=mesh,
        in_specs=(
            P(batch, None, None), P(batch, None), P(batch, None, None), P(batch, None), P(),
            matrix, matrix, matrix, matrix, matrix, vector, vector, vector, vector, vector,
            P("section", None, None),
        ),
        out_specs=(
            P("section", batch, None, None), P("section", batch, None, None), P(batch, None),
            matrix, matrix, matrix, matrix, matrix, vector, vector, vector, vector, vector,
            P("section", None, None),
        ),
        check_vma=False,
    )
```

time: 1040 us -> 439 us (0.42)
  matrix products: 499 us -> 4 us
  local copies, waits for them, and re-layouts: 258 us -> 42 us
  Pallas kernels: 0 us -> 103 us
  starting transfers between devices: 7.11 us -> 95.4 us
  other arithmetic: 104 us -> 38.4 us
  blocking collectives: 140 us -> 81.5 us
  waiting for transfers between devices: 3.17 us -> 49.6 us
    dot_general x143 -> x8, matrix products: 499 us -> 4 us  [the longest x1 2.15 us: dot_cols(): lax.dot_general(a, b, (((0,), (0,)), ((), ())), preferred_element_type=F32)]
    dynamic_slice x112 -> x7, local copies, waits for them, and re-layouts: 113 us -> 2.76 us  [the longest x4 1.38 us: own_part(): return lax.dynamic_slice_in_dim(vector, shard * size, size, 0)[None]]
    pallas_call x0 -> x8, Pallas kernels: none -> 103 us  [the longest x5 65.7 us: call(): pl.pallas_call(kernel, out_shape=[jax.ShapeDtypeStruct(shape, dtype) for...]
    psum x3 -> x0, blocking collectives: 91.5 us -> none  [the longest x1 78.4 us: per_device(): table_grad = lax.psum(table_local[None], ('fsdp', 'rep'))]
    ppermute x4 -> x52, starting transfers between devices: 5.78 us -> 95.4 us  [the longest x9 26 us: reduce_grads(): lax.ppermute(lax.dynamic_index_in_dim(low_parts, rank ^ j, 0, keepdims=Fa...]
    all_gather x3 -> x2, blocking collectives: 30.4 us -> 81.5 us  [the longest x1 42.1 us: per_device(): every = lax.all_gather(packed, ('fsdp', 'rep'), axis=0)]
    ppermute x4 -> x52, waiting for transfers between devices: 0.06 us -> 49.6 us  [the longest x9 22.2 us: reduce_grads(): lax.ppermute(sums[p].astype(BF16), ('section', 'fsdp'), one_section_pairs...]
    reduce_sum x41 -> x3, other arithmetic: 43 us -> 1.03 us  [the longest x1 0.91 us: per_device(): bias_sum = jnp.sum(small[:, 6:], axis=0).astype(BF16)]
  transfers between devices with their start and end apart: 18 -> 53, of which waited for: 1 -> 13; matrix products, arithmetic and copies ran while one was open for 62% -> 16% of each run, Pallas kernels for 0% -> 11%
where the time goes in v1:
time: 439 us; the launch traced here: 430 us
  Pallas kernels  103 us (23%)
  starting transfers between devices  95.4 us (22%)
  blocking collectives  81.5 us (19%)
  waiting for transfers between devices  49.6 us (11%)
  local copies, waits for them, and re-layouts  42 us (10%)
  other arithmetic  38.4 us (9%)
  between operations  15.9 us (4%)
    pallas_call x5, Pallas kernels, call(): pl.pallas_call(kernel, out_shape=[jax.ShapeDtypeStruct(shape, dtype) for...  65.7 us
    all_gather x1, blocking collectives, per_device(): every = lax.all_gather(packed, ('fsdp', 'rep'), axis=0)  42.1 us
    all_gather x1, blocking collectives, per_device(): cond_all = lax.all_gather(conditioning, ('fsdp', 'rep'), axis=0, tiled=True)  39.4 us
    ppermute x9, starting transfers between devices, reduce_grads(): lax.ppermute(lax.dynamic_index_in_dim(low_parts, rank ^ j, 0, keepdims=Fa...  26 us
    ppermute x9, waiting for transfers between devices, reduce_grads(): lax.ppermute(sums[p].astype(BF16), ('section', 'fsdp'), one_section_pairs...  22.2 us
    pallas_call x2, Pallas kernels, table_gradient(): pl.pallas_call(table_kernel, out_shape=jax.ShapeDtypeStruct((heads * LOW,...  21.5 us
    ppermute x9, starting transfers between devices, reduce_grads(): lax.ppermute(sums[p].astype(BF16), ('section', 'fsdp'), one_section_pairs...  20.8 us
    ppermute x9, starting transfers between devices, reduce_grads(): lax.ppermute(mine, names, one_section_pairs(layer, replicas, j))  20.7 us
  transfers between devices with their start and end apart: 53, of which 13 were waited for; matrix products, arithmetic and copies ran while one was open for 16% of the time, Pallas kernels for 11%

profile of v1, /device:TPU:0, one launch (start us, length us, event | category | flops | bytes accessed | tf_op | source)
XLA Modules:
  0.0 430.1 jit_solution(1950480903890187227)
XLA Ops:
  11.6 3.9 collective-permute-start.2
  33.8 39.4 %all-gather.2 = bf16[16,4,384]{2,1,0:T(4,128)(2,1)S(1)} all-gather(bf16[1,4,384]{2,1,0:T(4,128)(2,1)S(1)} %bitcast.229), channel_id=1, replica_groups=mesh['section'=2,'fsdp'=4,'rep'=4] {'fsdp','rep'}, dimensions={0}, use_global_device_ids=true | all-gather | bytes 52224 | tf_op jit(solution)/shard_map/all_gather | solution.py:764
  74.8 16.0 %shard_map.263 = bf16[6,256,256]{2,1,0:T(8,128)(2,1)} custom-call(bf16[256,32]{1,0:T(8,128)(2,1)} %bitcast.225, s32[256,256]{1,0:T(8,128)} %index.5), custom_call_target="tpu_custom_call" | custom-call | tf_op jit(solution)/shard_map/pallas_call | solution.py:497
  98.0 5.8 %collective-permute-done.13 = bf16[768,384]{1,0:T(8,128)(2,1)} collective-permute-done((bf16[768,384]{1,0:T(8,128)(2,1)}, bf16[768,384]{1,0:T(8,128)(2,1)}, u32[]{:S(2)}, u32[]{:S(2)}) %collective-permute-start.13) | collective-permute-done | bytes 589856 | tf_op jit(solution)/shard_map/ppermute | solution.py:655
  106.0 8.2 %collective-permute-done.14 = bf16[768,384]{1,0:T(8,128)(2,1)} collective-permute-done((bf16[768,384]{1,0:T(8,128)(2,1)}, bf16[768,384]{1,0:T(8,128)(2,1)}, u32[]{:S(2)}, u32[]{:S(2)}) %collective-permute-start.14) | collective-permute-done | bytes 589856 | tf_op jit(solution)/shard_map/ppermute | solution.py:655
  134.1 9.1 %shard_map.264 = (bf16[512,1152]{1,0:T(8,128)(2,1)}, bf16[2,6,256,256]{3,2,1,0:T(8,128)(2,1)}, bf16[512,384]{1,0:T(8,128)(2,1)}, f32[512,384]{1,0:T(8,128)}, f32[512,384]{1,0:T(8,128)}) custom-call(s32[2]{0:T(128)} %pad_add_fusion.pos, bf16[512,384]{1,0:T(8,128)(2,1)} %bitcast.180, f32[2,6,384]{2,1,0:T(8,128)} %reshape.314.mod, ...), custom_call_target="tpu_custom_call" | custom-call | tf_op jit(solution)/shard_map/pallas_call | solution.py:387
  143.3 3.9 copy.40
  147.1 9.4 %shard_map.265 = (bf16[512,1536]{1,0:T(8,128)(2,1)}, bf16[512,1536]{1,0:T(8,128)(2,1)}, f32[512,384]{1,0:T(8,128)}, bf16[512,384]{1,0:T(8,128)(2,1)}) custom-call(s32[2]{0:T(128)} %pad_add_fusion.pos, f32[512,384]{1,0:T(8,128)} %get-tuple-element.37.middle, f32[2,6,384]{2,1,0:T(8,128)} %reshape.314.mod, bf16[3072,384]{1,0:T(8,128)(2,1)} %copy-done.2, ...), custom_call_target="tpu_custom_call" | custom-call | tf_op jit(solution)/shard_map/pallas_call | solution.py:387
  156.6 24.9 %shard_map.266 = (bf16[512,384]{1,0:T(8,128)(2,1)}, bf16[512,384]{1,0:T(8,128)(2,1)}, f32[2,8,384]{2,1,0:T(8,128)}, f32[2,8,384]{2,1,0:T(8,128)}, bf16[6,256,256...) custom-call(s32[2]{0:T(128)} %pad_add_fusion.pos, bf16[512,384]{1,0:T(8,128)(2,1)} %get-tuple-element.38.h, ...), custom_call_target="tpu_custom_call" | custom-call | tf_op jit(solution)/shard_map/pallas_call | solution.py:387
  181.5 11.1 %shard_map.267 = (f32[512,384]{1,0:T(8,128)}, f32[2,8,384]{2,1,0:T(8,128)}, bf16[3072,384]{1,0:T(8,128)(2,1)}) custom-call(s32[2]{0:T(128)} %pad_add_fusion.pos, bf16[512,384]{1,0:T(8,128)(2,1)} %get-tuple-element.44.grad, f32[512,384]{1,0:T(8,128)} %get-tuple-element.37.middle, f32[2,6,384]{2,1,0:T(8,128)} %reshape.314.mod, bf16[3072,384]{1,0:T(8,128)(2,1)} %copy-done.2, ...), custom_call_target="tpu_custom_call" | custom-call | tf_op jit(solution)/shard_map/pallas_call | solution.py:387
  192.6 11.1 %shard_map.268 = (f32[512,384]{1,0:T(8,128)}, f32[2,8,384]{2,1,0:T(8,128)}, bf16[6,256,256]{2,1,0:T(8,128)(2,1)}, bf16[1536,384]{1,0:T(8,128)(2,1)}) custom-call(s32[2]{0:T(128)} %pad_add_fusion.pos, bf16[512,384]{1,0:T(8,128)(2,1)} %bitcast.181, f32[2,6,384]{2,1,0:T(8,128)} %reshape.314.mod, bf16[1536,384]{1,0:T(8,128)(2,1)} %constant_dynamic-update-slice_fusion.own.own_a, ...), custom_call_target="tpu_custom_call" | custom-call | tf_op jit(solution)/shard_map/pallas_call | solution.py:387
  209.2 10.7 %shard_map.270 = f32[192,32]{1,0:T(8,128)} custom-call(bf16[6,256,256]{2,1,0:T(8,128)(2,1)} %get-tuple-element.55.scores, s32[256,256]{1,0:T(8,128)} %index.5), custom_call_target="tpu_custom_call" | custom-call | tf_op jit(solution)/shard_map/pallas_call | solution.py:532
  219.9 10.8 %shard_map.269 = f32[192,32]{1,0:T(8,128)} custom-call(bf16[6,256,256]{2,1,0:T(8,128)(2,1)} %get-tuple-element.54.scores, s32[256,256]{1,0:T(8,128)} %index.5), custom_call_target="tpu_custom_call" | custom-call | tf_op jit(solution)/shard_map/pallas_call | solution.py:532
  239.8 3.7 collective-permute-start.32
  250.9 2.7 collective-permute-start.20
  254.5 42.1 %all-gather.3 = bf16[16,50,384]{2,1,0:T(8,128)(2,1)S(1)} all-gather(bf16[1,50,384]{2,1,0:T(8,128)(2,1)S(1)} %maximum_bitcast_fusion.2), channel_id=3, replica_groups=mesh['section'=2,'fsdp'=4,'rep'=4] {'fsdp','rep'}, dimensions={0}, use_global_device_ids=true | all-gather | bytes 652800 | tf_op jit(solution)/shard_map/all_gather | solution.py:760
  303.3 5.0 %collective-permute-start.23 = (bf16[384,384]{1,0:T(8,128)(2,1)S(1)}, bf16[384,384]{1,0:T(8,128)(2,1)}, u32[]{:S(2)}, u32[]{:S(2)}) collective-permute-start(bf16[384,384]{1,0:T(8,128)(2,1)S(1)} %get-tuple-element.68), channel_id=1, source_target_pairs={{0,4},{4,0},{8,12},{12,8},{1,5},{5,1},{9,13},{13,9},{2,6},{6,2},{1... | collective-permute-start | bytes 884744 | tf_op jit(solution)/shard_map/ppermute | solution.py:571
  319.6 4.9 %collective-permute-start.27 = (bf16[96,384]{1,0:T(8,128)(2,1)S(1)}, bf16[96,384]{1,0:T(8,128)(2,1)S(1)}, u32[]{:S(2)}, u32[]{:S(2)}) collective-permute-start(bf16[96,384]{1,0:T(8,128)(2,1)S(1)} %get-tuple-element.107), channel_id=1, source_target_pairs={{0,2},{1,3},{2,0},{3,1},{4,6},{5,7},{6,4},{7,5},{8,10},{9,11},{10,... | collective-permute-start | bytes 221192 | tf_op jit(solution)/shard_map/ppermute | solution.py:582
  324.5 3.3 collective-permute-start.26
  335.3 4.3 collective-permute-start.45
  342.0 2.7 collective-permute-start.43
  347.2 6.1 %collective-permute-done.45 = bf16[768,384]{1,0:T(8,128)(2,1)S(1)} collective-permute-done((bf16[768,384]{1,0:T(8,128)(2,1)S(1)}, bf16[768,384]{1,0:T(8,128)(2,1)S(1)}, u32[]{:S(2)}, u32[]{:S(2)}) %collective-permute-start.45) | collective-permute-done | bytes 589856 | tf_op jit(solution)/shard_map/ppermute | solution.py:571
  354.0 16.2 %collective-permute-done.44 = bf16[768,384]{1,0:T(8,128)(2,1)S(1)} collective-permute-done((bf16[768,384]{1,0:T(8,128)(2,1)S(1)}, bf16[768,384]{1,0:T(8,128)(2,1)S(1)}, u32[]{:S(2)}, u32[]{:S(2)}) %collective-permute-start.44) | collective-permute-done | bytes 589856 | tf_op jit(solution)/shard_map/ppermute | solution.py:571
  373.3 3.5 collective-permute-start.30
  376.9 2.5 collective-permute-start.29
  379.4 2.5 collective-permute-done.30
  381.8 3.3 collective-permute-start.48
  386.2 5.6 %collective-permute-start.47 = (bf16[192,384]{1,0:T(8,128)(2,1)S(1)}, bf16[192,384]{1,0:T(8,128)(2,1)S(1)}, u32[]{:S(2)}, u32[]{:S(2)}) collective-permute-start(bf16[192,384]{1,0:T(8,128)(2,1)S(1)} %get-tuple-element.98), channel_id=1, source_target_pairs={{0,2},{1,3},{2,0},{3,1},{4,6},{5,7},{6,4},{7,5},{8,10},{9,11},{10,... | collective-permute-start | bytes 442376 | tf_op jit(solution)/shard_map/ppermute | solution.py:582
  391.9 4.9 %collective-permute-start.46 = (bf16[192,384]{1,0:T(8,128)(2,1)S(1)}, bf16[192,384]{1,0:T(8,128)(2,1)S(1)}, u32[]{:S(2)}, u32[]{:S(2)}) collective-permute-start(bf16[192,384]{1,0:T(8,128)(2,1)S(1)} %get-tuple-element.96), channel_id=1, source_target_pairs={{0,1},{1,0},{2,3},{3,2},{4,5},{5,4},{6,7},{7,6},{8,9},{9,8},{10,11... | collective-permute-start | bytes 442376 | tf_op jit(solution)/shard_map/ppermute | solution.py:582
  397.6 2.6 collective-permute-done.46
  400.3 4.2 collective-permute-start.51
  404.5 4.4 %collective-permute-start.50 = (bf16[192,384]{1,0:T(8,128)(2,1)S(1)}, bf16[192,384]{1,0:T(8,128)(2,1)S(1)}, u32[]{:S(2)}, u32[]{:S(2)}) collective-permute-start(bf16[192,384]{1,0:T(8,128)(2,1)S(1)} %fusion.11), channel_id=1, source_target_pairs={{0,3},{1,2},{2,1},{3,0},{4,7},{5,6},{6,5},{7,4},{8,11},{9,10},{10,... | collective-permute-start | bytes 442376 | tf_op jit(solution)/shard_map/ppermute | solution.py:592
  (320 shorter events, 125.4 us)
Async XLA Ops:
  7.2 136.0 %all-gather.6.cloned.1.call-start = ((), (), s32[]{:S(2)}) async-start(), calls=%async_computation | async-start | bytes 2211840 | tf_op jit(solution)/shard_map/all_gather | solution.py:659
  11.6 79.4 %collective-permute-start.2 = (bf16[2880]{0:T(1024)(128)(2,1)S(1)}, bf16[2880]{0:T(1024)(128)(2,1)S(1)}, u32[]{:S(2)}, u32[]{:S(2)}) collective-permute-start(bf16[2880]{0:T(1024)(128)(2,1)S(1)} %concatenate.118), channel_id=1, source_target_pairs={{0,12},{4,8},{8,4},{12,0},{1,13},{5,9},{9,5},{13,1},{2,14},{6,10},... | collective-permute-start | bytes 17288 | tf_op jit(solution)/shard_map/ppermute | solution.py:645
  15.5 75.4 %collective-permute-start.1 = (bf16[2880]{0:T(1024)(128)(2,1)S(1)}, bf16[2880]{0:T(1024)(128)(2,1)S(1)}, u32[]{:S(2)}, u32[]{:S(2)}) collective-permute-start(bf16[2880]{0:T(1024)(128)(2,1)S(1)} %concatenate.118), channel_id=1, source_target_pairs={{0,8},{4,12},{8,0},{12,4},{1,9},{5,13},{9,1},{13,5},{2,10},{6,14},... | collective-permute-start | bytes 17288 | tf_op jit(solution)/shard_map/ppermute | solution.py:645
  16.0 76.6 %collective-permute-start = (bf16[2880]{0:T(1024)(128)(2,1)S(1)}, bf16[2880]{0:T(1024)(128)(2,1)S(1)}, u32[]{:S(2)}, u32[]{:S(2)}) collective-permute-start(bf16[2880]{0:T(1024)(128)(2,1)S(1)} %concatenate.118), channel_id=1, source_target_pairs={{0,4},{4,0},{8,12},{12,8},{1,5},{5,1},{9,13},{13,9},{2,6},{6,2},{1... | collective-permute-start | bytes 17288 | tf_op jit(solution)/shard_map/ppermute | solution.py:645
  19.3 102.5 %collective-permute-start.8 = (bf16[384,384]{1,0:T(8,128)(2,1)}, bf16[384,384]{1,0:T(8,128)(2,1)}, u32[]{:S(2)}, u32[]{:S(2)}) collective-permute-start(bf16[384,384]{1,0:T(8,128)(2,1)} %pad_maximum_fusion), channel_id=1, source_target_pairs={{0,4},{4,0},{8,12},{12,8},{1,5},{5,1},{9,13},{13,9},{2,6},{6,2},{1... | collective-permute-start | bytes 884744 | tf_op jit(solution)/shard_map/ppermute | solution.py:646
  21.2 102.9 %collective-permute-start.9 = (bf16[384,384]{1,0:T(8,128)(2,1)}, bf16[384,384]{1,0:T(8,128)(2,1)}, u32[]{:S(2)}, u32[]{:S(2)}) collective-permute-start(bf16[384,384]{1,0:T(8,128)(2,1)} %pad_maximum_fusion), channel_id=1, source_target_pairs={{0,8},{4,12},{8,0},{12,4},{1,9},{5,13},{9,1},{13,5},{2,10},{6,14},... | collective-permute-start | bytes 884744 | tf_op jit(solution)/shard_map/ppermute | solution.py:646
  90.8 13.0 %collective-permute-start.13 = (bf16[768,384]{1,0:T(8,128)(2,1)}, bf16[768,384]{1,0:T(8,128)(2,1)}, u32[]{:S(2)}, u32[]{:S(2)}) collective-permute-start(bf16[768,384]{1,0:T(8,128)(2,1)} %get-tuple-element.108), channel_id=1, source_target_pairs={{0,4},{4,0},{8,12},{12,8},{1,5},{5,1},{9,13},{13,9},{2,6},{6,2},{1... | collective-permute-start | bytes 1769480 | tf_op jit(solution)/shard_map/ppermute | solution.py:655
  91.0 23.2 %collective-permute-start.14 = (bf16[768,384]{1,0:T(8,128)(2,1)}, bf16[768,384]{1,0:T(8,128)(2,1)}, u32[]{:S(2)}, u32[]{:S(2)}) collective-permute-start(bf16[768,384]{1,0:T(8,128)(2,1)} %get-tuple-element.108), channel_id=1, source_target_pairs={{0,8},{4,12},{8,0},{12,4},{1,9},{5,13},{9,1},{13,5},{2,10},{6,14},... | collective-permute-start | bytes 1769480 | tf_op jit(solution)/shard_map/ppermute | solution.py:655
  95.0 22.8 %collective-permute-start.15 = (bf16[768,384]{1,0:T(8,128)(2,1)}, bf16[768,384]{1,0:T(8,128)(2,1)S(1)}, u32[]{:S(2)}, u32[]{:S(2)}) collective-permute-start(bf16[768,384]{1,0:T(8,128)(2,1)} %get-tuple-element.108), channel_id=1, source_target_pairs={{0,12},{4,8},{8,4},{12,0},{1,13},{5,9},{9,5},{13,1},{2,14},{6,10},... | collective-permute-start | bytes 1769480 | tf_op jit(solution)/shard_map/ppermute | solution.py:655
  103.8 16.1 %collective-permute-start.5 = (f32[4,2304]{1,0:T(4,128)S(1)}, f32[4,2304]{1,0:T(4,128)S(1)}, u32[]{:S(2)}, u32[]{:S(2)}) collective-permute-start(f32[4,2304]{1,0:T(4,128)S(1)} %get-tuple-element.117), channel_id=1, source_target_pairs={{0,12},{4,8},{8,4},{12,0},{1,13},{5,9},{9,5},{13,1},{2,14},{6,10},... | collective-permute-start | bytes 110600 | tf_op jit(solution)/shard_map/ppermute | solution.py:654
  121.8 25.3 %collective-permute-start.16 = (bf16[3072,384]{1,0:T(8,128)(2,1)S(1)}, bf16[3072,384]{1,0:T(8,128)(2,1)}, u32[]{:S(2)}, u32[]{:S(2)}) collective-permute-start(bf16[3072,384]{1,0:T(8,128)(2,1)S(1)} %constant_dynamic-update-slice_fusion.7.own.own_m), channel_id=1, source_target_pairs={{0,16},{16,0},{1,17},{17,1},{2,18},{18,2},{3,19},{19,3},{4,20},{20... | collective-permute-start | bytes 7077896 | tf_op jit(solution)/shard_map/ppermute | solution.py:540
  207.9 95.5 %collective-permute-start.18 = (bf16[512,384]{1,0:T(8,128)(2,1)}, bf16[512,384]{1,0:T(8,128)(2,1)}, u32[]{:S(2)}, u32[]{:S(2)}) collective-permute-start(bf16[512,384]{1,0:T(8,128)(2,1)} %convert_select_fusion.1), channel_id=1, source_target_pairs={{0,16},{16,0},{1,17},{17,1},{2,18},{18,2},{3,19},{19,3},{4,20},{20... | collective-permute-start | bytes 1179656 | tf_op jit(solution)/shard_map/ppermute | solution.py:540
  209.2 38.5 %collective-permute-start.19 = (f32[2,16,384]{2,1,0:T(8,128)}, f32[2,16,384]{2,1,0:T(8,128)}, u32[]{:S(2)}, u32[]{:S(2)}) collective-permute-start(f32[2,16,384]{2,1,0:T(8,128)} %get-tuple-element.119), channel_id=1, source_target_pairs={{0,16},{16,0},{1,17},{17,1},{2,18},{18,2},{3,19},{19,3},{4,20},{20... | collective-permute-start | bytes 147464 | tf_op jit(solution)/shard_map/ppermute | solution.py:540
  231.7 13.2 %collective-permute-start.21 = (f32[192,32]{1,0:T(8,128)S(1)}, f32[192,32]{1,0:T(8,128)S(1)}, u32[]{:S(2)}, u32[]{:S(2)}) collective-permute-start(f32[192,32]{1,0:T(8,128)S(1)} %broadcast_select_fusion.4), channel_id=1, source_target_pairs={{0,16},{16,0},{1,17},{17,1},{2,18},{18,2},{3,19},{19,3},{4,20},{20... | collective-permute-start | bytes 73736 | tf_op jit(solution)/shard_map/ppermute | solution.py:540
  239.8 102.2 %collective-permute-start.32 = (bf16[4608,384]{1,0:T(8,128)(2,1)}, bf16[4608,384]{1,0:T(8,128)(2,1)}, u32[]{:S(2)}, u32[]{:S(2)}) collective-permute-start(bf16[4608,384]{1,0:T(8,128)(2,1)} %constant_dynamic-update-slice_fusion.10), channel_id=1, source_target_pairs={{0,16},{1,17},{2,18},{3,19},{4,20},{5,21},{6,22},{7,23},{8,24},{9,... | collective-permute-start | bytes 10616840 | tf_op jit(solution)/shard_map/ppermute | solution.py:563
  243.5 53.5 %collective-permute-start.22 = (bf16[1536,384]{1,0:T(8,128)(2,1)}, bf16[1536,384]{1,0:T(8,128)(2,1)S(1)}, u32[]{:S(2)}, u32[]{:S(2)}) collective-permute-start(bf16[1536,384]{1,0:T(8,128)(2,1)} %get-tuple-element.56), channel_id=1, source_target_pairs={{16,0},{17,1},{18,2},{19,3},{20,4},{21,5},{22,6},{23,7},{24,8},{25... | collective-permute-start | bytes 3538952 | tf_op jit(solution)/shard_map/ppermute | solution.py:563
  244.8 88.0 %collective-permute-start.42 = (bf16[3072,384]{1,0:T(8,128)(2,1)}, bf16[3072,384]{1,0:T(8,128)(2,1)}, u32[]{:S(2)}, u32[]{:S(2)}) collective-permute-start(bf16[3072,384]{1,0:T(8,128)(2,1)} %get-tuple-element.59), channel_id=1, source_target_pairs={{16,0},{17,1},{18,2},{19,3},{20,4},{21,5},{22,6},{23,7},{24,8},{25... | collective-permute-start | bytes 7077896 | tf_op jit(solution)/shard_map/ppermute | solution.py:563
  250.9 50.1 %collective-permute-start.20 = (f32[4,384]{1,0:T(4,128)}, f32[4,384]{1,0:T(4,128)S(1)}, u32[]{:S(2)}, u32[]{:S(2)}) collective-permute-start(f32[4,384]{1,0:T(4,128)} %fusion), channel_id=1, source_target_pairs={{0,16},{16,0},{1,17},{17,1},{2,18},{18,2},{3,19},{19,3},{4,20},{20... | collective-permute-start | bytes 18440 | tf_op jit(solution)/shard_map/ppermute | solution.py:540
  299.1 17.0 %collective-permute-start.25 = (bf16[384,384]{1,0:T(8,128)(2,1)}, bf16[384,384]{1,0:T(8,128)(2,1)S(1)}, u32[]{:S(2)}, u32[]{:S(2)}) collective-permute-start(bf16[384,384]{1,0:T(8,128)(2,1)} %get-tuple-element.69), channel_id=1, source_target_pairs={{0,12},{4,8},{8,4},{12,0},{1,13},{5,9},{9,5},{13,1},{2,14},{6,10},... | collective-permute-start | bytes 884744 | tf_op jit(solution)/shard_map/ppermute | solution.py:571
  301.0 15.1 %collective-permute-start.24 = (bf16[384,384]{1,0:T(8,128)(2,1)S(1)}, bf16[384,384]{1,0:T(8,128)(2,1)S(1)}, u32[]{:S(2)}, u32[]{:S(2)}) collective-permute-start(bf16[384,384]{1,0:T(8,128)(2,1)S(1)} %get-tuple-element.70), channel_id=1, source_target_pairs={{0,8},{4,12},{8,0},{12,4},{1,9},{5,13},{9,1},{13,5},{2,10},{6,14},... | collective-permute-start | bytes 884744 | tf_op jit(solution)/shard_map/ppermute | solution.py:571
  303.3 12.8 %collective-permute-start.23 = (bf16[384,384]{1,0:T(8,128)(2,1)S(1)}, bf16[384,384]{1,0:T(8,128)(2,1)}, u32[]{:S(2)}, u32[]{:S(2)}) collective-permute-start(bf16[384,384]{1,0:T(8,128)(2,1)S(1)} %get-tuple-element.68), channel_id=1, source_target_pairs={{0,4},{4,0},{8,12},{12,8},{1,5},{5,1},{9,13},{13,9},{2,6},{6,2},{1... | collective-permute-start | bytes 884744 | tf_op jit(solution)/shard_map/ppermute | solution.py:571
  317.5 11.5 %collective-permute-start.28 = (bf16[96,384]{1,0:T(8,128)(2,1)S(1)}, bf16[96,384]{1,0:T(8,128)(2,1)S(1)}, u32[]{:S(2)}, u32[]{:S(2)}) collective-permute-start(bf16[96,384]{1,0:T(8,128)(2,1)S(1)} %get-tuple-element.106), channel_id=1, source_target_pairs={{0,3},{1,2},{2,1},{3,0},{4,7},{5,6},{6,5},{7,4},{8,11},{9,10},{10,... | collective-permute-start | bytes 221192 | tf_op jit(solution)/shard_map/ppermute | solution.py:582
  329.1 44.2 %collective-permute-start.17 = (bf16[512,384]{1,0:T(8,128)(2,1)S(1)}, bf16[512,384]{1,0:T(8,128)(2,1)S(1)}, u32[]{:S(2)}, u32[]{:S(2)}) collective-permute-start(bf16[512,384]{1,0:T(8,128)(2,1)S(1)} %copy-done.23), channel_id=1, source_target_pairs={{0,16},{16,0},{1,17},{17,1},{2,18},{18,2},{3,19},{19,3},{4,20},{20... | collective-permute-start | bytes 1179656 | tf_op jit(solution)/shard_map/ppermute | solution.py:540
  330.8 46.0 %collective-permute-start.31 = (bf16[96,384]{1,0:T(8,128)(2,1)S(1)}, bf16[96,384]{1,0:T(8,128)(2,1)S(1)}, u32[]{:S(2)}, u32[]{:S(2)}) collective-permute-start(bf16[96,384]{1,0:T(8,128)(2,1)S(1)} %fusion.14), channel_id=1, source_target_pairs={{0,2},{1,3},{2,0},{3,1},{4,6},{5,7},{6,4},{7,5},{8,10},{9,11},{10,... | collective-permute-start | bytes 221192 | tf_op jit(solution)/shard_map/ppermute | solution.py:592
  335.3 18.0 %collective-permute-start.45 = (bf16[768,384]{1,0:T(8,128)(2,1)S(1)}, bf16[768,384]{1,0:T(8,128)(2,1)S(1)}, u32[]{:S(2)}, u32[]{:S(2)}) collective-permute-start(bf16[768,384]{1,0:T(8,128)(2,1)S(1)} %get-tuple-element.63), channel_id=1, source_target_pairs={{0,12},{4,8},{8,4},{12,0},{1,13},{5,9},{9,5},{13,1},{2,14},{6,10},... | collective-permute-start | bytes 1769480 | tf_op jit(solution)/shard_map/ppermute | solution.py:571
  339.6 30.6 %collective-permute-start.44 = (bf16[768,384]{1,0:T(8,128)(2,1)S(1)}, bf16[768,384]{1,0:T(8,128)(2,1)S(1)}, u32[]{:S(2)}, u32[]{:S(2)}) collective-permute-start(bf16[768,384]{1,0:T(8,128)(2,1)S(1)} %get-tuple-element.64), channel_id=1, source_target_pairs={{0,8},{4,12},{8,0},{12,4},{1,9},{5,13},{9,1},{13,5},{2,10},{6,14},... | collective-permute-start | bytes 1769480 | tf_op jit(solution)/shard_map/ppermute | solution.py:571
  342.0 28.8 %collective-permute-start.43 = (bf16[768,384]{1,0:T(8,128)(2,1)S(1)}, bf16[768,384]{1,0:T(8,128)(2,1)S(1)}, u32[]{:S(2)}, u32[]{:S(2)}) collective-permute-start(bf16[768,384]{1,0:T(8,128)(2,1)S(1)} %get-tuple-element.62), channel_id=1, source_target_pairs={{0,4},{4,0},{8,12},{12,8},{1,5},{5,1},{9,13},{13,9},{2,6},{6,2},{1... | collective-permute-start | bytes 1769480 | tf_op jit(solution)/shard_map/ppermute | solution.py:571
  353.2 55.7 %collective-permute-start.35 = (bf16[1152,384]{1,0:T(8,128)(2,1)S(1)}, bf16[1152,384]{1,0:T(8,128)(2,1)S(1)}, u32[]{:S(2)}, u32[]{:S(2)}) collective-permute-start(bf16[1152,384]{1,0:T(8,128)(2,1)S(1)} %get-tuple-element.66), channel_id=1, source_target_pairs={{16,28},{20,24},{24,20},{28,16},{17,29},{21,25},{25,21},{29,17},{1... | collective-permute-start | bytes 2654216 | tf_op jit(solution)/shard_map/ppermute | solution.py:571
  370.1 40.7 %collective-permute-start.34 = (bf16[1152,384]{1,0:T(8,128)(2,1)S(1)}, bf16[1152,384]{1,0:T(8,128)(2,1)S(1)}, u32[]{:S(2)}, u32[]{:S(2)}) collective-permute-start(bf16[1152,384]{1,0:T(8,128)(2,1)S(1)} %get-tuple-element.67), channel_id=1, source_target_pairs={{16,24},{20,28},{24,16},{28,20},{17,25},{21,29},{25,17},{29,21},{1... | collective-permute-start | bytes 2654216 | tf_op jit(solution)/shard_map/ppermute | solution.py:571
  370.9 40.0 %collective-permute-start.33 = (bf16[1152,384]{1,0:T(8,128)(2,1)S(1)}, bf16[1152,384]{1,0:T(8,128)(2,1)S(1)}, u32[]{:S(2)}, u32[]{:S(2)}) collective-permute-start(bf16[1152,384]{1,0:T(8,128)(2,1)S(1)} %get-tuple-element.65), channel_id=1, source_target_pairs={{16,20},{20,16},{24,28},{28,24},{17,21},{21,17},{25,29},{29,25},{1... | collective-permute-start | bytes 2654216 | tf_op jit(solution)/shard_map/ppermute | solution.py:571
  386.2 11.4 %collective-permute-start.47 = (bf16[192,384]{1,0:T(8,128)(2,1)S(1)}, bf16[192,384]{1,0:T(8,128)(2,1)S(1)}, u32[]{:S(2)}, u32[]{:S(2)}) collective-permute-start(bf16[192,384]{1,0:T(8,128)(2,1)S(1)} %get-tuple-element.98), channel_id=1, source_target_pairs={{0,2},{1,3},{2,0},{3,1},{4,6},{5,7},{6,4},{7,5},{8,10},{9,11},{10,... | collective-permute-start | bytes 442376 | tf_op jit(solution)/shard_map/ppermute | solution.py:582
  400.3 13.9 %collective-permute-start.51 = (bf16[192,384]{1,0:T(8,128)(2,1)S(1)}, bf16[192,384]{1,0:T(8,128)(2,1)S(1)}, u32[]{:S(2)}, u32[]{:S(2)}) collective-permute-start(bf16[192,384]{1,0:T(8,128)(2,1)S(1)} %fusion.11), channel_id=1, source_target_pairs={{0,2},{1,3},{2,0},{3,1},{4,6},{5,7},{6,4},{7,5},{8,10},{9,11},{10,... | collective-permute-start | bytes 442376 | tf_op jit(solution)/shard_map/ppermute | solution.py:592
  (57 other events, 696.7 us)
Sparse Core Ops, SparseCore 0:
  22.9 32.1 all-gather.5

commit v2 on v1

v2 whole, which is shorter than its diff:
```python
import functools

import jax
import jax.numpy as jnp
from jax import lax
from jax.experimental import pallas as pl
from jax.experimental.pallas import tpu as pltpu
from jax.sharding import PartitionSpec as P

EPSILON = 1e-06
F32 = jnp.float32
BF16 = jnp.bfloat16
VMEM_BYTES = 58 * 1024 * 1024
LOW_BITS = 6
LOW = 1 << LOW_BITS
HIGH = 16


def dot(a, b):
    return jnp.dot(a, b, preferred_element_type=F32)


def dot_rows(a, b):
    return lax.dot_general(a, b, (((1,), (1,)), ((), ())), preferred_element_type=F32)


def dot_cols(a, b):
    return lax.dot_general(a, b, (((0,), (0,)), ((), ())), preferred_element_type=F32)


def norm_parts(v):
    centre = v - jnp.mean(v, axis=-1, keepdims=True)
    inverse = lax.rsqrt(jnp.mean(centre * centre, axis=-1, keepdims=True) + EPSILON)
    return centre * inverse, inverse


def norm_back(d_normed, scale, normed, inverse):
    d = d_normed * (1.0 + scale)
    return inverse * (
        d
        - jnp.mean(d, axis=-1, keepdims=True)
        - normed * jnp.mean(d * normed, axis=-1, keepdims=True)
    )


def col_sum(v):
    return jnp.sum(v, axis=0, keepdims=True)


def half_masks(width):
    lane = lax.broadcasted_iota(jnp.int32, (1, width), 1)
    first = jnp.where(lane < width // 2, 1.0, 0.0)
    return first.astype(BF16), (1.0 - first).astype(BF16)


def block_targets(mats, off, q):
    w_qkv, w_proj, w_fc1, w_fc2 = mats
    model = w_proj.shape[0]
    targets = [w_qkv.at[pl.ds(off, q), pl.ds(c * model, model)] for c in range(3)]
    targets.append(w_proj.at[pl.ds(off, q), :])
    targets += [w_fc1.at[pl.ds(off, q), pl.ds(c * model, model)] for c in range(4)]
    targets.append(w_fc2.at[pl.ds(off * 4, 4 * q), :])
    return targets


def weight_count(refs):
    return 9 if refs == 2 else 31


def weight_loads(layer, section, shard, refs, mats, sems):
    model = mats[1].shape[0]
    plans = []
    own_layer = section == layer
    if len(refs) == 2:
        targets = block_targets(mats, 0, model)
        for i, target in enumerate(targets):
            rows = pl.ds(i * model, 4 * model if i == 8 else model)
            plans.append((own_layer, refs[0].at[rows, :], refs[1].at[rows, :], target, i < 4))
    else:
        own, other, mine, theirs = refs[:4], refs[4:8], refs[8:11], refs[11:14]
        q = own[0].shape[0]
        off = pl.multiple_of(shard * q, 16)
        whole = [
            mats[0].at[pl.ds(off, q), :], mats[1].at[pl.ds(off, q), :],
            mats[2].at[pl.ds(off, q), :], mats[3].at[pl.ds(pl.multiple_of(off * 4, 16), 4 * q), :],
        ]
        for i in range(4):
            plans.append((own_layer, own[i], other[i], whole[i], i < 2))
        for p in range(1, 4):
            targets = block_targets(mats, pl.multiple_of((shard ^ p) * q, 16), q)
            for i, target in enumerate(targets):
                at = i if i < 6 else i - 6
                rows = pl.ds(at * q, 4 * q if i == 8 else q)
                half = 0 if i < 6 else 1
                plans.append((section == half, mine[p - 1].at[rows, :], theirs[p - 1].at[rows, :], target, i < 4))
    waits = ([], [])
    for i, (condition, first, second, target, early) in enumerate(plans):
        one = pltpu.make_async_copy(first, target, sems.at[i])
        two = pltpu.make_async_copy(second, target, sems.at[i])
        pl.when(condition)(one.start)
        pl.when(jnp.logical_not(condition))(two.start)
        waits[0 if early else 1].append(one)
    return waits


def wait_all(copies):
    for copy in copies:
        copy.wait()


def pack_attention(out_ref, g_qkv, g_proj, shard, pieces, stride, first):
    model = g_proj.shape[0]
    q = model // pieces
    for p in range(pieces):
        off = pl.multiple_of((shard ^ p) * q, 16) if pieces > 1 else 0
        at = (stride * p + first) * q
        for c in range(3):
            out_ref[at + c * q : at + (c + 1) * q, :] = g_qkv[pl.ds(off, q), c * model : (c + 1) * model]
        out_ref[at + 3 * q : at + 4 * q, :] = g_proj[pl.ds(off, q), :]


def pack_mlp(out_ref, g_fc1, g_fc2, shard, pieces, stride, first):
    model = g_fc1.shape[0]
    q = model // pieces
    for p in range(pieces):
        off = pl.multiple_of((shard ^ p) * q, 16) if pieces > 1 else 0
        at = (stride * p + first) * q
        for c in range(4):
            out_ref[at + c * q : at + (c + 1) * q, :] = g_fc1[pl.ds(off, q), c * model : (c + 1) * model]
        out_ref[at + 4 * q : at + 8 * q, :] = g_fc2[pl.ds(pl.multiple_of(off * 4, 16), 4 * q), :]


class Modulation:
    def __init__(self, line, model):
        self.line, self.model = line, model

    def __getitem__(self, key):
        b, rows, _ = key
        return self.line[:, pl.ds(pl.multiple_of((6 * b + rows.start) * self.model, 128), self.model)]


def bias_at(line, samples, model, start, size):
    return line[:, (6 * samples + start) * model : (6 * samples + start + size) * model]


def attention_forward(b, length, h, mod, bias, w_qkv, w_proj, b_qkv, b_proj, qkv, probs, att, branch, middle):
    model = w_proj.shape[0]
    heads = bias.shape[0]
    pair = 2 * model // heads
    rows = pl.ds(pl.multiple_of(b * length, length), length)
    masks = half_masks(pair)
    x = h[rows, :].astype(F32)
    normed, _ = norm_parts(x)
    normed_low = (normed * (1.0 + mod[b, 1:2, :]) + mod[b, 0:1, :]).astype(BF16)
    qkv[rows, :] = (dot(normed_low, w_qkv[...]) + b_qkv[...]).astype(BF16)
    for j in range(heads // 2):
        q_pair = qkv[rows, j * pair : (j + 1) * pair] * BF16((pair // 2) ** (-0.5))
        k_pair = qkv[rows, model + j * pair : model + (j + 1) * pair]
        v_pair = qkv[rows, 2 * model + j * pair : 2 * model + (j + 1) * pair]
        total = None
        for e in range(2):
            scores = dot_rows(q_pair * masks[e], k_pair) + bias[2 * j + e].astype(F32)
            raised = jnp.exp(scores - jnp.max(scores, axis=-1, keepdims=True))
            p = (raised * (1.0 / jnp.sum(raised, axis=-1, keepdims=True))).astype(BF16)
            probs[b, 2 * j + e] = p
            part = dot(p, v_pair * masks[e])
            total = part if total is None else total + part
        att[rows, j * pair : (j + 1) * pair] = total.astype(BF16)
    out = dot(att[rows, :], w_proj[...]) + b_proj[...]
    branch[rows, :] = out
    middle[rows, :] = x + mod[b, 2:3, :] * out


def mlp_forward(b, length, middle, mod, w_fc1, w_fc2, b_fc1, b_fc2, act, slope, out_branch, layer_out):
    model = w_fc1.shape[0]
    rows = pl.ds(pl.multiple_of(b * length, length), length)
    mid = middle[rows, :]
    normed, _ = norm_parts(mid)
    normed_low = (normed * (1.0 + mod[b, 4:5, :]) + mod[b, 3:4, :]).astype(BF16)
    total = b_fc2[...]
    for c in range(w_fc1.shape[1] // model):
        cols = slice(c * model, (c + 1) * model)
        v = dot(normed_low, w_fc1[:, cols]) + b_fc1[:, cols]
        square = v * v
        t = jnp.tanh(0.7978845608028654 * v * (1.0 + 0.044715 * square))
        half = 0.5 * (1.0 + t)
        a = (v * half).astype(BF16)
        act[rows, cols] = a
        slope[rows, cols] = (
            half
            + 0.5 * v * (1.0 - t * t) * (0.7978845608028654 + (3 * 0.044715 * 0.7978845608028654) * square)
        ).astype(BF16)
        total = total + dot(a, w_fc2[cols, :])
    out_branch[rows, :] = total
    layer_out[rows, :] = (mid + mod[b, 5:6, :] * total).astype(layer_out.dtype)


def mlp_backward(b, length, grad, middle, mod, w_fc1, w_fc2, act, slope, out_branch, d_middle, small, normed_low, d_pre, d_ob):
    model = w_fc1.shape[0]
    rows = pl.ds(pl.multiple_of(b * length, length), length)
    g = grad[rows, :].astype(F32)
    small[b, 2:3, :] = col_sum(g * out_branch[rows, :])
    d_out = g * mod[b, 5:6, :]
    d_out_low = d_out.astype(BF16)
    d_ob[rows, :] = d_out_low
    small[b, 3:4, :] = col_sum(d_out_low.astype(F32))
    normed, inverse = norm_parts(middle[rows, :])
    normed_low[rows, :] = (normed * (1.0 + mod[b, 4:5, :]) + mod[b, 3:4, :]).astype(BF16)
    d_normed = None
    for c in range(w_fc1.shape[1] // model):
        cols = slice(c * model, (c + 1) * model)
        d_act = dot_rows(d_out_low, w_fc2[cols, :])
        d_low = (d_act * slope[rows, cols].astype(F32)).astype(BF16)
        d_pre[rows, cols] = d_low
        small[b, 4 + c : 5 + c, :] = col_sum(d_low.astype(F32))
        part = dot_rows(d_low, w_fc1[:, cols])
        d_normed = part if d_normed is None else d_normed + part
    small[b, 0:1, :] = col_sum(d_normed)
    small[b, 1:2, :] = col_sum(d_normed * normed)
    d_middle[rows, :] = norm_back(d_normed, mod[b, 4:5, :], normed, inverse) + g


def mlp_weight_grads(normed_low, d_pre, act, d_ob, g_fc1, g_fc2):
    model = g_fc1.shape[0]
    for c in range(g_fc1.shape[1] // model):
        cols = slice(c * model, (c + 1) * model)
        g_fc1[:, cols] = dot_cols(normed_low[...], d_pre[:, cols]).astype(BF16)
        g_fc2[cols, :] = dot_cols(act[:, cols], d_ob[...]).astype(BF16)


def attention_backward(b, length, h, mod, w_qkv, w_proj, qkv, probs, att, branch, d_middle, d_in, small, score_sum, normed_low, d_qkv, d_br):
    model = w_proj.shape[0]
    heads = probs.shape[1]
    pair = 2 * model // heads
    scale = F32((pair // 2) ** (-0.5))
    rows = pl.ds(pl.multiple_of(b * length, length), length)
    masks = half_masks(pair)
    d_mid = d_middle[rows, :]
    small[b, 2:3, :] = col_sum(d_mid * branch[rows, :])
    d_branch = (d_mid * mod[b, 2:3, :]).astype(BF16)
    d_br[rows, :] = d_branch
    small[b, 5:6, :] = col_sum(d_branch.astype(F32))
    d_att = dot_rows(d_branch, w_proj[...]).astype(BF16)
    for j in range(heads // 2):
        q_pair = qkv[rows, j * pair : (j + 1) * pair]
        k_pair = qkv[rows, model + j * pair : model + (j + 1) * pair]
        v_pair = qkv[rows, 2 * model + j * pair : 2 * model + (j + 1) * pair]
        d_pair = d_att[:, j * pair : (j + 1) * pair]
        d_q = d_k = d_v = None
        for e in range(2):
            p_low = probs[b, 2 * j + e]
            p = p_low.astype(F32)
            d_here = d_pair * masks[e]
            d_p = dot_rows(d_here, v_pair)
            d_s = (p * (d_p - jnp.sum(d_p * p, axis=-1, keepdims=True))).astype(BF16)
            score_sum[2 * j + e] += d_s.astype(F32)
            v_part = dot_cols(p_low, d_here)
            q_part = dot(d_s, k_pair * masks[e])
            k_part = dot_cols(d_s, q_pair * masks[e])
            d_v = v_part if d_v is None else d_v + v_part
            d_q = q_part if d_q is None else d_q + q_part
            d_k = k_part if d_k is None else d_k + k_part
        d_qkv[rows, j * pair : (j + 1) * pair] = (d_q * scale).astype(BF16)
        d_qkv[rows, model + j * pair : model + (j + 1) * pair] = (d_k * scale).astype(BF16)
        d_qkv[rows, 2 * model + j * pair : 2 * model + (j + 1) * pair] = d_v.astype(BF16)
    small[b, 3:4, :] = col_sum(d_qkv[rows, :model].astype(F32))
    small[b, 4:5, :] = col_sum(d_qkv[rows, 2 * model :].astype(F32))
    small[b, 6:8, :] = jnp.zeros((2, model), F32)
    d_normed = dot_rows(d_qkv[rows, :], w_qkv[...])
    normed, inverse = norm_parts(h[rows, :].astype(F32))
    normed_low[rows, :] = (normed * (1.0 + mod[b, 1:2, :]) + mod[b, 0:1, :]).astype(BF16)
    small[b, 0:1, :] = col_sum(d_normed)
    small[b, 1:2, :] = col_sum(d_normed * normed)
    d_in[rows, :] = (norm_back(d_normed, mod[b, 1:2, :], normed, inverse) + d_mid).astype(d_in.dtype)


def attention_weight_grads(normed_low, d_qkv, att, d_br, g_qkv, g_proj):
    model = g_proj.shape[0]
    for c in range(3):
        cols = slice(c * model, (c + 1) * model)
        g_qkv[:, cols] = dot_cols(normed_low[...], d_qkv[:, cols]).astype(BF16)
    g_proj[...] = dot_cols(att[...], d_br[...]).astype(BF16)


def each_sample(count, body):
    def step(b, carry):
        body(b)
        return carry

    lax.fori_loop(0, count, step, 0)


def set_line(line, layer, section, own_line, other_line):
    line[...] = jnp.where(section == layer, own_line[...], other_line[...])


def start_bias(layer, section, own, other, bias, sem):
    one = pltpu.make_async_copy(own, bias, sem)
    two = pltpu.make_async_copy(other, bias, sem)
    pl.when(section == layer)(one.start)
    pl.when(section != layer)(two.start)
    return one


def line_biases(line, samples, model):
    q_bias = bias_at(line, samples, model, 0, 1)
    v_bias = bias_at(line, samples, model, 1, 1)
    b_qkv = jnp.concatenate([q_bias, jnp.zeros_like(q_bias), v_bias], axis=1)
    return b_qkv, bias_at(line, samples, model, 2, 1), bias_at(line, samples, model, 3, 4), bias_at(line, samples, model, 7, 1)


def forward_kernel(layer, length, n_weights, pos, h, own_line, other_line, own_bias, other_bias, *rest):
    refs, rest = rest[:n_weights], rest[n_weights:]
    (qkv, probs, att, branch, middle, act, slope, out_branch, layer_out,
     w_qkv, w_proj, w_fc1, w_fc2, bias, line, sems) = rest
    section, shard = pos[0], pos[1]
    model = h.shape[1]
    samples = h.shape[0] // length
    got_bias = start_bias(layer, section, own_bias, other_bias, bias, sems.at[weight_count(n_weights)])
    for_attention, for_mlp = weight_loads(layer, section, shard, refs, (w_qkv, w_proj, w_fc1, w_fc2), sems)
    set_line(line, layer, section, own_line, other_line)
    mod = Modulation(line, model)
    b_qkv, b_proj, b_fc1, b_fc2 = line_biases(line, samples, model)
    got_bias.wait()
    wait_all(for_attention)
    each_sample(
        samples,
        lambda b: attention_forward(b, length, h, mod, bias, w_qkv, w_proj, b_qkv, b_proj, qkv, probs, att, branch, middle),
    )
    wait_all(for_mlp)
    each_sample(
        samples,
        lambda b: mlp_forward(b, length, middle, mod, w_fc1, w_fc2, b_fc1, b_fc2, act, slope, out_branch, layer_out),
    )


def both_kernel(layer, pieces, length, n_weights, pos, h, grad, own_line, other_line, own_bias, other_bias, *rest):
    refs, rest = rest[:n_weights], rest[n_weights:]
    (layer_out, d_in, small_a, small_m, scores, pack,
     w_qkv, w_proj, w_fc1, w_fc2, bias, line, qkv, probs, att, branch, middle, act, slope, out_branch,
     d_middle, normed_low, d_pre, d_ob, d_qkv, score_sum, g_qkv, g_proj, g_fc1, g_fc2, sems) = rest
    section, shard = pos[0], pos[1]
    model = h.shape[1]
    samples = h.shape[0] // length
    got_bias = start_bias(layer, section, own_bias, other_bias, bias, sems.at[weight_count(n_weights)])
    for_attention, for_mlp = weight_loads(layer, section, shard, refs, (w_qkv, w_proj, w_fc1, w_fc2), sems)
    set_line(line, layer, section, own_line, other_line)
    mod = Modulation(line, model)
    b_qkv, b_proj, b_fc1, b_fc2 = line_biases(line, samples, model)
    got_bias.wait()
    wait_all(for_attention)
    each_sample(
        samples,
        lambda b: attention_forward(b, length, h, mod, bias, w_qkv, w_proj, b_qkv, b_proj, qkv, probs, att, branch, middle),
    )
    wait_all(for_mlp)

    def mlp(b):
        mlp_forward(b, length, middle, mod, w_fc1, w_fc2, b_fc1, b_fc2, act, slope, out_branch, layer_out)
        mlp_backward(b, length, grad, middle, mod, w_fc1, w_fc2, act, slope, out_branch, d_middle, small_m, normed_low, d_pre, d_ob)

    each_sample(samples, mlp)
    mlp_weight_grads(normed_low, d_pre, act, d_ob, g_fc1, g_fc2)
    pack_mlp(pack, g_fc1, g_fc2, shard, pieces, 12, 4)
    score_sum[...] = jnp.zeros_like(score_sum)
    each_sample(
        samples,
        lambda b: attention_backward(b, length, h, mod, w_qkv, w_proj, qkv, probs, att, branch, d_middle, d_in, small_a, score_sum, normed_low, d_qkv, d_ob),
    )
    scores[...] = score_sum[...].astype(BF16)
    attention_weight_grads(normed_low, d_qkv, att, d_ob, g_qkv, g_proj)
    pack_attention(pack, g_qkv, g_proj, shard, pieces, 12, 0)


def backward_mlp_kernel(layer, pieces, length, n_weights, pos, grad, middle, own_line, other_line, act, slope, out_branch, *rest):
    refs, rest = rest[:n_weights], rest[n_weights:]
    (d_middle, small, pack,
     w_qkv, w_proj, w_fc1, w_fc2, line, normed_low, d_pre, d_ob, g_fc1, g_fc2, sems) = rest
    section, shard = pos[0], pos[1]
    for_attention, for_mlp = weight_loads(layer, section, shard, refs, (w_qkv, w_proj, w_fc1, w_fc2), sems)
    set_line(line, layer, section, own_line, other_line)
    mod = Modulation(line, middle.shape[1])
    wait_all(for_mlp)
    each_sample(
        middle.shape[0] // length,
        lambda b: mlp_backward(b, length, grad, middle, mod, w_fc1, w_fc2, act, slope, out_branch, d_middle, small, normed_low, d_pre, d_ob),
    )
    mlp_weight_grads(normed_low, d_pre, act, d_ob, g_fc1, g_fc2)
    pack_mlp(pack, g_fc1, g_fc2, shard, pieces, 8, 0)
    wait_all(for_attention)


def backward_attention_kernel(layer, pieces, length, n_weights, n_after, pos, h, own_line, other_line, qkv, probs, att, branch, d_middle, *rest):
    refs, rest = rest[:n_weights], rest[n_weights + n_after :]
    (d_in, small, scores, pack,
     w_qkv, w_proj, w_fc1, w_fc2, line, normed_low, d_qkv, d_br, score_sum, g_qkv, g_proj, sems) = rest
    section, shard = pos[0], pos[1]
    for_attention, for_mlp = weight_loads(layer, section, shard, refs, (w_qkv, w_proj, w_fc1, w_fc2), sems)
    set_line(line, layer, section, own_line, other_line)
    mod = Modulation(line, h.shape[1])
    score_sum[...] = jnp.zeros_like(score_sum)
    wait_all(for_attention)
    each_sample(
        h.shape[0] // length,
        lambda b: attention_backward(b, length, h, mod, w_qkv, w_proj, qkv, probs, att, branch, d_middle, d_in, small, score_sum, normed_low, d_qkv, d_br),
    )
    scores[...] = score_sum[...].astype(BF16)
    attention_weight_grads(normed_low, d_qkv, att, d_br, g_qkv, g_proj)
    pack_attention(pack, g_qkv, g_proj, shard, pieces, 4, 0)
    wait_all(for_mlp)


def call(kernel, pos, operands, in_hbm, outs, scratch, sems=0):
    specs = [pl.BlockSpec(memory_space=pltpu.SMEM)]
    specs += [pl.BlockSpec(memory_space=pltpu.VMEM) for _ in operands]
    specs += [pl.BlockSpec(memory_space=pl.ANY) for _ in in_hbm]
    shapes = [pltpu.VMEM(shape, dtype) for shape, dtype in scratch]
    if sems:
        shapes.append(pltpu.SemaphoreType.DMA((sems,)))
    return pl.pallas_call(
        kernel,
        out_shape=[jax.ShapeDtypeStruct(shape, dtype) for shape, dtype in outs],
        in_specs=specs,
        out_specs=[pl.BlockSpec(memory_space=pltpu.VMEM) for _ in outs],
        scratch_shapes=shapes,
        compiler_params=pltpu.CompilerParams(vmem_limit_bytes=VMEM_BYTES),
    )(pos, *operands, *in_hbm)


class Sizes:
    def __init__(self, samples, length, model, heads, hidden, pieces):
        self.samples, self.length, self.model = samples, length, model
        self.heads, self.hidden, self.pieces = heads, hidden, pieces
        self.rows = samples * length
        self.line = ((1, (6 * samples + 4 + hidden // model) * model), F32)
        self.weights = [
            ((model, 3 * model), BF16), ((model, model), BF16), ((model, hidden), BF16), ((hidden, model), BF16),
        ]
        self.bias = ((heads, length, length), BF16)
        self.probs = ((samples, heads, length, length), BF16)
        self.low = ((self.rows, model), BF16)
        self.full = ((self.rows, model), F32)
        self.qkv = ((self.rows, 3 * model), BF16)
        self.wide = ((self.rows, hidden), BF16)
        self.small = ((samples, 8, model), F32)


def forward_layer(layer, z, pos, h, lines, biases, weights):
    def kernel(pos_ref, h_ref, a, b, *rest):
        forward_kernel(layer, z.length, len(weights), pos_ref, h_ref, a, b, *rest)

    return call(
        kernel, pos, (h, *lines), (*biases, *weights),
        [z.qkv, z.probs, z.low, z.full, z.full, z.wide, z.wide, z.full, z.low],
        [*z.weights, z.bias, z.line], weight_count(len(weights)) + 1,
    )


def both_ways(layer, z, pos, h, grad, lines, biases, weights):
    return call(
        functools.partial(both_kernel, layer, z.pieces, z.length, len(weights)),
        pos, (h, grad, *lines), (*biases, *weights),
        [z.low, z.low, z.small, z.small, z.bias, ((12 * z.model, z.model), BF16)],
        [*z.weights, z.bias, z.line, z.qkv, z.probs, z.low, z.full, z.full, z.wide, z.wide, z.full,
         z.full, z.low, z.wide, z.low, z.qkv, (z.bias[0], F32), *z.weights],
        weight_count(len(weights)) + 1,
    )


def backward_mlp(layer, z, pos, grad, middle, lines, act, slope, out_branch, weights):
    return call(
        functools.partial(backward_mlp_kernel, layer, z.pieces, z.length, len(weights)),
        pos, (grad, middle, *lines, act, slope, out_branch), weights,
        [z.full, z.small, ((8 * z.model, z.model), BF16)],
        [*z.weights, z.line, z.low, z.wide, z.low, *z.weights[2:]],
        weight_count(len(weights)),
    )


def backward_attention(layer, z, pos, h, lines, qkv, probs, att, branch, d_middle, weights, after):
    return call(
        functools.partial(backward_attention_kernel, layer, z.pieces, z.length, len(weights), len(after)),
        pos, (h, *lines, qkv, probs, att, branch, d_middle), (*weights, *after),
        [z.full, z.small, z.bias, ((4 * z.model, z.model), BF16)],
        [*z.weights, z.line, z.low, z.qkv, z.low, (z.bias[0], F32), *z.weights[:2]],
        weight_count(len(weights)),
    )


def half_kernel(pos, *refs):
    own, other, outs = refs[:4], refs[4:8], refs[8:]
    section = pos[0]
    model = outs[0].shape[1]
    q = own[0].shape[0]
    for layer in range(2):
        out = outs[layer]
        for source, here in ((own, section == layer), (other, section != layer)):
            qkv, proj, fc1, fc2 = source

            @pl.when(jnp.logical_and(here, section == 0))
            def _():
                for c in range(3):
                    out[c * q : (c + 1) * q, :] = qkv[:, c * model : (c + 1) * model]
                out[3 * q : 4 * q, :] = proj[...]
                for c in range(2):
                    out[(4 + c) * q : (5 + c) * q, :] = fc1[:, c * model : (c + 1) * model]

            @pl.when(jnp.logical_and(here, section == 1))
            def _():
                for c in range(2):
                    out[c * q : (c + 1) * q, :] = fc1[:, (2 + c) * model : (3 + c) * model]
                out[2 * q : 6 * q, :] = fc2[...]


def halves(pos, own, other):
    q, model = own[1].shape
    shape = ((6 * q, model), BF16)
    return call(half_kernel, pos, (*own, *other), (), [shape, shape], [])


def lookup_kernel(table, index, out, work):
    heads, length = out.shape[0], out.shape[1]
    high_count = table.shape[0] // 8
    values = table[...]
    low_id = lax.broadcasted_iota(jnp.int32, (LOW, length), 0)

    def step(i, carry):
        block = index[pl.ds(pl.multiple_of(i * 8, 8), 8), :]
        for r in range(8):
            entry = block[r : r + 1, :]
            picks = jnp.where(low_id == (entry & (LOW - 1)), 1.0, 0.0).astype(BF16)
            found = dot(values, picks).reshape(high_count, 8, length)
            high = jnp.broadcast_to(entry >> LOW_BITS, (8, length))
            bit = high_count // 2
            while bit:
                chosen = (high & bit) != 0
                found = jnp.where(chosen[None], found[bit : 2 * bit], found[:bit])
                bit //= 2
            for head in range(heads):
                work[head, pl.ds(i * 8 + r, 1), :] = found[0, head : head + 1, :]
        return carry

    lax.fori_loop(0, length // 8, step, 0)
    out[...] = work[...].astype(BF16)


def lookup(table, index):
    heads, entries = table.shape
    high_count = HIGH
    padded = jnp.pad(table, ((0, 8 - heads), (0, high_count * LOW - entries)))
    rows = jnp.transpose(padded.reshape(8, high_count, LOW), (1, 0, 2)).reshape(high_count * 8, LOW)
    length = index.shape[0]
    return pl.pallas_call(
        lookup_kernel,
        out_shape=jax.ShapeDtypeStruct((heads, length, length), BF16),
        scratch_shapes=[pltpu.VMEM((heads, length, length), F32)],
        compiler_params=pltpu.CompilerParams(vmem_limit_bytes=VMEM_BYTES),
    )(rows, index)


def table_kernel(scores_a, scores_b, index, *rest):
    out = rest[-1]
    heads, length = scores_a.shape[0], scores_a.shape[1]
    out[...] = jnp.zeros_like(out)
    low_ids = lax.broadcasted_iota(jnp.int32, (LOW, length), 0)
    high_ids = lax.broadcasted_iota(jnp.int32, (HIGH, length), 0)

    def step(i, carry):
        rows = pl.ds(pl.multiple_of(i * 16, 16), 16)
        entries = index[rows, :]
        block = [scores[head, rows, :].astype(F32) for scores in (scores_a, scores_b) for head in range(heads)]
        total = None
        for r in range(16):
            entry = entries[r : r + 1, :]
            low = jnp.where(low_ids == (entry & (LOW - 1)), 1.0, 0.0).astype(BF16)
            high = high_ids == (entry >> LOW_BITS)
            left = jnp.concatenate([jnp.where(high, part[r : r + 1, :], 0.0) for part in block], axis=0).astype(BF16)
            part = dot_rows(left, low)
            total = part if total is None else total + part
        out[...] += total
        return carry

    lax.fori_loop(0, length // 16, step, 0)


def table_gradients(scores_a, scores_b, index, after):
    heads = scores_a.shape[0]
    total = pl.pallas_call(
        table_kernel,
        out_shape=jax.ShapeDtypeStruct((2 * heads * HIGH, LOW), F32),
        in_specs=[pl.BlockSpec(memory_space=pltpu.VMEM)] * 3 + [pl.BlockSpec(memory_space=pl.ANY)] * len(after),
        out_specs=pl.BlockSpec(memory_space=pltpu.VMEM),
        compiler_params=pltpu.CompilerParams(vmem_limit_bytes=VMEM_BYTES),
    )(scores_a, scores_b, index, *after)
    return total[: heads * HIGH], total[heads * HIGH :]


def swap_section(value):
    return lax.ppermute(value, "section", [(0, 1), (1, 0)])


def pairs_of(count, step):
    return [(i, i ^ step) for i in range(count)]


def by_rank(pieces, rank):
    stack = jnp.stack(pieces)
    count = len(pieces)
    bit = 1
    while bit < count:
        moved = jnp.stack([stack[i ^ bit] for i in range(count)])
        stack = jnp.where((rank & bit) != 0, moved, stack)
        bit *= 2
    return stack


def one_section_pairs(layer, count, step):
    return [(layer * count + i, layer * count + (i ^ step)) for i in range(count)]


def section_sums(pack, layer, shards):
    other = lax.ppermute(pack, "section", [(1 - layer, layer)])
    size = pack.shape[0] // shards
    return [
        pack[p * size : (p + 1) * size].astype(F32) + other[p * size : (p + 1) * size].astype(F32)
        for p in range(shards)
    ]


def send_pieces(sums, layer):
    shards = len(sums)
    low = [x.astype(BF16) for x in sums[1:]]
    got = [
        lax.ppermute(low[p - 1], ("section", "fsdp"), one_section_pairs(layer, shards, p))
        for p in range(1, shards)
    ]
    return low, got


def add_pieces(own, got):
    total = own
    for piece in got:
        total = total + piece.astype(F32)
    return total


def replica_total(total, layer, rank):
    replicas = lax.axis_size("rep")
    size = total.shape[0]
    parts = total.reshape(replicas, size // replicas, -1)
    low_parts = parts.astype(BF16)
    mine = lax.dynamic_index_in_dim(parts, rank, 0, keepdims=False)
    names = ("section", "rep")
    got = [
        lax.ppermute(
            lax.dynamic_index_in_dim(low_parts, rank ^ j, 0, keepdims=False),
            names, one_section_pairs(layer, replicas, j),
        )
        for j in range(1, replicas)
    ]
    mine = add_pieces(mine, got).astype(BF16)
    quarters = [mine] + [
        lax.ppermute(mine, names, one_section_pairs(layer, replicas, j)) for j in range(1, replicas)
    ]
    return by_rank(quarters, rank).reshape(size, -1)


def unpack_attention(pack):
    q = pack.shape[0] // 4
    return jnp.concatenate([pack[c * q : (c + 1) * q] for c in range(3)], axis=1), pack[3 * q :]


def unpack_mlp(pack):
    q = pack.shape[0] // 8
    return jnp.concatenate([pack[c * q : (c + 1) * q] for c in range(4)], axis=1), pack[4 * q :]


def from_peers(value, axis):
    return [lax.ppermute(value, axis, pairs_of(lax.axis_size(axis), p)) for p in range(1, lax.axis_size(axis))]


def pair_sum(values):
    while len(values) > 1:
        values = [values[i] + values[i + 1] for i in range(0, len(values), 2)]
    return values[0]


def per_device(inputs, conditioning, cotangent, micro_sizes, relative_bias_index,
               w_ada, w_qkv, w_proj, w_fc1, w_fc2, b_ada, b_qv, b_proj, b_fc1, b_fc2, bias_table):
    section = lax.axis_index("section")
    shard = lax.axis_index("fsdp")
    rank = lax.axis_index("rep")
    shards, replicas = lax.axis_size("fsdp"), lax.axis_size("rep")
    direct = shards == 4 and replicas == 4
    is_first = section == 0
    samples, length, model = inputs.shape
    heads, entries = bias_table.shape[1:]
    half = samples // 2
    z = Sizes(half, length, model, heads, 4 * model, shards if direct else 1)
    pos = jnp.stack([section, shard]).astype(jnp.int32)

    def mine(first, second):
        return jnp.where(is_first, first, second)

    def own_samples(array):
        return lax.dynamic_slice_in_dim(array, section * half, half, 0)

    def in_order(own, other):
        return jnp.where(is_first, jnp.concatenate([own, other]), jnp.concatenate([other, own]))

    own_raw = [w_qkv[0], w_proj[0], w_fc1[0], w_fc2[0]]
    cond_size = conditioning.size
    width = model // shards
    w_ada_all = lax.all_gather(w_ada[0], "fsdp", axis=0, tiled=True)
    if direct:
        row = jnp.concatenate([conditioning.reshape(1, -1), b_ada, b_qv, b_proj, b_fc1, b_fc2], axis=1)
        rows = [row] + from_peers(row, "fsdp")
        other_raw = [swap_section(w) for w in own_raw]
        half0, half1 = halves(pos, own_raw, other_raw)
        got0 = from_peers(half0, "fsdp")
        cond_pieces = jnp.stack([r[0, :cond_size].reshape(samples, model) for r in rows])
        acts = jax.nn.silu(cond_pieces.astype(F32)).astype(BF16)
        acts = lax.dynamic_slice_in_dim(acts, shard * width, width, 2)
        partial = lax.dot_general(acts, w_ada[0], (((2,), (0,)), ((), ())), preferred_element_type=F32)
        modulation = partial[0]
        for p in range(1, shards):
            modulation = modulation + lax.ppermute(partial[p], "fsdp", pairs_of(shards, p))
        got1 = from_peers(half1, "fsdp")
        weights0 = own_raw + other_raw + got0 + [swap_section(w) for w in got0]
        weights1 = own_raw + other_raw + got1 + [swap_section(w) for w in got1]
        bias_rows = by_rank([r[0, cond_size:] for r in rows], shard)
    else:
        row = jnp.concatenate([b_ada, b_qv, b_proj, b_fc1, b_fc2], axis=1)
        bias_rows = lax.all_gather(row[0], "fsdp", axis=0)
        whole = [lax.all_gather(w, "fsdp", axis=0, tiled=True) for w in own_raw]
        own_whole = jnp.concatenate(
            [whole[0][:, c * model : (c + 1) * model] for c in range(3)] + [whole[1]]
            + [whole[2][:, c * model : (c + 1) * model] for c in range(4)] + [whole[3]]
        )
        weights0 = weights1 = [own_whole, swap_section(own_whole)]
        acts = jax.nn.silu(conditioning.astype(F32)).astype(BF16)
        modulation = dot(acts, w_ada_all)
    cuts = [b_ada.shape[1], b_qv.shape[1], b_proj.shape[1], b_fc1.shape[1], b_fc2.shape[1]]
    biases, at = [], 0
    for cut in cuts:
        biases.append(bias_rows[:, at : at + cut].reshape(1, -1).astype(F32))
        at += cut
    modulation = modulation + biases[0]
    other_samples = lax.dynamic_slice_in_dim(modulation, (1 - section) * half, half, 0)
    own_line = jnp.concatenate([own_samples(modulation).reshape(1, -1)] + biases[1:], axis=1)
    other_line = swap_section(jnp.concatenate([other_samples.reshape(1, -1)] + biases[1:], axis=1))
    lines = (own_line, other_line)
    bias_own = lookup(bias_table[0], relative_bias_index)
    bias_heads = (bias_own, swap_section(bias_own))

    live = (jnp.arange(half)[:, None, None] < lax.dynamic_index_in_dim(micro_sizes[0], section, 0)).astype(BF16)
    h0 = own_samples(inputs).reshape(half * length, model)
    grad1 = (own_samples(cotangent) * live).reshape(half * length, model)

    qkv, probs, att, branch, middle, act, slope, out_branch, h1 = forward_layer(0, z, pos, h0, lines, bias_heads, weights0)
    out1, d_h1, small_a1, small_m1, scores1, pack1 = both_ways(1, z, pos, h1, grad1, lines, bias_heads, weights1)
    d_middle, small_m0, pack_m0 = backward_mlp(0, z, pos, d_h1, middle, lines, act, slope, out_branch, weights0)
    if direct:
        sums1 = section_sums(pack1, 1, shards)
        low1, got1 = send_pieces(sums1, 1)
        after = low1
    else:
        after = []
    d_h0, small_a0, scores0, pack_a0 = backward_attention(
        0, z, pos, h0, lines, qkv, probs, att, branch, d_middle, weights0, after
    )

    if direct:
        sums_m0 = section_sums(pack_m0, 0, shards)
        low_m0, got_m0 = send_pieces(sums_m0, 0)
        sums_a0 = section_sums(pack_a0, 0, shards)
        low_a0, got_a0 = send_pieces(sums_a0, 0)
        done1 = replica_total(add_pieces(sums1[0], got1), 1, rank)
        total0 = jnp.concatenate([add_pieces(sums_a0[0], got_a0), add_pieces(sums_m0[0], got_m0)])
        done0 = replica_total(total0, 0, rank)
        done = mine(done0, done1).astype(F32)
        g_qkv, g_proj = unpack_attention(done[:model])
        g_fc1, g_fc2 = unpack_mlp(done[model:])
        after = got1 + low_a0 + low_m0
    else:
        pack0 = jnp.concatenate([pack_a0, pack_m0])
        total = (mine(pack0, pack1).astype(F32) + swap_section(mine(pack1, pack0)).astype(F32)).astype(BF16)
        grads = unpack_attention(total[: 4 * model]) + unpack_mlp(total[4 * model :])
        grads = [lax.psum_scatter(g, "fsdp", scatter_dimension=0, tiled=True) for g in grads]
        g_qkv, g_proj, g_fc1, g_fc2 = [g.astype(F32) for g in lax.psum(tuple(grads), "rep")]

    other_out = swap_section(mine(out1, h1))
    activations = in_order(mine(h1, out1).reshape(half, length, model), other_out.reshape(half, length, model))
    other_in = swap_section(mine(d_h1, d_h0.astype(BF16)))
    input_grads = in_order(
        mine(d_h0, d_h1.astype(F32)).reshape(half, length, model),
        other_in.astype(F32).reshape(half, length, model),
    )

    tables = table_gradients(scores0, scores1, relative_bias_index, after)
    smalls = [
        jnp.concatenate([small_a0[:, :3], small_m0, small_a0[:, 3:]], axis=1),
        jnp.concatenate([small_a1[:, :3], small_m1, small_a1[:, 3:]], axis=1),
    ]
    small = in_order(mine(smalls[0], smalls[1]), swap_section(mine(smalls[1], smalls[0])))
    table = mine(tables[0], tables[1]) + swap_section(mine(tables[1], tables[0]))
    low = small[:, :6].astype(BF16)
    w_rows = w_ada_all.reshape(model, 6, model)
    d_act = sum(dot_rows(low[:, i], w_rows[:, i]) for i in range(6))
    cond = conditioning.astype(F32)
    gate = jax.nn.sigmoid(cond)
    cond_part = d_act * (gate * (1.0 + cond * (1.0 - gate)))
    cond_grad = cond_part + swap_section(cond_part)

    kept = jnp.concatenate([low, conditioning[:, None]], axis=1).reshape(-1, model)
    summed = jnp.concatenate([jnp.sum(small[:, 6:14], axis=0), table.reshape(-1, model)])
    if direct:
        both = jnp.concatenate([kept, summed.astype(BF16)])
        plane = [both] + from_peers(both, "fsdp")
        count = kept.shape[0]
        summed = pair_sum([p[count:].astype(F32) for p in plane])
        both = jnp.concatenate([p[:count] for p in plane] + [summed.astype(BF16)])
        every = [both] + from_peers(both, "rep")
        count = count * shards
        summed = pair_sum([p[count:].astype(F32) for p in every])
        kept = by_rank([p[:count] for p in every], rank).reshape(-1, 7, model)
    else:
        kept = lax.all_gather(kept, ("fsdp", "rep"), axis=0, tiled=True).reshape(-1, 7, model)
        summed = lax.psum(summed, ("fsdp", "rep"))
    act_all = jax.nn.silu(kept[:, 6].astype(F32)).astype(BF16)
    act_cols = lax.dynamic_slice_in_dim(act_all, shard * width, width, 1)
    g_ada = jnp.concatenate([dot_cols(act_cols, kept[:, i]) for i in range(6)], axis=1)
    g_b_ada = jnp.sum(kept[:, :6].astype(F32), axis=0).reshape(-1)
    g_b_fc2, g_b_fc1 = summed[0], summed[1:5].reshape(-1)
    g_b_qv, g_b_proj = summed[5:7].reshape(-1), summed[7]
    g_table = summed[8:].reshape(heads, HIGH * LOW)[:, :entries]

    def own_part(vector):
        size = vector.shape[0] // shards
        return lax.dynamic_slice_in_dim(vector, shard * size, size, 0)[None]

    return (
        activations[None], input_grads[None], cond_grad,
        g_ada[None], g_qkv[None], g_proj[None], g_fc1[None], g_fc2[None],
        own_part(g_b_ada), own_part(g_b_qv), own_part(g_b_proj), own_part(g_b_fc1), own_part(g_b_fc2),
        g_table[None],
    )


def solution(mesh):
    batch = ("fsdp", "rep")
    matrix = P("section", "fsdp", None)
    vector = P("section", "fsdp")
    return jax.shard_map(
        per_device,
        mesh=mesh,
        in_specs=(
            P(batch, None, None), P(batch, None), P(batch, None, None), P(batch, None), P(),
            matrix, matrix, matrix, matrix, matrix, vector, vector, vector, vector, vector,
            P("section", None, None),
        ),
        out_specs=(
            P("section", batch, None, None), P("section", batch, None, None), P(batch, None),
            matrix, matrix, matrix, matrix, matrix, vector, vector, vector, vector, vector,
            P("section", None, None),
        ),
        check_vma=False,
    )
```

time: 439 us -> 351 us (0.80)
  blocking collectives: 81.5 us -> 0 us
  waiting for transfers between devices: 49.6 us -> 70.8 us
  local copies, waits for them, and re-layouts: 42 us -> 23.8 us
  Pallas kernels: 103 us -> 89.8 us
  starting transfers between devices: 95.4 us -> 107 us
  other arithmetic: 38.4 us -> 32.6 us
    all_gather x2 -> x0, blocking collectives: 81.5 us -> none  [the longest x1 42.1 us: per_device(): every = lax.all_gather(packed, ('fsdp', 'rep'), axis=0)]
    ppermute x10 -> x17, starting transfers between devices: 4.54 us -> 20.5 us  [swap_section(): return lax.ppermute(value, 'section', [(0, 1), (1, 0)])]
    all_gather x1, waiting for transfers between devices: 0.02 us -> 13.4 us  [per_device(): w_ada_all = lax.all_gather(w_ada[0], 'fsdp', axis=0, tiled=True)]
    pallas_call x2 -> x1, Pallas kernels: 21.5 us -> 11.1 us  [table_gradients(): pl.pallas_call(table_kernel, out_shape=jax.ShapeDtypeStruct((2 * heads *...]
    unnamed x93 -> x117, local copies, waits for them, and re-layouts: 14.6 us -> 5.28 us
    select_n x8 -> x6, other arithmetic: 7.96 us -> 1.8 us  [mine(): return jnp.where(is_first, first, second)]
    slice x17 -> x10, local copies, waits for them, and re-layouts: 6.85 us -> 0.74 us  [the longest x1 0.61 us: per_device(): g_table = summed[8:].reshape(heads, HIGH * LOW)[:, :entries]]
    ppermute x10 -> x17, waiting for transfers between devices: 1.09 us -> 6.16 us  [swap_section(): return lax.ppermute(value, 'section', [(0, 1), (1, 0)])]
  transfers between devices with their start and end apart: 53 -> 60, of which waited for: 13 -> 19; matrix products, arithmetic and copies ran while one was open for 16% -> 14% of each run, Pallas kernels for 11% -> 15%
where the time goes in v2:
time: 351 us; the launch traced here: 345 us
  starting transfers between devices  107 us (30%)
  Pallas kernels  89.8 us (26%)
  waiting for transfers between devices  70.8 us (20%)
  other arithmetic  32.6 us (9%)
  local copies, waits for them, and re-layouts  23.8 us (7%)
  between operations  15.8 us (5%)
  matrix products  6 us (2%)
    pallas_call x5, Pallas kernels, call(): pl.pallas_call(kernel, out_shape=[jax.ShapeDtypeStruct(shape, dtype) for...  67.4 us
    ppermute x15, waiting for transfers between devices, from_peers(): lax.ppermute(value, axis, pairs_of(lax.axis_size(axis), p))  35.2 us
    ppermute x15, starting transfers between devices, from_peers(): lax.ppermute(value, axis, pairs_of(lax.axis_size(axis), p))  28.4 us
    ppermute x9, starting transfers between devices, send_pieces(): lax.ppermute(low[p - 1], ('section', 'fsdp'), one_section_pairs(layer, sh...  23.3 us
    ppermute x17, starting transfers between devices, swap_section(): return lax.ppermute(value, 'section', [(0, 1), (1, 0)])  20.5 us
    all_gather x1, waiting for transfers between devices, per_device(): w_ada_all = lax.all_gather(w_ada[0], 'fsdp', axis=0, tiled=True)  13.4 us
    ppermute x6, starting transfers between devices, replica_total(): lax.ppermute(lax.dynamic_index_in_dim(low_parts, rank ^ j, 0, keepdims=Fa...  12.8 us
    ppermute x6, starting transfers between devices, replica_total(): lax.ppermute(mine, names, one_section_pairs(layer, replicas, j))  11.2 us
  transfers between devices with their start and end apart: 60, of which 19 were waited for; matrix products, arithmetic and copies ran while one was open for 14% of the time, Pallas kernels for 15%

profile of v2, /device:TPU:0, one launch (start us, length us, event | category | flops | bytes accessed | tf_op | source)
XLA Modules:
  0.0 345.4 jit_solution(6605182999875696746)
XLA Ops:
  8.9 4.0 %collective-permute-start.2 = (bf16[1,2880]{1,0:T(2,128)(2,1)S(1)}, bf16[1,2880]{1,0:T(2,128)(2,1)S(1)}, u32[]{:S(2)}, u32[]{:S(2)}) collective-permute-start(bf16[1,2880]{1,0:T(2,128)(2,1)S(1)} %concatenate.103), channel_id=1, source_target_pairs={{0,12},{4,8},{8,4},{12,0},{1,13},{5,9},{9,5},{13,1},{2,14},{6,10},... | collective-permute-start | bytes 17288 | tf_op jit(solution)/shard_map/ppermute | solution.py:679
  15.0 11.2 %shard_map.263.rest_0_.own_bias = bf16[6,256,256]{2,1,0:T(8,128)(2,1)} custom-call(bf16[128,64]{1,0:T(8,128)(2,1)} %bitcast.245, s32[256,256]{1,0:T(8,128)} %index.3), custom_call_target="tpu_custom_call" | custom-call | tf_op jit(solution)/shard_map/pallas_call | solution.py:553
  29.7 2.9 collective-permute-start.5
  47.5 7.9 %collective-permute-done.12.rest_10_.rest_8_ = bf16[576,384]{1,0:T(8,128)(2,1)S(1)} collective-permute-done((bf16[576,384]{1,0:T(8,128)(2,1)}, bf16[576,384]{1,0:T(8,128)(2,1)S(1)}, u32[]{:S(2)}, u32[]{:S(2)}) %collective-permute-start.12) | collective-permute-done | bytes 442400 | tf_op jit(solution)/shard_map/ppermute | solution.py:679
  56.7 10.7 %collective-permute-start.20 = (bf16[576,384]{1,0:T(8,128)(2,1)}, bf16[576,384]{1,0:T(8,128)(2,1)}, u32[]{:S(2)}, u32[]{:S(2)}) collective-permute-start(bf16[576,384]{1,0:T(8,128)(2,1)} %get-tuple-element.40), channel_id=1, source_target_pairs={{0,12},{4,8},{8,4},{12,0},{1,13},{5,9},{9,5},{13,1},{2,14},{6,10},... | collective-permute-start | bytes 1327112 | tf_op jit(solution)/shard_map/ppermute | solution.py:679
  68.0 6.3 %collective-permute-done.18.rest_8_ = bf16[576,384]{1,0:T(8,128)(2,1)S(1)} collective-permute-done((bf16[576,384]{1,0:T(8,128)(2,1)}, bf16[576,384]{1,0:T(8,128)(2,1)S(1)}, u32[]{:S(2)}, u32[]{:S(2)}) %collective-permute-start.18) | collective-permute-done | bytes 442400 | tf_op jit(solution)/shard_map/ppermute | solution.py:679
  75.0 8.9 %collective-permute-done.20.rest_10_ = bf16[576,384]{1,0:T(8,128)(2,1)} collective-permute-done((bf16[576,384]{1,0:T(8,128)(2,1)}, bf16[576,384]{1,0:T(8,128)(2,1)}, u32[]{:S(2)}, u32[]{:S(2)}) %collective-permute-start.20) | collective-permute-done | bytes 442400 | tf_op jit(solution)/shard_map/ppermute | solution.py:679
  88.7 15.2 %shard_map.265 = (bf16[512,1152]{1,0:T(8,128)(2,1)}, bf16[2,6,256,256]{3,2,1,0:T(8,128)(2,1)}, bf16[512,384]{1,0:T(8,128)(2,1)}, f32[512,384]{1,0:T(8,128)}, f32...) custom-call(s32[2]{0:T(128)} %pad_add_fusion.pos.pos_ref, ...), custom_call_target="tpu_custom_call" | custom-call | tf_op jit(solution)/shard_map/pallas_call | solution.py:420
  105.0 25.5 %shard_map.266 = (bf16[512,384]{1,0:T(8,128)(2,1)}, bf16[512,384]{1,0:T(8,128)(2,1)}, f32[2,8,384]{2,1,0:T(8,128)}, f32[2,8,384]{2,1,0:T(8,128)}, bf16[6,256,256...) custom-call(s32[2]{0:T(128)} %pad_add_fusion.pos.pos_ref, bf16[512,384]{1,0:T(8,128)(2,1)} %get-tuple-element.39.h, ...), custom_call_target="tpu_custom_call" | custom-call | tf_op jit(solution)/shard_map/pallas_call | solution.py:420
  130.5 4.2 %collective-permute-start.25 = (bf16[4608,384]{1,0:T(8,128)(2,1)}, bf16[4608,384]{1,0:T(8,128)(2,1)}, u32[]{:S(2)}, u32[]{:S(2)}) collective-permute-start(bf16[4608,384]{1,0:T(8,128)(2,1)} %get-tuple-element.52), channel_id=1, source_target_pairs={{0,16},{1,17},{2,18},{3,19},{4,20},{5,21},{6,22},{7,23},{8,24},{9,... | collective-permute-start | bytes 10616840 | tf_op jit(solution)/shard_map/ppermute | solution.py:622
  134.8 11.8 %shard_map.267 = (f32[512,384]{1,0:T(8,128)}, f32[2,8,384]{2,1,0:T(8,128)}, bf16[3072,384]{1,0:T(8,128)(2,1)}) custom-call(s32[2]{0:T(128)} %pad_add_fusion.pos.pos_ref, bf16[512,384]{1,0:T(8,128)(2,1)} %get-tuple-element.46.grad, f32[512,384]{1,0:T(8,128)} %get-tuple-element.47.middle, f32[1,7680]{1,0:T(1,128)} %copy-done.32, f32[1,7680]{1,0:T(1,128)} %copy-done.33, ...), custom_call_target="tpu_custom_call" | custom-call | tf_op jit(solution)/shard_map/pallas_call | solution.py:420
  150.7 2.9 collective-permute-done.24
  154.6 13.4 %all-gather.3.cloned.1.call-done = bf16[1,384,2304]{2,1,0:T(8,128)(2,1)} async-done(((bf16[1,96,2304]{2,1,0:T(8,128)(2,1)}), bf16[1,384,2304]{2,1,0:T(8,128)(2,1)}) %all-gather.3.cloned.1.call-update) | async-done | bytes 1769488 | tf_op jit(solution)/shard_map/all_gather | solution.py:714
  168.0 2.8 copy.41
  173.4 3.4 collective-permute-start.46
  176.8 3.4 collective-permute-start.45
  182.6 3.6 %add_convert_fusion = (bf16[1152,384]{1,0:T(8,128)(2,1)}, bf16[1152,384]{1,0:T(8,128)(2,1)}, bf16[1152,384]{1,0:T(8,128)(2,1)}) fusion(bf16[4608,384]{1,0:T(8,128)(2,1)} %collective-permute-done.25, bf16[4608,384]{1,0:T(8,128)(2,1)S(1)} %copy-done.15), kind=kLoop, calls=%fused_computation.2 | loop fusion | flops 5308416 | bytes 7962624 | tf_op jit(solution)/shard_map/convert_element_type | solution.py:632
  186.3 12.4 %shard_map.268 = (f32[512,384]{1,0:T(8,128)}, f32[2,8,384]{2,1,0:T(8,128)}, bf16[6,256,256]{2,1,0:T(8,128)(2,1)}, bf16[1536,384]{1,0:T(8,128)(2,1)}) custom-call(s32[2]{0:T(128)} %pad_add_fusion.pos.pos_ref, bf16[512,384]{1,0:T(8,128)(2,1)} %bitcast.216, f32[1,7680]{1,0:T(1,128)} %copy-done.32, f32[1,7680]{1,0:T(1,128)} %copy-done.33, ...), custom_call_target="tpu_custom_call" | custom-call | tf_op jit(solution)/shard_map/pallas_call | solution.py:420
  200.3 2.9 convert_add_fusion.1
  209.8 4.1 %collective-permute-start.28 = (f32[4,384]{1,0:T(4,128)S(1)}, f32[4,384]{1,0:T(4,128)S(1)}, u32[]{:S(2)}, u32[]{:S(2)}) collective-permute-start(f32[4,384]{1,0:T(4,128)S(1)} %fusion), channel_id=1, source_target_pairs={{0,16},{16,0},{1,17},{17,1},{2,18},{18,2},{3,19},{19,3},{4,20},{20... | collective-permute-start | bytes 18440 | tf_op jit(solution)/shard_map/ppermute | solution.py:599
  223.4 11.1 %shard_map.269 = f32[192,64]{1,0:T(8,128)} custom-call(bf16[6,256,256]{2,1,0:T(8,128)(2,1)} %get-tuple-element.58.scores_a, bf16[6,256,256]{2,1,0:T(8,128)(2,1)} %get-tuple-element.59.scores_b, s32[256,256]{1,0:T(8,128)} %index.3, bf16[1152,384]{1,0:T(8,128)(2,1)} %collective-permute-done.29.rest_0_, bf16[1152,384]{1,0:T(8,128)(2,1)} %collective-permute-done.30.rest_1_, ...), custom_call_target="tpu_custom_call" | custom-call | tf_op jit(solution)/shard_map/pallas_call | solution.py:588
  235.4 12.4 %collective-permute-start.34 = (f32[96,64]{1,0:T(8,128)S(1)}, f32[96,64]{1,0:T(8,128)S(1)}, u32[]{:S(2)}, u32[]{:S(2)}) collective-permute-start(f32[96,64]{1,0:T(8,128)S(1)} %slice_select_fusion), channel_id=1, source_target_pairs={{0,16},{16,0},{1,17},{17,1},{2,18},{18,2},{3,19},{19,3},{4,20},{20... | collective-permute-start | bytes 73736 | tf_op jit(solution)/shard_map/ppermute | solution.py:599
  259.1 3.4 collective-permute-start.43
  265.5 3.4 collective-permute-start.41
  273.2 7.2 %collective-permute-done.40 = bf16[136,384]{1,0:T(8,128)(2,1)S(1)} collective-permute-done((bf16[136,384]{1,0:T(8,128)(2,1)S(1)}, bf16[136,384]{1,0:T(8,128)(2,1)S(1)}, u32[]{:S(2)}, u32[]{:S(2)}) %collective-permute-start.40) | collective-permute-done | bytes 104480 | tf_op jit(solution)/shard_map/ppermute | solution.py:679
  280.7 4.3 %collective-permute-done.38 = bf16[136,384]{1,0:T(8,128)(2,1)S(1)} collective-permute-done((bf16[136,384]{1,0:T(8,128)(2,1)S(1)}, bf16[136,384]{1,0:T(8,128)(2,1)S(1)}, u32[]{:S(2)}, u32[]{:S(2)}) %collective-permute-start.38) | collective-permute-done | bytes 104480 | tf_op jit(solution)/shard_map/ppermute | solution.py:679
  300.5 5.0 %collective-permute-start.49 = (bf16[288,384]{1,0:T(8,128)(2,1)S(1)}, bf16[288,384]{1,0:T(8,128)(2,1)S(1)}, u32[]{:S(2)}, u32[]{:S(2)}) collective-permute-start(bf16[288,384]{1,0:T(8,128)(2,1)S(1)} %get-tuple-element.89), channel_id=1, source_target_pairs={{0,3},{1,2},{2,1},{3,0},{4,7},{5,6},{6,5},{7,4},{8,11},{9,10},{10,... | collective-permute-start | bytes 663560 | tf_op jit(solution)/shard_map/ppermute | solution.py:655
  307.4 3.2 collective-permute-start.47
  310.8 4.4 %collective-permute-done.48 = bf16[288,384]{1,0:T(8,128)(2,1)S(1)} collective-permute-done((bf16[288,384]{1,0:T(8,128)(2,1)S(1)}, bf16[288,384]{1,0:T(8,128)(2,1)S(1)}, u32[]{:S(2)}, u32[]{:S(2)}) %collective-permute-start.48) | collective-permute-done | bytes 221216 | tf_op jit(solution)/shard_map/ppermute | solution.py:655
  320.2 3.7 %collective-permute-start.51 = (bf16[288,384]{1,0:T(8,128)(2,1)S(1)}, bf16[288,384]{1,0:T(8,128)(2,1)S(1)}, u32[]{:S(2)}, u32[]{:S(2)}) collective-permute-start(bf16[288,384]{1,0:T(8,128)(2,1)S(1)} %fusion.7), channel_id=1, source_target_pairs={{0,3},{1,2},{2,1},{3,0},{4,7},{5,6},{6,5},{7,4},{8,11},{9,10},{10,... | collective-permute-start | bytes 663560 | tf_op jit(solution)/shard_map/ppermute | solution.py:663
  323.9 3.0 collective-permute-start.50
  327.1 3.6 %collective-permute-done.52 = bf16[288,384]{1,0:T(8,128)(2,1)S(1)} collective-permute-done((bf16[288,384]{1,0:T(8,128)(2,1)S(1)}, bf16[288,384]{1,0:T(8,128)(2,1)S(1)}, u32[]{:S(2)}, u32[]{:S(2)}) %collective-permute-start.52) | collective-permute-done | bytes 221216 | tf_op jit(solution)/shard_map/ppermute | solution.py:663
  (339 shorter events, 107.6 us)
Async XLA Ops:
  7.2 160.8 %all-gather.3.cloned.1.call-start = ((), (), s32[]{:S(2)}) async-start(), calls=%async_computation | async-start | bytes 2211840 | tf_op jit(solution)/shard_map/all_gather | solution.py:714
  8.9 19.2 %collective-permute-start.2 = (bf16[1,2880]{1,0:T(2,128)(2,1)S(1)}, bf16[1,2880]{1,0:T(2,128)(2,1)S(1)}, u32[]{:S(2)}, u32[]{:S(2)}) collective-permute-start(bf16[1,2880]{1,0:T(2,128)(2,1)S(1)} %concatenate.103), channel_id=1, source_target_pairs={{0,12},{4,8},{8,4},{12,0},{1,13},{5,9},{9,5},{13,1},{2,14},{6,10},... | collective-permute-start | bytes 17288 | tf_op jit(solution)/shard_map/ppermute | solution.py:679
  12.9 15.3 %collective-permute-start.1 = (bf16[1,2880]{1,0:T(2,128)(2,1)S(1)}, bf16[1,2880]{1,0:T(2,128)(2,1)S(1)}, u32[]{:S(2)}, u32[]{:S(2)}) collective-permute-start(bf16[1,2880]{1,0:T(2,128)(2,1)S(1)} %concatenate.103), channel_id=1, source_target_pairs={{0,8},{4,12},{8,0},{12,4},{1,9},{5,13},{9,1},{13,5},{2,10},{6,14},... | collective-permute-start | bytes 17288 | tf_op jit(solution)/shard_map/ppermute | solution.py:679
  13.4 14.8 %collective-permute-start = (bf16[1,2880]{1,0:T(2,128)(2,1)S(1)}, bf16[1,2880]{1,0:T(2,128)(2,1)S(1)}, u32[]{:S(2)}, u32[]{:S(2)}) collective-permute-start(bf16[1,2880]{1,0:T(2,128)(2,1)S(1)} %concatenate.103), channel_id=1, source_target_pairs={{0,4},{4,0},{8,12},{12,8},{1,5},{5,1},{9,13},{13,9},{2,6},{6,2},{1... | collective-permute-start | bytes 17288 | tf_op jit(solution)/shard_map/ppermute | solution.py:679
  26.2 57.7 %collective-permute-start.7 = (bf16[6,256,256]{2,1,0:T(8,128)(2,1)}, bf16[6,256,256]{2,1,0:T(8,128)(2,1)}, u32[]{:S(2)}, u32[]{:S(2)}) collective-permute-start(bf16[6,256,256]{2,1,0:T(8,128)(2,1)} %shard_map.263.rest_0_.own_bias), channel_id=1, source_target_pairs={{0,16},{16,0},{1,17},{17,1},{2,18},{18,2},{3,19},{19,3},{4,20},{20... | collective-permute-start | bytes 2359304 | tf_op jit(solution)/shard_map/ppermute | solution.py:599
  42.1 13.2 %collective-permute-start.12 = (bf16[576,384]{1,0:T(8,128)(2,1)}, bf16[576,384]{1,0:T(8,128)(2,1)S(1)}, u32[]{:S(2)}, u32[]{:S(2)}) collective-permute-start(bf16[576,384]{1,0:T(8,128)(2,1)} %get-tuple-element.38), channel_id=1, source_target_pairs={{0,4},{4,0},{8,12},{12,8},{1,5},{5,1},{9,13},{13,9},{2,6},{6,2},{1... | collective-permute-start | bytes 1327112 | tf_op jit(solution)/shard_map/ppermute | solution.py:679
  42.7 14.0 %collective-permute-start.13 = (bf16[576,384]{1,0:T(8,128)(2,1)}, bf16[576,384]{1,0:T(8,128)(2,1)S(1)}, u32[]{:S(2)}, u32[]{:S(2)}) collective-permute-start(bf16[576,384]{1,0:T(8,128)(2,1)} %get-tuple-element.38), channel_id=1, source_target_pairs={{0,8},{4,12},{8,0},{12,4},{1,9},{5,13},{9,1},{13,5},{2,10},{6,14},... | collective-permute-start | bytes 1327112 | tf_op jit(solution)/shard_map/ppermute | solution.py:679
  44.0 23.4 %collective-permute-start.14 = (bf16[576,384]{1,0:T(8,128)(2,1)}, bf16[576,384]{1,0:T(8,128)(2,1)S(1)}, u32[]{:S(2)}, u32[]{:S(2)}) collective-permute-start(bf16[576,384]{1,0:T(8,128)(2,1)} %get-tuple-element.38), channel_id=1, source_target_pairs={{0,12},{4,8},{8,4},{12,0},{1,13},{5,9},{9,5},{13,1},{2,14},{6,10},... | collective-permute-start | bytes 1327112 | tf_op jit(solution)/shard_map/ppermute | solution.py:679
  46.9 27.4 %collective-permute-start.18 = (bf16[576,384]{1,0:T(8,128)(2,1)}, bf16[576,384]{1,0:T(8,128)(2,1)S(1)}, u32[]{:S(2)}, u32[]{:S(2)}) collective-permute-start(bf16[576,384]{1,0:T(8,128)(2,1)} %get-tuple-element.40), channel_id=1, source_target_pairs={{0,4},{4,0},{8,12},{12,8},{1,5},{5,1},{9,13},{13,9},{2,6},{6,2},{1... | collective-permute-start | bytes 1327112 | tf_op jit(solution)/shard_map/ppermute | solution.py:679
  55.4 19.6 %collective-permute-start.19 = (bf16[576,384]{1,0:T(8,128)(2,1)}, bf16[576,384]{1,0:T(8,128)(2,1)S(1)}, u32[]{:S(2)}, u32[]{:S(2)}) collective-permute-start(bf16[576,384]{1,0:T(8,128)(2,1)} %get-tuple-element.40), channel_id=1, source_target_pairs={{0,8},{4,12},{8,0},{12,4},{1,9},{5,13},{9,1},{13,5},{2,10},{6,14},... | collective-permute-start | bytes 1327112 | tf_op jit(solution)/shard_map/ppermute | solution.py:679
  56.7 27.2 %collective-permute-start.20 = (bf16[576,384]{1,0:T(8,128)(2,1)}, bf16[576,384]{1,0:T(8,128)(2,1)}, u32[]{:S(2)}, u32[]{:S(2)}) collective-permute-start(bf16[576,384]{1,0:T(8,128)(2,1)} %get-tuple-element.40), channel_id=1, source_target_pairs={{0,12},{4,8},{8,4},{12,0},{1,13},{5,9},{9,5},{13,1},{2,14},{6,10},... | collective-permute-start | bytes 1327112 | tf_op jit(solution)/shard_map/ppermute | solution.py:679
  67.4 17.0 %collective-permute-start.15 = (bf16[576,384]{1,0:T(8,128)(2,1)S(1)}, bf16[576,384]{1,0:T(8,128)(2,1)S(1)}, u32[]{:S(2)}, u32[]{:S(2)}) collective-permute-start(bf16[576,384]{1,0:T(8,128)(2,1)S(1)} %collective-permute-done.12.rest_10_.rest_8_), channel_id=1, source_target_pairs={{0,16},{16,0},{1,17},{17,1},{2,18},{18,2},{3,19},{19,3},{4,20},{20... | collective-permute-start | bytes 1327112 | tf_op jit(solution)/shard_map/ppermute | solution.py:599
  74.4 13.4 %collective-permute-start.16 = (bf16[576,384]{1,0:T(8,128)(2,1)S(1)}, bf16[576,384]{1,0:T(8,128)(2,1)S(1)}, u32[]{:S(2)}, u32[]{:S(2)}) collective-permute-start(bf16[576,384]{1,0:T(8,128)(2,1)S(1)} %collective-permute-done.13.rest_11_.rest_9_), channel_id=1, source_target_pairs={{0,16},{16,0},{1,17},{17,1},{2,18},{18,2},{3,19},{19,3},{4,20},{20... | collective-permute-start | bytes 1327112 | tf_op jit(solution)/shard_map/ppermute | solution.py:599
  75.0 12.8 %collective-permute-start.17 = (bf16[576,384]{1,0:T(8,128)(2,1)S(1)}, bf16[576,384]{1,0:T(8,128)(2,1)S(1)}, u32[]{:S(2)}, u32[]{:S(2)}) collective-permute-start(bf16[576,384]{1,0:T(8,128)(2,1)S(1)} %collective-permute-done.14.rest_12_.rest_10_), channel_id=1, source_target_pairs={{0,16},{16,0},{1,17},{17,1},{2,18},{18,2},{3,19},{19,3},{4,20},{20... | collective-permute-start | bytes 1327112 | tf_op jit(solution)/shard_map/ppermute | solution.py:599
  83.9 20.1 %collective-permute-start.21 = (bf16[576,384]{1,0:T(8,128)(2,1)S(1)}, bf16[576,384]{1,0:T(8,128)(2,1)S(1)}, u32[]{:S(2)}, u32[]{:S(2)}) collective-permute-start(bf16[576,384]{1,0:T(8,128)(2,1)S(1)} %collective-permute-done.18.rest_8_), channel_id=1, source_target_pairs={{0,16},{16,0},{1,17},{17,1},{2,18},{18,2},{3,19},{19,3},{4,20},{20... | collective-permute-start | bytes 1327112 | tf_op jit(solution)/shard_map/ppermute | solution.py:599
  83.9 20.1 %collective-permute-start.22 = (bf16[576,384]{1,0:T(8,128)(2,1)S(1)}, bf16[576,384]{1,0:T(8,128)(2,1)S(1)}, u32[]{:S(2)}, u32[]{:S(2)}) collective-permute-start(bf16[576,384]{1,0:T(8,128)(2,1)S(1)} %collective-permute-done.19.rest_9_), channel_id=1, source_target_pairs={{0,16},{16,0},{1,17},{17,1},{2,18},{18,2},{3,19},{19,3},{4,20},{20... | collective-permute-start | bytes 1327112 | tf_op jit(solution)/shard_map/ppermute | solution.py:599
  84.4 19.6 %collective-permute-start.23 = (bf16[576,384]{1,0:T(8,128)(2,1)}, bf16[576,384]{1,0:T(8,128)(2,1)S(1)}, u32[]{:S(2)}, u32[]{:S(2)}) collective-permute-start(bf16[576,384]{1,0:T(8,128)(2,1)} %collective-permute-done.20.rest_10_), channel_id=1, source_target_pairs={{0,16},{16,0},{1,17},{17,1},{2,18},{18,2},{3,19},{19,3},{4,20},{20... | collective-permute-start | bytes 1327112 | tf_op jit(solution)/shard_map/ppermute | solution.py:599
  130.5 52.1 %collective-permute-start.25 = (bf16[4608,384]{1,0:T(8,128)(2,1)}, bf16[4608,384]{1,0:T(8,128)(2,1)}, u32[]{:S(2)}, u32[]{:S(2)}) collective-permute-start(bf16[4608,384]{1,0:T(8,128)(2,1)} %get-tuple-element.52), channel_id=1, source_target_pairs={{0,16},{1,17},{2,18},{3,19},{4,20},{5,21},{6,22},{7,23},{8,24},{9,... | collective-permute-start | bytes 10616840 | tf_op jit(solution)/shard_map/ppermute | solution.py:622
  146.6 24.2 %collective-permute-start.33 = (bf16[3072,384]{1,0:T(8,128)(2,1)}, bf16[3072,384]{1,0:T(8,128)(2,1)}, u32[]{:S(2)}, u32[]{:S(2)}) collective-permute-start(bf16[3072,384]{1,0:T(8,128)(2,1)} %get-tuple-element.61), channel_id=1, source_target_pairs={{16,0},{17,1},{18,2},{19,3},{20,4},{21,5},{22,6},{23,7},{24,8},{25... | collective-permute-start | bytes 7077896 | tf_op jit(solution)/shard_map/ppermute | solution.py:622
  173.4 26.9 %collective-permute-start.46 = (bf16[768,384]{1,0:T(8,128)(2,1)S(1)}, bf16[768,384]{1,0:T(8,128)(2,1)S(1)}, u32[]{:S(2)}, u32[]{:S(2)}) collective-permute-start(bf16[768,384]{1,0:T(8,128)(2,1)S(1)} %get-tuple-element.67.rest_8_), channel_id=1, source_target_pairs={{0,12},{4,8},{8,4},{12,0},{1,13},{5,9},{9,5},{13,1},{2,14},{6,10},... | collective-permute-start | bytes 1769480 | tf_op jit(solution)/shard_map/ppermute | solution.py:634
  176.8 23.6 %collective-permute-start.45 = (bf16[768,384]{1,0:T(8,128)(2,1)S(1)}, bf16[768,384]{1,0:T(8,128)(2,1)S(1)}, u32[]{:S(2)}, u32[]{:S(2)}) collective-permute-start(bf16[768,384]{1,0:T(8,128)(2,1)S(1)} %get-tuple-element.68.rest_7_), channel_id=1, source_target_pairs={{0,8},{4,12},{8,0},{12,4},{1,9},{5,13},{9,1},{13,5},{2,10},{6,14},... | collective-permute-start | bytes 1769480 | tf_op jit(solution)/shard_map/ppermute | solution.py:634
  180.1 20.2 %collective-permute-start.44 = (bf16[768,384]{1,0:T(8,128)(2,1)S(1)}, bf16[768,384]{1,0:T(8,128)(2,1)}, u32[]{:S(2)}, u32[]{:S(2)}) collective-permute-start(bf16[768,384]{1,0:T(8,128)(2,1)S(1)} %get-tuple-element.69.rest_6_), channel_id=1, source_target_pairs={{0,4},{4,0},{8,12},{12,8},{1,5},{5,1},{9,13},{13,9},{2,6},{6,2},{1... | collective-permute-start | bytes 1769480 | tf_op jit(solution)/shard_map/ppermute | solution.py:634
  203.2 14.8 %collective-permute-start.29 = (bf16[1152,384]{1,0:T(8,128)(2,1)}, bf16[1152,384]{1,0:T(8,128)(2,1)}, u32[]{:S(2)}, u32[]{:S(2)}) collective-permute-start(bf16[1152,384]{1,0:T(8,128)(2,1)} %get-tuple-element.66.rest_14_), channel_id=1, source_target_pairs={{16,20},{20,16},{24,28},{28,24},{17,21},{21,17},{25,29},{29,25},{1... | collective-permute-start | bytes 2654216 | tf_op jit(solution)/shard_map/ppermute | solution.py:634
  205.0 13.1 %collective-permute-start.30 = (bf16[1152,384]{1,0:T(8,128)(2,1)}, bf16[1152,384]{1,0:T(8,128)(2,1)}, u32[]{:S(2)}, u32[]{:S(2)}) collective-permute-start(bf16[1152,384]{1,0:T(8,128)(2,1)} %get-tuple-element.65.rest_15_), channel_id=1, source_target_pairs={{16,24},{20,28},{24,16},{28,20},{17,25},{21,29},{25,17},{29,21},{1... | collective-permute-start | bytes 2654216 | tf_op jit(solution)/shard_map/ppermute | solution.py:634
  206.6 11.5 %collective-permute-start.31 = (bf16[1152,384]{1,0:T(8,128)(2,1)S(1)}, bf16[1152,384]{1,0:T(8,128)(2,1)}, u32[]{:S(2)}, u32[]{:S(2)}) collective-permute-start(bf16[1152,384]{1,0:T(8,128)(2,1)S(1)} %copy-done.14), channel_id=1, source_target_pairs={{16,28},{20,24},{24,20},{28,16},{17,29},{21,25},{25,21},{29,17},{1... | collective-permute-start | bytes 2654216 | tf_op jit(solution)/shard_map/ppermute | solution.py:634
  235.4 16.0 %collective-permute-start.34 = (f32[96,64]{1,0:T(8,128)S(1)}, f32[96,64]{1,0:T(8,128)S(1)}, u32[]{:S(2)}, u32[]{:S(2)}) collective-permute-start(f32[96,64]{1,0:T(8,128)S(1)} %slice_select_fusion), channel_id=1, source_target_pairs={{0,16},{16,0},{1,17},{17,1},{2,18},{18,2},{3,19},{19,3},{4,20},{20... | collective-permute-start | bytes 73736 | tf_op jit(solution)/shard_map/ppermute | solution.py:599
  258.3 13.0 %collective-permute-start.56 = (bf16[288,384]{1,0:T(8,128)(2,1)S(1)}, bf16[288,384]{1,0:T(8,128)(2,1)S(1)}, u32[]{:S(2)}, u32[]{:S(2)}) collective-permute-start(bf16[288,384]{1,0:T(8,128)(2,1)S(1)} %fusion.4), channel_id=1, source_target_pairs={{16,17},{17,16},{18,19},{19,18},{20,21},{21,20},{22,23},{23,22},{2... | collective-permute-start | bytes 663560 | tf_op jit(solution)/shard_map/ppermute | solution.py:663
  259.1 39.5 %collective-permute-start.43 = (bf16[384,384]{1,0:T(8,128)(2,1)S(1)}, bf16[384,384]{1,0:T(8,128)(2,1)}, u32[]{:S(2)}, u32[]{:S(2)}) collective-permute-start(bf16[384,384]{1,0:T(8,128)(2,1)S(1)} %copy-done.27), channel_id=1, source_target_pairs={{0,12},{4,8},{8,4},{12,0},{1,13},{5,9},{9,5},{13,1},{2,14},{6,10},... | collective-permute-start | bytes 884744 | tf_op jit(solution)/shard_map/ppermute | solution.py:634
  262.4 36.2 %collective-permute-start.42 = (bf16[384,384]{1,0:T(8,128)(2,1)S(1)}, bf16[384,384]{1,0:T(8,128)(2,1)}, u32[]{:S(2)}, u32[]{:S(2)}) collective-permute-start(bf16[384,384]{1,0:T(8,128)(2,1)S(1)} %copy-done.26), channel_id=1, source_target_pairs={{0,8},{4,12},{8,0},{12,4},{1,9},{5,13},{9,1},{13,5},{2,10},{6,14},... | collective-permute-start | bytes 884744 | tf_op jit(solution)/shard_map/ppermute | solution.py:634
  265.5 33.2 %collective-permute-start.41 = (bf16[384,384]{1,0:T(8,128)(2,1)S(1)}, bf16[384,384]{1,0:T(8,128)(2,1)}, u32[]{:S(2)}, u32[]{:S(2)}) collective-permute-start(bf16[384,384]{1,0:T(8,128)(2,1)S(1)} %copy-done.25), channel_id=1, source_target_pairs={{0,4},{4,0},{8,12},{12,8},{1,5},{5,1},{9,13},{13,9},{2,6},{6,2},{1... | collective-permute-start | bytes 884744 | tf_op jit(solution)/shard_map/ppermute | solution.py:634
  268.9 11.5 %collective-permute-start.40 = (bf16[136,384]{1,0:T(8,128)(2,1)S(1)}, bf16[136,384]{1,0:T(8,128)(2,1)S(1)}, u32[]{:S(2)}, u32[]{:S(2)}) collective-permute-start(bf16[136,384]{1,0:T(8,128)(2,1)S(1)} %concatenate.123), channel_id=1, source_target_pairs={{0,2},{1,3},{2,0},{3,1},{4,6},{5,7},{6,4},{7,5},{8,10},{9,11},{10,... | collective-permute-start | bytes 313352 | tf_op jit(solution)/shard_map/ppermute | solution.py:679
  317.6 13.0 %collective-permute-start.52 = (bf16[288,384]{1,0:T(8,128)(2,1)S(1)}, bf16[288,384]{1,0:T(8,128)(2,1)S(1)}, u32[]{:S(2)}, u32[]{:S(2)}) collective-permute-start(bf16[288,384]{1,0:T(8,128)(2,1)S(1)} %fusion.7), channel_id=1, source_target_pairs={{0,2},{1,3},{2,0},{3,1},{4,6},{5,7},{6,4},{7,5},{8,10},{9,11},{10,... | collective-permute-start | bytes 663560 | tf_op jit(solution)/shard_map/ppermute | solution.py:663
  (81 other events, 955.4 us)
Sparse Core Ops, SparseCore 0:
  134.9 33.1 all-gather.2

commit v3 on v2

--- a/solution.py
+++ b/solution.py
@@ -64,43 +64,44 @@
 
 
 def weight_count(refs):
-    return 9 if refs == 2 else 31
+    return 9 if refs == 2 else 36
 
 
 def weight_loads(layer, section, shard, refs, mats, sems):
     model = mats[1].shape[0]
     plans = []
-    own_layer = section == layer
     if len(refs) == 2:
-        targets = block_targets(mats, 0, model)
-        for i, target in enumerate(targets):
+        for i, target in enumerate(block_targets(mats, 0, model)):
             rows = pl.ds(i * model, 4 * model if i == 8 else model)
-            plans.append((own_layer, refs[0].at[rows, :], refs[1].at[rows, :], target, i < 4))
+            plans.append((refs[0].at[rows, :], refs[1].at[rows, :], target, i < 4))
     else:
-        own, other, mine, theirs = refs[:4], refs[4:8], refs[8:11], refs[11:14]
-        q = own[0].shape[0]
-        off = pl.multiple_of(shard * q, 16)
-        whole = [
-            mats[0].at[pl.ds(off, q), :], mats[1].at[pl.ds(off, q), :],
-            mats[2].at[pl.ds(off, q), :], mats[3].at[pl.ds(pl.multiple_of(off * 4, 16), 4 * q), :],
-        ]
-        for i in range(4):
-            plans.append((own_layer, own[i], other[i], whole[i], i < 2))
-        for p in range(1, 4):
+        count = len(refs) // 2
+        q = refs[0].shape[0] // 12
+        for p in range(4):
             targets = block_targets(mats, pl.multiple_of((shard ^ p) * q, 16), q)
             for i, target in enumerate(targets):
-                at = i if i < 6 else i - 6
+                which, at = p, i
+                if p == 3 and i >= 6:
+                    which, at = 4, i - 6
                 rows = pl.ds(at * q, 4 * q if i == 8 else q)
-                half = 0 if i < 6 else 1
-                plans.append((section == half, mine[p - 1].at[rows, :], theirs[p - 1].at[rows, :], target, i < 4))
-    waits = ([], [])
-    for i, (condition, first, second, target, early) in enumerate(plans):
-        one = pltpu.make_async_copy(first, target, sems.at[i])
-        two = pltpu.make_async_copy(second, target, sems.at[i])
-        pl.when(condition)(one.start)
-        pl.when(jnp.logical_not(condition))(two.start)
-        waits[0 if early else 1].append(one)
-    return waits
+                plans.append((refs[which].at[rows, :], refs[count + which].at[rows, :], target, i < 4))
+    ones = [pltpu.make_async_copy(x[0], x[2], sems.at[i]) for i, x in enumerate(plans)]
+    twos = [pltpu.make_async_copy(x[1], x[2], sems.at[i]) for i, x in enumerate(plans)]
+
+    @pl.when(section == layer)
+    def _():
+        for copy in ones:
+            copy.start()
+
+    @pl.when(section != layer)
+    def _():
+        for copy in twos:
+            copy.start()
+
+    return (
+        [copy for copy, x in zip(ones, plans) if x[3]],
+        [copy for copy, x in zip(ones, plans) if not x[3]],
+    )
 
 
 def wait_all(copies):
@@ -108,26 +109,41 @@
         copy.wait()
 
 
-def pack_attention(out_ref, g_qkv, g_proj, shard, pieces, stride, first):
+def put_half(refs, section, half, at, value):
+    keep, send = refs
+    rows = slice(at, at + value.shape[0])
+
+    @pl.when(section == half)
+    def _():
+        keep[rows, :] = value
+
+    @pl.when(section != half)
+    def _():
+        send[rows, :] = value
+
+
+def pack_attention(refs, section, g_qkv, g_proj, shard, pieces, stride, first):
     model = g_proj.shape[0]
     q = model // pieces
     for p in range(pieces):
         off = pl.multiple_of((shard ^ p) * q, 16) if pieces > 1 else 0
         at = (stride * p + first) * q
         for c in range(3):
-            out_ref[at + c * q : at + (c + 1) * q, :] = g_qkv[pl.ds(off, q), c * model : (c + 1) * model]
-        out_ref[at + 3 * q : at + 4 * q, :] = g_proj[pl.ds(off, q), :]
-
-
-def pack_mlp(out_ref, g_fc1, g_fc2, shard, pieces, stride, first):
+            value = g_qkv[pl.ds(off, q), c * model : (c + 1) * model]
+            put_half(refs, section, c // 2, at + (c % 2) * q, value)
+        put_half(refs, section, 1, at + q, g_proj[pl.ds(off, q), :])
+
+
+def pack_mlp(refs, section, g_fc1, g_fc2, shard, pieces, stride, first):
     model = g_fc1.shape[0]
     q = model // pieces
     for p in range(pieces):
         off = pl.multiple_of((shard ^ p) * q, 16) if pieces > 1 else 0
         at = (stride * p + first) * q
         for c in range(4):
-            out_ref[at + c * q : at + (c + 1) * q, :] = g_fc1[pl.ds(off, q), c * model : (c + 1) * model]
-        out_ref[at + 4 * q : at + 8 * q, :] = g_fc2[pl.ds(pl.multiple_of(off * 4, 16), 4 * q), :]
+            value = g_fc1[pl.ds(off, q), c * model : (c + 1) * model]
+            put_half(refs, section, 0, at + c * q, value)
+        put_half(refs, section, 1, at, g_fc2[pl.ds(pl.multiple_of(off * 4, 16), 4 * q), :])
 
 
 class Modulation:
@@ -336,7 +352,7 @@
 
 def both_kernel(layer, pieces, length, n_weights, pos, h, grad, own_line, other_line, own_bias, other_bias, *rest):
     refs, rest = rest[:n_weights], rest[n_weights:]
-    (layer_out, d_in, small_a, small_m, scores, pack,
+    (layer_out, d_in, small_a, small_m, scores, keep, send,
      w_qkv, w_proj, w_fc1, w_fc2, bias, line, qkv, probs, att, branch, middle, act, slope, out_branch,
      d_middle, normed_low, d_pre, d_ob, d_qkv, score_sum, g_qkv, g_proj, g_fc1, g_fc2, sems) = rest
     section, shard = pos[0], pos[1]
@@ -361,7 +377,7 @@
 
     each_sample(samples, mlp)
     mlp_weight_grads(normed_low, d_pre, act, d_ob, g_fc1, g_fc2)
-    pack_mlp(pack, g_fc1, g_fc2, shard, pieces, 12, 4)
+    pack_mlp((keep, send), section, g_fc1, g_fc2, shard, pieces, 6, 2)
     score_sum[...] = jnp.zeros_like(score_sum)
     each_sample(
         samples,
@@ -369,12 +385,12 @@
     )
     scores[...] = score_sum[...].astype(BF16)
     attention_weight_grads(normed_low, d_qkv, att, d_ob, g_qkv, g_proj)
-    pack_attention(pack, g_qkv, g_proj, shard, pieces, 12, 0)
+    pack_attention((keep, send), section, g_qkv, g_proj, shard, pieces, 6, 0)
 
 
 def backward_mlp_kernel(layer, pieces, length, n_weights, pos, grad, middle, own_line, other_line, act, slope, out_branch, *rest):
     refs, rest = rest[:n_weights], rest[n_weights:]
-    (d_middle, small, pack,
+    (d_middle, small, keep, send,
      w_qkv, w_proj, w_fc1, w_fc2, line, normed_low, d_pre, d_ob, g_fc1, g_fc2, sems) = rest
     section, shard = pos[0], pos[1]
     for_attention, for_mlp = weight_loads(layer, section, shard, refs, (w_qkv, w_proj, w_fc1, w_fc2), sems)
@@ -386,13 +402,13 @@
         lambda b: mlp_backward(b, length, grad, middle, mod, w_fc1, w_fc2, act, slope, out_branch, d_middle, small, normed_low, d_pre, d_ob),
     )
     mlp_weight_grads(normed_low, d_pre, act, d_ob, g_fc1, g_fc2)
-    pack_mlp(pack, g_fc1, g_fc2, shard, pieces, 8, 0)
+    pack_mlp((keep, send), section, g_fc1, g_fc2, shard, pieces, 4, 0)
     wait_all(for_attention)
 
 
 def backward_attention_kernel(layer, pieces, length, n_weights, n_after, pos, h, own_line, other_line, qkv, probs, att, branch, d_middle, *rest):
     refs, rest = rest[:n_weights], rest[n_weights + n_after :]
-    (d_in, small, scores, pack,
+    (d_in, small, scores, keep, send,
      w_qkv, w_proj, w_fc1, w_fc2, line, normed_low, d_qkv, d_br, score_sum, g_qkv, g_proj, sems) = rest
     section, shard = pos[0], pos[1]
     for_attention, for_mlp = weight_loads(layer, section, shard, refs, (w_qkv, w_proj, w_fc1, w_fc2), sems)
@@ -406,7 +422,7 @@
     )
     scores[...] = score_sum[...].astype(BF16)
     attention_weight_grads(normed_low, d_qkv, att, d_br, g_qkv, g_proj)
-    pack_attention(pack, g_qkv, g_proj, shard, pieces, 4, 0)
+    pack_attention((keep, send), section, g_qkv, g_proj, shard, pieces, 2, 0)
     wait_all(for_mlp)
 
 
@@ -444,6 +460,9 @@
         self.wide = ((self.rows, hidden), BF16)
         self.small = ((samples, 8, model), F32)
 
+    def pack(self, blocks):
+        return [((blocks * self.model, self.model), BF16)] * 2
+
 
 def forward_layer(layer, z, pos, h, lines, biases, weights):
     def kernel(pos_ref, h_ref, a, b, *rest):
@@ -460,7 +479,7 @@
     return call(
         functools.partial(both_kernel, layer, z.pieces, z.length, len(weights)),
         pos, (h, grad, *lines), (*biases, *weights),
-        [z.low, z.low, z.small, z.small, z.bias, ((12 * z.model, z.model), BF16)],
+        [z.low, z.low, z.small, z.small, z.bias, *z.pack(6)],
         [*z.weights, z.bias, z.line, z.qkv, z.probs, z.low, z.full, z.full, z.wide, z.wide, z.full,
          z.full, z.low, z.wide, z.low, z.qkv, (z.bias[0], F32), *z.weights],
         weight_count(len(weights)) + 1,
@@ -471,54 +490,49 @@
     return call(
         functools.partial(backward_mlp_kernel, layer, z.pieces, z.length, len(weights)),
         pos, (grad, middle, *lines, act, slope, out_branch), weights,
-        [z.full, z.small, ((8 * z.model, z.model), BF16)],
+        [z.full, z.small, *z.pack(4)],
         [*z.weights, z.line, z.low, z.wide, z.low, *z.weights[2:]],
         weight_count(len(weights)),
     )
 
 
-def backward_attention(layer, z, pos, h, lines, qkv, probs, att, branch, d_middle, weights, after):
+def backward_attention(layer, z, pos, h, lines, qkv, probs, att, branch, d_middle, weights, earlier):
     return call(
-        functools.partial(backward_attention_kernel, layer, z.pieces, z.length, len(weights), len(after)),
-        pos, (h, *lines, qkv, probs, att, branch, d_middle), (*weights, *after),
-        [z.full, z.small, z.bias, ((4 * z.model, z.model), BF16)],
+        functools.partial(backward_attention_kernel, layer, z.pieces, z.length, len(weights), len(earlier)),
+        pos, (h, *lines, qkv, probs, att, branch, d_middle), (*weights, *earlier),
+        [z.full, z.small, z.bias, *z.pack(2)],
         [*z.weights, z.line, z.low, z.qkv, z.low, (z.bias[0], F32), *z.weights[:2]],
         weight_count(len(weights)),
     )
 
 
-def half_kernel(pos, *refs):
-    own, other, outs = refs[:4], refs[4:8], refs[8:]
-    section = pos[0]
-    model = outs[0].shape[1]
-    q = own[0].shape[0]
-    for layer in range(2):
-        out = outs[layer]
-        for source, here in ((own, section == layer), (other, section != layer)):
-            qkv, proj, fc1, fc2 = source
-
-            @pl.when(jnp.logical_and(here, section == 0))
-            def _():
-                for c in range(3):
-                    out[c * q : (c + 1) * q, :] = qkv[:, c * model : (c + 1) * model]
-                out[3 * q : 4 * q, :] = proj[...]
-                for c in range(2):
-                    out[(4 + c) * q : (5 + c) * q, :] = fc1[:, c * model : (c + 1) * model]
-
-            @pl.when(jnp.logical_and(here, section == 1))
-            def _():
-                for c in range(2):
-                    out[c * q : (c + 1) * q, :] = fc1[:, (2 + c) * model : (3 + c) * model]
-                out[2 * q : 6 * q, :] = fc2[...]
-
-
-def halves(pos, own, other):
+def pack_kernel(pos, qkv, proj, fc1, fc2, out):
+    q, model = proj.shape
+    for c in range(3):
+        out[c * q : (c + 1) * q, :] = qkv[:, c * model : (c + 1) * model]
+    out[3 * q : 4 * q, :] = proj[...]
+    for c in range(4):
+        out[(4 + c) * q : (5 + c) * q, :] = fc1[:, c * model : (c + 1) * model]
+    out[8 * q : 12 * q, :] = fc2[...]
+
+
+def pack_shard(pos, own):
     q, model = own[1].shape
-    shape = ((6 * q, model), BF16)
-    return call(half_kernel, pos, (*own, *other), (), [shape, shape], [])
-
-
-def lookup_kernel(table, index, out, work):
+    return call(pack_kernel, pos, own, (), [((12 * q, model), BF16)], [])[0]
+
+
+def after(values, others):
+    return pl.pallas_call(
+        lambda *refs: None,
+        out_shape=[jax.ShapeDtypeStruct(v.shape, v.dtype) for v in values],
+        in_specs=[pl.BlockSpec(memory_space=pl.ANY)] * (len(values) + len(others)),
+        out_specs=[pl.BlockSpec(memory_space=pl.ANY)] * len(values),
+        input_output_aliases={i: i for i in range(len(values))},
+    )(*values, *others)
+
+
+def lookup_kernel(table, index, *rest):
+    out, work = rest[-2:]
     heads, length = out.shape[0], out.shape[1]
     high_count = table.shape[0] // 8
     values = table[...]
@@ -544,7 +558,7 @@
     out[...] = work[...].astype(BF16)
 
 
-def lookup(table, index):
+def lookup(table, index, earlier):
     heads, entries = table.shape
     high_count = HIGH
     padded = jnp.pad(table, ((0, 8 - heads), (0, high_count * LOW - entries)))
@@ -553,14 +567,16 @@
     return pl.pallas_call(
         lookup_kernel,
         out_shape=jax.ShapeDtypeStruct((heads, length, length), BF16),
+        in_specs=[pl.BlockSpec(memory_space=pltpu.VMEM)] * 2 + [pl.BlockSpec(memory_space=pl.ANY)] * len(earlier),
+        out_specs=pl.BlockSpec(memory_space=pltpu.VMEM),
         scratch_shapes=[pltpu.VMEM((heads, length, length), F32)],
         compiler_params=pltpu.CompilerParams(vmem_limit_bytes=VMEM_BYTES),
-    )(rows, index)
-
-
-def table_kernel(scores_a, scores_b, index, *rest):
+    )(rows, index, *earlier)
+
+
+def table_kernel(scores, index, *rest):
     out = rest[-1]
-    heads, length = scores_a.shape[0], scores_a.shape[1]
+    heads, length = scores.shape[0], scores.shape[1]
     out[...] = jnp.zeros_like(out)
     low_ids = lax.broadcasted_iota(jnp.int32, (LOW, length), 0)
     high_ids = lax.broadcasted_iota(jnp.int32, (HIGH, length), 0)
@@ -568,7 +584,7 @@
     def step(i, carry):
         rows = pl.ds(pl.multiple_of(i * 16, 16), 16)
         entries = index[rows, :]
-        block = [scores[head, rows, :].astype(F32) for scores in (scores_a, scores_b) for head in range(heads)]
+        block = [scores[head, rows, :].astype(F32) for head in range(heads)]
         total = None
         for r in range(16):
             entry = entries[r : r + 1, :]
@@ -583,16 +599,15 @@
     lax.fori_loop(0, length // 16, step, 0)
 
 
-def table_gradients(scores_a, scores_b, index, after):
-    heads = scores_a.shape[0]
-    total = pl.pallas_call(
+def table_gradient(scores, index, earlier):
+    heads = scores.shape[0]
+    return pl.pallas_call(
         table_kernel,
-        out_shape=jax.ShapeDtypeStruct((2 * heads * HIGH, LOW), F32),
-        in_specs=[pl.BlockSpec(memory_space=pltpu.VMEM)] * 3 + [pl.BlockSpec(memory_space=pl.ANY)] * len(after),
+        out_shape=jax.ShapeDtypeStruct((heads * HIGH, LOW), F32),
+        in_specs=[pl.BlockSpec(memory_space=pltpu.VMEM)] * 2 + [pl.BlockSpec(memory_space=pl.ANY)] * len(earlier),
         out_specs=pl.BlockSpec(memory_space=pltpu.VMEM),
         compiler_params=pltpu.CompilerParams(vmem_limit_bytes=VMEM_BYTES),
-    )(scores_a, scores_b, index, *after)
-    return total[: heads * HIGH], total[heads * HIGH :]
+    )(scores, index, *earlier)
 
 
 def swap_section(value):
@@ -614,27 +629,22 @@
     return stack
 
 
-def one_section_pairs(layer, count, step):
-    return [(layer * count + i, layer * count + (i ^ step)) for i in range(count)]
-
-
-def section_sums(pack, layer, shards):
-    other = lax.ppermute(pack, "section", [(1 - layer, layer)])
-    size = pack.shape[0] // shards
+def section_sums(keep, send, shards):
+    other = swap_section(send)
+    size = keep.shape[0] // shards
     return [
-        pack[p * size : (p + 1) * size].astype(F32) + other[p * size : (p + 1) * size].astype(F32)
+        keep[p * size : (p + 1) * size].astype(F32) + other[p * size : (p + 1) * size].astype(F32)
         for p in range(shards)
     ]
 
 
-def send_pieces(sums, layer):
-    shards = len(sums)
-    low = [x.astype(BF16) for x in sums[1:]]
-    got = [
-        lax.ppermute(low[p - 1], ("section", "fsdp"), one_section_pairs(layer, shards, p))
-        for p in range(1, shards)
-    ]
-    return low, got
+def low_pieces(sums):
+    return [x.astype(BF16) for x in sums[1:]]
+
+
+def to_peers(messages, axis):
+    count = lax.axis_size(axis)
+    return [lax.ppermute(messages[p - 1], axis, pairs_of(count, p)) for p in range(1, count)]
 
 
 def add_pieces(own, got):
@@ -644,35 +654,30 @@
     return total
 
 
-def replica_total(total, layer, rank):
+def replica_parts(total, rank):
     replicas = lax.axis_size("rep")
-    size = total.shape[0]
-    parts = total.reshape(replicas, size // replicas, -1)
-    low_parts = parts.astype(BF16)
+    parts = total.reshape(replicas, total.shape[0] // replicas, -1)
+    low = parts.astype(BF16)
     mine = lax.dynamic_index_in_dim(parts, rank, 0, keepdims=False)
-    names = ("section", "rep")
-    got = [
-        lax.ppermute(
-            lax.dynamic_index_in_dim(low_parts, rank ^ j, 0, keepdims=False),
-            names, one_section_pairs(layer, replicas, j),
-        )
-        for j in range(1, replicas)
-    ]
-    mine = add_pieces(mine, got).astype(BF16)
-    quarters = [mine] + [
-        lax.ppermute(mine, names, one_section_pairs(layer, replicas, j)) for j in range(1, replicas)
-    ]
-    return by_rank(quarters, rank).reshape(size, -1)
-
-
-def unpack_attention(pack):
-    q = pack.shape[0] // 4
-    return jnp.concatenate([pack[c * q : (c + 1) * q] for c in range(3)], axis=1), pack[3 * q :]
-
-
-def unpack_mlp(pack):
-    q = pack.shape[0] // 8
-    return jnp.concatenate([pack[c * q : (c + 1) * q] for c in range(4)], axis=1), pack[4 * q :]
+    return mine, [lax.dynamic_index_in_dim(low, rank ^ j, 0, keepdims=False) for j in range(1, replicas)]
+
+
+def replica_whole(mine, rank):
+    quarters = [mine] + from_peers(mine, "rep")
+    return by_rank(quarters, rank).reshape(-1, mine.shape[1])
+
+
+def unpack(pack):
+    q = pack.shape[0] // 12
+    unit = [pack[c * q : (c + 1) * q] for c in range(8)]
+    return (
+        jnp.concatenate([unit[0], unit[1], unit[6]], axis=1), unit[7],
+        jnp.concatenate(unit[2:6], axis=1), pack[8 * q :],
+    )
+
+
+def pad_rows(value):
+    return jnp.pad(value, ((0, -value.shape[0] % 16), (0, 0)))
 
 
 def from_peers(value, axis):
@@ -711,13 +716,17 @@
     own_raw = [w_qkv[0], w_proj[0], w_fc1[0], w_fc2[0]]
     cond_size = conditioning.size
     width = model // shards
-    w_ada_all = lax.all_gather(w_ada[0], "fsdp", axis=0, tiled=True)
     if direct:
         row = jnp.concatenate([conditioning.reshape(1, -1), b_ada, b_qv, b_proj, b_fc1, b_fc2], axis=1)
         rows = [row] + from_peers(row, "fsdp")
-        other_raw = [swap_section(w) for w in own_raw]
-        half0, half1 = halves(pos, own_raw, other_raw)
-        got0 = from_peers(half0, "fsdp")
+        own_pack = pack_shard(pos, own_raw)
+        middle_row = own_pack.shape[0] // 2
+        got_x = lax.ppermute(own_pack, "fsdp", pairs_of(shards, 1))
+        got_y = lax.ppermute(own_pack, "fsdp", pairs_of(shards, 2))
+        got_first = lax.ppermute(got_x[:middle_row], "fsdp", pairs_of(shards, 2))
+        got_second = lax.ppermute(got_y[middle_row:], "fsdp", pairs_of(shards, 1))
+        own_weights = [own_pack, got_x, got_y, got_first, got_second]
+        weights = own_weights + [swap_section(w) for w in own_weights]
         cond_pieces = jnp.stack([r[0, :cond_size].reshape(samples, model) for r in rows])
         acts = jax.nn.silu(cond_pieces.astype(F32)).astype(BF16)
         acts = lax.dynamic_slice_in_dim(acts, shard * width, width, 2)
@@ -725,21 +734,17 @@
         modulation = partial[0]
         for p in range(1, shards):
             modulation = modulation + lax.ppermute(partial[p], "fsdp", pairs_of(shards, p))
-        got1 = from_peers(half1, "fsdp")
-        weights0 = own_raw + other_raw + got0 + [swap_section(w) for w in got0]
-        weights1 = own_raw + other_raw + got1 + [swap_section(w) for w in got1]
         bias_rows = by_rank([r[0, cond_size:] for r in rows], shard)
+        bias_own = lookup(bias_table[0], relative_bias_index, [own_pack, partial])
     else:
         row = jnp.concatenate([b_ada, b_qv, b_proj, b_fc1, b_fc2], axis=1)
         bias_rows = lax.all_gather(row[0], "fsdp", axis=0)
         whole = [lax.all_gather(w, "fsdp", axis=0, tiled=True) for w in own_raw]
-        own_whole = jnp.concatenate(
-            [whole[0][:, c * model : (c + 1) * model] for c in range(3)] + [whole[1]]
-            + [whole[2][:, c * model : (c + 1) * model] for c in range(4)] + [whole[3]]
-        )
-        weights0 = weights1 = [own_whole, swap_section(own_whole)]
+        own_whole = pack_shard(pos, whole)
+        weights = [own_whole, swap_section(own_whole)]
         acts = jax.nn.silu(conditioning.astype(F32)).astype(BF16)
-        modulation = dot(acts, w_ada_all)
+        modulation = dot(acts, lax.all_gather(w_ada[0], "fsdp", axis=0, tiled=True))
+        bias_own = lookup(bias_table[0], relative_bias_index, [])
     cuts = [b_ada.shape[1], b_qv.shape[1], b_proj.shape[1], b_fc1.shape[1], b_fc2.shape[1]]
     biases, at = [], 0
     for cut in cuts:
@@ -750,44 +755,34 @@
     own_line = jnp.concatenate([own_samples(modulation).reshape(1, -1)] + biases[1:], axis=1)
     other_line = swap_section(jnp.concatenate([other_samples.reshape(1, -1)] + biases[1:], axis=1))
     lines = (own_line, other_line)
-    bias_own = lookup(bias_table[0], relative_bias_index)
     bias_heads = (bias_own, swap_section(bias_own))
 
     live = (jnp.arange(half)[:, None, None] < lax.dynamic_index_in_dim(micro_sizes[0], section, 0)).astype(BF16)
     h0 = own_samples(inputs).reshape(half * length, model)
     grad1 = (own_samples(cotangent) * live).reshape(half * length, model)
 
-    qkv, probs, att, branch, middle, act, slope, out_branch, h1 = forward_layer(0, z, pos, h0, lines, bias_heads, weights0)
-    out1, d_h1, small_a1, small_m1, scores1, pack1 = both_ways(1, z, pos, h1, grad1, lines, bias_heads, weights1)
-    d_middle, small_m0, pack_m0 = backward_mlp(0, z, pos, d_h1, middle, lines, act, slope, out_branch, weights0)
+    qkv, probs, att, branch, middle, act, slope, out_branch, h1 = forward_layer(0, z, pos, h0, lines, bias_heads, weights)
+    w_ada_later = after([w_ada[0]], [h1])[0]
+    w_ada_all = lax.all_gather(w_ada_later, "fsdp", axis=0, tiled=True)
+    out1, d_h1, small_a1, small_m1, scores1, keep1, send1 = both_ways(1, z, pos, h1, grad1, lines, bias_heads, weights)
+    d_middle, small_m0, keep_m0, send_m0 = backward_mlp(0, z, pos, d_h1, middle, lines, act, slope, out_branch, weights)
+    pieces = z.pieces
+    sums1 = section_sums(keep1, send1, pieces)
+    sums_m0 = section_sums(keep_m0, send_m0, pieces)
+    low1, low_m0 = low_pieces(sums1), low_pieces(sums_m0)
+    table1 = table_gradient(scores1, relative_bias_index, low1)
+    d_h0, small_a0, scores0, keep_a0, send_a0 = backward_attention(
+        0, z, pos, h0, lines, qkv, probs, att, branch, d_middle, weights, [table1, w_ada_all, *low_m0]
+    )
+    sums_a0 = section_sums(keep_a0, send_a0, pieces)
     if direct:
-        sums1 = section_sums(pack1, 1, shards)
-        low1, got1 = send_pieces(sums1, 1)
-        after = low1
+        got1 = to_peers(low1, "fsdp")
+        got_m0 = to_peers(low_m0, "fsdp")
+        part1, others1 = replica_parts(add_pieces(sums1[0], got1), rank)
+        table0 = table_gradient(scores0, relative_bias_index, others1)
+        half1 = replica_whole(add_pieces(part1, to_peers(others1, "rep")).astype(BF16), rank)
     else:
-        after = []
-    d_h0, small_a0, scores0, pack_a0 = backward_attention(
-        0, z, pos, h0, lines, qkv, probs, att, branch, d_middle, weights0, after
-    )
-
-    if direct:
-        sums_m0 = section_sums(pack_m0, 0, shards)
-        low_m0, got_m0 = send_pieces(sums_m0, 0)
-        sums_a0 = section_sums(pack_a0, 0, shards)
-        low_a0, got_a0 = send_pieces(sums_a0, 0)
-        done1 = replica_total(add_pieces(sums1[0], got1), 1, rank)
-        total0 = jnp.concatenate([add_pieces(sums_a0[0], got_a0), add_pieces(sums_m0[0], got_m0)])
-        done0 = replica_total(total0, 0, rank)
-        done = mine(done0, done1).astype(F32)
-        g_qkv, g_proj = unpack_attention(done[:model])
-        g_fc1, g_fc2 = unpack_mlp(done[model:])
-        after = got1 + low_a0 + low_m0
-    else:
-        pack0 = jnp.concatenate([pack_a0, pack_m0])
-        total = (mine(pack0, pack1).astype(F32) + swap_section(mine(pack1, pack0)).astype(F32)).astype(BF16)
-        grads = unpack_attention(total[: 4 * model]) + unpack_mlp(total[4 * model :])
-        grads = [lax.psum_scatter(g, "fsdp", scatter_dimension=0, tiled=True) for g in grads]
-        g_qkv, g_proj, g_fc1, g_fc2 = [g.astype(F32) for g in lax.psum(tuple(grads), "rep")]
+        table0 = table_gradient(scores0, relative_bias_index, [])
 
     other_out = swap_section(mine(out1, h1))
     activations = in_order(mine(h1, out1).reshape(half, length, model), other_out.reshape(half, length, model))
@@ -797,7 +792,7 @@
         other_in.astype(F32).reshape(half, length, model),
     )
 
-    tables = table_gradients(scores0, scores1, relative_bias_index, after)
+    tables = (table0, table1)
     smalls = [
         jnp.concatenate([small_a0[:, :3], small_m0, small_a0[:, 3:]], axis=1),
         jnp.concatenate([small_a1[:, :3], small_m1, small_a1[:, 3:]], axis=1),
@@ -815,18 +810,34 @@
     kept = jnp.concatenate([low, conditioning[:, None]], axis=1).reshape(-1, model)
     summed = jnp.concatenate([jnp.sum(small[:, 6:14], axis=0), table.reshape(-1, model)])
     if direct:
-        both = jnp.concatenate([kept, summed.astype(BF16)])
-        plane = [both] + from_peers(both, "fsdp")
-        count = kept.shape[0]
-        summed = pair_sum([p[count:].astype(F32) for p in plane])
-        both = jnp.concatenate([p[:count] for p in plane] + [summed.astype(BF16)])
-        every = [both] + from_peers(both, "rep")
-        count = count * shards
-        summed = pair_sum([p[count:].astype(F32) for p in every])
+        both = pad_rows(jnp.concatenate([kept, summed.astype(BF16)]))
+        low_a0 = low_pieces(sums_a0)
+        size, count, end = sums_a0[0].shape[0], kept.shape[0], kept.shape[0] + summed.shape[0]
+        got = to_peers([jnp.concatenate([x, both]) for x in low_a0], "fsdp")
+        total0 = jnp.concatenate([
+            add_pieces(sums_a0[0], [x[:size] for x in got]), add_pieces(sums_m0[0], got_m0)
+        ])
+        plane = [both] + [x[size:] for x in got]
+        summed = pair_sum([p[count:end].astype(F32) for p in plane])
+        both = pad_rows(jnp.concatenate([p[:count] for p in plane] + [summed.astype(BF16)]))
+        part0, others0 = replica_parts(total0, rank)
+        got = to_peers([jnp.concatenate([x, both]) for x in others0], "rep")
+        size = part0.shape[0]
+        half0 = replica_whole(add_pieces(part0, [x[:size] for x in got]).astype(BF16), rank)
+        every = [both] + [x[size:] for x in got]
+        count, end = count * shards, count * shards + summed.shape[0]
+        summed = pair_sum([p[count:end].astype(F32) for p in every])
         kept = by_rank([p[:count] for p in every], rank).reshape(-1, 7, model)
+        grads = [g.astype(F32) for g in unpack(in_order(mine(half0, half1), swap_section(mine(half1, half0))))]
     else:
         kept = lax.all_gather(kept, ("fsdp", "rep"), axis=0, tiled=True).reshape(-1, 7, model)
         summed = lax.psum(summed, ("fsdp", "rep"))
+        half0 = jnp.concatenate([sums_a0[0], sums_m0[0]]).astype(BF16)
+        half1 = sums1[0].astype(BF16)
+        whole = unpack(in_order(mine(half0, half1), swap_section(mine(half1, half0))))
+        whole = [lax.psum_scatter(g, "fsdp", scatter_dimension=0, tiled=True) for g in whole]
+        grads = [g.astype(F32) for g in lax.psum(tuple(whole), "rep")]
+    g_qkv, g_proj, g_fc1, g_fc2 = grads
     act_all = jax.nn.silu(kept[:, 6].astype(F32)).astype(BF16)
     act_cols = lax.dynamic_slice_in_dim(act_all, shard * width, width, 1)
     g_ada = jnp.concatenate([dot_cols(act_cols, kept[:, i]) for i in range(6)], axis=1)

time: 351 us -> 280 us (0.80); the launches traced: 345 us -> 279 us
  starting transfers between devices: 107 us -> 46.1 us
  local copies, waits for them, and re-layouts: 23.8 us -> 16.3 us
  Pallas kernels: 89.8 us -> 94.6 us
  waiting for transfers between devices: 70.8 us -> 74.8 us
  matrix products: 6 us -> 2.45 us
    ppermute x24 -> x19, waiting for transfers between devices: 12.6 us -> 67 us  [the longest x15 56.2 us: to_peers(): lax.ppermute(messages[p - 1], axis, pairs_of(count, p))]
    ppermute x15 -> x9, waiting for transfers between devices: 35.2 us -> 2.82 us  [from_peers(): lax.ppermute(value, axis, pairs_of(lax.axis_size(axis), p))]
    ppermute x24 -> x19, starting transfers between devices: 54.1 us -> 25.9 us  [the longest x15 20.3 us: to_peers(): lax.ppermute(messages[p - 1], axis, pairs_of(count, p))]
    ppermute x17 -> x16, starting transfers between devices: 20.5 us -> 3.18 us  [swap_section(): return lax.ppermute(value, 'section', [(0, 1), (1, 0)])]
    ppermute x15 -> x9, starting transfers between devices: 28.4 us -> 13.4 us  [from_peers(): lax.ppermute(value, axis, pairs_of(lax.axis_size(axis), p))]
    all_gather x1, waiting for transfers between devices: 13.4 us -> 0.01 us  [per_device(): w_ada_all = lax.all_gather(w_ada_later, 'fsdp', axis=0, tiled=True)]
    ppermute x17 -> x16, waiting for transfers between devices: 6.16 us -> 1.41 us  [swap_section(): return lax.ppermute(value, 'section', [(0, 1), (1, 0)])]
    pallas_call x1 -> x3, Pallas kernels: 11.1 us -> 15.3 us  [the longest x2 15.3 us: table_gradient(): pl.pallas_call(table_kernel, out_shape=jax.ShapeDtypeStruct((heads * HIGH...]
  transfers between devices with their start and end apart: 60 -> 48, of which waited for: 19 -> 16; matrix products, arithmetic and copies ran while one was open for 14% -> 13% of each run, Pallas kernels for 15% -> 15%
where the time goes in v3:
time: 280 us; the launch traced here: 279 us
  Pallas kernels  94.6 us (34%)
  waiting for transfers between devices  74.8 us (27%)
  starting transfers between devices  46.1 us (16%)
  other arithmetic  29.9 us (11%)
  local copies, waits for them, and re-layouts  16.3 us (6%)
  between operations  15.2 us (5%)
    pallas_call x5, Pallas kernels, call(): pl.pallas_call(kernel, out_shape=[jax.ShapeDtypeStruct(shape, dtype) for...  68.1 us
    ppermute x15, waiting for transfers between devices, to_peers(): lax.ppermute(messages[p - 1], axis, pairs_of(count, p))  56.2 us
    ppermute x15, starting transfers between devices, to_peers(): lax.ppermute(messages[p - 1], axis, pairs_of(count, p))  20.3 us
    pallas_call x2, Pallas kernels, table_gradient(): pl.pallas_call(table_kernel, out_shape=jax.ShapeDtypeStruct((heads * HIGH...  15.3 us
    ppermute x9, starting transfers between devices, from_peers(): lax.ppermute(value, axis, pairs_of(lax.axis_size(axis), p))  13.4 us
    pallas_call x1, Pallas kernels, lookup(): pl.pallas_call(lookup_kernel, out_shape=jax.ShapeDtypeStruct((heads, leng...  11.2 us
    ppermute x1, waiting for transfers between devices, per_device(): got_first = lax.ppermute(got_x[:middle_row], 'fsdp', pairs_of(shards, 2))  9.44 us
  transfers between devices with their start and end apart: 48, of which 16 were waited for; matrix products, arithmetic and copies ran while one was open for 13% of the time, Pallas kernels for 15%

profile of v3, /device:TPU:0, one launch (start us, length us, event | category | flops | bytes accessed | tf_op | source)
XLA Modules:
  0.0 279.3 jit_solution(5679641053420539103)
XLA Ops:
  9.8 3.0 %collective-permute-start = (bf16[1,2880]{1,0:T(2,128)(2,1)S(1)}, bf16[1,2880]{1,0:T(2,128)(2,1)S(1)}, u32[]{:S(2)}, u32[]{:S(2)}) collective-permute-start(bf16[1,2880]{1,0:T(2,128)(2,1)S(1)} %concatenate.155), channel_id=1, source_target_pairs={{0,4},{4,0},{8,12},{12,8},{1,5},{5,1},{9,13},{13,9},{2,6},{6,2},{1... | collective-permute-start | bytes 17288 | tf_op jit(solution)/shard_map/ppermute | solution.py:684
  15.0 2.2 shard_map.263.rest_0_.rest_2_
  17.2 1.9 collective-permute-start.8
  23.1 2.9 %collective-permute-start.5 = (f32[4,2304]{1,0:T(4,128)S(1)}, f32[4,2304]{1,0:T(4,128)S(1)}, u32[]{:S(2)}, u32[]{:S(2)}) collective-permute-start(f32[4,2304]{1,0:T(4,128)S(1)} %get-tuple-element.107), channel_id=1, source_target_pairs={{0,12},{4,8},{8,4},{12,0},{1,13},{5,9},{9,5},{13,1},{2,14},{6,10},... | collective-permute-start | bytes 110600 | tf_op jit(solution)/shard_map/ppermute | solution.py:736
  26.4 11.2 %shard_map.264.rest_0_.own_bias = bf16[6,256,256]{2,1,0:T(8,128)(2,1)} custom-call(bf16[128,64]{1,0:T(8,128)(2,1)} %bitcast.241, s32[256,256]{1,0:T(8,128)} %index.5, bf16[1152,384]{1,0:T(8,128)(2,1)} %shard_map.263.rest_0_.rest_2_, f32[4,4,2304]{2,1,0:T(4,128)} %copy-done.17), custom_call_target="tpu_custom_call" | custom-call | tf_op jit(solution)/shard_map/pallas_call | solution.py:567
  37.6 1.8 collective-permute-done.3
  39.4 1.8 collective-permute-done.4
  45.7 9.4 %collective-permute-done.10.rest_5_.rest_3_ = bf16[576,384]{1,0:T(8,128)(2,1)} collective-permute-done((bf16[576,384]{1,0:T(8,128)(2,1)S(1)}, bf16[576,384]{1,0:T(8,128)(2,1)}, u32[]{:S(2)}, u32[]{:S(2)}) %collective-permute-start.10) | collective-permute-done | bytes 442400 | tf_op jit(solution)/shard_map/ppermute | solution.py:726
  57.7 2.1 dynamic-slice_multiply_fusion
  60.8 15.2 %shard_map.265 = (bf16[512,1152]{1,0:T(8,128)(2,1)}, bf16[2,6,256,256]{3,2,1,0:T(8,128)(2,1)}, bf16[512,384]{1,0:T(8,128)(2,1)}, f32[512,384]{1,0:T(8,128)}, f32...) custom-call(s32[2]{0:T(128)} %pad_add_fusion.pos.pos_ref, ...), custom_call_target="tpu_custom_call" | custom-call | tf_op jit(solution)/shard_map/pallas_call | solution.py:436
  75.9 26.0 %shard_map.266 = (bf16[512,384]{1,0:T(8,128)(2,1)}, bf16[512,384]{1,0:T(8,128)(2,1)}, f32[2,8,384]{2,1,0:T(8,128)}, f32[2,8,384]{2,1,0:T(8,128)}, bf16[6,256,256...) custom-call(s32[2]{0:T(128)} %pad_add_fusion.pos.pos_ref, ...), custom_call_target="tpu_custom_call" | custom-call | tf_op jit(solution)/shard_map/pallas_call | solution.py:436
  102.5 12.1 %shard_map.267 = (f32[512,384]{1,0:T(8,128)}, f32[2,8,384]{2,1,0:T(8,128)}, bf16[1536,384]{1,0:T(8,128)(2,1)}, bf16[1536,384]{1,0:T(8,128)(2,1)}) custom-call(s32[2]{0:T(128)} %pad_add_fusion.pos.pos_ref, bf16[512,384]{1,0:T(8,128)(2,1)} %get-tuple-element.45.grad, f32[512,384]{1,0:T(8,128)} %get-tuple-element.46.middle, f32[1,7680]{1,0:T(1,128)} %copy-done.27, ...), custom_call_target="tpu_custom_call" | custom-call | tf_op jit(solution)/shard_map/pallas_call | solution.py:436
  114.7 1.8 add_convert_fusion
  121.9 11.8 %collective-permute-done.24 = bf16[576,384]{1,0:T(8,128)(2,1)} collective-permute-done((bf16[576,384]{1,0:T(8,128)(2,1)S(1)}, bf16[576,384]{1,0:T(8,128)(2,1)}, u32[]{:S(2)}, u32[]{:S(2)}) %collective-permute-start.24) | collective-permute-done | bytes 442400 | tf_op jit(solution)/shard_map/ppermute | solution.py:647
  133.7 2.7 collective-permute-done.25
  136.4 11.8 %collective-permute-done.26 = bf16[576,384]{1,0:T(8,128)(2,1)} collective-permute-done((bf16[576,384]{1,0:T(8,128)(2,1)S(1)}, bf16[576,384]{1,0:T(8,128)(2,1)}, u32[]{:S(2)}, u32[]{:S(2)}) %collective-permute-start.26) | collective-permute-done | bytes 442400 | tf_op jit(solution)/shard_map/ppermute | solution.py:647
  156.7 2.6 collective-permute-start.41
  161.2 5.6 %collective-permute-done.41 = bf16[144,384]{1,0:T(8,128)(2,1)S(1)} collective-permute-done((bf16[144,384]{1,0:T(8,128)(2,1)S(1)}, bf16[144,384]{1,0:T(8,128)(2,1)S(1)}, u32[]{:S(2)}, u32[]{:S(2)}) %collective-permute-start.41) | collective-permute-done | bytes 110624 | tf_op jit(solution)/shard_map/ppermute | solution.py:647
  166.9 1.9 collective-permute-start.43
  168.8 3.4 %collective-permute-start.44 = (bf16[144,384]{1,0:T(8,128)(2,1)S(1)}, bf16[144,384]{1,0:T(8,128)(2,1)S(1)}, u32[]{:S(2)}, u32[]{:S(2)}) collective-permute-start(bf16[144,384]{1,0:T(8,128)(2,1)S(1)} %fusion.8), channel_id=1, source_target_pairs={{0,3},{1,2},{2,1},{3,0},{4,7},{5,6},{6,5},{7,4},{8,11},{9,10},{10,... | collective-permute-start | bytes 331784 | tf_op jit(solution)/shard_map/ppermute | solution.py:684
  172.2 2.0 convert_add_fusion.1
  174.2 7.6 %shard_map.268.rest_10_ = f32[96,64]{1,0:T(8,128)} custom-call(bf16[6,256,256]{2,1,0:T(8,128)(2,1)} %get-tuple-element.51.scores, s32[256,256]{1,0:T(8,128)} %index.5, bf16[576,384]{1,0:T(8,128)(2,1)} %copy-done.16, bf16[576,384]{1,0:T(8,128)(2,1)} %copy-done.15, bf16[576,384]{1,0:T(8,128)(2,1)} %copy-done.14), custom_call_target="tpu_custom_call" | custom-call | tf_op jit(solution)/shard_map/pallas_call | solution.py:604
  183.4 12.6 %shard_map.270 = (f32[512,384]{1,0:T(8,128)}, f32[2,8,384]{2,1,0:T(8,128)}, bf16[6,256,256]{2,1,0:T(8,128)(2,1)}, bf16[768,384]{1,0:T(8,128)(2,1)}, bf16[768,384]{1,0:T(8,128)(2,1)}) custom-call(s32[2]{0:T(128)} %pad_add_fusion.pos.pos_ref, bf16[512,384]{1,0:T(8,128)(2,1)} %bitcast.214, f32[1,7680]{1,0:T(1,128)} %copy-done.27, f32[1,7680]{1,0:T(1,128)} %copy-done.29, ...), custom_call_target="tpu_custom_call" | custom-call | tf_op jit(solution)/shard_map/pallas_call | solution.py:436
  197.7 7.6 %shard_map.271 = f32[96,64]{1,0:T(8,128)} custom-call(bf16[6,256,256]{2,1,0:T(8,128)(2,1)} %get-tuple-element.63.scores, s32[256,256]{1,0:T(8,128)} %index.5, bf16[144,384]{1,0:T(8,128)(2,1)} %copy-done.32, bf16[144,384]{1,0:T(8,128)(2,1)} %copy-done.31, bf16[144,384]{1,0:T(8,128)(2,1)} %copy-done.30), custom_call_target="tpu_custom_call" | custom-call | tf_op jit(solution)/shard_map/pallas_call | solution.py:604
  208.0 2.0 convert_select_fusion.1
  221.9 2.5 collective-permute-done.28
  224.4 3.3 %collective-permute-done.29 = bf16[256,384]{1,0:T(8,128)(2,1)S(1)} collective-permute-done((bf16[256,384]{1,0:T(8,128)(2,1)S(1)}, bf16[256,384]{1,0:T(8,128)(2,1)S(1)}, u32[]{:S(2)}, u32[]{:S(2)}) %collective-permute-start.29) | collective-permute-done | bytes 196640 | tf_op jit(solution)/shard_map/ppermute | solution.py:647
  232.6 3.4 %collective-permute-start.35 = (bf16[288,384]{1,0:T(8,128)(2,1)S(1)}, bf16[288,384]{1,0:T(8,128)(2,1)S(1)}, u32[]{:S(2)}, u32[]{:S(2)}) collective-permute-start(bf16[288,384]{1,0:T(8,128)(2,1)S(1)} %get-tuple-element.112), channel_id=1, source_target_pairs={{0,3},{1,2},{2,1},{3,0},{4,7},{5,6},{6,5},{7,4},{8,11},{9,10},{10,... | collective-permute-start | bytes 663560 | tf_op jit(solution)/shard_map/ppermute | solution.py:647
  238.6 8.5 %collective-permute-done.35 = bf16[288,384]{1,0:T(8,128)(2,1)S(1)} collective-permute-done((bf16[288,384]{1,0:T(8,128)(2,1)S(1)}, bf16[288,384]{1,0:T(8,128)(2,1)S(1)}, u32[]{:S(2)}, u32[]{:S(2)}) %collective-permute-start.35) | collective-permute-done | bytes 221216 | tf_op jit(solution)/shard_map/ppermute | solution.py:647
  247.1 7.0 %collective-permute-done.36 = bf16[288,384]{1,0:T(8,128)(2,1)S(1)} collective-permute-done((bf16[288,384]{1,0:T(8,128)(2,1)S(1)}, bf16[288,384]{1,0:T(8,128)(2,1)S(1)}, u32[]{:S(2)}, u32[]{:S(2)}) %collective-permute-start.36) | collective-permute-done | bytes 221216 | tf_op jit(solution)/shard_map/ppermute | solution.py:647
  254.3 2.7 collective-permute-start.38
  263.6 2.8 %collective-permute-done.39 = bf16[144,384]{1,0:T(8,128)(2,1)S(1)} collective-permute-done((bf16[144,384]{1,0:T(8,128)(2,1)S(1)}, bf16[144,384]{1,0:T(8,128)(2,1)S(1)}, u32[]{:S(2)}, u32[]{:S(2)}) %collective-permute-start.39) | collective-permute-done | bytes 110624 | tf_op jit(solution)/shard_map/ppermute | solution.py:684
  (324 shorter events, 71.0 us)
Async XLA Ops:
  7.3 176.1 %all-gather.2.cloned.1.call-start = ((), (), s32[]{:S(2)}) async-start(), calls=%async_computation | async-start | bytes 2211840 | tf_op jit(solution)/shard_map/all_gather | solution.py:766
  9.8 11.7 %collective-permute-start = (bf16[1,2880]{1,0:T(2,128)(2,1)S(1)}, bf16[1,2880]{1,0:T(2,128)(2,1)S(1)}, u32[]{:S(2)}, u32[]{:S(2)}) collective-permute-start(bf16[1,2880]{1,0:T(2,128)(2,1)S(1)} %concatenate.155), channel_id=1, source_target_pairs={{0,4},{4,0},{8,12},{12,8},{1,5},{5,1},{9,13},{13,9},{2,6},{6,2},{1... | collective-permute-start | bytes 17288 | tf_op jit(solution)/shard_map/ppermute | solution.py:684
  17.2 25.6 %collective-permute-start.8 = (bf16[1152,384]{1,0:T(8,128)(2,1)}, bf16[1152,384]{1,0:T(8,128)(2,1)S(1)}, u32[]{:S(2)}, u32[]{:S(2)}) collective-permute-start(bf16[1152,384]{1,0:T(8,128)(2,1)} %shard_map.263.rest_0_.rest_2_), channel_id=1, source_target_pairs={{0,4},{4,0},{8,12},{12,8},{1,5},{5,1},{9,13},{13,9},{2,6},{6,2},{1... | collective-permute-start | bytes 2654216 | tf_op jit(solution)/shard_map/ppermute | solution.py:724
  19.1 25.3 %collective-permute-start.9 = (bf16[1152,384]{1,0:T(8,128)(2,1)}, bf16[1152,384]{1,0:T(8,128)(2,1)S(1)}, u32[]{:S(2)}, u32[]{:S(2)}) collective-permute-start(bf16[1152,384]{1,0:T(8,128)(2,1)} %shard_map.263.rest_0_.rest_2_), channel_id=1, source_target_pairs={{0,8},{4,12},{8,0},{12,4},{1,9},{5,13},{9,1},{13,5},{2,10},{6,14},... | collective-permute-start | bytes 2654216 | tf_op jit(solution)/shard_map/ppermute | solution.py:725
  22.4 17.0 %collective-permute-start.3 = (f32[4,2304]{1,0:T(4,128)S(1)}, f32[4,2304]{1,0:T(4,128)S(1)}, u32[]{:S(2)}, u32[]{:S(2)}) collective-permute-start(f32[4,2304]{1,0:T(4,128)S(1)} %get-tuple-element.106), channel_id=1, source_target_pairs={{0,4},{4,0},{8,12},{12,8},{1,5},{5,1},{9,13},{13,9},{2,6},{6,2},{1... | collective-permute-start | bytes 110600 | tf_op jit(solution)/shard_map/ppermute | solution.py:736
  23.0 18.2 %collective-permute-start.4 = (f32[4,2304]{1,0:T(4,128)S(1)}, f32[4,2304]{1,0:T(4,128)S(1)}, u32[]{:S(2)}, u32[]{:S(2)}) collective-permute-start(f32[4,2304]{1,0:T(4,128)S(1)} %get-tuple-element.108), channel_id=1, source_target_pairs={{0,8},{4,12},{8,0},{12,4},{1,9},{5,13},{9,1},{13,5},{2,10},{6,14},... | collective-permute-start | bytes 110600 | tf_op jit(solution)/shard_map/ppermute | solution.py:736
  23.1 18.1 %collective-permute-start.5 = (f32[4,2304]{1,0:T(4,128)S(1)}, f32[4,2304]{1,0:T(4,128)S(1)}, u32[]{:S(2)}, u32[]{:S(2)}) collective-permute-start(f32[4,2304]{1,0:T(4,128)S(1)} %get-tuple-element.107), channel_id=1, source_target_pairs={{0,12},{4,8},{8,4},{12,0},{1,13},{5,9},{9,5},{13,1},{2,14},{6,10},... | collective-permute-start | bytes 110600 | tf_op jit(solution)/shard_map/ppermute | solution.py:736
  42.2 17.6 %collective-permute-start.12 = (bf16[1152,384]{1,0:T(8,128)(2,1)S(1)}, bf16[1152,384]{1,0:T(8,128)(2,1)S(1)}, u32[]{:S(2)}, u32[]{:S(2)}) collective-permute-start(bf16[1152,384]{1,0:T(8,128)(2,1)S(1)} %copy-done.2), channel_id=1, source_target_pairs={{0,16},{16,0},{1,17},{17,1},{2,18},{18,2},{3,19},{19,3},{4,20},{20... | collective-permute-start | bytes 2654216 | tf_op jit(solution)/shard_map/ppermute | solution.py:614
  42.8 12.3 %collective-permute-start.10 = (bf16[576,384]{1,0:T(8,128)(2,1)S(1)}, bf16[576,384]{1,0:T(8,128)(2,1)}, u32[]{:S(2)}, u32[]{:S(2)}) collective-permute-start(bf16[576,384]{1,0:T(8,128)(2,1)S(1)} %slice.501), channel_id=1, source_target_pairs={{0,8},{4,12},{8,0},{12,4},{1,9},{5,13},{9,1},{13,5},{2,10},{6,14},... | collective-permute-start | bytes 1327112 | tf_op jit(solution)/shard_map/ppermute | solution.py:726
  44.5 12.0 %collective-permute-start.11 = (bf16[576,384]{1,0:T(8,128)(2,1)S(1)}, bf16[576,384]{1,0:T(8,128)(2,1)}, u32[]{:S(2)}, u32[]{:S(2)}) collective-permute-start(bf16[576,384]{1,0:T(8,128)(2,1)S(1)} %slice.502), channel_id=1, source_target_pairs={{0,4},{4,0},{8,12},{12,8},{1,5},{5,1},{9,13},{13,9},{2,6},{6,2},{1... | collective-permute-start | bytes 1327112 | tf_op jit(solution)/shard_map/ppermute | solution.py:727
  45.1 14.8 %collective-permute-start.13 = (bf16[1152,384]{1,0:T(8,128)(2,1)S(1)}, bf16[1152,384]{1,0:T(8,128)(2,1)}, u32[]{:S(2)}, u32[]{:S(2)}) collective-permute-start(bf16[1152,384]{1,0:T(8,128)(2,1)S(1)} %collective-permute-done.8.rest_3_.rest_1_), channel_id=1, source_target_pairs={{0,16},{16,0},{1,17},{17,1},{2,18},{18,2},{3,19},{19,3},{4,20},{20... | collective-permute-start | bytes 2654216 | tf_op jit(solution)/shard_map/ppermute | solution.py:614
  45.7 14.2 %collective-permute-start.14 = (bf16[1152,384]{1,0:T(8,128)(2,1)S(1)}, bf16[1152,384]{1,0:T(8,128)(2,1)}, u32[]{:S(2)}, u32[]{:S(2)}) collective-permute-start(bf16[1152,384]{1,0:T(8,128)(2,1)S(1)} %collective-permute-done.9.rest_4_.rest_2_), channel_id=1, source_target_pairs={{0,16},{16,0},{1,17},{17,1},{2,18},{18,2},{3,19},{19,3},{4,20},{20... | collective-permute-start | bytes 2654216 | tf_op jit(solution)/shard_map/ppermute | solution.py:614
  101.9 12.7 %collective-permute-start.18 = (bf16[2304,384]{1,0:T(8,128)(2,1)}, bf16[2304,384]{1,0:T(8,128)(2,1)}, u32[]{:S(2)}, u32[]{:S(2)}) collective-permute-start(bf16[2304,384]{1,0:T(8,128)(2,1)} %get-tuple-element.53), channel_id=1, source_target_pairs={{0,16},{16,0},{1,17},{17,1},{2,18},{18,2},{3,19},{19,3},{4,20},{20... | collective-permute-start | bytes 5308424 | tf_op jit(solution)/shard_map/ppermute | solution.py:614
  114.6 37.1 %collective-permute-start.19 = (bf16[1536,384]{1,0:T(8,128)(2,1)}, bf16[1536,384]{1,0:T(8,128)(2,1)}, u32[]{:S(2)}, u32[]{:S(2)}) collective-permute-start(bf16[1536,384]{1,0:T(8,128)(2,1)} %get-tuple-element.55), channel_id=1, source_target_pairs={{0,16},{16,0},{1,17},{17,1},{2,18},{18,2},{3,19},{19,3},{4,20},{20... | collective-permute-start | bytes 3538952 | tf_op jit(solution)/shard_map/ppermute | solution.py:614
  116.5 17.1 %collective-permute-start.24 = (bf16[576,384]{1,0:T(8,128)(2,1)S(1)}, bf16[576,384]{1,0:T(8,128)(2,1)}, u32[]{:S(2)}, u32[]{:S(2)}) collective-permute-start(bf16[576,384]{1,0:T(8,128)(2,1)S(1)} %get-tuple-element.68.rest_0_), channel_id=1, source_target_pairs={{0,4},{4,0},{8,12},{12,8},{1,5},{5,1},{9,13},{13,9},{2,6},{6,2},{1... | collective-permute-start | bytes 1327112 | tf_op jit(solution)/shard_map/ppermute | solution.py:647
  117.1 19.2 %collective-permute-start.25 = (bf16[576,384]{1,0:T(8,128)(2,1)S(1)}, bf16[576,384]{1,0:T(8,128)(2,1)}, u32[]{:S(2)}, u32[]{:S(2)}) collective-permute-start(bf16[576,384]{1,0:T(8,128)(2,1)S(1)} %get-tuple-element.67.rest_1_), channel_id=1, source_target_pairs={{0,8},{4,12},{8,0},{12,4},{1,9},{5,13},{9,1},{13,5},{2,10},{6,14},... | collective-permute-start | bytes 1327112 | tf_op jit(solution)/shard_map/ppermute | solution.py:647
  118.3 29.9 %collective-permute-start.26 = (bf16[576,384]{1,0:T(8,128)(2,1)S(1)}, bf16[576,384]{1,0:T(8,128)(2,1)}, u32[]{:S(2)}, u32[]{:S(2)}) collective-permute-start(bf16[576,384]{1,0:T(8,128)(2,1)S(1)} %get-tuple-element.66.rest_2_), channel_id=1, source_target_pairs={{0,12},{4,8},{8,4},{12,0},{1,13},{5,9},{9,5},{13,1},{2,14},{6,10},... | collective-permute-start | bytes 1327112 | tf_op jit(solution)/shard_map/ppermute | solution.py:647
  121.8 34.8 %collective-permute-start.17 = (bf16[512,384]{1,0:T(8,128)(2,1)S(1)}, bf16[512,384]{1,0:T(8,128)(2,1)S(1)}, u32[]{:S(2)}, u32[]{:S(2)}) collective-permute-start(bf16[512,384]{1,0:T(8,128)(2,1)S(1)} %get-tuple-element.86), channel_id=1, source_target_pairs={{0,16},{16,0},{1,17},{17,1},{2,18},{18,2},{3,19},{19,3},{4,20},{20... | collective-permute-start | bytes 1179656 | tf_op jit(solution)/shard_map/ppermute | solution.py:614
  153.1 19.1 %collective-permute-start.31 = (bf16[384,384]{1,0:T(8,128)(2,1)S(1)}, bf16[384,384]{1,0:T(8,128)(2,1)S(1)}, u32[]{:S(2)}, u32[]{:S(2)}) collective-permute-start(bf16[384,384]{1,0:T(8,128)(2,1)S(1)} %get-tuple-element.71.rest_12_), channel_id=1, source_target_pairs={{0,4},{4,0},{8,12},{12,8},{1,5},{5,1},{9,13},{13,9},{2,6},{6,2},{1... | collective-permute-start | bytes 884744 | tf_op jit(solution)/shard_map/ppermute | solution.py:647
  154.4 17.8 %collective-permute-start.32 = (bf16[384,384]{1,0:T(8,128)(2,1)S(1)}, bf16[384,384]{1,0:T(8,128)(2,1)S(1)}, u32[]{:S(2)}, u32[]{:S(2)}) collective-permute-start(bf16[384,384]{1,0:T(8,128)(2,1)S(1)} %get-tuple-element.70.rest_13_), channel_id=1, source_target_pairs={{0,8},{4,12},{8,0},{12,4},{1,9},{5,13},{9,1},{13,5},{2,10},{6,14},... | collective-permute-start | bytes 884744 | tf_op jit(solution)/shard_map/ppermute | solution.py:647
  155.2 17.0 %collective-permute-start.33 = (bf16[384,384]{1,0:T(8,128)(2,1)S(1)}, bf16[384,384]{1,0:T(8,128)(2,1)S(1)}, u32[]{:S(2)}, u32[]{:S(2)}) collective-permute-start(bf16[384,384]{1,0:T(8,128)(2,1)S(1)} %get-tuple-element.69.rest_14_), channel_id=1, source_target_pairs={{0,12},{4,8},{8,4},{12,0},{1,13},{5,9},{9,5},{13,1},{2,14},{6,10},... | collective-permute-start | bytes 884744 | tf_op jit(solution)/shard_map/ppermute | solution.py:647
  156.7 10.2 %collective-permute-start.41 = (bf16[144,384]{1,0:T(8,128)(2,1)S(1)}, bf16[144,384]{1,0:T(8,128)(2,1)S(1)}, u32[]{:S(2)}, u32[]{:S(2)}) collective-permute-start(bf16[144,384]{1,0:T(8,128)(2,1)S(1)} %get-tuple-element.95.rest_1_), channel_id=1, source_target_pairs={{0,2},{1,3},{2,0},{3,1},{4,6},{5,7},{6,4},{7,5},{8,10},{9,11},{10,... | collective-permute-start | bytes 331784 | tf_op jit(solution)/shard_map/ppermute | solution.py:647
  166.9 15.0 %collective-permute-start.43 = (bf16[144,384]{1,0:T(8,128)(2,1)S(1)}, bf16[144,384]{1,0:T(8,128)(2,1)S(1)}, u32[]{:S(2)}, u32[]{:S(2)}) collective-permute-start(bf16[144,384]{1,0:T(8,128)(2,1)S(1)} %fusion.8), channel_id=1, source_target_pairs={{0,1},{1,0},{2,3},{3,2},{4,5},{5,4},{6,7},{7,6},{8,9},{9,8},{10,11... | collective-permute-start | bytes 331784 | tf_op jit(solution)/shard_map/ppermute | solution.py:684
  168.8 13.0 %collective-permute-start.44 = (bf16[144,384]{1,0:T(8,128)(2,1)S(1)}, bf16[144,384]{1,0:T(8,128)(2,1)S(1)}, u32[]{:S(2)}, u32[]{:S(2)}) collective-permute-start(bf16[144,384]{1,0:T(8,128)(2,1)S(1)} %fusion.8), channel_id=1, source_target_pairs={{0,3},{1,2},{2,1},{3,0},{4,7},{5,6},{6,5},{7,4},{8,11},{9,10},{10,... | collective-permute-start | bytes 331784 | tf_op jit(solution)/shard_map/ppermute | solution.py:684
  172.2 9.7 %collective-permute-start.45 = (bf16[144,384]{1,0:T(8,128)(2,1)S(1)}, bf16[144,384]{1,0:T(8,128)(2,1)S(1)}, u32[]{:S(2)}, u32[]{:S(2)}) collective-permute-start(bf16[144,384]{1,0:T(8,128)(2,1)S(1)} %fusion.8), channel_id=1, source_target_pairs={{0,2},{1,3},{2,0},{3,1},{4,6},{5,7},{6,4},{7,5},{8,10},{9,11},{10,... | collective-permute-start | bytes 331784 | tf_op jit(solution)/shard_map/ppermute | solution.py:684
  197.7 17.6 %collective-permute-start.23 = (bf16[768,384]{1,0:T(8,128)(2,1)}, bf16[768,384]{1,0:T(8,128)(2,1)}, u32[]{:S(2)}, u32[]{:S(2)}) collective-permute-start(bf16[768,384]{1,0:T(8,128)(2,1)} %get-tuple-element.62), channel_id=1, source_target_pairs={{0,16},{16,0},{1,17},{17,1},{2,18},{18,2},{3,19},{19,3},{4,20},{20... | collective-permute-start | bytes 1769480 | tf_op jit(solution)/shard_map/ppermute | solution.py:614
  209.9 10.9 %collective-permute-start.20 = (bf16[512,384]{1,0:T(8,128)(2,1)}, bf16[512,384]{1,0:T(8,128)(2,1)}, u32[]{:S(2)}, u32[]{:S(2)}) collective-permute-start(bf16[512,384]{1,0:T(8,128)(2,1)} %convert_select_fusion.1), channel_id=1, source_target_pairs={{0,16},{16,0},{1,17},{17,1},{2,18},{18,2},{3,19},{19,3},{4,20},{20... | collective-permute-start | bytes 1179656 | tf_op jit(solution)/shard_map/ppermute | solution.py:614
  218.0 9.6 %collective-permute-start.29 = (bf16[256,384]{1,0:T(8,128)(2,1)S(1)}, bf16[256,384]{1,0:T(8,128)(2,1)S(1)}, u32[]{:S(2)}, u32[]{:S(2)}) collective-permute-start(bf16[256,384]{1,0:T(8,128)(2,1)S(1)} %get-tuple-element.115), channel_id=1, source_target_pairs={{0,8},{4,12},{8,0},{12,4},{1,9},{5,13},{9,1},{13,5},{2,10},{6,14},... | collective-permute-start | bytes 589832 | tf_op jit(solution)/shard_map/ppermute | solution.py:647
  218.9 10.4 %collective-permute-start.30 = (bf16[256,384]{1,0:T(8,128)(2,1)S(1)}, bf16[256,384]{1,0:T(8,128)(2,1)S(1)}, u32[]{:S(2)}, u32[]{:S(2)}) collective-permute-start(bf16[256,384]{1,0:T(8,128)(2,1)S(1)} %get-tuple-element.116), channel_id=1, source_target_pairs={{0,12},{4,8},{8,4},{12,0},{1,13},{5,9},{9,5},{13,1},{2,14},{6,10},... | collective-permute-start | bytes 589832 | tf_op jit(solution)/shard_map/ppermute | solution.py:647
  232.6 14.5 %collective-permute-start.35 = (bf16[288,384]{1,0:T(8,128)(2,1)S(1)}, bf16[288,384]{1,0:T(8,128)(2,1)S(1)}, u32[]{:S(2)}, u32[]{:S(2)}) collective-permute-start(bf16[288,384]{1,0:T(8,128)(2,1)S(1)} %get-tuple-element.112), channel_id=1, source_target_pairs={{0,3},{1,2},{2,1},{3,0},{4,7},{5,6},{6,5},{7,4},{8,11},{9,10},{10,... | collective-permute-start | bytes 663560 | tf_op jit(solution)/shard_map/ppermute | solution.py:647
  235.9 18.1 %collective-permute-start.36 = (bf16[288,384]{1,0:T(8,128)(2,1)S(1)}, bf16[288,384]{1,0:T(8,128)(2,1)S(1)}, u32[]{:S(2)}, u32[]{:S(2)}) collective-permute-start(bf16[288,384]{1,0:T(8,128)(2,1)S(1)} %get-tuple-element.113), channel_id=1, source_target_pairs={{0,2},{1,3},{2,0},{3,1},{4,6},{5,7},{6,4},{7,5},{8,10},{9,11},{10,... | collective-permute-start | bytes 663560 | tf_op jit(solution)/shard_map/ppermute | solution.py:647
  257.0 9.4 %collective-permute-start.39 = (bf16[144,384]{1,0:T(8,128)(2,1)S(1)}, bf16[144,384]{1,0:T(8,128)(2,1)S(1)}, u32[]{:S(2)}, u32[]{:S(2)}) collective-permute-start(bf16[144,384]{1,0:T(8,128)(2,1)S(1)} %fusion.11), channel_id=1, source_target_pairs={{0,2},{1,3},{2,0},{3,1},{4,6},{5,7},{6,4},{7,5},{8,10},{9,11},{10,... | collective-permute-start | bytes 331784 | tf_op jit(solution)/shard_map/ppermute | solution.py:684
  (71 other events, 773.8 us)
Sparse Core Ops, SparseCore 0:
  102.6 45.9 all-gather.1

commit v4 on v3

--- a/solution.py
+++ b/solution.py
@@ -306,6 +306,43 @@
     lax.fori_loop(0, count, step, 0)
 
 
+def add_table(scores, index, out):
+    heads, length = scores.shape[0], scores.shape[1]
+    low_ids = lax.broadcasted_iota(jnp.int32, (LOW, length), 0)
+    high_ids = lax.broadcasted_iota(jnp.int32, (HIGH, length), 0)
+
+    def step(i, carry):
+        rows = pl.ds(pl.multiple_of(i * 16, 16), 16)
+        entries = index[rows, :]
+        block = [scores[head, rows, :].astype(F32) for head in range(heads)]
+        total = carry
+        for r in range(16):
+            entry = entries[r : r + 1, :]
+            low = jnp.where(low_ids == (entry & (LOW - 1)), 1.0, 0.0).astype(BF16)
+            high = high_ids == (entry >> LOW_BITS)
+            left = jnp.concatenate([jnp.where(high, part[r : r + 1, :], 0.0) for part in block], axis=0).astype(BF16)
+            total = total + dot_rows(left, low)
+        return total
+
+    total = lax.fori_loop(0, length // 16, step, jnp.zeros((heads * HIGH, LOW), F32))
+    out[...] = jnp.concatenate([total[head * HIGH : (head + 1) * HIGH] for head in range(heads)], axis=1)
+
+
+def table_kernel(scores, index, *rest):
+    add_table(scores, index, rest[-1])
+
+
+def table_gradient(scores, index, earlier):
+    heads = scores.shape[0]
+    return pl.pallas_call(
+        table_kernel,
+        out_shape=jax.ShapeDtypeStruct((HIGH, heads * LOW), F32),
+        in_specs=[pl.BlockSpec(memory_space=pltpu.VMEM)] * 2 + [pl.BlockSpec(memory_space=pl.ANY)] * len(earlier),
+        out_specs=pl.BlockSpec(memory_space=pltpu.VMEM),
+        compiler_params=pltpu.CompilerParams(vmem_limit_bytes=VMEM_BYTES),
+    )(scores, index, *earlier)
+
+
 def set_line(line, layer, section, own_line, other_line):
     line[...] = jnp.where(section == layer, own_line[...], other_line[...])
 
@@ -325,8 +362,8 @@
     return b_qkv, bias_at(line, samples, model, 2, 1), bias_at(line, samples, model, 3, 4), bias_at(line, samples, model, 7, 1)
 
 
-def forward_kernel(layer, length, n_weights, pos, h, own_line, other_line, own_bias, other_bias, *rest):
-    refs, rest = rest[:n_weights], rest[n_weights:]
+def forward_kernel(layer, length, n_weights, n_after, pos, h, own_line, other_line, own_bias, other_bias, *rest):
+    refs, rest = rest[:n_weights], rest[n_weights + n_after :]
     (qkv, probs, att, branch, middle, act, slope, out_branch, layer_out,
      w_qkv, w_proj, w_fc1, w_fc2, bias, line, sems) = rest
     section, shard = pos[0], pos[1]
@@ -386,10 +423,19 @@
     scores[...] = score_sum[...].astype(BF16)
     attention_weight_grads(normed_low, d_qkv, att, d_ob, g_qkv, g_proj)
     pack_attention((keep, send), section, g_qkv, g_proj, shard, pieces, 6, 0)
-
-
-def backward_mlp_kernel(layer, pieces, length, n_weights, pos, grad, middle, own_line, other_line, act, slope, out_branch, *rest):
-    refs, rest = rest[:n_weights], rest[n_weights:]
+    rows = slice(keep.shape[0], keep.shape[0] + h.shape[0])
+
+    @pl.when(section == 0)
+    def _():
+        send[rows, :] = layer_out[...]
+
+    @pl.when(section == 1)
+    def _():
+        send[rows, :] = h[...]
+
+
+def backward_mlp_kernel(layer, pieces, length, n_weights, n_after, pos, grad, middle, own_line, other_line, act, slope, out_branch, *rest):
+    refs, rest = rest[:n_weights], rest[n_weights + n_after :]
     (d_middle, small, keep, send,
      w_qkv, w_proj, w_fc1, w_fc2, line, normed_low, d_pre, d_ob, g_fc1, g_fc2, sems) = rest
     section, shard = pos[0], pos[1]
@@ -406,23 +452,47 @@
     wait_all(for_attention)
 
 
-def backward_attention_kernel(layer, pieces, length, n_weights, n_after, pos, h, own_line, other_line, qkv, probs, att, branch, d_middle, *rest):
+def backward_attention_kernel(layer, pieces, length, n_weights, n_after, pos, h, own_line, other_line, qkv, probs, att, branch, d_middle,
+                              index, d_h1, small_m0, small_a1, small_m1, table1, *rest):
     refs, rest = rest[:n_weights], rest[n_weights + n_after :]
-    (d_in, small, scores, keep, send,
-     w_qkv, w_proj, w_fc1, w_fc2, line, normed_low, d_qkv, d_br, score_sum, g_qkv, g_proj, sems) = rest
+    (d_in, keep, send, kept_small,
+     w_qkv, w_proj, w_fc1, w_fc2, line, small, table, normed_low, d_qkv, d_br, score_sum, g_qkv, g_proj, sems) = rest
     section, shard = pos[0], pos[1]
+    model = h.shape[1]
+    samples = h.shape[0] // length
     for_attention, for_mlp = weight_loads(layer, section, shard, refs, (w_qkv, w_proj, w_fc1, w_fc2), sems)
     set_line(line, layer, section, own_line, other_line)
-    mod = Modulation(line, h.shape[1])
+    mod = Modulation(line, model)
     score_sum[...] = jnp.zeros_like(score_sum)
     wait_all(for_attention)
     each_sample(
-        h.shape[0] // length,
+        samples,
         lambda b: attention_backward(b, length, h, mod, w_qkv, w_proj, qkv, probs, att, branch, d_middle, d_in, small, score_sum, normed_low, d_qkv, d_br),
     )
-    scores[...] = score_sum[...].astype(BF16)
     attention_weight_grads(normed_low, d_qkv, att, d_br, g_qkv, g_proj)
     pack_attention((keep, send), section, g_qkv, g_proj, shard, pieces, 2, 0)
+    add_table(score_sum, index, table)
+    at = keep.shape[0]
+    rows = slice(at, at + h.shape[0])
+    at += h.shape[0]
+    size = samples * 8
+    smalls = (
+        jnp.concatenate([small[...].reshape(size, model), small_m0[...].reshape(size, model), table[...]], axis=0),
+        jnp.concatenate([small_a1[...].reshape(size, model), small_m1[...].reshape(size, model), table1[...]], axis=0),
+    )
+
+    @pl.when(section == 0)
+    def _():
+        send[rows, :] = d_h1[...]
+        send[at:, :] = smalls[1].astype(BF16)
+        kept_small[...] = smalls[0]
+
+    @pl.when(section == 1)
+    def _():
+        send[rows, :] = d_in[...].astype(BF16)
+        send[at:, :] = smalls[0].astype(BF16)
+        kept_small[...] = smalls[1]
+
     wait_all(for_mlp)
 
 
@@ -460,16 +530,14 @@
         self.wide = ((self.rows, hidden), BF16)
         self.small = ((samples, 8, model), F32)
 
-    def pack(self, blocks):
-        return [((blocks * self.model, self.model), BF16)] * 2
-
-
-def forward_layer(layer, z, pos, h, lines, biases, weights):
-    def kernel(pos_ref, h_ref, a, b, *rest):
-        forward_kernel(layer, z.length, len(weights), pos_ref, h_ref, a, b, *rest)
-
+    def pack(self, blocks, more=0):
+        return [((blocks * self.model, self.model), BF16), ((blocks * self.model + more, self.model), BF16)]
+
+
+def forward_layer(layer, z, pos, h, lines, biases, weights, earlier):
     return call(
-        kernel, pos, (h, *lines), (*biases, *weights),
+        functools.partial(forward_kernel, layer, z.length, len(weights), len(earlier)),
+        pos, (h, *lines), (*biases, *weights, *earlier),
         [z.qkv, z.probs, z.low, z.full, z.full, z.wide, z.wide, z.full, z.low],
         [*z.weights, z.bias, z.line], weight_count(len(weights)) + 1,
     )
@@ -479,31 +547,204 @@
     return call(
         functools.partial(both_kernel, layer, z.pieces, z.length, len(weights)),
         pos, (h, grad, *lines), (*biases, *weights),
-        [z.low, z.low, z.small, z.small, z.bias, *z.pack(6)],
+        [z.low, z.low, z.small, z.small, z.bias, *z.pack(6, z.rows)],
         [*z.weights, z.bias, z.line, z.qkv, z.probs, z.low, z.full, z.full, z.wide, z.wide, z.full,
          z.full, z.low, z.wide, z.low, z.qkv, (z.bias[0], F32), *z.weights],
         weight_count(len(weights)) + 1,
     )
 
 
-def backward_mlp(layer, z, pos, grad, middle, lines, act, slope, out_branch, weights):
+def backward_mlp(layer, z, pos, grad, middle, lines, act, slope, out_branch, weights, earlier):
     return call(
-        functools.partial(backward_mlp_kernel, layer, z.pieces, z.length, len(weights)),
-        pos, (grad, middle, *lines, act, slope, out_branch), weights,
+        functools.partial(backward_mlp_kernel, layer, z.pieces, z.length, len(weights), len(earlier)),
+        pos, (grad, middle, *lines, act, slope, out_branch), (*weights, *earlier),
         [z.full, z.small, *z.pack(4)],
         [*z.weights, z.line, z.low, z.wide, z.low, *z.weights[2:]],
         weight_count(len(weights)),
     )
 
 
-def backward_attention(layer, z, pos, h, lines, qkv, probs, att, branch, d_middle, weights, earlier):
+def backward_attention(layer, z, pos, h, lines, qkv, probs, att, branch, d_middle, index, others, weights, earlier):
+    rows = 2 * 8 * z.samples + HIGH
     return call(
         functools.partial(backward_attention_kernel, layer, z.pieces, z.length, len(weights), len(earlier)),
-        pos, (h, *lines, qkv, probs, att, branch, d_middle), (*weights, *earlier),
-        [z.full, z.small, z.bias, *z.pack(2)],
-        [*z.weights, z.line, z.low, z.qkv, z.low, (z.bias[0], F32), *z.weights[:2]],
+        pos, (h, *lines, qkv, probs, att, branch, d_middle, index, *others), (*weights, *earlier),
+        [z.full, *z.pack(2, z.rows + rows), ((rows, z.model), F32)],
+        [*z.weights, z.line, z.small, ((HIGH, z.heads * LOW), F32), z.low, z.qkv, z.low, (z.bias[0], F32), *z.weights[:2]],
         weight_count(len(weights)),
     )
+
+
+def plane_kernel(samples, n_rows, pos, keep, other, kept_small, cond, own, own_small, *rest):
+    messages, work = rest[:3], rest[3]
+    section = pos[0]
+    size, model = own.shape
+    for p in range(4):
+        rows = slice(p * size, (p + 1) * size)
+        total = keep[rows, :].astype(F32) + other[rows, :].astype(F32)
+        if p == 0:
+            own[...] = total
+        else:
+            messages[p - 1][:size, :] = total.astype(BF16)
+    at = keep.shape[0] + n_rows
+    theirs = other[at:, :].astype(F32)
+    mine = kept_small[...]
+    each = samples // 2
+    work[...] = jnp.zeros_like(work)
+    for b in range(each):
+        for kind in range(6):
+            row = b * 8 + kind if kind < 3 else (each + b) * 8 + kind - 3
+            work[pl.ds(kind * samples + section * each + b, 1), :] = mine[row : row + 1, :]
+            work[pl.ds(kind * samples + (1 - section) * each + b, 1), :] = theirs[row : row + 1, :]
+    work[6 * samples : 7 * samples, :] = cond[...].astype(F32)
+    both = mine + theirs
+    bias_rows = sum(both[(each + b) * 8 + 3 : (each + b) * 8 + 8, :] for b in range(each))
+    more_rows = sum(both[b * 8 + 3 : b * 8 + 6, :] for b in range(each))
+    at = 7 * samples
+    work[at : at + 5, :] = bias_rows
+    work[at + 5 : at + 8, :] = more_rows
+    work[at + 8 : at + 8 + HIGH, :] = both[2 * each * 8 :, :]
+    small = work[...].astype(BF16)
+    own_small[...] = small
+    for message in messages:
+        message[size:, :] = small
+
+
+def plane_step(pos, keep, other, kept_small, cond, n_rows):
+    samples, model = cond.shape
+    size = keep.shape[0] // 4
+    small = -(-(7 * samples + 8 + HIGH) // 16) * 16
+    outs = [((size, model), F32), ((small, model), BF16)] + [((size + small, model), BF16)] * 3
+    return call(
+        functools.partial(plane_kernel, samples, n_rows), pos, (keep, other, kept_small, cond), (), outs,
+        [((small, model), F32)],
+    )
+
+
+def column_kernel(samples, pos, own, own_small, got_a, got_b, got_c, part, own_out, *rest):
+    messages, work = rest[:3], rest[3]
+    rank = pos[2]
+    size, model = own.shape
+    n = size // 4
+    got = (got_a, got_b, got_c)
+    for j in range(4):
+        at = pl.multiple_of((rank ^ j) * n, 16)
+        total = own[pl.ds(at, n), :]
+        for piece in got:
+            total = total + piece[pl.ds(at, n), :].astype(F32)
+        if j == 0:
+            part[...] = total
+        else:
+            messages[j - 1][:n, :] = total.astype(BF16)
+    smalls = [own_small[...].astype(F32)] + [piece[size:, :].astype(F32) for piece in got]
+    work[...] = jnp.zeros_like(work)
+    for p in range(4):
+        for kind in range(7):
+            at = (kind * 4 + p) * samples
+            work[at : at + samples, :] = smalls[p][kind * samples : (kind + 1) * samples, :]
+    at = 7 * samples
+    summed = (smalls[0] + smalls[1]) + (smalls[2] + smalls[3])
+    work[4 * at : 4 * at + 8 + HIGH, :] = summed[at : at + 8 + HIGH, :]
+    small = work[...].astype(BF16)
+    own_out[...] = small
+    for message in messages:
+        message[n:, :] = small
+
+
+def column_step(pos, own, own_small, got, samples):
+    size, model = own.shape
+    small = -(-(28 * samples + 8 + HIGH) // 16) * 16
+    outs = [((size // 4, model), F32), ((small, model), BF16)] + [((size // 4 + small, model), BF16)] * 3
+    return call(
+        functools.partial(column_kernel, samples), pos, (own, own_small, *got), (), outs, [((small, model), F32)]
+    )
+
+
+def finish_kernel(samples, width, pos, own_small, got_a, got_b, got_c, g_ada, g_b_ada, summed, work, whole):
+    shard, rank = pos[1], pos[2]
+    model = own_small.shape[1]
+    each = 4 * samples
+    n = got_a.shape[0] - own_small.shape[0]
+    pieces = [own_small[...]] + [piece[n:, :] for piece in (got_a, got_b, got_c)]
+    for j in range(4):
+        for kind in range(7):
+            at = pl.multiple_of(kind * 4 * each + (rank ^ j) * each, 16)
+            work[pl.ds(at, each), :] = pieces[j][kind * each : (kind + 1) * each, :].astype(F32)
+    cond = work[24 * each :, :]
+    act = (cond * (1.0 / (1.0 + jnp.exp(-cond)))).astype(BF16)
+    for kind in range(6):
+        rows = work[kind * 4 * each : (kind + 1) * 4 * each, :]
+        whole[...] = dot_cols(act, rows.astype(BF16))
+        cols = slice(kind * model, (kind + 1) * model)
+        g_ada[:, cols] = whole[pl.ds(pl.multiple_of(shard * width, 16), width), :]
+        g_b_ada[:, cols] = col_sum(rows)
+    at = 7 * each
+    rows = [piece[at : at + 8 + HIGH, :].astype(F32) for piece in pieces]
+    summed[...] = (rows[0] + rows[1]) + (rows[2] + rows[3])
+
+
+def finish_step(pos, own_small, got, samples, width):
+    model = own_small.shape[1]
+    return call(
+        functools.partial(finish_kernel, samples, width), pos, (own_small, *got), (),
+        [((width, 6 * model), F32), ((1, 6 * model), F32), ((8 + HIGH, model), F32)],
+        [((7 * 16 * samples, model), F32), ((model, model), F32)],
+    )
+
+
+def cond_kernel(samples, pos, small, cond, *rest):
+    out, w_ada = rest[-2:]
+    model = cond.shape[1]
+    for p, piece in enumerate(rest[:-2]):
+        q = piece.shape[0]
+        off = pl.multiple_of((pos[1] ^ p) * q, 16) if q < model else 0
+        w_ada[pl.ds(off, q), :] = piece[...]
+    total = None
+    for kind in range(6):
+        rows = small[...].astype(F32)[kind * samples : (kind + 1) * samples, :].astype(BF16)
+        part = dot_rows(rows, w_ada[:, kind * model : (kind + 1) * model])
+        total = part if total is None else total + part
+    c = cond[...].astype(F32)
+    gate = 1.0 / (1.0 + jnp.exp(-c))
+    out[...] = total * (gate * (1.0 + c * (1.0 - gate)))
+
+
+def cond_step(pos, small, w_ada, cond):
+    model = cond.shape[1]
+    return call(
+        functools.partial(cond_kernel, cond.shape[0]), pos, (small, cond, *w_ada), (), [(cond.shape, F32)],
+        [((model, w_ada[0].shape[1]), BF16)],
+    )[0]
+
+
+def halve_kernel(pos, own, got_a, got_b, got_c, keep, send):
+    bit = pos[2] & 1
+    n = own.shape[0] // 4
+    for high in range(2):
+        for out, low in ((keep, bit), (send, 1 - bit)):
+            rows = pl.ds(pl.multiple_of((2 * high + low) * n, 16), n)
+            total = own[rows, :]
+            for piece in (got_a, got_b, got_c):
+                total = total + piece[rows, :].astype(F32)
+            out[high * n : (high + 1) * n, :] = total.astype(out.dtype)
+
+
+def halve_step(pos, own, got):
+    shape = (own.shape[0] // 2, own.shape[1])
+    return call(halve_kernel, pos, (own, *got), (), [(shape, F32), (shape, BF16)], [])
+
+
+def quarter_kernel(pos, kept, got, keep, send):
+    bit = pos[2] >> 1
+    n = kept.shape[0] // 2
+    for out, high in ((keep, bit), (send, 1 - bit)):
+        rows = pl.ds(pl.multiple_of(high * n, 16), n)
+        out[...] = (kept[rows, :] + got[rows, :].astype(F32)).astype(out.dtype)
+
+
+def quarter_step(pos, kept, got):
+    shape = (kept.shape[0] // 2, kept.shape[1])
+    return call(quarter_kernel, pos, (kept, got), (), [(shape, F32), (shape, BF16)], [])
 
 
 def pack_kernel(pos, qkv, proj, fc1, fc2, out):
@@ -574,42 +815,6 @@
     )(rows, index, *earlier)
 
 
-def table_kernel(scores, index, *rest):
-    out = rest[-1]
-    heads, length = scores.shape[0], scores.shape[1]
-    out[...] = jnp.zeros_like(out)
-    low_ids = lax.broadcasted_iota(jnp.int32, (LOW, length), 0)
-    high_ids = lax.broadcasted_iota(jnp.int32, (HIGH, length), 0)
-
-    def step(i, carry):
-        rows = pl.ds(pl.multiple_of(i * 16, 16), 16)
-        entries = index[rows, :]
-        block = [scores[head, rows, :].astype(F32) for head in range(heads)]
-        total = None
-        for r in range(16):
-            entry = entries[r : r + 1, :]
-            low = jnp.where(low_ids == (entry & (LOW - 1)), 1.0, 0.0).astype(BF16)
-            high = high_ids == (entry >> LOW_BITS)
-            left = jnp.concatenate([jnp.where(high, part[r : r + 1, :], 0.0) for part in block], axis=0).astype(BF16)
-            part = dot_rows(left, low)
-            total = part if total is None else total + part
-        out[...] += total
-        return carry
-
-    lax.fori_loop(0, length // 16, step, 0)
-
-
-def table_gradient(scores, index, earlier):
-    heads = scores.shape[0]
-    return pl.pallas_call(
-        table_kernel,
-        out_shape=jax.ShapeDtypeStruct((heads * HIGH, LOW), F32),
-        in_specs=[pl.BlockSpec(memory_space=pltpu.VMEM)] * 2 + [pl.BlockSpec(memory_space=pl.ANY)] * len(earlier),
-        out_specs=pl.BlockSpec(memory_space=pltpu.VMEM),
-        compiler_params=pltpu.CompilerParams(vmem_limit_bytes=VMEM_BYTES),
-    )(scores, index, *earlier)
-
-
 def swap_section(value):
     return lax.ppermute(value, "section", [(0, 1), (1, 0)])
 
@@ -629,8 +834,7 @@
     return stack
 
 
-def section_sums(keep, send, shards):
-    other = swap_section(send)
+def section_sums(keep, other, shards):
     size = keep.shape[0] // shards
     return [
         keep[p * size : (p + 1) * size].astype(F32) + other[p * size : (p + 1) * size].astype(F32)
@@ -656,24 +860,20 @@
 
 def replica_parts(total, rank):
     replicas = lax.axis_size("rep")
-    parts = total.reshape(replicas, total.shape[0] // replicas, -1)
+    parts = total if total.ndim == 3 else total.reshape(replicas, total.shape[0] // replicas, -1)
     low = parts.astype(BF16)
     mine = lax.dynamic_index_in_dim(parts, rank, 0, keepdims=False)
     return mine, [lax.dynamic_index_in_dim(low, rank ^ j, 0, keepdims=False) for j in range(1, replicas)]
 
 
-def replica_whole(mine, rank):
-    quarters = [mine] + from_peers(mine, "rep")
-    return by_rank(quarters, rank).reshape(-1, mine.shape[1])
-
-
-def unpack(pack):
-    q = pack.shape[0] // 12
-    unit = [pack[c * q : (c + 1) * q] for c in range(8)]
-    return (
-        jnp.concatenate([unit[0], unit[1], unit[6]], axis=1), unit[7],
-        jnp.concatenate(unit[2:6], axis=1), pack[8 * q :],
-    )
+def unpack_attention(pack):
+    q = pack.shape[0] // 4
+    return jnp.concatenate([pack[c * q : (c + 1) * q] for c in range(3)], axis=1), pack[3 * q :]
+
+
+def unpack_mlp(pack):
+    q = pack.shape[0] // 8
+    return jnp.concatenate([pack[c * q : (c + 1) * q] for c in range(4)], axis=1), pack[4 * q :]
 
 
 def pad_rows(value):
@@ -702,7 +902,7 @@
     heads, entries = bias_table.shape[1:]
     half = samples // 2
     z = Sizes(half, length, model, heads, 4 * model, shards if direct else 1)
-    pos = jnp.stack([section, shard]).astype(jnp.int32)
+    pos = jnp.stack([section, shard, rank]).astype(jnp.int32)
 
     def mine(first, second):
         return jnp.where(is_first, first, second)
@@ -713,6 +913,9 @@
     def in_order(own, other):
         return jnp.where(is_first, jnp.concatenate([own, other]), jnp.concatenate([other, own]))
 
+    live = (jnp.arange(half)[:, None, None] < lax.dynamic_index_in_dim(micro_sizes[0], section, 0)).astype(BF16)
+    h0 = own_samples(inputs).reshape(half * length, model)
+    grad1 = (own_samples(cotangent) * live).reshape(half * length, model)
     own_raw = [w_qkv[0], w_proj[0], w_fc1[0], w_fc2[0]]
     cond_size = conditioning.size
     width = model // shards
@@ -731,11 +934,10 @@
         acts = jax.nn.silu(cond_pieces.astype(F32)).astype(BF16)
         acts = lax.dynamic_slice_in_dim(acts, shard * width, width, 2)
         partial = lax.dot_general(acts, w_ada[0], (((2,), (0,)), ((), ())), preferred_element_type=F32)
-        modulation = partial[0]
-        for p in range(1, shards):
-            modulation = modulation + lax.ppermute(partial[p], "fsdp", pairs_of(shards, p))
         bias_rows = by_rank([r[0, cond_size:] for r in rows], shard)
-        bias_own = lookup(bias_table[0], relative_bias_index, [own_pack, partial])
+        bias_own = lookup(bias_table[0], relative_bias_index, [own_pack, partial, h0, grad1])
+        parts = after(to_peers(partial[1:], "fsdp"), [got_x, got_y, bias_own])
+        modulation = add_pieces(partial[0], parts)
     else:
         row = jnp.concatenate([b_ada, b_qv, b_proj, b_fc1, b_fc2], axis=1)
         bias_rows = lax.all_gather(row[0], "fsdp", axis=0)
@@ -757,94 +959,116 @@
     lines = (own_line, other_line)
     bias_heads = (bias_own, swap_section(bias_own))
 
-    live = (jnp.arange(half)[:, None, None] < lax.dynamic_index_in_dim(micro_sizes[0], section, 0)).astype(BF16)
-    h0 = own_samples(inputs).reshape(half * length, model)
-    grad1 = (own_samples(cotangent) * live).reshape(half * length, model)
-
-    qkv, probs, att, branch, middle, act, slope, out_branch, h1 = forward_layer(0, z, pos, h0, lines, bias_heads, weights)
-    w_ada_later = after([w_ada[0]], [h1])[0]
-    w_ada_all = lax.all_gather(w_ada_later, "fsdp", axis=0, tiled=True)
+    if direct:
+        w_ada_later = after([w_ada[0]], weights[3:5])[0]
+        w_ada_pieces = [w_ada_later] + from_peers(w_ada_later, "fsdp")
+    else:
+        w_ada_pieces = [lax.all_gather(w_ada[0], "fsdp", axis=0, tiled=True)]
+    qkv, probs, att, branch, middle, act, slope, out_branch, h1 = forward_layer(0, z, pos, h0, lines, bias_heads, weights, w_ada_pieces[:1] if direct else [])
     out1, d_h1, small_a1, small_m1, scores1, keep1, send1 = both_ways(1, z, pos, h1, grad1, lines, bias_heads, weights)
-    d_middle, small_m0, keep_m0, send_m0 = backward_mlp(0, z, pos, d_h1, middle, lines, act, slope, out_branch, weights)
+    d_middle, small_m0, keep_m0, send_m0 = backward_mlp(0, z, pos, d_h1, middle, lines, act, slope, out_branch, weights, w_ada_pieces[1:])
     pieces = z.pieces
-    sums1 = section_sums(keep1, send1, pieces)
-    sums_m0 = section_sums(keep_m0, send_m0, pieces)
-    low1, low_m0 = low_pieces(sums1), low_pieces(sums_m0)
+    rows = half * length
+    other1 = swap_section(send1)
+    sums1 = section_sums(keep1, other1[: keep1.shape[0]], pieces)
+    low1 = low_pieces(sums1)
     table1 = table_gradient(scores1, relative_bias_index, low1)
-    d_h0, small_a0, scores0, keep_a0, send_a0 = backward_attention(
-        0, z, pos, h0, lines, qkv, probs, att, branch, d_middle, weights, [table1, w_ada_all, *low_m0]
-    )
-    sums_a0 = section_sums(keep_a0, send_a0, pieces)
+    other_m0 = after([swap_section(send_m0)], [table1])[0]
+    sums_m0 = section_sums(keep_m0, other_m0, pieces)
+    low_m0 = low_pieces(sums_m0)
     if direct:
-        got1 = to_peers(low1, "fsdp")
-        got_m0 = to_peers(low_m0, "fsdp")
-        part1, others1 = replica_parts(add_pieces(sums1[0], got1), rank)
-        table0 = table_gradient(scores0, relative_bias_index, others1)
-        half1 = replica_whole(add_pieces(part1, to_peers(others1, "rep")).astype(BF16), rank)
+        got1 = after(to_peers(low1, "fsdp"), [table1, *low_m0])
+        keep_z1, send_z1 = halve_step(pos, sums1[0], got1)
+        earlier = [table1, *low_m0, send_z1]
     else:
-        table0 = table_gradient(scores0, relative_bias_index, [])
-
-    other_out = swap_section(mine(out1, h1))
-    activations = in_order(mine(h1, out1).reshape(half, length, model), other_out.reshape(half, length, model))
-    other_in = swap_section(mine(d_h1, d_h0.astype(BF16)))
+        earlier = [table1, *low_m0]
+    d_h0, keep_a0, send_a0, kept_small = backward_attention(
+        0, z, pos, h0, lines, qkv, probs, att, branch, d_middle, relative_bias_index,
+        (d_h1, small_m0, small_a1, small_m1, table1), weights, earlier,
+    )
+    if direct:
+        got_z1, *got_m0 = after([lax.ppermute(send_z1, "rep", pairs_of(replicas, 1)), *to_peers(low_m0, "fsdp")], [d_h0])
+        send_a0 = after([send_a0], [got_z1, *got_m0])[0]
+    other_a0 = swap_section(send_a0)
+    size_a = keep_a0.shape[0]
+
+    def replica(value, step):
+        return lax.ppermute(value, "rep", pairs_of(replicas, step))
+
+    def ordered(own, other, bit):
+        return jnp.where(bit == 0, jnp.concatenate([own, other]), jnp.concatenate([other, own]))
+
+    if direct:
+        own_a0, own_small, *messages = plane_step(pos, keep_a0, other_a0, kept_small, conditioning, rows)
+        keep_z1, send_z1 = quarter_step(pos, keep_z1, got_z1)
+        keep_zm, send_zm = halve_step(pos, sums_m0[0], got_m0)
+        cond_part = cond_step(pos, after([own_small], [send_zm, send_z1])[0], w_ada_pieces, conditioning)
+        got = to_peers(messages, "fsdp")
+        part0, plane_small, *messages = column_step(pos, own_a0, own_small, got, samples)
+        got_z1, got_zm = after([replica(send_z1, 2), replica(send_zm, 1)], [plane_small])
+        quarter1 = (keep_z1 + got_z1.astype(F32)).astype(BF16)
+        keep_zm, send_zm = quarter_step(pos, keep_zm, got_zm)
+        got = to_peers(messages, "rep")
+        size = part0.shape[0]
+        quarter0 = add_pieces(part0, [x[:size] for x in got]).astype(BF16)
+        got_z1, got_zm = after([replica(quarter1, 2), replica(send_zm, 2)], [quarter0])
+        high, low = rank >> 1, rank & 1
+        pair1 = ordered(quarter1, got_z1, high)
+        quarter_m = (keep_zm + got_zm.astype(F32)).astype(BF16)
+        pair_m = ordered(quarter_m, replica(quarter_m, 2), high)
+        half_a0 = by_rank([quarter0] + from_peers(quarter0, "rep"), rank).reshape(-1, model)
+
+        def by_low(pair):
+            n = pair.shape[0] // 2
+            both = ordered(pair.reshape(1, 2, n, model), replica(pair, 1).reshape(1, 2, n, model), low)
+            return jnp.transpose(both, (1, 0, 2, 3)).reshape(-1, model)
+
+        half1, half_m0 = by_low(pair1), by_low(pair_m)
+        g_ada, g_b_ada, summed = finish_step(pos, plane_small, got, samples, width)
+        g_b_ada = g_b_ada[0]
+    else:
+        theirs = other_a0[size_a + rows :].astype(F32)
+        both = kept_small + theirs
+        cut = half * 8
+
+        def d_mod_of(values):
+            a, m = values[:cut].reshape(half, 8, model), values[cut : 2 * cut].reshape(half, 8, model)
+            return jnp.concatenate([a[:, :3], m[:, :3]], axis=1)
+
+        low = in_order(d_mod_of(kept_small), d_mod_of(theirs)).astype(BF16)
+        bias_rows = jnp.sum(both[: 2 * cut].reshape(2, half, 8, model), axis=1)
+        summed = jnp.concatenate([bias_rows[1, 3:8], bias_rows[0, 3:6], both[2 * cut :]])
+        cond_part = cond_step(pos, jnp.transpose(low, (1, 0, 2)).reshape(-1, model), w_ada_pieces, conditioning)
+        kept = jnp.concatenate([low, conditioning[:, None]], axis=1)
+        kept = lax.all_gather(kept, ("fsdp", "rep"), axis=0, tiled=True)
+        summed = lax.psum(summed, ("fsdp", "rep"))
+        act_all = jax.nn.silu(kept[:, 6].astype(F32)).astype(BF16)
+        act_cols = lax.dynamic_slice_in_dim(act_all, shard * width, width, 1)
+        g_ada = jnp.concatenate([dot_cols(act_cols, kept[:, i]) for i in range(6)], axis=1)
+        g_b_ada = jnp.sum(kept[:, :6].astype(F32), axis=0).reshape(-1)
+        sums_a0 = section_sums(keep_a0, other_a0[:size_a], pieces)
+        half_a0, half_m0, half1 = sums_a0[0].astype(BF16), sums_m0[0].astype(BF16), sums1[0].astype(BF16)
+    cond_grad = cond_part + swap_section(cond_part)
+    cut = half_a0.shape[0]
+    half_a1, half_m1 = half1[:cut], half1[cut:]
+    grads = unpack_mlp(in_order(mine(half_m0, half_m1), swap_section(mine(half_m1, half_m0))))
+    grads = unpack_attention(in_order(mine(half_a0, half_a1), swap_section(mine(half_a1, half_a0)))) + grads
+    if not direct:
+        grads = [lax.psum_scatter(g, "fsdp", scatter_dimension=0, tiled=True) for g in grads]
+        grads = lax.psum(tuple(grads), "rep")
+    g_qkv, g_proj, g_fc1, g_fc2 = [g.astype(F32) for g in grads]
+
+    activations = in_order(
+        mine(h1, out1).reshape(half, length, model), other1[keep1.shape[0] :].reshape(half, length, model)
+    )
     input_grads = in_order(
         mine(d_h0, d_h1.astype(F32)).reshape(half, length, model),
-        other_in.astype(F32).reshape(half, length, model),
-    )
-
-    tables = (table0, table1)
-    smalls = [
-        jnp.concatenate([small_a0[:, :3], small_m0, small_a0[:, 3:]], axis=1),
-        jnp.concatenate([small_a1[:, :3], small_m1, small_a1[:, 3:]], axis=1),
-    ]
-    small = in_order(mine(smalls[0], smalls[1]), swap_section(mine(smalls[1], smalls[0])))
-    table = mine(tables[0], tables[1]) + swap_section(mine(tables[1], tables[0]))
-    low = small[:, :6].astype(BF16)
-    w_rows = w_ada_all.reshape(model, 6, model)
-    d_act = sum(dot_rows(low[:, i], w_rows[:, i]) for i in range(6))
-    cond = conditioning.astype(F32)
-    gate = jax.nn.sigmoid(cond)
-    cond_part = d_act * (gate * (1.0 + cond * (1.0 - gate)))
-    cond_grad = cond_part + swap_section(cond_part)
-
-    kept = jnp.concatenate([low, conditioning[:, None]], axis=1).reshape(-1, model)
-    summed = jnp.concatenate([jnp.sum(small[:, 6:14], axis=0), table.reshape(-1, model)])
-    if direct:
-        both = pad_rows(jnp.concatenate([kept, summed.astype(BF16)]))
-        low_a0 = low_pieces(sums_a0)
-        size, count, end = sums_a0[0].shape[0], kept.shape[0], kept.shape[0] + summed.shape[0]
-        got = to_peers([jnp.concatenate([x, both]) for x in low_a0], "fsdp")
-        total0 = jnp.concatenate([
-            add_pieces(sums_a0[0], [x[:size] for x in got]), add_pieces(sums_m0[0], got_m0)
-        ])
-        plane = [both] + [x[size:] for x in got]
-        summed = pair_sum([p[count:end].astype(F32) for p in plane])
-        both = pad_rows(jnp.concatenate([p[:count] for p in plane] + [summed.astype(BF16)]))
-        part0, others0 = replica_parts(total0, rank)
-        got = to_peers([jnp.concatenate([x, both]) for x in others0], "rep")
-        size = part0.shape[0]
-        half0 = replica_whole(add_pieces(part0, [x[:size] for x in got]).astype(BF16), rank)
-        every = [both] + [x[size:] for x in got]
-        count, end = count * shards, count * shards + summed.shape[0]
-        summed = pair_sum([p[count:end].astype(F32) for p in every])
-        kept = by_rank([p[:count] for p in every], rank).reshape(-1, 7, model)
-        grads = [g.astype(F32) for g in unpack(in_order(mine(half0, half1), swap_section(mine(half1, half0))))]
-    else:
-        kept = lax.all_gather(kept, ("fsdp", "rep"), axis=0, tiled=True).reshape(-1, 7, model)
-        summed = lax.psum(summed, ("fsdp", "rep"))
-        half0 = jnp.concatenate([sums_a0[0], sums_m0[0]]).astype(BF16)
-        half1 = sums1[0].astype(BF16)
-        whole = unpack(in_order(mine(half0, half1), swap_section(mine(half1, half0))))
-        whole = [lax.psum_scatter(g, "fsdp", scatter_dimension=0, tiled=True) for g in whole]
-        grads = [g.astype(F32) for g in lax.psum(tuple(whole), "rep")]
-    g_qkv, g_proj, g_fc1, g_fc2 = grads
-    act_all = jax.nn.silu(kept[:, 6].astype(F32)).astype(BF16)
-    act_cols = lax.dynamic_slice_in_dim(act_all, shard * width, width, 1)
-    g_ada = jnp.concatenate([dot_cols(act_cols, kept[:, i]) for i in range(6)], axis=1)
-    g_b_ada = jnp.sum(kept[:, :6].astype(F32), axis=0).reshape(-1)
+        other_a0[size_a : size_a + rows].astype(F32).reshape(half, length, model),
+    )
+
     g_b_fc2, g_b_fc1 = summed[0], summed[1:5].reshape(-1)
     g_b_qv, g_b_proj = summed[5:7].reshape(-1), summed[7]
-    g_table = summed[8:].reshape(heads, HIGH * LOW)[:, :entries]
+    g_table = jnp.transpose(summed[8:].reshape(HIGH, heads, LOW), (1, 0, 2)).reshape(heads, HIGH * LOW)[:, :entries]
 
     def own_part(vector):
         size = vector.shape[0] // shards

time: 280 us -> 272 us (0.971)
  waiting for transfers between devices: 74.8 us -> 43.7 us
  Pallas kernels: 94.6 us -> 112 us
  local copies, waits for them, and re-layouts: 16.3 us -> 33.6 us
  between operations: 15.2 us -> 1.39 us
  starting transfers between devices: 46.1 us -> 54.1 us
  other arithmetic: 29.9 us -> 26 us
    ppermute x15, waiting for transfers between devices: 56.2 us -> 6.58 us  [to_peers(): lax.ppermute(messages[p - 1], axis, pairs_of(count, p))]
    pallas_call x5 -> x13, Pallas kernels: 68.1 us -> 92.6 us  [call(): pl.pallas_call(kernel, out_shape=[jax.ShapeDtypeStruct(shape, dtype) for...]
    ppermute x9, waiting for transfers between devices: 2.82 us -> 19.4 us  [from_peers(): lax.ppermute(value, axis, pairs_of(lax.axis_size(axis), p))]
    unnamed x119 -> x134, local copies, waits for them, and re-layouts: 4.64 us -> 14.3 us
    ppermute x3 -> x8, starting transfers between devices: 3.55 us -> 12.7 us  [the longest x7 11.1 us: replica(): return lax.ppermute(value, 'rep', pairs_of(replicas, step))]
    pallas_call x2 -> x1, Pallas kernels: 15.3 us -> 7.65 us  [table_gradient(): pl.pallas_call(table_kernel, out_shape=jax.ShapeDtypeStruct((HIGH, heads...]
    select_n x6 -> x4, other arithmetic: 4.78 us -> 0.26 us  [mine(): return jnp.where(is_first, first, second)]
    convert_element_type x4, local copies, waits for them, and re-layouts: 0.33 us -> 4.14 us  [per_device(): biases.append(bias_rows[:, at:at + cut].reshape(1, -1).astype(F32))]
  transfers between devices with their start and end apart: 48 -> 49, of which waited for: 16 -> 15; matrix products, arithmetic and copies ran while one was open for 13% -> 16% of each run, Pallas kernels for 15% -> 25%
where the time goes in v4:
time: 272 us; the launch traced here: 271 us
  Pallas kernels  112 us (41%)
  starting transfers between devices  54.1 us (20%)
  waiting for transfers between devices  43.7 us (16%)
  local copies, waits for them, and re-layouts  33.6 us (12%)
  other arithmetic  26 us (10%)
    pallas_call x13, Pallas kernels, call(): pl.pallas_call(kernel, out_shape=[jax.ShapeDtypeStruct(shape, dtype) for...  92.6 us
    ppermute x9, waiting for transfers between devices, from_peers(): lax.ppermute(value, axis, pairs_of(lax.axis_size(axis), p))  19.4 us
    ppermute x15, starting transfers between devices, to_peers(): lax.ppermute(messages[p - 1], axis, pairs_of(count, p))  18.5 us
    ppermute x9, starting transfers between devices, from_peers(): lax.ppermute(value, axis, pairs_of(lax.axis_size(axis), p))  16.1 us
    unnamed x134, local copies, waits for them, and re-layouts  14.3 us
    pallas_call x1, Pallas kernels, lookup(): pl.pallas_call(lookup_kernel, out_shape=jax.ShapeDtypeStruct((heads, leng...  11.2 us
    ppermute x7, starting transfers between devices, replica(): return lax.ppermute(value, 'rep', pairs_of(replicas, step))  11.1 us
    ppermute x1, waiting for transfers between devices, per_device(): got_first = lax.ppermute(got_x[:middle_row], 'fsdp', pairs_of(shards, 2))  9.93 us
  transfers between devices with their start and end apart: 49, of which 15 were waited for; matrix products, arithmetic and copies ran while one was open for 16% of the time, Pallas kernels for 25%

profile of v4, /device:TPU:0, one launch (start us, length us, event | category | flops | bytes accessed | tf_op | source)
XLA Modules:
  0.0 270.7 jit_solution(5857436765476195074)
XLA Ops:
  3.3 3.0 %collective-permute-start.1 = (bf16[1,2880]{1,0:T(2,128)(2,1)S(1)}, bf16[1,2880]{1,0:T(2,128)(2,1)S(1)}, u32[]{:S(2)}, u32[]{:S(2)}) collective-permute-start(bf16[1,2880]{1,0:T(2,128)(2,1)S(1)} %concatenate.132), channel_id=1, source_target_pairs={{0,8},{4,12},{8,0},{12,4},{1,9},{5,13},{9,1},{13,5},{2,10},{6,14},... | collective-permute-start | bytes 17288 | tf_op jit(solution)/shard_map/ppermute | solution.py:884
  8.4 2.2 shard_map.263.rest_0_
  10.7 1.9 collective-permute-start.6
  15.4 1.9 dynamic-slice_multiply_fusion
  22.1 2.9 %collective-permute-start.5 = (f32[4,2304]{1,0:T(4,128)}, f32[4,2304]{1,0:T(4,128)S(1)}, u32[]{:S(2)}, u32[]{:S(2)}) collective-permute-start(f32[4,2304]{1,0:T(4,128)} %get-tuple-element.168), channel_id=1, source_target_pairs={{0,12},{4,8},{8,4},{12,0},{1,13},{5,9},{9,5},{13,1},{2,14},{6,10},... | collective-permute-start | bytes 110600 | tf_op jit(solution)/shard_map/ppermute | solution.py:851
  36.2 11.2 %shard_map.264.refs_5_.own_bias = bf16[6,256,256]{2,1,0:T(8,128)(2,1)} custom-call(bf16[128,64]{1,0:T(8,128)(2,1)} %bitcast.131, s32[256,256]{1,0:T(8,128)} %index.5, bf16[1152,384]{1,0:T(8,128)(2,1)} %shard_map.263.rest_0_, f32[4,4,2304]{2,1,0:T(4,128)} %copy-done.26, bf16[512,384]{1,0:T(8,128)(2,1)} %bitcast.106, bf16[512,384]{1,0:T(8,128)(2,1)} %bitcast.109), custom_call_target="tpu_custom_call" | custom-call | tf_op jit(solution)/shard_map/pallas_call | solution.py:808
  54.5 9.9 %collective-permute-done.10.refs_1_.rest_3_ = bf16[576,384]{1,0:T(8,128)(2,1)} collective-permute-done((bf16[576,384]{1,0:T(8,128)(2,1)S(1)}, bf16[576,384]{1,0:T(8,128)(2,1)}, u32[]{:S(2)}, u32[]{:S(2)}) %collective-permute-start.10) | collective-permute-done | bytes 442400 | tf_op jit(solution)/shard_map/ppermute | solution.py:929
  68.2 15.1 %shard_map.267 = (bf16[512,1152]{1,0:T(8,128)(2,1)}, bf16[2,6,256,256]{3,2,1,0:T(8,128)(2,1)}, bf16[512,384]{1,0:T(8,128)(2,1)}, f32[512,384]{1,0:T(8,128)}, f32...) custom-call(s32[3]{0:T(128)} %pad_add_fusion.pos, ...), custom_call_target="tpu_custom_call" | custom-call | tf_op jit(solution)/shard_map/pallas_call | solution.py:506
  83.3 26.2 %shard_map.268 = (bf16[512,384]{1,0:T(8,128)(2,1)}, bf16[512,384]{1,0:T(8,128)(2,1)}, f32[2,8,384]{2,1,0:T(8,128)}, f32[2,8,384]{2,1,0:T(8,128)}, bf16[6,256,256...) custom-call(s32[3]{0:T(128)} %pad_add_fusion.pos, bf16[512,384]{1,0:T(8,128)(2,1)} %get-tuple-element.76.h, ...), custom_call_target="tpu_custom_call" | custom-call | tf_op jit(solution)/shard_map/pallas_call | solution.py:506
  113.2 9.5 %collective-permute-done.18.rest_10_.rest_1_ = bf16[96,2304]{1,0:T(8,128)(2,1)S(1)} collective-permute-done((bf16[96,2304]{1,0:T(8,128)(2,1)S(1)}, bf16[96,2304]{1,0:T(8,128)(2,1)S(1)}, u32[]{:S(2)}, u32[]{:S(2)}) %collective-permute-start.18) | collective-permute-done | bytes 442400 | tf_op jit(solution)/shard_map/ppermute | solution.py:884
  122.6 8.3 %collective-permute-done.19.rest_11_.rest_2_ = bf16[96,2304]{1,0:T(8,128)(2,1)S(1)} collective-permute-done((bf16[96,2304]{1,0:T(8,128)(2,1)S(1)}, bf16[96,2304]{1,0:T(8,128)(2,1)S(1)}, u32[]{:S(2)}, u32[]{:S(2)}) %collective-permute-start.19) | collective-permute-done | bytes 442400 | tf_op jit(solution)/shard_map/ppermute | solution.py:884
  133.4 12.0 %shard_map.269 = (f32[512,384]{1,0:T(8,128)}, f32[2,8,384]{2,1,0:T(8,128)}, bf16[1536,384]{1,0:T(8,128)(2,1)}, bf16[1536,384]{1,0:T(8,128)(2,1)}) custom-call(s32[3]{0:T(128)} %pad_add_fusion.pos, bf16[512,384]{1,0:T(8,128)(2,1)} %get-tuple-element.83.grad.d_h1, f32[512,384]{1,0:T(8,128)} %get-tuple-element.84.middle, f32[1,7680]{1,0:T(1,128)} %copy-done.27, ...), custom_call_target="tpu_custom_call" | custom-call | tf_op jit(solution)/shard_map/pallas_call | solution.py:506
  145.5 3.7 %convert_add_fusion = (f32[576,384]{1,0:T(8,128)}, bf16[576,384]{1,0:T(8,128)(2,1)S(1)}, bf16[576,384]{1,0:T(8,128)(2,1)S(1)}, bf16[576,384]{1,0:T(8,128)(2,1)}) fusion(bf16[2816,384]{1,0:T(8,128)(2,1)S(1)} %collective-permute-done.17, bf16[2304,384]{1,0:T(8,128)(2,1)} %get-tuple-element.93), kind=kLoop, calls=%fused_computation.1 | loop fusion | flops 3317760 | bytes 5750784 | tf_op jit(solution)/shard_map/add | solution.py:840
  152.7 7.6 %shard_map.270.refs_1_.refs_3_.table1.rest_10_ = f32[16,384]{1,0:T(8,128)} custom-call(bf16[6,256,256]{2,1,0:T(8,128)(2,1)} %get-tuple-element.92.scores, s32[256,256]{1,0:T(8,128)} %index.5, bf16[576,384]{1,0:T(8,128)(2,1)} %get-tuple-element.149.rest_0_, bf16[576,384]{1,0:T(8,128)(2,1)} %copy-done.21, bf16[576,384]{1,0:T(8,128)(2,1)} %copy-done.20), custom_call_target="tpu_custom_call" | custom-call | tf_op jit(solution)/shard_map/pallas_call | solution.py:337
  161.4 2.7 convert_add_fusion.1
  167.6 3.5 %collective-permute-done.23.refs_1_ = bf16[576,384]{1,0:T(8,128)(2,1)} collective-permute-done((bf16[576,384]{1,0:T(8,128)(2,1)S(1)}, bf16[576,384]{1,0:T(8,128)(2,1)}, u32[]{:S(2)}, u32[]{:S(2)}) %collective-permute-start.23) | collective-permute-done | bytes 442400 | tf_op jit(solution)/shard_map/ppermute | solution.py:851
  172.4 2.6 shard_map.273
  176.6 18.4 %shard_map.274 = (f32[512,384]{1,0:T(8,128)}, bf16[768,384]{1,0:T(8,128)(2,1)}, bf16[1328,384]{1,0:T(8,128)(2,1)}, f32[48,384]{1,0:T(8,128)}) custom-call(s32[3]{0:T(128)} %pad_add_fusion.pos, bf16[512,384]{1,0:T(8,128)(2,1)} %bitcast.108, f32[1,7680]{1,0:T(1,128)} %copy-done.27, f32[1,7680]{1,0:T(1,128)} %copy-done.29, ...), custom_call_target="tpu_custom_call" | custom-call | tf_op jit(solution)/shard_map/pallas_call | solution.py:506
  199.9 2.4 shard_map.277
  205.9 1.9 shard_map.279
  207.8 2.6 collective-permute-start.40
  210.4 2.2 shard_map.278
  215.6 2.2 shard_map.282
  219.0 1.9 collective-permute-start.35
  223.0 1.8 shard_map.285
  226.4 2.8 %shard_map.281 = f32[4,384]{1,0:T(4,128)} custom-call(s32[3]{0:T(128)} %pad_add_fusion.pos, bf16[64,384]{1,0:T(8,128)(2,1)} %shard_map.280.small, bf16[4,384]{1,0:T(4,128)(2,1)} %cond.3, bf16[96,2304]{1,0:T(8,128)(2,1)} %shard_map.266.rest_10_.rest_0_, bf16[96,2304]{1,0:T(8,128)(2,1)} %copy-done.22, bf16[96,2304]{1,0:T(8,128)(2,1)} %copy-done.23, ...), custom_call_target="tpu_custom_call" | custom-call | tf_op jit(solution)/shard_map/pallas_call | solution.py:506
  235.1 6.0 %collective-permute-start.37 = (bf16[48,384]{1,0:T(8,128)(2,1)}, bf16[48,384]{1,0:T(8,128)(2,1)S(1)}, u32[]{:S(2)}, u32[]{:S(2)}) collective-permute-start(bf16[48,384]{1,0:T(8,128)(2,1)} %add_convert_fusion.8.refs_2_), channel_id=1, source_target_pairs={{0,1},{1,0},{2,3},{3,2},{4,5},{5,4},{6,7},{7,6},{8,9},{9,8},{10,11... | collective-permute-start | bytes 110600 | tf_op jit(solution)/shard_map/ppermute | solution.py:884
  241.1 2.0 collective-permute-start.38
  243.2 2.8 %shard_map.283 = (f32[96,2304]{1,0:T(8,128)}, f32[1,2304]{1,0:T(1,128)}, f32[24,384]{1,0:T(8,128)}) custom-call(s32[3]{0:T(128)} %pad_add_fusion.pos, bf16[144,384]{1,0:T(8,128)(2,1)} %get-tuple-element.116.own_small.refs_2_, bf16[192,384]{1,0:T(8,128)(2,1)} %copy-done.35, bf16[192,384]{1,0:T(8,128)(2,1)} %copy-done.36, bf16[192,384]{1,0:T(8,128)(2,1)} %copy-done.37), custom_call_target="tpu_custom_call" | custom-call | tf_op jit(solution)/shard_map/pallas_call | solution.py:506
  251.1 3.0 %collective-permute-start.46 = (bf16[96,384]{1,0:T(8,128)(2,1)S(1)}, bf16[96,384]{1,0:T(8,128)(2,1)S(1)}, u32[]{:S(2)}, u32[]{:S(2)}) collective-permute-start(bf16[96,384]{1,0:T(8,128)(2,1)S(1)} %add_convert_fusion.7), channel_id=1, source_target_pairs={{0,2},{1,3},{2,0},{3,1},{4,6},{5,7},{6,4},{7,5},{8,10},{9,11},{10,... | collective-permute-start | bytes 221192 | tf_op jit(solution)/shard_map/ppermute | solution.py:996
  260.2 2.1 collective-permute-start.47
  263.2 2.2 collective-permute-done.47
  (309 shorter events, 90.7 us)
Async XLA Ops:
  3.3 16.2 %collective-permute-start.1 = (bf16[1,2880]{1,0:T(2,128)(2,1)S(1)}, bf16[1,2880]{1,0:T(2,128)(2,1)S(1)}, u32[]{:S(2)}, u32[]{:S(2)}) collective-permute-start(bf16[1,2880]{1,0:T(2,128)(2,1)S(1)} %concatenate.132), channel_id=1, source_target_pairs={{0,8},{4,12},{8,0},{12,4},{1,9},{5,13},{9,1},{13,5},{2,10},{6,14},... | collective-permute-start | bytes 17288 | tf_op jit(solution)/shard_map/ppermute | solution.py:884
  6.3 13.2 %collective-permute-start.2 = (bf16[1,2880]{1,0:T(2,128)(2,1)S(1)}, bf16[1,2880]{1,0:T(2,128)(2,1)S(1)}, u32[]{:S(2)}, u32[]{:S(2)}) collective-permute-start(bf16[1,2880]{1,0:T(2,128)(2,1)S(1)} %concatenate.132), channel_id=1, source_target_pairs={{0,12},{4,8},{8,4},{12,0},{1,13},{5,9},{9,5},{13,1},{2,14},{6,10},... | collective-permute-start | bytes 17288 | tf_op jit(solution)/shard_map/ppermute | solution.py:884
  10.7 37.4 %collective-permute-start.6 = (bf16[1152,384]{1,0:T(8,128)(2,1)}, bf16[1152,384]{1,0:T(8,128)(2,1)S(1)}, u32[]{:S(2)}, u32[]{:S(2)}) collective-permute-start(bf16[1152,384]{1,0:T(8,128)(2,1)} %shard_map.263.rest_0_), channel_id=1, source_target_pairs={{0,4},{4,0},{8,12},{12,8},{1,5},{5,1},{9,13},{13,9},{2,6},{6,2},{1... | collective-permute-start | bytes 2654216 | tf_op jit(solution)/shard_map/ppermute | solution.py:927
  12.6 35.5 %collective-permute-start.7 = (bf16[1152,384]{1,0:T(8,128)(2,1)}, bf16[1152,384]{1,0:T(8,128)(2,1)S(1)}, u32[]{:S(2)}, u32[]{:S(2)}) collective-permute-start(bf16[1152,384]{1,0:T(8,128)(2,1)} %shard_map.263.rest_0_), channel_id=1, source_target_pairs={{0,8},{4,12},{8,0},{12,4},{1,9},{5,13},{9,1},{13,5},{2,10},{6,14},... | collective-permute-start | bytes 2654216 | tf_op jit(solution)/shard_map/ppermute | solution.py:928
  21.5 26.0 %collective-permute-start.3 = (f32[4,2304]{1,0:T(4,128)}, f32[4,2304]{1,0:T(4,128)S(1)}, u32[]{:S(2)}, u32[]{:S(2)}) collective-permute-start(f32[4,2304]{1,0:T(4,128)} %get-tuple-element.170), channel_id=1, source_target_pairs={{0,4},{4,0},{8,12},{12,8},{1,5},{5,1},{9,13},{13,9},{2,6},{6,2},{1... | collective-permute-start | bytes 110600 | tf_op jit(solution)/shard_map/ppermute | solution.py:851
  22.0 25.5 %collective-permute-start.4 = (f32[4,2304]{1,0:T(4,128)}, f32[4,2304]{1,0:T(4,128)S(1)}, u32[]{:S(2)}, u32[]{:S(2)}) collective-permute-start(f32[4,2304]{1,0:T(4,128)} %get-tuple-element.169), channel_id=1, source_target_pairs={{0,8},{4,12},{8,0},{12,4},{1,9},{5,13},{9,1},{13,5},{2,10},{6,14},... | collective-permute-start | bytes 110600 | tf_op jit(solution)/shard_map/ppermute | solution.py:851
  22.1 25.9 %collective-permute-start.5 = (f32[4,2304]{1,0:T(4,128)}, f32[4,2304]{1,0:T(4,128)S(1)}, u32[]{:S(2)}, u32[]{:S(2)}) collective-permute-start(f32[4,2304]{1,0:T(4,128)} %get-tuple-element.168), channel_id=1, source_target_pairs={{0,12},{4,8},{8,4},{12,0},{1,13},{5,9},{9,5},{13,1},{2,14},{6,10},... | collective-permute-start | bytes 110600 | tf_op jit(solution)/shard_map/ppermute | solution.py:851
  47.5 18.4 %collective-permute-start.12 = (bf16[1152,384]{1,0:T(8,128)(2,1)S(1)}, bf16[1152,384]{1,0:T(8,128)(2,1)}, u32[]{:S(2)}, u32[]{:S(2)}) collective-permute-start(bf16[1152,384]{1,0:T(8,128)(2,1)S(1)} %copy-done.1), channel_id=1, source_target_pairs={{0,16},{16,0},{1,17},{17,1},{2,18},{18,2},{3,19},{19,3},{4,20},{20... | collective-permute-start | bytes 2654216 | tf_op jit(solution)/shard_map/ppermute | solution.py:819
  52.1 12.3 %collective-permute-start.10 = (bf16[576,384]{1,0:T(8,128)(2,1)S(1)}, bf16[576,384]{1,0:T(8,128)(2,1)}, u32[]{:S(2)}, u32[]{:S(2)}) collective-permute-start(bf16[576,384]{1,0:T(8,128)(2,1)S(1)} %slice.272), channel_id=1, source_target_pairs={{0,8},{4,12},{8,0},{12,4},{1,9},{5,13},{9,1},{13,5},{2,10},{6,14},... | collective-permute-start | bytes 1327112 | tf_op jit(solution)/shard_map/ppermute | solution.py:929
  53.9 14.0 %collective-permute-start.13 = (bf16[1152,384]{1,0:T(8,128)(2,1)S(1)}, bf16[1152,384]{1,0:T(8,128)(2,1)}, u32[]{:S(2)}, u32[]{:S(2)}) collective-permute-start(bf16[1152,384]{1,0:T(8,128)(2,1)S(1)} %copy-done.3), channel_id=1, source_target_pairs={{0,16},{16,0},{1,17},{17,1},{2,18},{18,2},{3,19},{19,3},{4,20},{20... | collective-permute-start | bytes 2654216 | tf_op jit(solution)/shard_map/ppermute | solution.py:819
  53.9 14.0 %collective-permute-start.14 = (bf16[1152,384]{1,0:T(8,128)(2,1)S(1)}, bf16[1152,384]{1,0:T(8,128)(2,1)}, u32[]{:S(2)}, u32[]{:S(2)}) collective-permute-start(bf16[1152,384]{1,0:T(8,128)(2,1)S(1)} %copy-done.5), channel_id=1, source_target_pairs={{0,16},{16,0},{1,17},{17,1},{2,18},{18,2},{3,19},{19,3},{4,20},{20... | collective-permute-start | bytes 2654216 | tf_op jit(solution)/shard_map/ppermute | solution.py:819
  109.5 35.9 %collective-permute-start.17 = (bf16[2816,384]{1,0:T(8,128)(2,1)}, bf16[2816,384]{1,0:T(8,128)(2,1)S(1)}, u32[]{:S(2)}, u32[]{:S(2)}) collective-permute-start(bf16[2816,384]{1,0:T(8,128)(2,1)} %get-tuple-element.78), channel_id=1, source_target_pairs={{0,16},{16,0},{1,17},{17,1},{2,18},{18,2},{3,19},{19,3},{4,20},{20... | collective-permute-start | bytes 6488072 | tf_op jit(solution)/shard_map/ppermute | solution.py:819
  109.7 13.0 %collective-permute-start.18 = (bf16[96,2304]{1,0:T(8,128)(2,1)S(1)}, bf16[96,2304]{1,0:T(8,128)(2,1)S(1)}, u32[]{:S(2)}, u32[]{:S(2)}) collective-permute-start(bf16[96,2304]{1,0:T(8,128)(2,1)S(1)} %copy-done.7), channel_id=1, source_target_pairs={{0,4},{4,0},{8,12},{12,8},{1,5},{5,1},{9,13},{13,9},{2,6},{6,2},{1... | collective-permute-start | bytes 1327112 | tf_op jit(solution)/shard_map/ppermute | solution.py:884
  110.0 21.0 %collective-permute-start.19 = (bf16[96,2304]{1,0:T(8,128)(2,1)S(1)}, bf16[96,2304]{1,0:T(8,128)(2,1)S(1)}, u32[]{:S(2)}, u32[]{:S(2)}) collective-permute-start(bf16[96,2304]{1,0:T(8,128)(2,1)S(1)} %copy-done.7), channel_id=1, source_target_pairs={{0,8},{4,12},{8,0},{12,4},{1,9},{5,13},{9,1},{13,5},{2,10},{6,14},... | collective-permute-start | bytes 1327112 | tf_op jit(solution)/shard_map/ppermute | solution.py:884
  111.7 20.9 %collective-permute-start.20 = (bf16[96,2304]{1,0:T(8,128)(2,1)S(1)}, bf16[96,2304]{1,0:T(8,128)(2,1)S(1)}, u32[]{:S(2)}, u32[]{:S(2)}) collective-permute-start(bf16[96,2304]{1,0:T(8,128)(2,1)S(1)} %copy-done.7), channel_id=1, source_target_pairs={{0,12},{4,8},{8,4},{12,0},{1,13},{5,9},{9,5},{13,1},{2,14},{6,10},... | collective-permute-start | bytes 1327112 | tf_op jit(solution)/shard_map/ppermute | solution.py:884
  145.4 15.0 %collective-permute-start.21 = (bf16[1536,384]{1,0:T(8,128)(2,1)}, bf16[1536,384]{1,0:T(8,128)(2,1)S(1)}, u32[]{:S(2)}, u32[]{:S(2)}) collective-permute-start(bf16[1536,384]{1,0:T(8,128)(2,1)} %get-tuple-element.95), channel_id=1, source_target_pairs={{0,16},{16,0},{1,17},{17,1},{2,18},{18,2},{3,19},{19,3},{4,20},{20... | collective-permute-start | bytes 3538952 | tf_op jit(solution)/shard_map/ppermute | solution.py:819
  149.1 17.4 %collective-permute-start.22 = (bf16[576,384]{1,0:T(8,128)(2,1)}, bf16[576,384]{1,0:T(8,128)(2,1)}, u32[]{:S(2)}, u32[]{:S(2)}) collective-permute-start(bf16[576,384]{1,0:T(8,128)(2,1)} %get-tuple-element.149.rest_0_), channel_id=1, source_target_pairs={{0,4},{4,0},{8,12},{12,8},{1,5},{5,1},{9,13},{13,9},{2,6},{6,2},{1... | collective-permute-start | bytes 1327112 | tf_op jit(solution)/shard_map/ppermute | solution.py:851
  150.1 20.9 %collective-permute-start.23 = (bf16[576,384]{1,0:T(8,128)(2,1)S(1)}, bf16[576,384]{1,0:T(8,128)(2,1)}, u32[]{:S(2)}, u32[]{:S(2)}) collective-permute-start(bf16[576,384]{1,0:T(8,128)(2,1)S(1)} %get-tuple-element.148.rest_1_), channel_id=1, source_target_pairs={{0,8},{4,12},{8,0},{12,4},{1,9},{5,13},{9,1},{13,5},{2,10},{6,14},... | collective-permute-start | bytes 1327112 | tf_op jit(solution)/shard_map/ppermute | solution.py:851
  151.6 20.8 %collective-permute-start.24 = (bf16[576,384]{1,0:T(8,128)(2,1)S(1)}, bf16[576,384]{1,0:T(8,128)(2,1)}, u32[]{:S(2)}, u32[]{:S(2)}) collective-permute-start(bf16[576,384]{1,0:T(8,128)(2,1)S(1)} %get-tuple-element.147.rest_2_), channel_id=1, source_target_pairs={{0,12},{4,8},{8,4},{12,0},{1,13},{5,9},{9,5},{13,1},{2,14},{6,10},... | collective-permute-start | bytes 1327112 | tf_op jit(solution)/shard_map/ppermute | solution.py:851
  164.0 31.0 %collective-permute-start.26 = (bf16[384,384]{1,0:T(8,128)(2,1)S(1)}, bf16[384,384]{1,0:T(8,128)(2,1)S(1)}, u32[]{:S(2)}, u32[]{:S(2)}) collective-permute-start(bf16[384,384]{1,0:T(8,128)(2,1)S(1)} %get-tuple-element.153.refs_4_.rest_11_), channel_id=1, source_target_pairs={{0,4},{4,0},{8,12},{12,8},{1,5},{5,1},{9,13},{13,9},{2,6},{6,2},{1... | collective-permute-start | bytes 884744 | tf_op jit(solution)/shard_map/ppermute | solution.py:851
  165.1 30.0 %collective-permute-start.27 = (bf16[384,384]{1,0:T(8,128)(2,1)S(1)}, bf16[384,384]{1,0:T(8,128)(2,1)S(1)}, u32[]{:S(2)}, u32[]{:S(2)}) collective-permute-start(bf16[384,384]{1,0:T(8,128)(2,1)S(1)} %get-tuple-element.152.refs_5_.rest_12_), channel_id=1, source_target_pairs={{0,8},{4,12},{8,0},{12,4},{1,9},{5,13},{9,1},{13,5},{2,10},{6,14},... | collective-permute-start | bytes 884744 | tf_op jit(solution)/shard_map/ppermute | solution.py:851
  166.6 28.5 %collective-permute-start.28 = (bf16[384,384]{1,0:T(8,128)(2,1)S(1)}, bf16[384,384]{1,0:T(8,128)(2,1)S(1)}, u32[]{:S(2)}, u32[]{:S(2)}) collective-permute-start(bf16[384,384]{1,0:T(8,128)(2,1)S(1)} %get-tuple-element.151.refs_6_.rest_13_), channel_id=1, source_target_pairs={{0,12},{4,8},{8,4},{12,0},{1,13},{5,9},{9,5},{13,1},{2,14},{6,10},... | collective-permute-start | bytes 884744 | tf_op jit(solution)/shard_map/ppermute | solution.py:851
  175.1 20.0 %collective-permute-start.25 = (bf16[288,384]{1,0:T(8,128)(2,1)}, bf16[288,384]{1,0:T(8,128)(2,1)S(1)}, u32[]{:S(2)}, u32[]{:S(2)}) collective-permute-start(bf16[288,384]{1,0:T(8,128)(2,1)} %get-tuple-element.99.rest_14_), channel_id=1, source_target_pairs={{0,1},{1,0},{2,3},{3,2},{4,5},{5,4},{6,7},{7,6},{8,9},{9,8},{10,11... | collective-permute-start | bytes 663560 | tf_op jit(solution)/shard_map/ppermute | solution.py:990
  207.8 14.5 %collective-permute-start.40 = (bf16[144,384]{1,0:T(8,128)(2,1)}, bf16[144,384]{1,0:T(8,128)(2,1)S(1)}, u32[]{:S(2)}, u32[]{:S(2)}) collective-permute-start(bf16[144,384]{1,0:T(8,128)(2,1)} %get-tuple-element.111.refs_2_), channel_id=1, source_target_pairs={{0,2},{1,3},{2,0},{3,1},{4,6},{5,7},{6,4},{7,5},{8,10},{9,11},{10,... | collective-permute-start | bytes 331784 | tf_op jit(solution)/shard_map/ppermute | solution.py:996
  217.8 15.3 %collective-permute-start.34 = (bf16[192,384]{1,0:T(8,128)(2,1)}, bf16[192,384]{1,0:T(8,128)(2,1)S(1)}, u32[]{:S(2)}, u32[]{:S(2)}) collective-permute-start(bf16[192,384]{1,0:T(8,128)(2,1)} %get-tuple-element.117), channel_id=1, source_target_pairs={{0,1},{1,0},{2,3},{3,2},{4,5},{5,4},{6,7},{7,6},{8,9},{9,8},{10,11... | collective-permute-start | bytes 442376 | tf_op jit(solution)/shard_map/ppermute | solution.py:851
  219.0 15.4 %collective-permute-start.35 = (bf16[192,384]{1,0:T(8,128)(2,1)}, bf16[192,384]{1,0:T(8,128)(2,1)S(1)}, u32[]{:S(2)}, u32[]{:S(2)}) collective-permute-start(bf16[192,384]{1,0:T(8,128)(2,1)} %get-tuple-element.118), channel_id=1, source_target_pairs={{0,2},{1,3},{2,0},{3,1},{4,6},{5,7},{6,4},{7,5},{8,10},{9,11},{10,... | collective-permute-start | bytes 442376 | tf_op jit(solution)/shard_map/ppermute | solution.py:851
  220.9 13.5 %collective-permute-start.36 = (bf16[192,384]{1,0:T(8,128)(2,1)}, bf16[192,384]{1,0:T(8,128)(2,1)S(1)}, u32[]{:S(2)}, u32[]{:S(2)}) collective-permute-start(bf16[192,384]{1,0:T(8,128)(2,1)} %get-tuple-element.119), channel_id=1, source_target_pairs={{0,3},{1,2},{2,1},{3,0},{4,7},{5,6},{6,5},{7,4},{8,11},{9,10},{10,... | collective-permute-start | bytes 442376 | tf_op jit(solution)/shard_map/ppermute | solution.py:851
  224.8 24.2 %collective-permute-start.43 = (bf16[96,384]{1,0:T(8,128)(2,1)}, bf16[96,384]{1,0:T(8,128)(2,1)S(1)}, u32[]{:S(2)}, u32[]{:S(2)}) collective-permute-start(bf16[96,384]{1,0:T(8,128)(2,1)} %get-tuple-element.126), channel_id=1, source_target_pairs={{0,2},{1,3},{2,0},{3,1},{4,6},{5,7},{6,4},{7,5},{8,10},{9,11},{10,... | collective-permute-start | bytes 221192 | tf_op jit(solution)/shard_map/ppermute | solution.py:996
  230.6 18.3 %collective-permute-start.42 = (bf16[144,384]{1,0:T(8,128)(2,1)S(1)}, bf16[144,384]{1,0:T(8,128)(2,1)S(1)}, u32[]{:S(2)}, u32[]{:S(2)}) collective-permute-start(bf16[144,384]{1,0:T(8,128)(2,1)S(1)} %add_convert_fusion.6), channel_id=1, source_target_pairs={{0,2},{1,3},{2,0},{3,1},{4,6},{5,7},{6,4},{7,5},{8,10},{9,11},{10,... | collective-permute-start | bytes 331784 | tf_op jit(solution)/shard_map/ppermute | solution.py:996
  235.1 24.1 %collective-permute-start.37 = (bf16[48,384]{1,0:T(8,128)(2,1)}, bf16[48,384]{1,0:T(8,128)(2,1)S(1)}, u32[]{:S(2)}, u32[]{:S(2)}) collective-permute-start(bf16[48,384]{1,0:T(8,128)(2,1)} %add_convert_fusion.8.refs_2_), channel_id=1, source_target_pairs={{0,1},{1,0},{2,3},{3,2},{4,5},{5,4},{6,7},{7,6},{8,9},{9,8},{10,11... | collective-permute-start | bytes 110600 | tf_op jit(solution)/shard_map/ppermute | solution.py:884
  241.1 18.1 %collective-permute-start.38 = (bf16[48,384]{1,0:T(8,128)(2,1)}, bf16[48,384]{1,0:T(8,128)(2,1)S(1)}, u32[]{:S(2)}, u32[]{:S(2)}) collective-permute-start(bf16[48,384]{1,0:T(8,128)(2,1)} %add_convert_fusion.8.refs_2_), channel_id=1, source_target_pairs={{0,3},{1,2},{2,1},{3,0},{4,7},{5,6},{6,5},{7,4},{8,11},{9,10},{10,... | collective-permute-start | bytes 110600 | tf_op jit(solution)/shard_map/ppermute | solution.py:884
  243.1 16.1 %collective-permute-start.39 = (bf16[48,384]{1,0:T(8,128)(2,1)}, bf16[48,384]{1,0:T(8,128)(2,1)S(1)}, u32[]{:S(2)}, u32[]{:S(2)}) collective-permute-start(bf16[48,384]{1,0:T(8,128)(2,1)} %add_convert_fusion.8.refs_2_), channel_id=1, source_target_pairs={{0,2},{1,3},{2,0},{3,1},{4,6},{5,7},{6,4},{7,5},{8,10},{9,11},{10,... | collective-permute-start | bytes 110600 | tf_op jit(solution)/shard_map/ppermute | solution.py:884
  (80 other events, 509.9 us)

commit v5 on v4

--- a/solution.py
+++ b/solution.py
@@ -339,8 +339,41 @@
         out_shape=jax.ShapeDtypeStruct((HIGH, heads * LOW), F32),
         in_specs=[pl.BlockSpec(memory_space=pltpu.VMEM)] * 2 + [pl.BlockSpec(memory_space=pl.ANY)] * len(earlier),
         out_specs=pl.BlockSpec(memory_space=pltpu.VMEM),
+        cost_estimate=cost(8),
         compiler_params=pltpu.CompilerParams(vmem_limit_bytes=VMEM_BYTES),
     )(scores, index, *earlier)
+
+
+def small_kernel(pos, scores, index, small_a0, small_m0, small_a1, small_m1, table1, *rest):
+    keep, send, table = rest[-3:]
+    size = small_a0.shape[0] * small_a0.shape[1]
+    add_table(scores, index, table)
+    parts = (
+        (small_a0[...], small_m0[...], table[...]),
+        (small_a1[...], small_m1[...], table1[...]),
+    )
+    rows = [
+        jnp.concatenate([x[0].reshape(size, -1), x[1].reshape(size, -1), x[2]], axis=0) for x in parts
+    ]
+
+    @pl.when(pos[0] == 0)
+    def _():
+        keep[...] = rows[0]
+        send[...] = rows[1].astype(BF16)
+
+    @pl.when(pos[0] == 1)
+    def _():
+        keep[...] = rows[1]
+        send[...] = rows[0].astype(BF16)
+
+
+def small_step(pos, scores, index, smalls, table1, earlier):
+    samples, _, model = smalls[0].shape
+    shape = (16 * samples + HIGH, model)
+    return call(
+        small_kernel, pos, (scores, index, *smalls, table1), earlier, [(shape, F32), (shape, BF16)],
+        [((HIGH, model), F32)], work=8,
+    )
 
 
 def set_line(line, layer, section, own_line, other_line):
@@ -387,8 +420,8 @@
     )
 
 
-def both_kernel(layer, pieces, length, n_weights, pos, h, grad, own_line, other_line, own_bias, other_bias, *rest):
-    refs, rest = rest[:n_weights], rest[n_weights:]
+def both_kernel(layer, pieces, length, n_weights, n_after, pos, h, grad, own_line, other_line, own_bias, other_bias, *rest):
+    refs, rest = rest[:n_weights], rest[n_weights + n_after :]
     (layer_out, d_in, small_a, small_m, scores, keep, send,
      w_qkv, w_proj, w_fc1, w_fc2, bias, line, qkv, probs, att, branch, middle, act, slope, out_branch,
      d_middle, normed_low, d_pre, d_ob, d_qkv, score_sum, g_qkv, g_proj, g_fc1, g_fc2, sems) = rest
@@ -452,51 +485,41 @@
     wait_all(for_attention)
 
 
-def backward_attention_kernel(layer, pieces, length, n_weights, n_after, pos, h, own_line, other_line, qkv, probs, att, branch, d_middle,
-                              index, d_h1, small_m0, small_a1, small_m1, table1, *rest):
+def backward_attention_kernel(layer, pieces, length, n_weights, n_after, pos, h, own_line, other_line, qkv, probs, att, branch, d_middle, d_h1, *rest):
     refs, rest = rest[:n_weights], rest[n_weights + n_after :]
-    (d_in, keep, send, kept_small,
-     w_qkv, w_proj, w_fc1, w_fc2, line, small, table, normed_low, d_qkv, d_br, score_sum, g_qkv, g_proj, sems) = rest
+    (d_in, small, scores, keep, send,
+     w_qkv, w_proj, w_fc1, w_fc2, line, normed_low, d_qkv, d_br, score_sum, g_qkv, g_proj, sems) = rest
     section, shard = pos[0], pos[1]
-    model = h.shape[1]
-    samples = h.shape[0] // length
     for_attention, for_mlp = weight_loads(layer, section, shard, refs, (w_qkv, w_proj, w_fc1, w_fc2), sems)
     set_line(line, layer, section, own_line, other_line)
-    mod = Modulation(line, model)
+    mod = Modulation(line, h.shape[1])
     score_sum[...] = jnp.zeros_like(score_sum)
     wait_all(for_attention)
     each_sample(
-        samples,
+        h.shape[0] // length,
         lambda b: attention_backward(b, length, h, mod, w_qkv, w_proj, qkv, probs, att, branch, d_middle, d_in, small, score_sum, normed_low, d_qkv, d_br),
     )
+    scores[...] = score_sum[...].astype(BF16)
     attention_weight_grads(normed_low, d_qkv, att, d_br, g_qkv, g_proj)
     pack_attention((keep, send), section, g_qkv, g_proj, shard, pieces, 2, 0)
-    add_table(score_sum, index, table)
-    at = keep.shape[0]
-    rows = slice(at, at + h.shape[0])
-    at += h.shape[0]
-    size = samples * 8
-    smalls = (
-        jnp.concatenate([small[...].reshape(size, model), small_m0[...].reshape(size, model), table[...]], axis=0),
-        jnp.concatenate([small_a1[...].reshape(size, model), small_m1[...].reshape(size, model), table1[...]], axis=0),
-    )
+    rows = slice(keep.shape[0], keep.shape[0] + h.shape[0])
 
     @pl.when(section == 0)
     def _():
         send[rows, :] = d_h1[...]
-        send[at:, :] = smalls[1].astype(BF16)
-        kept_small[...] = smalls[0]
 
     @pl.when(section == 1)
     def _():
         send[rows, :] = d_in[...].astype(BF16)
-        send[at:, :] = smalls[0].astype(BF16)
-        kept_small[...] = smalls[1]
 
     wait_all(for_mlp)
 
 
-def call(kernel, pos, operands, in_hbm, outs, scratch, sems=0):
+def cost(gigaflop):
+    return pl.CostEstimate(flops=int(gigaflop * 1e9), bytes_accessed=0, transcendentals=0)
+
+
+def call(kernel, pos, operands, in_hbm, outs, scratch, sems=0, work=2):
     specs = [pl.BlockSpec(memory_space=pltpu.SMEM)]
     specs += [pl.BlockSpec(memory_space=pltpu.VMEM) for _ in operands]
     specs += [pl.BlockSpec(memory_space=pl.ANY) for _ in in_hbm]
@@ -509,6 +532,7 @@
         in_specs=specs,
         out_specs=[pl.BlockSpec(memory_space=pltpu.VMEM) for _ in outs],
         scratch_shapes=shapes,
+        cost_estimate=cost(work),
         compiler_params=pltpu.CompilerParams(vmem_limit_bytes=VMEM_BYTES),
     )(pos, *operands, *in_hbm)
 
@@ -539,18 +563,18 @@
         functools.partial(forward_kernel, layer, z.length, len(weights), len(earlier)),
         pos, (h, *lines), (*biases, *weights, *earlier),
         [z.qkv, z.probs, z.low, z.full, z.full, z.wide, z.wide, z.full, z.low],
-        [*z.weights, z.bias, z.line], weight_count(len(weights)) + 1,
-    )
-
-
-def both_ways(layer, z, pos, h, grad, lines, biases, weights):
+        [*z.weights, z.bias, z.line], weight_count(len(weights)) + 1, work=15,
+    )
+
+
+def both_ways(layer, z, pos, h, grad, lines, biases, weights, earlier):
     return call(
-        functools.partial(both_kernel, layer, z.pieces, z.length, len(weights)),
-        pos, (h, grad, *lines), (*biases, *weights),
+        functools.partial(both_kernel, layer, z.pieces, z.length, len(weights), len(earlier)),
+        pos, (h, grad, *lines), (*biases, *weights, *earlier),
         [z.low, z.low, z.small, z.small, z.bias, *z.pack(6, z.rows)],
         [*z.weights, z.bias, z.line, z.qkv, z.probs, z.low, z.full, z.full, z.wide, z.wide, z.full,
          z.full, z.low, z.wide, z.low, z.qkv, (z.bias[0], F32), *z.weights],
-        weight_count(len(weights)) + 1,
+        weight_count(len(weights)) + 1, work=25,
     )
 
 
@@ -560,22 +584,74 @@
         pos, (grad, middle, *lines, act, slope, out_branch), (*weights, *earlier),
         [z.full, z.small, *z.pack(4)],
         [*z.weights, z.line, z.low, z.wide, z.low, *z.weights[2:]],
-        weight_count(len(weights)),
-    )
-
-
-def backward_attention(layer, z, pos, h, lines, qkv, probs, att, branch, d_middle, index, others, weights, earlier):
-    rows = 2 * 8 * z.samples + HIGH
+        weight_count(len(weights)), work=12,
+    )
+
+
+def backward_attention(layer, z, pos, h, lines, qkv, probs, att, branch, d_middle, d_h1, weights, earlier):
     return call(
         functools.partial(backward_attention_kernel, layer, z.pieces, z.length, len(weights), len(earlier)),
-        pos, (h, *lines, qkv, probs, att, branch, d_middle, index, *others), (*weights, *earlier),
-        [z.full, *z.pack(2, z.rows + rows), ((rows, z.model), F32)],
-        [*z.weights, z.line, z.small, ((HIGH, z.heads * LOW), F32), z.low, z.qkv, z.low, (z.bias[0], F32), *z.weights[:2]],
-        weight_count(len(weights)),
-    )
-
-
-def plane_kernel(samples, n_rows, pos, keep, other, kept_small, cond, own, own_small, *rest):
+        pos, (h, *lines, qkv, probs, att, branch, d_middle, d_h1), (*weights, *earlier),
+        [z.full, z.small, z.bias, *z.pack(2, z.rows)],
+        [*z.weights, z.line, z.low, z.qkv, z.low, (z.bias[0], F32), *z.weights[:2]],
+        weight_count(len(weights)), work=13,
+    )
+
+
+def partial_kernel(pos, w_ada, cond_a, cond_b, cond_c, cond_d, b_ada, b_qv, b_proj, b_fc1, b_fc2, *rest):
+    outs, whole = rest[-5:-1], rest[-1]
+    shard = pos[1]
+    q, wide = w_ada.shape
+    samples, model = cond_a.shape
+    whole[...] = jnp.zeros_like(whole)
+    whole[pl.ds(pl.multiple_of(shard * q, 16), q), :] = w_ada[...]
+    for cond, out in zip((cond_a, cond_b, cond_c, cond_d), outs):
+        c = cond[...].astype(F32)
+        act = (c * (1.0 / (1.0 + jnp.exp(-c)))).astype(BF16)
+        out[:, :wide] = dot(act, whole[...])
+        out[:, wide:] = jnp.zeros((samples, 2 * model), F32)
+        for f in range(4):
+            @pl.when(shard == f)
+            def _():
+                here = slice(f * b_ada.shape[1], (f + 1) * b_ada.shape[1])
+                out[:, here] += b_ada[...].astype(F32)
+                for bias, row, at in ((b_qv, 0, 0), (b_proj, 1, 0), (b_fc1, 1, model), (b_fc2, 3, model)):
+                    width = bias.shape[1]
+                    at += f * width
+                    row, at = row + at // (2 * model), wide + at % (2 * model)
+                    out[row : row + 1, at : at + width] = bias[...].astype(F32)
+
+
+def partial_step(pos, w_ada, conds, biases, earlier):
+    q, wide = w_ada.shape
+    samples, model = conds[0].shape
+    return call(
+        partial_kernel, pos, (w_ada, *conds, *biases), earlier, [((samples, wide + 2 * model), F32)] * 4,
+        [((4 * q, wide), BF16)],
+    )
+
+
+def line_kernel(pos, own, got_a, got_b, got_c, keep, send, total):
+    section = pos[0]
+    samples = own.shape[0]
+    each = samples // 2
+    model = own.shape[1] // 8
+    total[...] = (own[...] + got_a[...]) + (got_b[...] + got_c[...])
+    for out, side in ((keep, section), (send, 1 - section)):
+        for b in range(each):
+            out[:, b * 6 * model : (b + 1) * 6 * model] = total[pl.ds(side * each + b, 1), : 6 * model]
+        for row in range(samples):
+            at = (6 * each + 2 * row) * model
+            out[:, at : at + 2 * model] = total[row : row + 1, 6 * model :]
+
+
+def line_step(pos, own, got):
+    samples, model = own.shape[0], own.shape[1] // 8
+    shape = (1, (3 * samples + 8) * model)
+    return call(line_kernel, pos, (own, *got), (), [(shape, F32)] * 2, [(own.shape, F32)])
+
+
+def plane_kernel(samples, pos, keep, other, kept_small, other_small, cond, own, own_small, *rest):
     messages, work = rest[:3], rest[3]
     section = pos[0]
     size, model = own.shape
@@ -586,8 +662,7 @@
             own[...] = total
         else:
             messages[p - 1][:size, :] = total.astype(BF16)
-    at = keep.shape[0] + n_rows
-    theirs = other[at:, :].astype(F32)
+    theirs = other_small[...].astype(F32)
     mine = kept_small[...]
     each = samples // 2
     work[...] = jnp.zeros_like(work)
@@ -610,13 +685,13 @@
         message[size:, :] = small
 
 
-def plane_step(pos, keep, other, kept_small, cond, n_rows):
+def plane_step(pos, keep, other, kept_small, other_small, cond):
     samples, model = cond.shape
     size = keep.shape[0] // 4
     small = -(-(7 * samples + 8 + HIGH) // 16) * 16
     outs = [((size, model), F32), ((small, model), BF16)] + [((size + small, model), BF16)] * 3
     return call(
-        functools.partial(plane_kernel, samples, n_rows), pos, (keep, other, kept_small, cond), (), outs,
+        functools.partial(plane_kernel, samples), pos, (keep, other, kept_small, other_small, cond), (), outs,
         [((small, model), F32)],
     )
 
@@ -717,6 +792,39 @@
     )[0]
 
 
+def final_kernel(pos, own_a, own_m, other, g_qkv, g_proj, g_fc1, g_fc2):
+    section = pos[0]
+    q, model = g_proj.shape
+    cut = own_a.shape[0]
+
+    def write(first_a, first_m, second_a, second_m):
+        for c in range(2):
+            g_qkv[:, c * model : (c + 1) * model] = first_a[c * q : (c + 1) * q, :].astype(F32)
+        g_qkv[:, 2 * model : 3 * model] = second_a[:q, :].astype(F32)
+        g_proj[...] = second_a[q : 2 * q, :].astype(F32)
+        for c in range(4):
+            g_fc1[:, c * model : (c + 1) * model] = first_m[c * q : (c + 1) * q, :].astype(F32)
+        g_fc2[...] = second_m[...].astype(F32)
+
+    other_a, other_m = other.at[:cut, :], other.at[cut:, :]
+
+    @pl.when(section == 0)
+    def _():
+        write(own_a, own_m, other_a, other_m)
+
+    @pl.when(section == 1)
+    def _():
+        write(other_a, other_m, own_a, own_m)
+
+
+def final_step(pos, own_a, own_m, other):
+    q, model = own_a.shape[0] // 2, own_a.shape[1]
+    return call(
+        final_kernel, pos, (own_a, own_m, other), (),
+        [((q, 3 * model), F32), ((q, model), F32), ((q, 4 * model), F32), ((4 * q, model), F32)], [],
+    )
+
+
 def halve_kernel(pos, own, got_a, got_b, got_c, keep, send):
     bit = pos[2] & 1
     n = own.shape[0] // 4
@@ -811,6 +919,7 @@
         in_specs=[pl.BlockSpec(memory_space=pltpu.VMEM)] * 2 + [pl.BlockSpec(memory_space=pl.ANY)] * len(earlier),
         out_specs=pl.BlockSpec(memory_space=pltpu.VMEM),
         scratch_shapes=[pltpu.VMEM((heads, length, length), F32)],
+        cost_estimate=cost(11),
         compiler_params=pltpu.CompilerParams(vmem_limit_bytes=VMEM_BYTES),
     )(rows, index, *earlier)
 
@@ -917,27 +1026,20 @@
     h0 = own_samples(inputs).reshape(half * length, model)
     grad1 = (own_samples(cotangent) * live).reshape(half * length, model)
     own_raw = [w_qkv[0], w_proj[0], w_fc1[0], w_fc2[0]]
-    cond_size = conditioning.size
     width = model // shards
     if direct:
-        row = jnp.concatenate([conditioning.reshape(1, -1), b_ada, b_qv, b_proj, b_fc1, b_fc2], axis=1)
-        rows = [row] + from_peers(row, "fsdp")
+        conds = [conditioning] + from_peers(conditioning, "fsdp")
         own_pack = pack_shard(pos, own_raw)
         middle_row = own_pack.shape[0] // 2
         got_x = lax.ppermute(own_pack, "fsdp", pairs_of(shards, 1))
         got_y = lax.ppermute(own_pack, "fsdp", pairs_of(shards, 2))
+        bias_own = lookup(bias_table[0], relative_bias_index, [own_pack, h0, grad1])
+        partial = partial_step(pos, w_ada[0], conds, (b_ada, b_qv, b_proj, b_fc1, b_fc2), [bias_own])
         got_first = lax.ppermute(got_x[:middle_row], "fsdp", pairs_of(shards, 2))
         got_second = lax.ppermute(got_y[middle_row:], "fsdp", pairs_of(shards, 1))
         own_weights = [own_pack, got_x, got_y, got_first, got_second]
         weights = own_weights + [swap_section(w) for w in own_weights]
-        cond_pieces = jnp.stack([r[0, :cond_size].reshape(samples, model) for r in rows])
-        acts = jax.nn.silu(cond_pieces.astype(F32)).astype(BF16)
-        acts = lax.dynamic_slice_in_dim(acts, shard * width, width, 2)
-        partial = lax.dot_general(acts, w_ada[0], (((2,), (0,)), ((), ())), preferred_element_type=F32)
-        bias_rows = by_rank([r[0, cond_size:] for r in rows], shard)
-        bias_own = lookup(bias_table[0], relative_bias_index, [own_pack, partial, h0, grad1])
-        parts = after(to_peers(partial[1:], "fsdp"), [got_x, got_y, bias_own])
-        modulation = add_pieces(partial[0], parts)
+        own_line, send_line = line_step(pos, partial[0], after(to_peers(partial[1:], "fsdp"), [got_x, got_y]))
     else:
         row = jnp.concatenate([b_ada, b_qv, b_proj, b_fc1, b_fc2], axis=1)
         bias_rows = lax.all_gather(row[0], "fsdp", axis=0)
@@ -947,16 +1049,16 @@
         acts = jax.nn.silu(conditioning.astype(F32)).astype(BF16)
         modulation = dot(acts, lax.all_gather(w_ada[0], "fsdp", axis=0, tiled=True))
         bias_own = lookup(bias_table[0], relative_bias_index, [])
-    cuts = [b_ada.shape[1], b_qv.shape[1], b_proj.shape[1], b_fc1.shape[1], b_fc2.shape[1]]
-    biases, at = [], 0
-    for cut in cuts:
-        biases.append(bias_rows[:, at : at + cut].reshape(1, -1).astype(F32))
-        at += cut
-    modulation = modulation + biases[0]
-    other_samples = lax.dynamic_slice_in_dim(modulation, (1 - section) * half, half, 0)
-    own_line = jnp.concatenate([own_samples(modulation).reshape(1, -1)] + biases[1:], axis=1)
-    other_line = swap_section(jnp.concatenate([other_samples.reshape(1, -1)] + biases[1:], axis=1))
-    lines = (own_line, other_line)
+        cuts = [b_ada.shape[1], b_qv.shape[1], b_proj.shape[1], b_fc1.shape[1], b_fc2.shape[1]]
+        biases, at = [], 0
+        for cut in cuts:
+            biases.append(bias_rows[:, at : at + cut].reshape(1, -1).astype(F32))
+            at += cut
+        modulation = modulation + biases[0]
+        other_samples = lax.dynamic_slice_in_dim(modulation, (1 - section) * half, half, 0)
+        own_line = jnp.concatenate([own_samples(modulation).reshape(1, -1)] + biases[1:], axis=1)
+        send_line = jnp.concatenate([other_samples.reshape(1, -1)] + biases[1:], axis=1)
+    lines = (own_line, swap_section(send_line))
     bias_heads = (bias_own, swap_section(bias_own))
 
     if direct:
@@ -965,8 +1067,8 @@
     else:
         w_ada_pieces = [lax.all_gather(w_ada[0], "fsdp", axis=0, tiled=True)]
     qkv, probs, att, branch, middle, act, slope, out_branch, h1 = forward_layer(0, z, pos, h0, lines, bias_heads, weights, w_ada_pieces[:1] if direct else [])
-    out1, d_h1, small_a1, small_m1, scores1, keep1, send1 = both_ways(1, z, pos, h1, grad1, lines, bias_heads, weights)
-    d_middle, small_m0, keep_m0, send_m0 = backward_mlp(0, z, pos, d_h1, middle, lines, act, slope, out_branch, weights, w_ada_pieces[1:])
+    out1, d_h1, small_a1, small_m1, scores1, keep1, send1 = both_ways(1, z, pos, h1, grad1, lines, bias_heads, weights, w_ada_pieces[1:])
+    d_middle, small_m0, keep_m0, send_m0 = backward_mlp(0, z, pos, d_h1, middle, lines, act, slope, out_branch, weights, [])
     pieces = z.pieces
     rows = half * length
     other1 = swap_section(send1)
@@ -982,14 +1084,10 @@
         earlier = [table1, *low_m0, send_z1]
     else:
         earlier = [table1, *low_m0]
-    d_h0, keep_a0, send_a0, kept_small = backward_attention(
-        0, z, pos, h0, lines, qkv, probs, att, branch, d_middle, relative_bias_index,
-        (d_h1, small_m0, small_a1, small_m1, table1), weights, earlier,
-    )
-    if direct:
-        got_z1, *got_m0 = after([lax.ppermute(send_z1, "rep", pairs_of(replicas, 1)), *to_peers(low_m0, "fsdp")], [d_h0])
-        send_a0 = after([send_a0], [got_z1, *got_m0])[0]
-    other_a0 = swap_section(send_a0)
+    d_h0, small_a0, scores0, keep_a0, send_a0 = backward_attention(
+        0, z, pos, h0, lines, qkv, probs, att, branch, d_middle, d_h1, weights, earlier
+    )
+    smalls = (small_a0, small_m0, small_a1, small_m1)
     size_a = keep_a0.shape[0]
 
     def replica(value, step):
@@ -999,35 +1097,42 @@
         return jnp.where(bit == 0, jnp.concatenate([own, other]), jnp.concatenate([other, own]))
 
     if direct:
-        own_a0, own_small, *messages = plane_step(pos, keep_a0, other_a0, kept_small, conditioning, rows)
+        got_z1, *got_m0 = after([replica(send_z1, 1), *to_peers(low_m0, "fsdp")], [d_h0])
+        other_a0 = swap_section(after([send_a0], [got_z1, *got_m0])[0])
         keep_z1, send_z1 = quarter_step(pos, keep_z1, got_z1)
         keep_zm, send_zm = halve_step(pos, sums_m0[0], got_m0)
-        cond_part = cond_step(pos, after([own_small], [send_zm, send_z1])[0], w_ada_pieces, conditioning)
+        kept_small, send_small = small_step(pos, scores0, relative_bias_index, smalls, table1, [send_z1, send_zm])
+        other_small = swap_section(send_small)
+        other_a0, got_z1, got_zm = after([other_a0, replica(send_z1, 2), replica(send_zm, 1)], [kept_small])
+        own_a0, own_small, *messages = plane_step(pos, keep_a0, other_a0, kept_small, other_small, conditioning)
         got = to_peers(messages, "fsdp")
-        part0, plane_small, *messages = column_step(pos, own_a0, own_small, got, samples)
-        got_z1, got_zm = after([replica(send_z1, 2), replica(send_zm, 1)], [plane_small])
+        got_z1, got_zm = after([got_z1, got_zm], [own_small])
         quarter1 = (keep_z1 + got_z1.astype(F32)).astype(BF16)
         keep_zm, send_zm = quarter_step(pos, keep_zm, got_zm)
+        cond_part = cond_step(pos, after([own_small], [send_zm, quarter1])[0], w_ada_pieces, conditioning)
+        part0, plane_small, *messages = column_step(pos, own_a0, own_small, got, samples)
+        got_z1, got_zm = after([replica(quarter1, 2), replica(send_zm, 2)], [plane_small])
         got = to_peers(messages, "rep")
         size = part0.shape[0]
-        quarter0 = add_pieces(part0, [x[:size] for x in got]).astype(BF16)
-        got_z1, got_zm = after([replica(quarter1, 2), replica(send_zm, 2)], [quarter0])
         high, low = rank >> 1, rank & 1
-        pair1 = ordered(quarter1, got_z1, high)
-        quarter_m = (keep_zm + got_zm.astype(F32)).astype(BF16)
-        pair_m = ordered(quarter_m, replica(quarter_m, 2), high)
-        half_a0 = by_rank([quarter0] + from_peers(quarter0, "rep"), rank).reshape(-1, model)
 
         def by_low(pair):
             n = pair.shape[0] // 2
             both = ordered(pair.reshape(1, 2, n, model), replica(pair, 1).reshape(1, 2, n, model), low)
             return jnp.transpose(both, (1, 0, 2, 3)).reshape(-1, model)
 
-        half1, half_m0 = by_low(pair1), by_low(pair_m)
+        half1 = by_low(ordered(quarter1, got_z1, high))
+        quarter_m = (keep_zm + got_zm.astype(F32)).astype(BF16)
+        pair_m = ordered(quarter_m, replica(quarter_m, 2), high)
+        quarter0 = add_pieces(part0, [x[:size] for x in got]).astype(BF16)
+        half_m0 = by_low(pair_m)
+        half_a0 = by_rank([quarter0] + from_peers(quarter0, "rep"), rank).reshape(-1, model)
         g_ada, g_b_ada, summed = finish_step(pos, plane_small, got, samples, width)
         g_b_ada = g_b_ada[0]
     else:
-        theirs = other_a0[size_a + rows :].astype(F32)
+        other_a0 = swap_section(send_a0)
+        kept_small, send_small = small_step(pos, scores0, relative_bias_index, smalls, table1, [])
+        theirs = swap_section(send_small).astype(F32)
         both = kept_small + theirs
         cut = half * 8
 
@@ -1051,12 +1156,14 @@
     cond_grad = cond_part + swap_section(cond_part)
     cut = half_a0.shape[0]
     half_a1, half_m1 = half1[:cut], half1[cut:]
-    grads = unpack_mlp(in_order(mine(half_m0, half_m1), swap_section(mine(half_m1, half_m0))))
-    grads = unpack_attention(in_order(mine(half_a0, half_a1), swap_section(mine(half_a1, half_a0)))) + grads
+    grads = final_step(
+        pos, mine(half_a0, half_a1), mine(half_m0, half_m1),
+        swap_section(mine(jnp.concatenate([half_a1, half_m1]), jnp.concatenate([half_a0, half_m0]))),
+    )
     if not direct:
-        grads = [lax.psum_scatter(g, "fsdp", scatter_dimension=0, tiled=True) for g in grads]
-        grads = lax.psum(tuple(grads), "rep")
-    g_qkv, g_proj, g_fc1, g_fc2 = [g.astype(F32) for g in grads]
+        grads = [lax.psum_scatter(g.astype(BF16), "fsdp", scatter_dimension=0, tiled=True) for g in grads]
+        grads = [g.astype(F32) for g in lax.psum(tuple(grads), "rep")]
+    g_qkv, g_proj, g_fc1, g_fc2 = grads
 
     activations = in_order(
         mine(h1, out1).reshape(half, length, model), other1[keep1.shape[0] :].reshape(half, length, model)

time: 272 us -> 242 us (0.89)
  local copies, waits for them, and re-layouts: 33.6 us -> 19.1 us
  waiting for transfers between devices: 43.7 us -> 31.9 us
  other arithmetic: 26 us -> 14.9 us
  Pallas kernels: 112 us -> 121 us
    pallas_call x13 -> x17, Pallas kernels: 92.6 us -> 102 us  [call(): pl.pallas_call(kernel, out_shape=[jax.ShapeDtypeStruct(shape, dtype) for...]
    ppermute x9, waiting for transfers between devices: 19.4 us -> 10.1 us  [from_peers(): lax.ppermute(value, axis, pairs_of(lax.axis_size(axis), p))]
    unnamed x134 -> x108, local copies, waits for them, and re-layouts: 14.3 us -> 9.69 us
    ppermute x9, starting transfers between devices: 16.1 us -> 11.9 us  [from_peers(): lax.ppermute(value, axis, pairs_of(lax.axis_size(axis), p))]
    convert_element_type x4 -> x0, local copies, waits for them, and re-layouts: 4.14 us -> none  [per_device(): biases.append(bias_rows[:, at:at + cut].reshape(1, -1).astype(F32))]
    ppermute x15, waiting for transfers between devices: 6.58 us -> 10.7 us  [to_peers(): lax.ppermute(messages[p - 1], axis, pairs_of(count, p))]
    select_n x4 -> x2, other arithmetic: 3.47 us -> 0.09 us  [by_rank(): stack = jnp.where(rank & bit != 0, moved, stack)]
    convert_element_type x6 -> x0, other arithmetic: 3 us -> none  [the longest x2 1.66 us: per_device(): g_qkv, g_proj, g_fc1, g_fc2 = [g.astype(F32) for g in grads]]
  transfers between devices with their start and end apart: 49 -> 49, of which waited for: 15 -> 14; matrix products, arithmetic and copies ran while one was open for 16% -> 9% of each run, Pallas kernels for 25% -> 36%
where the time goes in v5:
time: 242 us; the launch traced here: 241 us
  Pallas kernels  121 us (50%)
  starting transfers between devices  52.7 us (22%)
  waiting for transfers between devices  31.9 us (13%)
  local copies, waits for them, and re-layouts  19.1 us (8%)
  other arithmetic  14.9 us (6%)
    pallas_call x17, Pallas kernels, call(): pl.pallas_call(kernel, out_shape=[jax.ShapeDtypeStruct(shape, dtype) for...  102 us
    ppermute x15, starting transfers between devices, to_peers(): lax.ppermute(messages[p - 1], axis, pairs_of(count, p))  18.5 us
    ppermute x8, starting transfers between devices, replica(): return lax.ppermute(value, 'rep', pairs_of(replicas, step))  12.3 us
    ppermute x9, starting transfers between devices, from_peers(): lax.ppermute(value, axis, pairs_of(lax.axis_size(axis), p))  11.9 us
    pallas_call x1, Pallas kernels, lookup(): pl.pallas_call(lookup_kernel, out_shape=jax.ShapeDtypeStruct((heads, leng...  11.2 us
    ppermute x15, waiting for transfers between devices, to_peers(): lax.ppermute(messages[p - 1], axis, pairs_of(count, p))  10.7 us
    ppermute x9, waiting for transfers between devices, from_peers(): lax.ppermute(value, axis, pairs_of(lax.axis_size(axis), p))  10.1 us
    unnamed x108, local copies, waits for them, and re-layouts  9.69 us
  transfers between devices with their start and end apart: 49, of which 14 were waited for; matrix products, arithmetic and copies ran while one was open for 9% of the time, Pallas kernels for 36%

profile of v5, /device:TPU:0, one launch (start us, length us, event | category | flops | bytes accessed | tf_op | source)
XLA Modules:
  0.0 241.1 jit_solution(8941861425371352953)
XLA Ops:
  3.1 2.3 shard_map.263.rest_0_
  5.4 2.9 %collective-permute-start.6 = (bf16[1152,384]{1,0:T(8,128)(2,1)}, bf16[1152,384]{1,0:T(8,128)(2,1)S(1)}, u32[]{:S(2)}, u32[]{:S(2)}) collective-permute-start(bf16[1152,384]{1,0:T(8,128)(2,1)} %shard_map.263.rest_0_), channel_id=1, source_target_pairs={{0,4},{4,0},{8,12},{12,8},{1,5},{5,1},{9,13},{13,9},{2,6},{6,2},{1... | collective-permute-start | bytes 2654216 | tf_op jit(solution)/shard_map/ppermute | solution.py:1034
  12.9 11.2 %shard_map.264.rest_0_.own_bias = bf16[6,256,256]{2,1,0:T(8,128)(2,1)} custom-call(bf16[128,64]{1,0:T(8,128)(2,1)} %bitcast.85, s32[256,256]{1,0:T(8,128)} %index.5, bf16[1152,384]{1,0:T(8,128)(2,1)} %shard_map.263.rest_0_, bf16[512,384]{1,0:T(8,128)(2,1)} %bitcast.69, bf16[512,384]{1,0:T(8,128)(2,1)} %bitcast.72), custom_call_target="tpu_custom_call" | custom-call | flops 11000000512 | tf_op jit(solution)/shard_map/pallas_call | solution.py:916
  24.7 3.6 %collective-permute-done.cond_b = bf16[4,384]{1,0:T(4,128)(2,1)S(1)} collective-permute-done((bf16[4,384]{1,0:T(4,128)(2,1)S(1)}, bf16[4,384]{1,0:T(4,128)(2,1)S(1)}, u32[]{:S(2)}, u32[]{:S(2)}) %collective-permute-start) | collective-permute-done | bytes 3104 | tf_op jit(solution)/shard_map/ppermute | solution.py:993
  28.3 2.7 %collective-permute-start.2 = (bf16[4,384]{1,0:T(4,128)(2,1)S(1)}, bf16[4,384]{1,0:T(4,128)(2,1)S(1)}, u32[]{:S(2)}, u32[]{:S(2)}) collective-permute-start(bf16[4,384]{1,0:T(4,128)(2,1)S(1)} %copy-done.49), channel_id=1, source_target_pairs={{0,12},{4,8},{8,4},{12,0},{1,13},{5,9},{9,5},{13,1},{2,14},{6,10},... | collective-permute-start | bytes 9224 | tf_op jit(solution)/shard_map/ppermute | solution.py:993
  33.4 3.4 %shard_map.265 = (f32[4,3072]{1,0:T(4,128)}, f32[4,3072]{1,0:T(4,128)}, f32[4,3072]{1,0:T(4,128)}, f32[4,3072]{1,0:T(4,128)}) custom-call(s32[3]{0:T(128)} %pad_add_fusion.pos, bf16[96,2304]{1,0:T(8,128)(2,1)} %bitcast.61, bf16[4,384]{1,0:T(4,128)(2,1)} %cond.3, bf16[4,384]{1,0:T(4,128)(2,1)} %copy-done.50, bf16[4,384]{1,0:T(4,128)(2,1)} %copy-done.51, ...), custom_call_target="tpu_custom_call" | custom-call | flops 2000000000 | tf_op jit(solution)/shard_map/pallas_call | solution.py:529
  36.8 2.1 collective-permute-start.3
  46.5 7.4 %collective-permute-done.10.refs_1_.rest_3_ = bf16[576,384]{1,0:T(8,128)(2,1)S(1)} collective-permute-done((bf16[576,384]{1,0:T(8,128)(2,1)S(1)}, bf16[576,384]{1,0:T(8,128)(2,1)S(1)}, u32[]{:S(2)}, u32[]{:S(2)}) %collective-permute-start.10) | collective-permute-done | bytes 442400 | tf_op jit(solution)/shard_map/ppermute | solution.py:1038
  61.6 15.1 %shard_map.269 = (bf16[512,1152]{1,0:T(8,128)(2,1)}, bf16[2,6,256,256]{3,2,1,0:T(8,128)(2,1)}, bf16[512,384]{1,0:T(8,128)(2,1)}, f32[512,384]{1,0:T(8,128)}, f32...) custom-call(s32[3]{0:T(128)} %pad_add_fusion.pos, ...), custom_call_target="tpu_custom_call" | custom-call | flops 15000000512 | tf_op jit(solution)/shard_map/pallas_call | solution.py:529
  76.8 4.7 %collective-permute-done.18.rest_11_.rest_2_ = bf16[96,2304]{1,0:T(8,128)(2,1)S(1)} collective-permute-done((bf16[96,2304]{1,0:T(8,128)(2,1)}, bf16[96,2304]{1,0:T(8,128)(2,1)S(1)}, u32[]{:S(2)}, u32[]{:S(2)}) %collective-permute-start.18) | collective-permute-done | bytes 442400 | tf_op jit(solution)/shard_map/ppermute | solution.py:993
  82.4 26.1 %shard_map.270 = (bf16[512,384]{1,0:T(8,128)(2,1)}, bf16[512,384]{1,0:T(8,128)(2,1)}, f32[2,8,384]{2,1,0:T(8,128)}, f32[2,8,384]{2,1,0:T(8,128)}, bf16[6,256,256...) custom-call(s32[3]{0:T(128)} %pad_add_fusion.pos, bf16[512,384]{1,0:T(8,128)(2,1)} %get-tuple-element.98.h, ...), custom_call_target="tpu_custom_call" | custom-call | flops 24999999488 | tf_op jit(solution)/shard_map/pallas_call | solution.py:529
  108.6 12.1 %shard_map.271 = (f32[512,384]{1,0:T(8,128)}, f32[2,8,384]{2,1,0:T(8,128)}, bf16[1536,384]{1,0:T(8,128)(2,1)}, bf16[1536,384]{1,0:T(8,128)(2,1)}) custom-call(s32[3]{0:T(128)} %pad_add_fusion.pos, bf16[512,384]{1,0:T(8,128)(2,1)} %get-tuple-element.105.grad.d_h1, f32[512,384]{1,0:T(8,128)} %get-tuple-element.106.middle, ...), custom_call_target="tpu_custom_call" | custom-call | flops 12000000000 | tf_op jit(solution)/shard_map/pallas_call | solution.py:529
  127.1 7.6 %shard_map.272.refs_1_.refs_3_.rest_10_.table1 = f32[16,384]{1,0:T(8,128)} custom-call(bf16[6,256,256]{2,1,0:T(8,128)(2,1)} %get-tuple-element.111.scores, s32[256,256]{1,0:T(8,128)} %index.5, bf16[576,384]{1,0:T(8,128)(2,1)} %get-tuple-element.181.rest_0_, bf16[576,384]{1,0:T(8,128)(2,1)} %get-tuple-element.180.rest_1_, ...), custom_call_target="tpu_custom_call" | custom-call | flops 8000000000 | tf_op jit(solution)/shard_map/pallas_call | solution.py:337
  135.8 2.7 %convert_add_fusion.1 = (f32[384,384]{1,0:T(8,128)}, bf16[384,384]{1,0:T(8,128)(2,1)S(1)}, bf16[384,384]{1,0:T(8,128)(2,1)S(1)}, bf16[384,384]{1,0:T(8,128)(2,1)S(1)}) fusion(bf16[1536,384]{1,0:T(8,128)(2,1)} %shard_map.273, bf16[1536,384]{1,0:T(8,128)(2,1)} %get-tuple-element.113), kind=kLoop, calls=%fused_computation.7 | loop fusion | flops 2211840 | bytes 3833856 | tf_op jit(solution)/shard_map/add | solution.py:949
  143.2 2.3 collective-permute-done.23.refs_1_
  146.5 2.6 %shard_map.275 = (f32[288,384]{1,0:T(8,128)}, bf16[288,384]{1,0:T(8,128)(2,1)}) custom-call(s32[3]{0:T(128)} %pad_add_fusion.pos, f32[576,384]{1,0:T(8,128)} %get-tuple-element.178.own, bf16[576,384]{1,0:T(8,128)(2,1)} %get-tuple-element.115.got_a, bf16[576,384]{1,0:T(8,128)(2,1)} %get-tuple-element.116.got_b, bf16[576,384]{1,0:T(8,128)(2,1)} %get-tuple-element.117.got_c), custom_call_target="tpu_custom_call" | custom-call | flops 2000000000 | tf_op jit(solution)/shard_map/pallas_call | solution.py:529
  150.6 12.6 %shard_map.276 = (f32[512,384]{1,0:T(8,128)}, f32[2,8,384]{2,1,0:T(8,128)}, bf16[6,256,256]{2,1,0:T(8,128)(2,1)}, bf16[768,384]{1,0:T(8,128)(2,1)}, bf16[1280,384]{1,0:T(8,128)(2,1)}) custom-call(s32[3]{0:T(128)} %pad_add_fusion.pos, bf16[512,384]{1,0:T(8,128)(2,1)} %bitcast.71, f32[1,7680]{1,0:T(1,128)} %get-tuple-element.96.own_line, ...), custom_call_target="tpu_custom_call" | custom-call | flops 12999999488 | tf_op jit(solution)/shard_map/pallas_call | solution.py:529
  164.1 2.2 shard_map.280
  168.6 2.6 %collective-permute-start.30 = (bf16[144,384]{1,0:T(8,128)(2,1)}, bf16[144,384]{1,0:T(8,128)(2,1)S(1)}, u32[]{:S(2)}, u32[]{:S(2)}) collective-permute-start(bf16[144,384]{1,0:T(8,128)(2,1)} %get-tuple-element.126.rest_0_), channel_id=1, source_target_pairs={{0,2},{1,3},{2,0},{3,1},{4,6},{5,7},{6,4},{7,5},{8,10},{9,11},{10,... | collective-permute-start | bytes 331784 | tf_op jit(solution)/shard_map/ppermute | solution.py:1094
  171.2 8.1 %shard_map.281 = (f32[48,384]{1,0:T(8,128)}, bf16[48,384]{1,0:T(8,128)(2,1)}) custom-call(s32[3]{0:T(128)} %pad_add_fusion.pos, bf16[6,256,256]{2,1,0:T(8,128)(2,1)} %get-tuple-element.128.scores, s32[256,256]{1,0:T(8,128)} %index.5, f32[2,8,384]{2,1,0:T(8,128)} %get-tuple-element.129.small_a0, f32[2,8,384]{2,1,0:T(8,128)} %get-tuple-element.130.small_m0, ...), custom_call_target="tpu_custom_call" | custom-call | flops 8000000000 | tf_op jit(solution)/shard_map/pallas_call | solution.py:529
  182.6 2.4 %shard_map.283 = (f32[192,384]{1,0:T(8,128)}, bf16[64,384]{1,0:T(8,128)(2,1)}, bf16[256,384]{1,0:T(8,128)(2,1)}, bf16[256,384]{1,0:T(8,128)(2,1)}, bf16[256,384]{1,0:T(8,128)(2,1)}) custom-call(s32[3]{0:T(128)} %pad_add_fusion.pos, bf16[768,384]{1,0:T(8,128)(2,1)} %get-tuple-element.135.keep, bf16[1280,384]{1,0:T(8,128)(2,1)} %get-tuple-element.134.other, ...), custom_call_target="tpu_custom_call" | custom-call | flops 2000000000 | tf_op jit(solution)/shard_map/pallas_call | solution.py:529
  191.6 2.6 %collective-permute-start.44 = (bf16[96,384]{1,0:T(8,128)(2,1)}, bf16[96,384]{1,0:T(8,128)(2,1)S(1)}, u32[]{:S(2)}, u32[]{:S(2)}) collective-permute-start(bf16[96,384]{1,0:T(8,128)(2,1)} %get-tuple-element.142.refs_1_), channel_id=1, source_target_pairs={{0,2},{1,3},{2,0},{3,1},{4,6},{5,7},{6,4},{7,5},{8,10},{9,11},{10,... | collective-permute-start | bytes 221192 | tf_op jit(solution)/shard_map/ppermute | solution.py:1094
  195.5 3.1 %collective-permute-done.35.got_b = bf16[256,384]{1,0:T(8,128)(2,1)S(1)} collective-permute-done((bf16[256,384]{1,0:T(8,128)(2,1)}, bf16[256,384]{1,0:T(8,128)(2,1)S(1)}, u32[]{:S(2)}, u32[]{:S(2)}) %collective-permute-start.35) | collective-permute-done | bytes 196640 | tf_op jit(solution)/shard_map/ppermute | solution.py:960
  199.3 2.1 shard_map.288
  203.0 2.6 %collective-permute-start.46 = (bf16[96,384]{1,0:T(8,128)(2,1)S(1)}, bf16[96,384]{1,0:T(8,128)(2,1)S(1)}, u32[]{:S(2)}, u32[]{:S(2)}) collective-permute-start(bf16[96,384]{1,0:T(8,128)(2,1)S(1)} %add_convert_fusion.7), channel_id=1, source_target_pairs={{0,2},{1,3},{2,0},{3,1},{4,6},{5,7},{6,4},{7,5},{8,10},{9,11},{10,... | collective-permute-start | bytes 221192 | tf_op jit(solution)/shard_map/ppermute | solution.py:1094
  207.6 2.4 %collective-permute-start.39 = (bf16[192,384]{1,0:T(8,128)(2,1)}, bf16[192,384]{1,0:T(8,128)(2,1)S(1)}, u32[]{:S(2)}, u32[]{:S(2)}) collective-permute-start(bf16[192,384]{1,0:T(8,128)(2,1)} %get-tuple-element.152), channel_id=1, source_target_pairs={{0,3},{1,2},{2,1},{3,0},{4,7},{5,6},{6,5},{7,4},{8,11},{9,10},{10,... | collective-permute-start | bytes 442376 | tf_op jit(solution)/shard_map/ppermute | solution.py:960
  210.0 2.8 %shard_map.287 = f32[4,384]{1,0:T(4,128)} custom-call(s32[3]{0:T(128)} %pad_add_fusion.pos, bf16[64,384]{1,0:T(8,128)(2,1)} %shard_map.286.small, bf16[4,384]{1,0:T(4,128)(2,1)} %cond.3, bf16[96,2304]{1,0:T(8,128)(2,1)} %shard_map.268.rest_10_.rest_0_, bf16[96,2304]{1,0:T(8,128)(2,1)} %copy-done.39, bf16[96,2304]{1,0:T(8,128)(2,1)} %copy-done.40, ...), custom_call_target="tpu_custom_call" | custom-call | flops 2000000000 | tf_op jit(solution)/shard_map/pallas_call | solution.py:529
  217.6 2.3 collective-permute-done.38.got_b
  219.9 2.7 %collective-permute-start.40 = (bf16[48,384]{1,0:T(8,128)(2,1)S(1)}, bf16[48,384]{1,0:T(8,128)(2,1)S(1)}, u32[]{:S(2)}, u32[]{:S(2)}) collective-permute-start(bf16[48,384]{1,0:T(8,128)(2,1)S(1)} %add_convert_fusion.8), channel_id=1, source_target_pairs={{0,1},{1,0},{2,3},{3,2},{4,5},{5,4},{6,7},{7,6},{8,9},{9,8},{10,11... | collective-permute-start | bytes 110600 | tf_op jit(solution)/shard_map/ppermute | solution.py:993
  222.6 2.5 %collective-permute-start.41 = (bf16[48,384]{1,0:T(8,128)(2,1)S(1)}, bf16[48,384]{1,0:T(8,128)(2,1)S(1)}, u32[]{:S(2)}, u32[]{:S(2)}) collective-permute-start(bf16[48,384]{1,0:T(8,128)(2,1)S(1)} %add_convert_fusion.8), channel_id=1, source_target_pairs={{0,3},{1,2},{2,1},{3,0},{4,7},{5,6},{6,5},{7,4},{8,11},{9,10},{10,... | collective-permute-start | bytes 110600 | tf_op jit(solution)/shard_map/ppermute | solution.py:993
  225.1 2.8 %shard_map.289 = (f32[96,2304]{1,0:T(8,128)}, f32[1,2304]{1,0:T(1,128)}, f32[24,384]{1,0:T(8,128)}) custom-call(s32[3]{0:T(128)} %pad_add_fusion.pos, bf16[144,384]{1,0:T(8,128)(2,1)} %get-tuple-element.149.own_small.refs_2_, bf16[192,384]{1,0:T(8,128)(2,1)} %copy-done.35, bf16[192,384]{1,0:T(8,128)(2,1)} %copy-done.36, bf16[192,384]{1,0:T(8,128)(2,1)} %copy-done.37), custom_call_target="tpu_custom_call" | custom-call | flops 2000000000 | tf_op jit(solution)/shard_map/pallas_call | solution.py:529
  238.6 2.5 %shard_map.291 = (f32[96,1152]{1,0:T(8,128)}, f32[96,384]{1,0:T(8,128)}, f32[96,1536]{1,0:T(8,128)}, f32[384,384]{1,0:T(8,128)}) custom-call(s32[3]{0:T(128)} %pad_add_fusion.pos, bf16[192,384]{1,0:T(8,128)(2,1)} %slice_select_fusion.1.own_a, bf16[384,384]{1,0:T(8,128)(2,1)} %slice_select_fusion.own_m, bf16[576,384]{1,0:T(8,128)(2,1)} %copy-done.43), custom_call_target="tpu_custom_call" | custom-call | flops 2000000000 | tf_op jit(solution)/shard_map/pallas_call | solution.py:529
  (251 shorter events, 74.6 us)
Async XLA Ops:
  5.4 34.9 %collective-permute-start.6 = (bf16[1152,384]{1,0:T(8,128)(2,1)}, bf16[1152,384]{1,0:T(8,128)(2,1)S(1)}, u32[]{:S(2)}, u32[]{:S(2)}) collective-permute-start(bf16[1152,384]{1,0:T(8,128)(2,1)} %shard_map.263.rest_0_), channel_id=1, source_target_pairs={{0,4},{4,0},{8,12},{12,8},{1,5},{5,1},{9,13},{13,9},{2,6},{6,2},{1... | collective-permute-start | bytes 2654216 | tf_op jit(solution)/shard_map/ppermute | solution.py:1034
  8.4 32.0 %collective-permute-start.7 = (bf16[1152,384]{1,0:T(8,128)(2,1)}, bf16[1152,384]{1,0:T(8,128)(2,1)S(1)}, u32[]{:S(2)}, u32[]{:S(2)}) collective-permute-start(bf16[1152,384]{1,0:T(8,128)(2,1)} %shard_map.263.rest_0_), channel_id=1, source_target_pairs={{0,8},{4,12},{8,0},{12,4},{1,9},{5,13},{9,1},{13,5},{2,10},{6,14},... | collective-permute-start | bytes 2654216 | tf_op jit(solution)/shard_map/ppermute | solution.py:1035
  24.1 21.8 %collective-permute-start.9 = (bf16[6,256,256]{2,1,0:T(8,128)(2,1)}, bf16[6,256,256]{2,1,0:T(8,128)(2,1)S(1)}, u32[]{:S(2)}, u32[]{:S(2)}) collective-permute-start(bf16[6,256,256]{2,1,0:T(8,128)(2,1)} %shard_map.264.rest_0_.own_bias), channel_id=1, source_target_pairs={{0,16},{16,0},{1,17},{17,1},{2,18},{18,2},{3,19},{19,3},{4,20},{20... | collective-permute-start | bytes 2359304 | tf_op jit(solution)/shard_map/ppermute | solution.py:928
  40.4 16.2 %collective-permute-start.12 = (bf16[1152,384]{1,0:T(8,128)(2,1)}, bf16[1152,384]{1,0:T(8,128)(2,1)}, u32[]{:S(2)}, u32[]{:S(2)}) collective-permute-start(bf16[1152,384]{1,0:T(8,128)(2,1)} %shard_map.263.rest_0_), channel_id=1, source_target_pairs={{0,16},{16,0},{1,17},{17,1},{2,18},{18,2},{3,19},{19,3},{4,20},{20... | collective-permute-start | bytes 2654216 | tf_op jit(solution)/shard_map/ppermute | solution.py:928
  41.4 12.5 %collective-permute-start.10 = (bf16[576,384]{1,0:T(8,128)(2,1)S(1)}, bf16[576,384]{1,0:T(8,128)(2,1)S(1)}, u32[]{:S(2)}, u32[]{:S(2)}) collective-permute-start(bf16[576,384]{1,0:T(8,128)(2,1)S(1)} %slice.142), channel_id=1, source_target_pairs={{0,8},{4,12},{8,0},{12,4},{1,9},{5,13},{9,1},{13,5},{2,10},{6,14},... | collective-permute-start | bytes 1327112 | tf_op jit(solution)/shard_map/ppermute | solution.py:1038
  43.2 11.7 %collective-permute-start.11 = (bf16[576,384]{1,0:T(8,128)(2,1)S(1)}, bf16[576,384]{1,0:T(8,128)(2,1)S(1)}, u32[]{:S(2)}, u32[]{:S(2)}) collective-permute-start(bf16[576,384]{1,0:T(8,128)(2,1)S(1)} %slice.143), channel_id=1, source_target_pairs={{0,4},{4,0},{8,12},{12,8},{1,5},{5,1},{9,13},{13,9},{2,6},{6,2},{1... | collective-permute-start | bytes 1327112 | tf_op jit(solution)/shard_map/ppermute | solution.py:1039
  46.0 15.6 %collective-permute-start.13 = (bf16[1152,384]{1,0:T(8,128)(2,1)S(1)}, bf16[1152,384]{1,0:T(8,128)(2,1)}, u32[]{:S(2)}, u32[]{:S(2)}) collective-permute-start(bf16[1152,384]{1,0:T(8,128)(2,1)S(1)} %collective-permute-done.6.refs_3_.rest_1_), channel_id=1, source_target_pairs={{0,16},{16,0},{1,17},{17,1},{2,18},{18,2},{3,19},{19,3},{4,20},{20... | collective-permute-start | bytes 2654216 | tf_op jit(solution)/shard_map/ppermute | solution.py:928
  46.0 15.6 %collective-permute-start.14 = (bf16[1152,384]{1,0:T(8,128)(2,1)S(1)}, bf16[1152,384]{1,0:T(8,128)(2,1)}, u32[]{:S(2)}, u32[]{:S(2)}) collective-permute-start(bf16[1152,384]{1,0:T(8,128)(2,1)S(1)} %collective-permute-done.7.refs_4_.rest_2_), channel_id=1, source_target_pairs={{0,16},{16,0},{1,17},{17,1},{2,18},{18,2},{3,19},{19,3},{4,20},{20... | collective-permute-start | bytes 2654216 | tf_op jit(solution)/shard_map/ppermute | solution.py:928
  58.1 18.6 %collective-permute-start.17 = (bf16[96,2304]{1,0:T(8,128)(2,1)}, bf16[96,2304]{1,0:T(8,128)(2,1)S(1)}, u32[]{:S(2)}, u32[]{:S(2)}) collective-permute-start(bf16[96,2304]{1,0:T(8,128)(2,1)} %shard_map.268.rest_10_.rest_0_), channel_id=1, source_target_pairs={{0,4},{4,0},{8,12},{12,8},{1,5},{5,1},{9,13},{13,9},{2,6},{6,2},{1... | collective-permute-start | bytes 1327112 | tf_op jit(solution)/shard_map/ppermute | solution.py:993
  59.6 21.8 %collective-permute-start.18 = (bf16[96,2304]{1,0:T(8,128)(2,1)}, bf16[96,2304]{1,0:T(8,128)(2,1)S(1)}, u32[]{:S(2)}, u32[]{:S(2)}) collective-permute-start(bf16[96,2304]{1,0:T(8,128)(2,1)} %shard_map.268.rest_10_.rest_0_), channel_id=1, source_target_pairs={{0,8},{4,12},{8,0},{12,4},{1,9},{5,13},{9,1},{13,5},{2,10},{6,14},... | collective-permute-start | bytes 1327112 | tf_op jit(solution)/shard_map/ppermute | solution.py:993
  60.3 21.1 %collective-permute-start.19 = (bf16[96,2304]{1,0:T(8,128)(2,1)}, bf16[96,2304]{1,0:T(8,128)(2,1)S(1)}, u32[]{:S(2)}, u32[]{:S(2)}) collective-permute-start(bf16[96,2304]{1,0:T(8,128)(2,1)} %shard_map.268.rest_10_.rest_0_), channel_id=1, source_target_pairs={{0,12},{4,8},{8,4},{12,0},{1,13},{5,9},{9,5},{13,1},{2,14},{6,10},... | collective-permute-start | bytes 1327112 | tf_op jit(solution)/shard_map/ppermute | solution.py:993
  108.5 13.5 %collective-permute-start.20 = (bf16[2816,384]{1,0:T(8,128)(2,1)}, bf16[2816,384]{1,0:T(8,128)(2,1)S(1)}, u32[]{:S(2)}, u32[]{:S(2)}) collective-permute-start(bf16[2816,384]{1,0:T(8,128)(2,1)} %get-tuple-element.100), channel_id=1, source_target_pairs={{0,16},{16,0},{1,17},{17,1},{2,18},{18,2},{3,19},{19,3},{4,20},{20... | collective-permute-start | bytes 6488072 | tf_op jit(solution)/shard_map/ppermute | solution.py:928
  120.7 14.1 %collective-permute-start.21 = (bf16[1536,384]{1,0:T(8,128)(2,1)}, bf16[1536,384]{1,0:T(8,128)(2,1)S(1)}, u32[]{:S(2)}, u32[]{:S(2)}) collective-permute-start(bf16[1536,384]{1,0:T(8,128)(2,1)} %get-tuple-element.114), channel_id=1, source_target_pairs={{0,16},{16,0},{1,17},{17,1},{2,18},{18,2},{3,19},{19,3},{4,20},{20... | collective-permute-start | bytes 3538952 | tf_op jit(solution)/shard_map/ppermute | solution.py:928
  123.6 17.6 %collective-permute-start.22 = (bf16[576,384]{1,0:T(8,128)(2,1)}, bf16[576,384]{1,0:T(8,128)(2,1)}, u32[]{:S(2)}, u32[]{:S(2)}) collective-permute-start(bf16[576,384]{1,0:T(8,128)(2,1)} %get-tuple-element.181.rest_0_), channel_id=1, source_target_pairs={{0,4},{4,0},{8,12},{12,8},{1,5},{5,1},{9,13},{13,9},{2,6},{6,2},{1... | collective-permute-start | bytes 1327112 | tf_op jit(solution)/shard_map/ppermute | solution.py:960
  124.2 21.3 %collective-permute-start.23 = (bf16[576,384]{1,0:T(8,128)(2,1)}, bf16[576,384]{1,0:T(8,128)(2,1)}, u32[]{:S(2)}, u32[]{:S(2)}) collective-permute-start(bf16[576,384]{1,0:T(8,128)(2,1)} %get-tuple-element.180.rest_1_), channel_id=1, source_target_pairs={{0,8},{4,12},{8,0},{12,4},{1,9},{5,13},{9,1},{13,5},{2,10},{6,14},... | collective-permute-start | bytes 1327112 | tf_op jit(solution)/shard_map/ppermute | solution.py:960
  125.2 21.2 %collective-permute-start.24 = (bf16[576,384]{1,0:T(8,128)(2,1)}, bf16[576,384]{1,0:T(8,128)(2,1)}, u32[]{:S(2)}, u32[]{:S(2)}) collective-permute-start(bf16[576,384]{1,0:T(8,128)(2,1)} %get-tuple-element.179.rest_2_), channel_id=1, source_target_pairs={{0,12},{4,8},{8,4},{12,0},{1,13},{5,9},{9,5},{13,1},{2,14},{6,10},... | collective-permute-start | bytes 1327112 | tf_op jit(solution)/shard_map/ppermute | solution.py:960
  138.6 24.6 %collective-permute-start.26 = (bf16[384,384]{1,0:T(8,128)(2,1)S(1)}, bf16[384,384]{1,0:T(8,128)(2,1)S(1)}, u32[]{:S(2)}, u32[]{:S(2)}) collective-permute-start(bf16[384,384]{1,0:T(8,128)(2,1)S(1)} %get-tuple-element.185.refs_4_.rest_11_), channel_id=1, source_target_pairs={{0,4},{4,0},{8,12},{12,8},{1,5},{5,1},{9,13},{13,9},{2,6},{6,2},{1... | collective-permute-start | bytes 884744 | tf_op jit(solution)/shard_map/ppermute | solution.py:960
  139.1 24.1 %collective-permute-start.27 = (bf16[384,384]{1,0:T(8,128)(2,1)S(1)}, bf16[384,384]{1,0:T(8,128)(2,1)}, u32[]{:S(2)}, u32[]{:S(2)}) collective-permute-start(bf16[384,384]{1,0:T(8,128)(2,1)S(1)} %get-tuple-element.184.refs_5_.rest_12_), channel_id=1, source_target_pairs={{0,8},{4,12},{8,0},{12,4},{1,9},{5,13},{9,1},{13,5},{2,10},{6,14},... | collective-permute-start | bytes 884744 | tf_op jit(solution)/shard_map/ppermute | solution.py:960
  141.3 22.0 %collective-permute-start.28 = (bf16[384,384]{1,0:T(8,128)(2,1)S(1)}, bf16[384,384]{1,0:T(8,128)(2,1)S(1)}, u32[]{:S(2)}, u32[]{:S(2)}) collective-permute-start(bf16[384,384]{1,0:T(8,128)(2,1)S(1)} %get-tuple-element.183.refs_6_.rest_13_), channel_id=1, source_target_pairs={{0,12},{4,8},{8,4},{12,0},{1,13},{5,9},{9,5},{13,1},{2,14},{6,10},... | collective-permute-start | bytes 884744 | tf_op jit(solution)/shard_map/ppermute | solution.py:960
  149.0 14.2 %collective-permute-start.25 = (bf16[288,384]{1,0:T(8,128)(2,1)}, bf16[288,384]{1,0:T(8,128)(2,1)S(1)}, u32[]{:S(2)}, u32[]{:S(2)}) collective-permute-start(bf16[288,384]{1,0:T(8,128)(2,1)} %get-tuple-element.118.rest_14_), channel_id=1, source_target_pairs={{0,1},{1,0},{2,3},{3,2},{4,5},{5,4},{6,7},{7,6},{8,9},{9,8},{10,11... | collective-permute-start | bytes 663560 | tf_op jit(solution)/shard_map/ppermute | solution.py:1094
  166.3 13.6 %collective-permute-start.31 = (bf16[192,384]{1,0:T(8,128)(2,1)}, bf16[192,384]{1,0:T(8,128)(2,1)S(1)}, u32[]{:S(2)}, u32[]{:S(2)}) collective-permute-start(bf16[192,384]{1,0:T(8,128)(2,1)} %get-tuple-element.127.rest_1_), channel_id=1, source_target_pairs={{0,1},{1,0},{2,3},{3,2},{4,5},{5,4},{6,7},{7,6},{8,9},{9,8},{10,11... | collective-permute-start | bytes 442376 | tf_op jit(solution)/shard_map/ppermute | solution.py:1094
  168.6 11.3 %collective-permute-start.30 = (bf16[144,384]{1,0:T(8,128)(2,1)}, bf16[144,384]{1,0:T(8,128)(2,1)S(1)}, u32[]{:S(2)}, u32[]{:S(2)}) collective-permute-start(bf16[144,384]{1,0:T(8,128)(2,1)} %get-tuple-element.126.rest_0_), channel_id=1, source_target_pairs={{0,2},{1,3},{2,0},{3,1},{4,6},{5,7},{6,4},{7,5},{8,10},{9,11},{10,... | collective-permute-start | bytes 331784 | tf_op jit(solution)/shard_map/ppermute | solution.py:1094
  185.9 15.5 %collective-permute-start.43 = (bf16[144,384]{1,0:T(8,128)(2,1)S(1)}, bf16[144,384]{1,0:T(8,128)(2,1)S(1)}, u32[]{:S(2)}, u32[]{:S(2)}) collective-permute-start(bf16[144,384]{1,0:T(8,128)(2,1)S(1)} %add_convert_fusion.6.refs_2_), channel_id=1, source_target_pairs={{0,2},{1,3},{2,0},{3,1},{4,6},{5,7},{6,4},{7,5},{8,10},{9,11},{10,... | collective-permute-start | bytes 331784 | tf_op jit(solution)/shard_map/ppermute | solution.py:1094
  187.8 10.7 %collective-permute-start.35 = (bf16[256,384]{1,0:T(8,128)(2,1)}, bf16[256,384]{1,0:T(8,128)(2,1)S(1)}, u32[]{:S(2)}, u32[]{:S(2)}) collective-permute-start(bf16[256,384]{1,0:T(8,128)(2,1)} %get-tuple-element.147), channel_id=1, source_target_pairs={{0,8},{4,12},{8,0},{12,4},{1,9},{5,13},{9,1},{13,5},{2,10},{6,14},... | collective-permute-start | bytes 589832 | tf_op jit(solution)/shard_map/ppermute | solution.py:960
  203.0 13.2 %collective-permute-start.46 = (bf16[96,384]{1,0:T(8,128)(2,1)S(1)}, bf16[96,384]{1,0:T(8,128)(2,1)S(1)}, u32[]{:S(2)}, u32[]{:S(2)}) collective-permute-start(bf16[96,384]{1,0:T(8,128)(2,1)S(1)} %add_convert_fusion.7), channel_id=1, source_target_pairs={{0,2},{1,3},{2,0},{3,1},{4,6},{5,7},{6,4},{7,5},{8,10},{9,11},{10,... | collective-permute-start | bytes 221192 | tf_op jit(solution)/shard_map/ppermute | solution.py:1094
  205.6 12.0 %collective-permute-start.37 = (bf16[192,384]{1,0:T(8,128)(2,1)}, bf16[192,384]{1,0:T(8,128)(2,1)S(1)}, u32[]{:S(2)}, u32[]{:S(2)}) collective-permute-start(bf16[192,384]{1,0:T(8,128)(2,1)} %get-tuple-element.150), channel_id=1, source_target_pairs={{0,1},{1,0},{2,3},{3,2},{4,5},{5,4},{6,7},{7,6},{8,9},{9,8},{10,11... | collective-permute-start | bytes 442376 | tf_op jit(solution)/shard_map/ppermute | solution.py:960
  207.2 12.7 %collective-permute-start.38 = (bf16[192,384]{1,0:T(8,128)(2,1)}, bf16[192,384]{1,0:T(8,128)(2,1)S(1)}, u32[]{:S(2)}, u32[]{:S(2)}) collective-permute-start(bf16[192,384]{1,0:T(8,128)(2,1)} %get-tuple-element.151), channel_id=1, source_target_pairs={{0,2},{1,3},{2,0},{3,1},{4,6},{5,7},{6,4},{7,5},{8,10},{9,11},{10,... | collective-permute-start | bytes 442376 | tf_op jit(solution)/shard_map/ppermute | solution.py:960
  207.6 12.3 %collective-permute-start.39 = (bf16[192,384]{1,0:T(8,128)(2,1)}, bf16[192,384]{1,0:T(8,128)(2,1)S(1)}, u32[]{:S(2)}, u32[]{:S(2)}) collective-permute-start(bf16[192,384]{1,0:T(8,128)(2,1)} %get-tuple-element.152), channel_id=1, source_target_pairs={{0,3},{1,2},{2,1},{3,0},{4,7},{5,6},{6,5},{7,4},{8,11},{9,10},{10,... | collective-permute-start | bytes 442376 | tf_op jit(solution)/shard_map/ppermute | solution.py:960
  214.2 21.5 %collective-permute-start.45 = (bf16[288,384]{1,0:T(8,128)(2,1)S(1)}, bf16[288,384]{1,0:T(8,128)(2,1)S(1)}, u32[]{:S(2)}, u32[]{:S(2)}) collective-permute-start(bf16[288,384]{1,0:T(8,128)(2,1)S(1)} %maximum_select_fusion.5), channel_id=1, source_target_pairs={{0,1},{1,0},{2,3},{3,2},{4,5},{5,4},{6,7},{7,6},{8,9},{9,8},{10,11... | collective-permute-start | bytes 663560 | tf_op jit(solution)/shard_map/ppermute | solution.py:1094
  216.2 19.4 %collective-permute-start.47 = (bf16[192,384]{1,0:T(8,128)(2,1)S(1)}, bf16[192,384]{1,0:T(8,128)(2,1)S(1)}, u32[]{:S(2)}, u32[]{:S(2)}) collective-permute-start(bf16[192,384]{1,0:T(8,128)(2,1)S(1)} %maximum_select_fusion.8), channel_id=1, source_target_pairs={{0,1},{1,0},{2,3},{3,2},{4,5},{5,4},{6,7},{7,6},{8,9},{9,8},{10,11... | collective-permute-start | bytes 442376 | tf_op jit(solution)/shard_map/ppermute | solution.py:1094
  219.9 15.6 %collective-permute-start.40 = (bf16[48,384]{1,0:T(8,128)(2,1)S(1)}, bf16[48,384]{1,0:T(8,128)(2,1)S(1)}, u32[]{:S(2)}, u32[]{:S(2)}) collective-permute-start(bf16[48,384]{1,0:T(8,128)(2,1)S(1)} %add_convert_fusion.8), channel_id=1, source_target_pairs={{0,1},{1,0},{2,3},{3,2},{4,5},{5,4},{6,7},{7,6},{8,9},{9,8},{10,11... | collective-permute-start | bytes 110600 | tf_op jit(solution)/shard_map/ppermute | solution.py:993
  222.6 12.9 %collective-permute-start.41 = (bf16[48,384]{1,0:T(8,128)(2,1)S(1)}, bf16[48,384]{1,0:T(8,128)(2,1)S(1)}, u32[]{:S(2)}, u32[]{:S(2)}) collective-permute-start(bf16[48,384]{1,0:T(8,128)(2,1)S(1)} %add_convert_fusion.8), channel_id=1, source_target_pairs={{0,3},{1,2},{2,1},{3,0},{4,7},{5,6},{6,5},{7,4},{8,11},{9,10},{10,... | collective-permute-start | bytes 110600 | tf_op jit(solution)/shard_map/ppermute | solution.py:993
  (70 other events, 386.1 us)

commit v6 on v5

--- a/solution.py
+++ b/solution.py
@@ -306,15 +306,16 @@
     lax.fori_loop(0, count, step, 0)
 
 
-def add_table(scores, index, out):
-    heads, length = scores.shape[0], scores.shape[1]
+def add_tables(all_scores, index, outs):
+    heads, length = all_scores[0].shape[0], all_scores[0].shape[1]
     low_ids = lax.broadcasted_iota(jnp.int32, (LOW, length), 0)
     high_ids = lax.broadcasted_iota(jnp.int32, (HIGH, length), 0)
+    count = len(all_scores) * heads
 
     def step(i, carry):
         rows = pl.ds(pl.multiple_of(i * 16, 16), 16)
         entries = index[rows, :]
-        block = [scores[head, rows, :].astype(F32) for head in range(heads)]
+        block = [scores[head, rows, :].astype(F32) for scores in all_scores for head in range(heads)]
         total = carry
         for r in range(16):
             entry = entries[r : r + 1, :]
@@ -324,32 +325,18 @@
             total = total + dot_rows(left, low)
         return total
 
-    total = lax.fori_loop(0, length // 16, step, jnp.zeros((heads * HIGH, LOW), F32))
-    out[...] = jnp.concatenate([total[head * HIGH : (head + 1) * HIGH] for head in range(heads)], axis=1)
-
-
-def table_kernel(scores, index, *rest):
-    add_table(scores, index, rest[-1])
-
-
-def table_gradient(scores, index, earlier):
-    heads = scores.shape[0]
-    return pl.pallas_call(
-        table_kernel,
-        out_shape=jax.ShapeDtypeStruct((HIGH, heads * LOW), F32),
-        in_specs=[pl.BlockSpec(memory_space=pltpu.VMEM)] * 2 + [pl.BlockSpec(memory_space=pl.ANY)] * len(earlier),
-        out_specs=pl.BlockSpec(memory_space=pltpu.VMEM),
-        cost_estimate=cost(8),
-        compiler_params=pltpu.CompilerParams(vmem_limit_bytes=VMEM_BYTES),
-    )(scores, index, *earlier)
-
-
-def small_kernel(pos, scores, index, small_a0, small_m0, small_a1, small_m1, table1, *rest):
-    keep, send, table = rest[-3:]
+    total = lax.fori_loop(0, length // 16, step, jnp.zeros((count * HIGH, LOW), F32))
+    parts = [total[i * HIGH : (i + 1) * HIGH] for i in range(count)]
+    for layer, out in enumerate(outs):
+        out[...] = jnp.concatenate(parts[layer * heads : (layer + 1) * heads], axis=1)
+
+
+def small_kernel(pos, scores0, scores1, index, small_a0, small_m0, small_a1, small_m1, *rest):
+    keep, send, table0, table1 = rest[-4:]
     size = small_a0.shape[0] * small_a0.shape[1]
-    add_table(scores, index, table)
+    add_tables((scores0, scores1), index, (table0, table1))
     parts = (
-        (small_a0[...], small_m0[...], table[...]),
+        (small_a0[...], small_m0[...], table0[...]),
         (small_a1[...], small_m1[...], table1[...]),
     )
     rows = [
@@ -367,12 +354,12 @@
         send[...] = rows[0].astype(BF16)
 
 
-def small_step(pos, scores, index, smalls, table1, earlier):
+def small_step(pos, scores0, scores1, index, smalls, earlier):
     samples, _, model = smalls[0].shape
     shape = (16 * samples + HIGH, model)
     return call(
-        small_kernel, pos, (scores, index, *smalls, table1), earlier, [(shape, F32), (shape, BF16)],
-        [((HIGH, model), F32)], work=8,
+        small_kernel, pos, (scores0, scores1, index, *smalls), earlier, [(shape, F32), (shape, BF16)],
+        [((HIGH, model), F32)] * 2, work=12,
     )
 
 
@@ -649,6 +636,32 @@
     samples, model = own.shape[0], own.shape[1] // 8
     shape = (1, (3 * samples + 8) * model)
     return call(line_kernel, pos, (own, *got), (), [(shape, F32)] * 2, [(own.shape, F32)])
+
+
+def first_kernel(keep1, other1, keep_m, other_m, own, *messages):
+    pieces = 4
+    size1, size_m = keep1.shape[0] // pieces, keep_m.shape[0] // pieces
+    n1, nm = size1 // 4, size_m // 4
+    for p in range(pieces):
+        for k in range(4):
+            at = k * (n1 + nm)
+            for keep, other, first, n, to in (
+                (keep1, other1, p * size1 + k * n1, n1, at), (keep_m, other_m, p * size_m + k * nm, nm, at + n1)
+            ):
+                total = keep[first : first + n, :].astype(F32) + other[first : first + n, :].astype(F32)
+                if p == 0:
+                    own[to : to + n, :] = total
+                else:
+                    messages[p - 1][to : to + n, :] = total.astype(BF16)
+
+
+def first_step(keep1, other1, keep_m, other_m):
+    shape = ((keep1.shape[0] + keep_m.shape[0]) // 4, keep1.shape[1])
+    return pl.pallas_call(
+        first_kernel,
+        out_shape=[jax.ShapeDtypeStruct(shape, F32)] + [jax.ShapeDtypeStruct(shape, BF16)] * 3,
+        compiler_params=pltpu.CompilerParams(vmem_limit_bytes=VMEM_BYTES),
+    )(keep1, other1, keep_m, other_m)
 
 
 def plane_kernel(samples, pos, keep, other, kept_small, other_small, cond, own, own_small, *rest):
@@ -735,7 +748,8 @@
     )
 
 
-def finish_kernel(samples, width, pos, own_small, got_a, got_b, got_c, g_ada, g_b_ada, summed, work, whole):
+def finish_kernel(samples, width, pos, own_small, got_a, got_b, got_c,
+                  g_ada, g_b_ada, g_b_qv, g_b_proj, g_b_fc1, g_b_fc2, g_table, work, whole, row):
     shard, rank = pos[1], pos[2]
     model = own_small.shape[1]
     each = 4 * samples
@@ -752,18 +766,38 @@
         whole[...] = dot_cols(act, rows.astype(BF16))
         cols = slice(kind * model, (kind + 1) * model)
         g_ada[:, cols] = whole[pl.ds(pl.multiple_of(shard * width, 16), width), :]
-        g_b_ada[:, cols] = col_sum(rows)
+        row[:, cols] = col_sum(rows)
     at = 7 * each
     rows = [piece[at : at + 8 + HIGH, :].astype(F32) for piece in pieces]
-    summed[...] = (rows[0] + rows[1]) + (rows[2] + rows[3])
-
-
-def finish_step(pos, own_small, got, samples, width):
+    summed = (rows[0] + rows[1]) + (rows[2] + rows[3])
+    for c in range(4):
+        row[:, (6 + c) * model : (7 + c) * model] = summed[1 + c : 2 + c, :]
+    row[:, 10 * model : 11 * model] = summed[5:6, :]
+    row[:, 11 * model : 12 * model] = summed[6:7, :]
+    row[:, 12 * model : 13 * model] = summed[7:8, :]
+    row[:, 13 * model : 14 * model] = summed[0:1, :]
+    for f in range(4):
+        @pl.when(shard == f)
+        def _():
+            for out, start in ((g_b_ada, 0), (g_b_fc1, 6), (g_b_qv, 10), (g_b_proj, 12), (g_b_fc2, 13)):
+                size = out.shape[1]
+                out[...] = row[:, start * model + f * size : start * model + (f + 1) * size]
+    heads, entries = g_table.shape
+    for high in range(-(-entries // LOW)):
+        size = min(LOW, entries - high * LOW)
+        for head in range(heads):
+            g_table[head : head + 1, high * LOW : high * LOW + size] = summed[
+                8 + high : 9 + high, head * LOW : head * LOW + size
+            ]
+
+
+def finish_step(pos, own_small, got, samples, width, heads, entries):
     model = own_small.shape[1]
+    sizes = [6 * width, 2 * width, width, 4 * width, width]
     return call(
         functools.partial(finish_kernel, samples, width), pos, (own_small, *got), (),
-        [((width, 6 * model), F32), ((1, 6 * model), F32), ((8 + HIGH, model), F32)],
-        [((7 * 16 * samples, model), F32), ((model, model), F32)],
+        [((width, 6 * model), F32)] + [((1, size), F32) for size in sizes] + [((heads, entries), F32)],
+        [((7 * 16 * samples, model), F32), ((model, model), F32), ((1, 14 * model), F32)],
     )
 
 
@@ -855,7 +889,7 @@
     return call(quarter_kernel, pos, (kept, got), (), [(shape, F32), (shape, BF16)], [])
 
 
-def pack_kernel(pos, qkv, proj, fc1, fc2, out):
+def pack_kernel(qkv, proj, fc1, fc2, out):
     q, model = proj.shape
     for c in range(3):
         out[c * q : (c + 1) * q, :] = qkv[:, c * model : (c + 1) * model]
@@ -865,9 +899,13 @@
     out[8 * q : 12 * q, :] = fc2[...]
 
 
-def pack_shard(pos, own):
+def pack_shard(own):
     q, model = own[1].shape
-    return call(pack_kernel, pos, own, (), [((12 * q, model), BF16)], [])[0]
+    return pl.pallas_call(
+        pack_kernel,
+        out_shape=jax.ShapeDtypeStruct((12 * q, model), BF16),
+        compiler_params=pltpu.CompilerParams(vmem_limit_bytes=VMEM_BYTES),
+    )(*own)
 
 
 def after(values, others):
@@ -1029,12 +1067,13 @@
     width = model // shards
     if direct:
         conds = [conditioning] + from_peers(conditioning, "fsdp")
-        own_pack = pack_shard(pos, own_raw)
+        own_pack = pack_shard(own_raw)
         middle_row = own_pack.shape[0] // 2
         got_x = lax.ppermute(own_pack, "fsdp", pairs_of(shards, 1))
         got_y = lax.ppermute(own_pack, "fsdp", pairs_of(shards, 2))
-        bias_own = lookup(bias_table[0], relative_bias_index, [own_pack, h0, grad1])
-        partial = partial_step(pos, w_ada[0], conds, (b_ada, b_qv, b_proj, b_fc1, b_fc2), [bias_own])
+        partial = partial_step(pos, w_ada[0], conds, (b_ada, b_qv, b_proj, b_fc1, b_fc2), [own_pack])
+        table = after([bias_table[0]], [own_pack])[0]
+        bias_own = lookup(table, relative_bias_index, [h0, grad1, *partial])
         got_first = lax.ppermute(got_x[:middle_row], "fsdp", pairs_of(shards, 2))
         got_second = lax.ppermute(got_y[middle_row:], "fsdp", pairs_of(shards, 1))
         own_weights = [own_pack, got_x, got_y, got_first, got_second]
@@ -1044,7 +1083,7 @@
         row = jnp.concatenate([b_ada, b_qv, b_proj, b_fc1, b_fc2], axis=1)
         bias_rows = lax.all_gather(row[0], "fsdp", axis=0)
         whole = [lax.all_gather(w, "fsdp", axis=0, tiled=True) for w in own_raw]
-        own_whole = pack_shard(pos, whole)
+        own_whole = pack_shard(whole)
         weights = [own_whole, swap_section(own_whole)]
         acts = jax.nn.silu(conditioning.astype(F32)).astype(BF16)
         modulation = dot(acts, lax.all_gather(w_ada[0], "fsdp", axis=0, tiled=True))
@@ -1072,18 +1111,14 @@
     pieces = z.pieces
     rows = half * length
     other1 = swap_section(send1)
-    sums1 = section_sums(keep1, other1[: keep1.shape[0]], pieces)
-    low1 = low_pieces(sums1)
-    table1 = table_gradient(scores1, relative_bias_index, low1)
-    other_m0 = after([swap_section(send_m0)], [table1])[0]
-    sums_m0 = section_sums(keep_m0, other_m0, pieces)
-    low_m0 = low_pieces(sums_m0)
+    other_m0 = swap_section(send_m0)
     if direct:
-        got1 = after(to_peers(low1, "fsdp"), [table1, *low_m0])
-        keep_z1, send_z1 = halve_step(pos, sums1[0], got1)
-        earlier = [table1, *low_m0, send_z1]
+        own_first, *first_messages = first_step(keep1, other1, keep_m0, other_m0)
+        earlier = first_messages
     else:
-        earlier = [table1, *low_m0]
+        sums1 = section_sums(keep1, other1[: keep1.shape[0]], pieces)
+        sums_m0 = section_sums(keep_m0, other_m0, pieces)
+        earlier = []
     d_h0, small_a0, scores0, keep_a0, send_a0 = backward_attention(
         0, z, pos, h0, lines, qkv, probs, att, branch, d_middle, d_h1, weights, earlier
     )
@@ -1097,41 +1132,37 @@
         return jnp.where(bit == 0, jnp.concatenate([own, other]), jnp.concatenate([other, own]))
 
     if direct:
-        got_z1, *got_m0 = after([replica(send_z1, 1), *to_peers(low_m0, "fsdp")], [d_h0])
-        other_a0 = swap_section(after([send_a0], [got_z1, *got_m0])[0])
-        keep_z1, send_z1 = quarter_step(pos, keep_z1, got_z1)
-        keep_zm, send_zm = halve_step(pos, sums_m0[0], got_m0)
-        kept_small, send_small = small_step(pos, scores0, relative_bias_index, smalls, table1, [send_z1, send_zm])
+        kept_small, send_small = small_step(pos, scores0, scores1, relative_bias_index, smalls, [])
         other_small = swap_section(send_small)
-        other_a0, got_z1, got_zm = after([other_a0, replica(send_z1, 2), replica(send_zm, 1)], [kept_small])
+        other_a0 = after([swap_section(send_a0)], [kept_small])[0]
         own_a0, own_small, *messages = plane_step(pos, keep_a0, other_a0, kept_small, other_small, conditioning)
         got = to_peers(messages, "fsdp")
-        got_z1, got_zm = after([got_z1, got_zm], [own_small])
-        quarter1 = (keep_z1 + got_z1.astype(F32)).astype(BF16)
-        keep_zm, send_zm = quarter_step(pos, keep_zm, got_zm)
-        cond_part = cond_step(pos, after([own_small], [send_zm, quarter1])[0], w_ada_pieces, conditioning)
+        got_first = after(to_peers(first_messages, "fsdp"), [own_small])
+        keep_z, send_z = halve_step(pos, own_first, got_first)
+        cond_part = cond_step(pos, after([own_small], [send_z])[0], w_ada_pieces, conditioning)
         part0, plane_small, *messages = column_step(pos, own_a0, own_small, got, samples)
-        got_z1, got_zm = after([replica(quarter1, 2), replica(send_zm, 2)], [plane_small])
+        got_z = after([replica(send_z, 1)], [plane_small])[0]
+        keep_z, send_z = quarter_step(pos, keep_z, got_z)
         got = to_peers(messages, "rep")
         size = part0.shape[0]
         high, low = rank >> 1, rank & 1
-
-        def by_low(pair):
-            n = pair.shape[0] // 2
-            both = ordered(pair.reshape(1, 2, n, model), replica(pair, 1).reshape(1, 2, n, model), low)
-            return jnp.transpose(both, (1, 0, 2, 3)).reshape(-1, model)
-
-        half1 = by_low(ordered(quarter1, got_z1, high))
-        quarter_m = (keep_zm + got_zm.astype(F32)).astype(BF16)
-        pair_m = ordered(quarter_m, replica(quarter_m, 2), high)
         quarter0 = add_pieces(part0, [x[:size] for x in got]).astype(BF16)
-        half_m0 = by_low(pair_m)
+        got_z = after([replica(send_z, 2)], [quarter0])[0]
+        quarter = (keep_z + got_z.astype(F32)).astype(BF16)
+        pair = ordered(quarter, replica(quarter, 2), high)
         half_a0 = by_rank([quarter0] + from_peers(quarter0, "rep"), rank).reshape(-1, model)
-        g_ada, g_b_ada, summed = finish_step(pos, plane_small, got, samples, width)
-        g_b_ada = g_b_ada[0]
+        n = pair.shape[0] // 2
+        quarters = ordered(pair.reshape(1, 2, n, model), replica(pair, 1).reshape(1, 2, n, model), low)
+        quarters = jnp.transpose(quarters, (1, 0, 2, 3)).reshape(4, n, model)
+        n = 3 * n // 5
+        half1 = quarters[:, :n].reshape(-1, model)
+        half_m0 = quarters[:, n:].reshape(-1, model)
+        g_ada, g_b_ada, g_b_qv, g_b_proj, g_b_fc1, g_b_fc2, g_table = finish_step(
+            pos, plane_small, got, samples, width, heads, entries
+        )
     else:
         other_a0 = swap_section(send_a0)
-        kept_small, send_small = small_step(pos, scores0, relative_bias_index, smalls, table1, [])
+        kept_small, send_small = small_step(pos, scores0, scores1, relative_bias_index, smalls, [])
         theirs = swap_section(send_small).astype(F32)
         both = kept_small + theirs
         cut = half * 8
@@ -1151,6 +1182,11 @@
         act_cols = lax.dynamic_slice_in_dim(act_all, shard * width, width, 1)
         g_ada = jnp.concatenate([dot_cols(act_cols, kept[:, i]) for i in range(6)], axis=1)
         g_b_ada = jnp.sum(kept[:, :6].astype(F32), axis=0).reshape(-1)
+        vectors = [g_b_ada, summed[5:7].reshape(-1), summed[7], summed[1:5].reshape(-1), summed[0]]
+        g_b_ada, g_b_qv, g_b_proj, g_b_fc1, g_b_fc2 = [
+            lax.dynamic_slice_in_dim(v, shard * (v.shape[0] // shards), v.shape[0] // shards, 0)[None] for v in vectors
+        ]
+        g_table = jnp.transpose(summed[8:].reshape(HIGH, heads, LOW), (1, 0, 2)).reshape(heads, HIGH * LOW)[:, :entries]
         sums_a0 = section_sums(keep_a0, other_a0[:size_a], pieces)
         half_a0, half_m0, half1 = sums_a0[0].astype(BF16), sums_m0[0].astype(BF16), sums1[0].astype(BF16)
     cond_grad = cond_part + swap_section(cond_part)
@@ -1173,18 +1209,10 @@
         other_a0[size_a : size_a + rows].astype(F32).reshape(half, length, model),
     )
 
-    g_b_fc2, g_b_fc1 = summed[0], summed[1:5].reshape(-1)
-    g_b_qv, g_b_proj = summed[5:7].reshape(-1), summed[7]
-    g_table = jnp.transpose(summed[8:].reshape(HIGH, heads, LOW), (1, 0, 2)).reshape(heads, HIGH * LOW)[:, :entries]
-
-    def own_part(vector):
-        size = vector.shape[0] // shards
-        return lax.dynamic_slice_in_dim(vector, shard * size, size, 0)[None]
-
     return (
         activations[None], input_grads[None], cond_grad,
         g_ada[None], g_qkv[None], g_proj[None], g_fc1[None], g_fc2[None],
-        own_part(g_b_ada), own_part(g_b_qv), own_part(g_b_proj), own_part(g_b_fc1), own_part(g_b_fc2),
+        g_b_ada, g_b_qv, g_b_proj, g_b_fc1, g_b_fc2,
         g_table[None],
     )
 

time: 242 us -> 235 us (0.971)
  waiting for transfers between devices: 31.9 us -> 48.3 us
  starting transfers between devices: 52.7 us -> 42.3 us
  other arithmetic: 14.9 us -> 8.46 us
  local copies, waits for them, and re-layouts: 19.1 us -> 15.4 us
    ppermute x8 -> x4, waiting for transfers between devices: 0.02 us -> 15.1 us  [replica(): return lax.ppermute(value, 'rep', pairs_of(replicas, step))]
    ppermute x8 -> x4, starting transfers between devices: 12.3 us -> 5.13 us  [replica(): return lax.ppermute(value, 'rep', pairs_of(replicas, step))]
    ppermute x9, waiting for transfers between devices: 10.1 us -> 4.96 us  [from_peers(): lax.ppermute(value, axis, pairs_of(lax.axis_size(axis), p))]
    add x2 -> x0, other arithmetic: 4.37 us -> none  [section_sums(): keep[p * size:(p + 1) * size].astype(F32)]
    ppermute x15 -> x12, starting transfers between devices: 18.5 us -> 14.9 us  [to_peers(): lax.ppermute(messages[p - 1], axis, pairs_of(count, p))]
    dynamic_slice x5 -> x0, local copies, waits for them, and re-layouts: 3.22 us -> none  [own_part(): return lax.dynamic_slice_in_dim(vector, shard * size, size, 0)[None]]
    slice x4 -> x2, local copies, waits for them, and re-layouts: 2.94 us -> 0.08 us  [the longest x1 0.05 us: per_device(): half1 = quarters[:, :n].reshape(-1, model)]
    ppermute x15 -> x12, waiting for transfers between devices: 10.7 us -> 13.2 us  [to_peers(): lax.ppermute(messages[p - 1], axis, pairs_of(count, p))]
  transfers between devices with their start and end apart: 49 -> 42, of which waited for: 14 -> 15; matrix products, arithmetic and copies ran while one was open for 9% -> 5% of each run, Pallas kernels for 36% -> 36%
where the time goes in v6:
time: 235 us; the launch traced here: 234 us
  Pallas kernels  119 us (51%)
  waiting for transfers between devices  48.3 us (21%)
  starting transfers between devices  42.3 us (18%)
  local copies, waits for them, and re-layouts  15.4 us (7%)
  other arithmetic  8.46 us (4%)
    pallas_call x14, Pallas kernels, call(): pl.pallas_call(kernel, out_shape=[jax.ShapeDtypeStruct(shape, dtype) for...  100 us
    ppermute x4, waiting for transfers between devices, replica(): return lax.ppermute(value, 'rep', pairs_of(replicas, step))  15.1 us
    ppermute x12, starting transfers between devices, to_peers(): lax.ppermute(messages[p - 1], axis, pairs_of(count, p))  14.9 us
    ppermute x9, starting transfers between devices, from_peers(): lax.ppermute(value, axis, pairs_of(lax.axis_size(axis), p))  14.1 us
    ppermute x12, waiting for transfers between devices, to_peers(): lax.ppermute(messages[p - 1], axis, pairs_of(count, p))  13.2 us
    unnamed x91, local copies, waits for them, and re-layouts  12 us
    pallas_call x1, Pallas kernels, lookup(): pl.pallas_call(lookup_kernel, out_shape=jax.ShapeDtypeStruct((heads, leng...  11.3 us
    ppermute x1, waiting for transfers between devices, per_device(): got_first = lax.ppermute(got_x[:middle_row], 'fsdp', pairs_of(shards, 2))  8.41 us
  transfers between devices with their start and end apart: 42, of which 15 were waited for; matrix products, arithmetic and copies ran while one was open for 5% of the time, Pallas kernels for 36%

profile of v6, /device:TPU:0, one launch (start us, length us, event | category | flops | bytes accessed | tf_op | source)
XLA Modules:
  0.0 234.3 jit_solution(9713780445061290937)
XLA Ops:
  0.7 1.9 copy.61
  3.9 2.9 %collective-permute-start = (bf16[4,384]{1,0:T(4,128)(2,1)}, bf16[4,384]{1,0:T(4,128)(2,1)S(1)}, u32[]{:S(2)}, u32[]{:S(2)}) collective-permute-start(bf16[4,384]{1,0:T(4,128)(2,1)} %cond.3), channel_id=1, source_target_pairs={{0,4},{4,0},{8,12},{12,8},{1,5},{5,1},{9,13},{13,9},{2,6},{6,2},{1... | collective-permute-start | bytes 9224 | tf_op jit(solution)/shard_map/ppermute | solution.py:1031
  8.4 2.2 shard_map.263.rest_0_.refs_1_
  10.6 2.0 collective-permute-start.6
  19.0 3.4 %shard_map.264 = (f32[4,3072]{1,0:T(4,128)}, f32[4,3072]{1,0:T(4,128)}, f32[4,3072]{1,0:T(4,128)}, f32[4,3072]{1,0:T(4,128)}) custom-call(s32[3]{0:T(128)} %pad_add_fusion.pos, bf16[96,2304]{1,0:T(8,128)(2,1)} %bitcast.50, bf16[4,384]{1,0:T(4,128)(2,1)} %cond.3, bf16[4,384]{1,0:T(4,128)(2,1)} %copy-done.41, bf16[4,384]{1,0:T(4,128)(2,1)} %copy-done.42, ...), custom_call_target="tpu_custom_call" | custom-call | flops 2000000000 | tf_op jit(solution)/shard_map/pallas_call | solution.py:516
  22.5 11.3 %shard_map.268.own_bias = bf16[6,256,256]{2,1,0:T(8,128)(2,1)} custom-call(bf16[128,64]{1,0:T(8,128)(2,1)} %bitcast.76, s32[256,256]{1,0:T(8,128)} %index.3, bf16[512,384]{1,0:T(8,128)(2,1)} %bitcast.58, bf16[512,384]{1,0:T(8,128)(2,1)} %bitcast.61, f32[4,3072]{1,0:T(4,128)} %get-tuple-element.82.own.rest_2_, f32[4,3072]{1,0:T(4,128)} %get-tuple-element.83.rest_3_, ...), custom_call_target="tpu_custom_call" | custom-call | flops 11000000512 | tf_op jit(solution)/shard_map/pallas_call | solution.py:954
  34.7 2.7 %collective-permute-start.5 = (f32[4,3072]{1,0:T(4,128)S(1)}, f32[4,3072]{1,0:T(4,128)S(1)}, u32[]{:S(2)}, u32[]{:S(2)}) collective-permute-start(f32[4,3072]{1,0:T(4,128)S(1)} %copy-done.36), channel_id=1, source_target_pairs={{0,12},{4,8},{8,4},{12,0},{1,13},{5,9},{9,5},{13,1},{2,14},{6,10},... | collective-permute-start | bytes 147464 | tf_op jit(solution)/shard_map/ppermute | solution.py:998
  41.8 8.4 %collective-permute-done.10.refs_1_.rest_3_ = bf16[576,384]{1,0:T(8,128)(2,1)S(1)} collective-permute-done((bf16[576,384]{1,0:T(8,128)(2,1)S(1)}, bf16[576,384]{1,0:T(8,128)(2,1)S(1)}, u32[]{:S(2)}, u32[]{:S(2)}) %collective-permute-start.10) | collective-permute-done | bytes 442400 | tf_op jit(solution)/shard_map/ppermute | solution.py:1077
  50.2 2.5 %collective-permute-done.11.refs_2_.rest_4_ = bf16[576,384]{1,0:T(8,128)(2,1)} collective-permute-done((bf16[576,384]{1,0:T(8,128)(2,1)S(1)}, bf16[576,384]{1,0:T(8,128)(2,1)}, u32[]{:S(2)}, u32[]{:S(2)}) %collective-permute-start.11) | collective-permute-done | bytes 442400 | tf_op jit(solution)/shard_map/ppermute | solution.py:1078
  55.9 1.8 collective-permute-start.17
  59.4 15.1 %shard_map.270 = (bf16[512,1152]{1,0:T(8,128)(2,1)}, bf16[2,6,256,256]{3,2,1,0:T(8,128)(2,1)}, bf16[512,384]{1,0:T(8,128)(2,1)}, f32[512,384]{1,0:T(8,128)}, f32...) custom-call(s32[3]{0:T(128)} %pad_add_fusion.pos, ...), custom_call_target="tpu_custom_call" | custom-call | flops 15000000512 | tf_op jit(solution)/shard_map/pallas_call | solution.py:516
  74.5 4.9 %collective-permute-done.18.rest_11_.rest_2_ = bf16[96,2304]{1,0:T(8,128)(2,1)S(1)} collective-permute-done((bf16[96,2304]{1,0:T(8,128)(2,1)}, bf16[96,2304]{1,0:T(8,128)(2,1)S(1)}, u32[]{:S(2)}, u32[]{:S(2)}) %collective-permute-start.18) | collective-permute-done | bytes 442400 | tf_op jit(solution)/shard_map/ppermute | solution.py:1031
  80.4 26.1 %shard_map.271 = (bf16[512,384]{1,0:T(8,128)(2,1)}, bf16[512,384]{1,0:T(8,128)(2,1)}, f32[2,8,384]{2,1,0:T(8,128)}, f32[2,8,384]{2,1,0:T(8,128)}, bf16[6,256,256...) custom-call(s32[3]{0:T(128)} %pad_add_fusion.pos, bf16[512,384]{1,0:T(8,128)(2,1)} %get-tuple-element.91.h, ...), custom_call_target="tpu_custom_call" | custom-call | flops 24999999488 | tf_op jit(solution)/shard_map/pallas_call | solution.py:516
  106.6 12.0 %shard_map.272 = (f32[512,384]{1,0:T(8,128)}, f32[2,8,384]{2,1,0:T(8,128)}, bf16[1536,384]{1,0:T(8,128)(2,1)}, bf16[1536,384]{1,0:T(8,128)(2,1)}) custom-call(s32[3]{0:T(128)} %pad_add_fusion.pos, bf16[512,384]{1,0:T(8,128)(2,1)} %get-tuple-element.98.grad.d_h1, f32[512,384]{1,0:T(8,128)} %get-tuple-element.99.middle, f32[1,7680]{1,0:T(1,128)} %get-tuple-element.89.own_line, ...), custom_call_target="tpu_custom_call" | custom-call | flops 12000000000 | tf_op jit(solution)/shard_map/pallas_call | solution.py:516
  119.2 2.8 %collective-permute-done.21.other_m = bf16[1536,384]{1,0:T(8,128)(2,1)} collective-permute-done((bf16[1536,384]{1,0:T(8,128)(2,1)}, bf16[1536,384]{1,0:T(8,128)(2,1)}, u32[]{:S(2)}, u32[]{:S(2)}) %collective-permute-start.21) | collective-permute-done | bytes 1179680 | tf_op jit(solution)/shard_map/ppermute | solution.py:966
  123.4 4.8 %shard_map.273 = (f32[960,384]{1,0:T(8,128)}, bf16[960,384]{1,0:T(8,128)(2,1)}, bf16[960,384]{1,0:T(8,128)(2,1)}, bf16[960,384]{1,0:T(8,128)(2,1)}) custom-call(bf16[2304,384]{1,0:T(8,128)(2,1)} %get-tuple-element.104.keep1, bf16[2816,384]{1,0:T(8,128)(2,1)} %copy-done.2, bf16[1536,384]{1,0:T(8,128)(2,1)} %get-tuple-element.105.keep_m, ...), custom_call_target="tpu_custom_call" | custom-call | tf_op jit(solution)/shard_map/pallas_call | solution.py:660
  131.7 12.6 %shard_map.274 = (f32[512,384]{1,0:T(8,128)}, f32[2,8,384]{2,1,0:T(8,128)}, bf16[6,256,256]{2,1,0:T(8,128)(2,1)}, bf16[768,384]{1,0:T(8,128)(2,1)}, bf16[1280,384]{1,0:T(8,128)(2,1)}) custom-call(s32[3]{0:T(128)} %pad_add_fusion.pos, bf16[512,384]{1,0:T(8,128)(2,1)} %bitcast.60, f32[1,7680]{1,0:T(1,128)} %get-tuple-element.89.own_line, ...), custom_call_target="tpu_custom_call" | custom-call | flops 12999999488 | tf_op jit(solution)/shard_map/pallas_call | solution.py:516
  144.3 11.6 %shard_map.275 = (f32[48,384]{1,0:T(8,128)}, bf16[48,384]{1,0:T(8,128)(2,1)}) custom-call(s32[3]{0:T(128)} %pad_add_fusion.pos, bf16[6,256,256]{2,1,0:T(8,128)(2,1)} %get-tuple-element.112.scores0, bf16[6,256,256]{2,1,0:T(8,128)(2,1)} %get-tuple-element.113.scores1, s32[256,256]{1,0:T(8,128)} %index.3, f32[2,8,384]{2,1,0:T(8,128)} %get-tuple-element.114.small_a0, ...), custom_call_target="tpu_custom_call" | custom-call | flops 12000000000 | tf_op jit(solution)/shard_map/pallas_call | solution.py:516
  158.1 2.5 %shard_map.277 = (f32[192,384]{1,0:T(8,128)}, bf16[64,384]{1,0:T(8,128)(2,1)}, bf16[256,384]{1,0:T(8,128)(2,1)}, bf16[256,384]{1,0:T(8,128)(2,1)}, bf16[256,384]{1,0:T(8,128)(2,1)}) custom-call(s32[3]{0:T(128)} %pad_add_fusion.pos, bf16[768,384]{1,0:T(8,128)(2,1)} %get-tuple-element.119.keep, bf16[1280,384]{1,0:T(8,128)(2,1)} %shard_map.276.other, ...), custom_call_target="tpu_custom_call" | custom-call | flops 2000000000 | tf_op jit(solution)/shard_map/pallas_call | solution.py:516
  166.2 3.3 %shard_map.279 = (f32[480,384]{1,0:T(8,128)}, bf16[480,384]{1,0:T(8,128)(2,1)}) custom-call(s32[3]{0:T(128)} %pad_add_fusion.pos, f32[960,384]{1,0:T(8,128)} %get-tuple-element.122.own, bf16[960,384]{1,0:T(8,128)(2,1)} %get-tuple-element.123.got_a, bf16[960,384]{1,0:T(8,128)(2,1)} %get-tuple-element.124.got_b, bf16[960,384]{1,0:T(8,128)(2,1)} %get-tuple-element.125.got_c), custom_call_target="tpu_custom_call" | custom-call | flops 2000000000 | tf_op jit(solution)/shard_map/pallas_call | solution.py:516
  173.6 2.1 shard_map.282
  175.7 2.8 %shard_map.281 = f32[4,384]{1,0:T(4,128)} custom-call(s32[3]{0:T(128)} %pad_add_fusion.pos, bf16[64,384]{1,0:T(8,128)(2,1)} %shard_map.280.small, bf16[4,384]{1,0:T(4,128)(2,1)} %cond.3, bf16[96,2304]{1,0:T(8,128)(2,1)} %shard_map.269.rest_10_.rest_0_, bf16[96,2304]{1,0:T(8,128)(2,1)} %copy-done.26, bf16[96,2304]{1,0:T(8,128)(2,1)} %copy-done.27, ...), custom_call_target="tpu_custom_call" | custom-call | flops 2000000000 | tf_op jit(solution)/shard_map/pallas_call | solution.py:516
  181.3 2.6 %collective-permute-start.32 = (bf16[192,384]{1,0:T(8,128)(2,1)S(1)}, bf16[192,384]{1,0:T(8,128)(2,1)S(1)}, u32[]{:S(2)}, u32[]{:S(2)}) collective-permute-start(bf16[192,384]{1,0:T(8,128)(2,1)S(1)} %copy-done.34), channel_id=1, source_target_pairs={{0,2},{1,3},{2,0},{3,1},{4,6},{5,7},{6,4},{7,5},{8,10},{9,11},{10,... | collective-permute-start | bytes 442376 | tf_op jit(solution)/shard_map/ppermute | solution.py:998
  185.5 2.1 shard_map.285
  187.6 1.7 collective-permute-start.38
  189.3 9.9 %collective-permute-done.32.got_b = bf16[192,384]{1,0:T(8,128)(2,1)S(1)} collective-permute-done((bf16[192,384]{1,0:T(8,128)(2,1)S(1)}, bf16[192,384]{1,0:T(8,128)(2,1)S(1)}, u32[]{:S(2)}, u32[]{:S(2)}) %collective-permute-start.32) | collective-permute-done | bytes 147488 | tf_op jit(solution)/shard_map/ppermute | solution.py:998
  199.3 4.8 %collective-permute-start.36 = (bf16[48,384]{1,0:T(8,128)(2,1)S(1)}, bf16[48,384]{1,0:T(8,128)(2,1)S(1)}, u32[]{:S(2)}, u32[]{:S(2)}) collective-permute-start(bf16[48,384]{1,0:T(8,128)(2,1)S(1)} %add_convert_fusion.1.refs_1_), channel_id=1, source_target_pairs={{0,2},{1,3},{2,0},{3,1},{4,6},{5,7},{6,4},{7,5},{8,10},{9,11},{10,... | collective-permute-start | bytes 110600 | tf_op jit(solution)/shard_map/ppermute | solution.py:1031
  208.5 1.8 collective-permute-start.39
  210.3 2.8 %shard_map.283 = (f32[96,2304]{1,0:T(8,128)}, f32[1,576]{1,0:T(1,128)}, f32[1,192]{1,0:T(1,128)}, f32[1,96]{1,0:T(1,128)}, f32[1,384]{1,0:T(1,128)}, /*index=5*/f32[1,96]{1,0:T(1,128)}, f32[6,961]{1,0:T(8,128)}) custom-call(s32[3]{0:T(128)} %pad_add_fusion.pos, bf16[144,384]{1,0:T(8,128)(2,1)} %get-tuple-element.131.own_small.refs_1_, ...), custom_call_target="tpu_custom_call" | custom-call | flops 2000000000 | tf_op jit(solution)/shard_map/pallas_call | solution.py:516
  214.5 3.9 %collective-permute-done.39 = bf16[240,384]{1,0:T(8,128)(2,1)S(1)} collective-permute-done((bf16[240,384]{1,0:T(8,128)(2,1)S(1)}, bf16[240,384]{1,0:T(8,128)(2,1)S(1)}, u32[]{:S(2)}, u32[]{:S(2)}) %collective-permute-start.39) | collective-permute-done | bytes 184352 | tf_op jit(solution)/shard_map/ppermute | solution.py:1129
  218.8 9.9 %collective-permute-done.40 = bf16[480,384]{1,0:T(8,128)(2,1)S(1)} collective-permute-done((bf16[480,384]{1,0:T(8,128)(2,1)S(1)}, bf16[480,384]{1,0:T(8,128)(2,1)S(1)}, u32[]{:S(2)}, u32[]{:S(2)}) %collective-permute-start.40) | collective-permute-done | bytes 368672 | tf_op jit(solution)/shard_map/ppermute | solution.py:1129
  231.8 2.5 %shard_map.287 = (f32[96,1152]{1,0:T(8,128)}, f32[96,384]{1,0:T(8,128)}, f32[96,1536]{1,0:T(8,128)}, f32[384,384]{1,0:T(8,128)}) custom-call(s32[3]{0:T(128)} %pad_add_fusion.pos, bf16[192,384]{1,0:T(8,128)(2,1)} %slice_select_fusion.1.own_a, bf16[384,384]{1,0:T(8,128)(2,1)} %slice_select_fusion.own_m, bf16[576,384]{1,0:T(8,128)(2,1)} %copy-done.29), custom_call_target="tpu_custom_call" | custom-call | flops 2000000000 | tf_op jit(solution)/shard_map/pallas_call | solution.py:516
  (199 shorter events, 51.6 us)
Async XLA Ops:
  3.9 14.5 %collective-permute-start = (bf16[4,384]{1,0:T(4,128)(2,1)}, bf16[4,384]{1,0:T(4,128)(2,1)S(1)}, u32[]{:S(2)}, u32[]{:S(2)}) collective-permute-start(bf16[4,384]{1,0:T(4,128)(2,1)} %cond.3), channel_id=1, source_target_pairs={{0,4},{4,0},{8,12},{12,8},{1,5},{5,1},{9,13},{13,9},{2,6},{6,2},{1... | collective-permute-start | bytes 9224 | tf_op jit(solution)/shard_map/ppermute | solution.py:1031
  6.9 11.6 %collective-permute-start.1 = (bf16[4,384]{1,0:T(4,128)(2,1)}, bf16[4,384]{1,0:T(4,128)(2,1)S(1)}, u32[]{:S(2)}, u32[]{:S(2)}) collective-permute-start(bf16[4,384]{1,0:T(4,128)(2,1)} %cond.3), channel_id=1, source_target_pairs={{0,8},{4,12},{8,0},{12,4},{1,9},{5,13},{9,1},{13,5},{2,10},{6,14},... | collective-permute-start | bytes 9224 | tf_op jit(solution)/shard_map/ppermute | solution.py:1031
  8.4 10.1 %collective-permute-start.2 = (bf16[4,384]{1,0:T(4,128)(2,1)}, bf16[4,384]{1,0:T(4,128)(2,1)S(1)}, u32[]{:S(2)}, u32[]{:S(2)}) collective-permute-start(bf16[4,384]{1,0:T(4,128)(2,1)} %cond.3), channel_id=1, source_target_pairs={{0,12},{4,8},{8,4},{12,0},{1,13},{5,9},{9,5},{13,1},{2,14},{6,10},... | collective-permute-start | bytes 9224 | tf_op jit(solution)/shard_map/ppermute | solution.py:1031
  10.6 24.1 %collective-permute-start.6 = (bf16[1152,384]{1,0:T(8,128)(2,1)}, bf16[1152,384]{1,0:T(8,128)(2,1)S(1)}, u32[]{:S(2)}, u32[]{:S(2)}) collective-permute-start(bf16[1152,384]{1,0:T(8,128)(2,1)} %shard_map.263.rest_0_.refs_1_), channel_id=1, source_target_pairs={{0,4},{4,0},{8,12},{12,8},{1,5},{5,1},{9,13},{13,9},{2,6},{6,2},{1... | collective-permute-start | bytes 2654216 | tf_op jit(solution)/shard_map/ppermute | solution.py:1072
  12.5 24.8 %collective-permute-start.7 = (bf16[1152,384]{1,0:T(8,128)(2,1)}, bf16[1152,384]{1,0:T(8,128)(2,1)S(1)}, u32[]{:S(2)}, u32[]{:S(2)}) collective-permute-start(bf16[1152,384]{1,0:T(8,128)(2,1)} %shard_map.263.rest_0_.refs_1_), channel_id=1, source_target_pairs={{0,8},{4,12},{8,0},{12,4},{1,9},{5,13},{9,1},{13,5},{2,10},{6,14},... | collective-permute-start | bytes 2654216 | tf_op jit(solution)/shard_map/ppermute | solution.py:1073
  37.4 16.9 %collective-permute-start.12 = (bf16[1152,384]{1,0:T(8,128)(2,1)S(1)}, bf16[1152,384]{1,0:T(8,128)(2,1)}, u32[]{:S(2)}, u32[]{:S(2)}) collective-permute-start(bf16[1152,384]{1,0:T(8,128)(2,1)S(1)} %copy-done.1), channel_id=1, source_target_pairs={{0,16},{16,0},{1,17},{17,1},{2,18},{18,2},{3,19},{19,3},{4,20},{20... | collective-permute-start | bytes 2654216 | tf_op jit(solution)/shard_map/ppermute | solution.py:966
  37.9 12.2 %collective-permute-start.10 = (bf16[576,384]{1,0:T(8,128)(2,1)S(1)}, bf16[576,384]{1,0:T(8,128)(2,1)S(1)}, u32[]{:S(2)}, u32[]{:S(2)}) collective-permute-start(bf16[576,384]{1,0:T(8,128)(2,1)S(1)} %slice.57), channel_id=1, source_target_pairs={{0,8},{4,12},{8,0},{12,4},{1,9},{5,13},{9,1},{13,5},{2,10},{6,14},... | collective-permute-start | bytes 1327112 | tf_op jit(solution)/shard_map/ppermute | solution.py:1077
  39.6 18.0 %collective-permute-start.13 = (bf16[1152,384]{1,0:T(8,128)(2,1)S(1)}, bf16[1152,384]{1,0:T(8,128)(2,1)}, u32[]{:S(2)}, u32[]{:S(2)}) collective-permute-start(bf16[1152,384]{1,0:T(8,128)(2,1)S(1)} %collective-permute-done.6.refs_3_.rest_1_), channel_id=1, source_target_pairs={{0,16},{16,0},{1,17},{17,1},{2,18},{18,2},{3,19},{19,3},{4,20},{20... | collective-permute-start | bytes 2654216 | tf_op jit(solution)/shard_map/ppermute | solution.py:966
  39.8 19.2 %collective-permute-start.14 = (bf16[1152,384]{1,0:T(8,128)(2,1)S(1)}, bf16[1152,384]{1,0:T(8,128)(2,1)}, u32[]{:S(2)}, u32[]{:S(2)}) collective-permute-start(bf16[1152,384]{1,0:T(8,128)(2,1)S(1)} %collective-permute-done.7.refs_4_.rest_2_), channel_id=1, source_target_pairs={{0,16},{16,0},{1,17},{17,1},{2,18},{18,2},{3,19},{19,3},{4,20},{20... | collective-permute-start | bytes 2654216 | tf_op jit(solution)/shard_map/ppermute | solution.py:966
  40.1 12.5 %collective-permute-start.11 = (bf16[576,384]{1,0:T(8,128)(2,1)S(1)}, bf16[576,384]{1,0:T(8,128)(2,1)}, u32[]{:S(2)}, u32[]{:S(2)}) collective-permute-start(bf16[576,384]{1,0:T(8,128)(2,1)S(1)} %slice.58), channel_id=1, source_target_pairs={{0,4},{4,0},{8,12},{12,8},{1,5},{5,1},{9,13},{13,9},{2,6},{6,2},{1... | collective-permute-start | bytes 1327112 | tf_op jit(solution)/shard_map/ppermute | solution.py:1078
  50.2 9.2 %collective-permute-start.15 = (bf16[576,384]{1,0:T(8,128)(2,1)S(1)}, bf16[576,384]{1,0:T(8,128)(2,1)}, u32[]{:S(2)}, u32[]{:S(2)}) collective-permute-start(bf16[576,384]{1,0:T(8,128)(2,1)S(1)} %collective-permute-done.10.refs_1_.rest_3_), channel_id=1, source_target_pairs={{0,16},{16,0},{1,17},{17,1},{2,18},{18,2},{3,19},{19,3},{4,20},{20... | collective-permute-start | bytes 1327112 | tf_op jit(solution)/shard_map/ppermute | solution.py:966
  55.9 18.6 %collective-permute-start.17 = (bf16[96,2304]{1,0:T(8,128)(2,1)}, bf16[96,2304]{1,0:T(8,128)(2,1)S(1)}, u32[]{:S(2)}, u32[]{:S(2)}) collective-permute-start(bf16[96,2304]{1,0:T(8,128)(2,1)} %shard_map.269.rest_10_.rest_0_), channel_id=1, source_target_pairs={{0,4},{4,0},{8,12},{12,8},{1,5},{5,1},{9,13},{13,9},{2,6},{6,2},{1... | collective-permute-start | bytes 1327112 | tf_op jit(solution)/shard_map/ppermute | solution.py:1031
  57.6 21.8 %collective-permute-start.18 = (bf16[96,2304]{1,0:T(8,128)(2,1)}, bf16[96,2304]{1,0:T(8,128)(2,1)S(1)}, u32[]{:S(2)}, u32[]{:S(2)}) collective-permute-start(bf16[96,2304]{1,0:T(8,128)(2,1)} %shard_map.269.rest_10_.rest_0_), channel_id=1, source_target_pairs={{0,8},{4,12},{8,0},{12,4},{1,9},{5,13},{9,1},{13,5},{2,10},{6,14},... | collective-permute-start | bytes 1327112 | tf_op jit(solution)/shard_map/ppermute | solution.py:1031
  58.9 20.5 %collective-permute-start.19 = (bf16[96,2304]{1,0:T(8,128)(2,1)}, bf16[96,2304]{1,0:T(8,128)(2,1)S(1)}, u32[]{:S(2)}, u32[]{:S(2)}) collective-permute-start(bf16[96,2304]{1,0:T(8,128)(2,1)} %shard_map.269.rest_10_.rest_0_), channel_id=1, source_target_pairs={{0,12},{4,8},{8,4},{12,0},{1,13},{5,9},{9,5},{13,1},{2,14},{6,10},... | collective-permute-start | bytes 1327112 | tf_op jit(solution)/shard_map/ppermute | solution.py:1031
  106.5 15.5 %collective-permute-start.20 = (bf16[2816,384]{1,0:T(8,128)(2,1)}, bf16[2816,384]{1,0:T(8,128)(2,1)S(1)}, u32[]{:S(2)}, u32[]{:S(2)}) collective-permute-start(bf16[2816,384]{1,0:T(8,128)(2,1)} %get-tuple-element.93), channel_id=1, source_target_pairs={{0,16},{16,0},{1,17},{17,1},{2,18},{18,2},{3,19},{19,3},{4,20},{20... | collective-permute-start | bytes 6488072 | tf_op jit(solution)/shard_map/ppermute | solution.py:966
  128.2 34.5 %collective-permute-start.24 = (bf16[960,384]{1,0:T(8,128)(2,1)}, bf16[960,384]{1,0:T(8,128)(2,1)}, u32[]{:S(2)}, u32[]{:S(2)}) collective-permute-start(bf16[960,384]{1,0:T(8,128)(2,1)} %get-tuple-element.107.rest_10_), channel_id=1, source_target_pairs={{0,4},{4,0},{8,12},{12,8},{1,5},{5,1},{9,13},{13,9},{2,6},{6,2},{1... | collective-permute-start | bytes 2211848 | tf_op jit(solution)/shard_map/ppermute | solution.py:998
  129.0 37.2 %collective-permute-start.25 = (bf16[960,384]{1,0:T(8,128)(2,1)}, bf16[960,384]{1,0:T(8,128)(2,1)}, u32[]{:S(2)}, u32[]{:S(2)}) collective-permute-start(bf16[960,384]{1,0:T(8,128)(2,1)} %get-tuple-element.108.rest_11_), channel_id=1, source_target_pairs={{0,8},{4,12},{8,0},{12,4},{1,9},{5,13},{9,1},{13,5},{2,10},{6,14},... | collective-permute-start | bytes 2211848 | tf_op jit(solution)/shard_map/ppermute | solution.py:998
  130.2 36.0 %collective-permute-start.26 = (bf16[960,384]{1,0:T(8,128)(2,1)}, bf16[960,384]{1,0:T(8,128)(2,1)}, u32[]{:S(2)}, u32[]{:S(2)}) collective-permute-start(bf16[960,384]{1,0:T(8,128)(2,1)} %get-tuple-element.109.rest_12_), channel_id=1, source_target_pairs={{0,12},{4,8},{8,4},{12,0},{1,13},{5,9},{9,5},{13,1},{2,14},{6,10},... | collective-permute-start | bytes 2211848 | tf_op jit(solution)/shard_map/ppermute | solution.py:998
  144.2 12.3 %collective-permute-start.22 = (bf16[1280,384]{1,0:T(8,128)(2,1)}, bf16[1280,384]{1,0:T(8,128)(2,1)S(1)}, u32[]{:S(2)}, u32[]{:S(2)}) collective-permute-start(bf16[1280,384]{1,0:T(8,128)(2,1)} %get-tuple-element.111), channel_id=1, source_target_pairs={{0,16},{16,0},{1,17},{17,1},{2,18},{18,2},{3,19},{19,3},{4,20},{20... | collective-permute-start | bytes 2949128 | tf_op jit(solution)/shard_map/ppermute | solution.py:966
  160.6 10.5 %collective-permute-start.28 = (bf16[256,384]{1,0:T(8,128)(2,1)}, bf16[256,384]{1,0:T(8,128)(2,1)S(1)}, u32[]{:S(2)}, u32[]{:S(2)}) collective-permute-start(bf16[256,384]{1,0:T(8,128)(2,1)} %get-tuple-element.128), channel_id=1, source_target_pairs={{0,4},{4,0},{8,12},{12,8},{1,5},{5,1},{9,13},{13,9},{2,6},{6,2},{1... | collective-permute-start | bytes 589832 | tf_op jit(solution)/shard_map/ppermute | solution.py:998
  161.4 10.2 %collective-permute-start.29 = (bf16[256,384]{1,0:T(8,128)(2,1)}, bf16[256,384]{1,0:T(8,128)(2,1)S(1)}, u32[]{:S(2)}, u32[]{:S(2)}) collective-permute-start(bf16[256,384]{1,0:T(8,128)(2,1)} %get-tuple-element.129), channel_id=1, source_target_pairs={{0,8},{4,12},{8,0},{12,4},{1,9},{5,13},{9,1},{13,5},{2,10},{6,14},... | collective-permute-start | bytes 589832 | tf_op jit(solution)/shard_map/ppermute | solution.py:998
  162.6 10.3 %collective-permute-start.30 = (bf16[256,384]{1,0:T(8,128)(2,1)}, bf16[256,384]{1,0:T(8,128)(2,1)S(1)}, u32[]{:S(2)}, u32[]{:S(2)}) collective-permute-start(bf16[256,384]{1,0:T(8,128)(2,1)} %get-tuple-element.130), channel_id=1, source_target_pairs={{0,12},{4,8},{8,4},{12,0},{1,13},{5,9},{9,5},{13,1},{2,14},{6,10},... | collective-permute-start | bytes 589832 | tf_op jit(solution)/shard_map/ppermute | solution.py:998
  169.5 15.3 %collective-permute-start.37 = (bf16[480,384]{1,0:T(8,128)(2,1)}, bf16[480,384]{1,0:T(8,128)(2,1)S(1)}, u32[]{:S(2)}, u32[]{:S(2)}) collective-permute-start(bf16[480,384]{1,0:T(8,128)(2,1)} %get-tuple-element.126.refs_1_), channel_id=1, source_target_pairs={{0,1},{1,0},{2,3},{3,2},{4,5},{5,4},{6,7},{7,6},{8,9},{9,8},{10,11... | collective-permute-start | bytes 1105928 | tf_op jit(solution)/shard_map/ppermute | solution.py:1129
  179.8 9.5 %collective-permute-start.31 = (bf16[192,384]{1,0:T(8,128)(2,1)S(1)}, bf16[192,384]{1,0:T(8,128)(2,1)S(1)}, u32[]{:S(2)}, u32[]{:S(2)}) collective-permute-start(bf16[192,384]{1,0:T(8,128)(2,1)S(1)} %copy-done.35), channel_id=1, source_target_pairs={{0,1},{1,0},{2,3},{3,2},{4,5},{5,4},{6,7},{7,6},{8,9},{9,8},{10,11... | collective-permute-start | bytes 442376 | tf_op jit(solution)/shard_map/ppermute | solution.py:998
  181.3 17.9 %collective-permute-start.32 = (bf16[192,384]{1,0:T(8,128)(2,1)S(1)}, bf16[192,384]{1,0:T(8,128)(2,1)S(1)}, u32[]{:S(2)}, u32[]{:S(2)}) collective-permute-start(bf16[192,384]{1,0:T(8,128)(2,1)S(1)} %copy-done.34), channel_id=1, source_target_pairs={{0,2},{1,3},{2,0},{3,1},{4,6},{5,7},{6,4},{7,5},{8,10},{9,11},{10,... | collective-permute-start | bytes 442376 | tf_op jit(solution)/shard_map/ppermute | solution.py:998
  183.9 15.3 %collective-permute-start.33 = (bf16[192,384]{1,0:T(8,128)(2,1)S(1)}, bf16[192,384]{1,0:T(8,128)(2,1)S(1)}, u32[]{:S(2)}, u32[]{:S(2)}) collective-permute-start(bf16[192,384]{1,0:T(8,128)(2,1)S(1)} %copy-done.33), channel_id=1, source_target_pairs={{0,3},{1,2},{2,1},{3,0},{4,7},{5,6},{6,5},{7,4},{8,11},{9,10},{10,... | collective-permute-start | bytes 442376 | tf_op jit(solution)/shard_map/ppermute | solution.py:998
  187.6 19.1 %collective-permute-start.38 = (bf16[240,384]{1,0:T(8,128)(2,1)}, bf16[240,384]{1,0:T(8,128)(2,1)S(1)}, u32[]{:S(2)}, u32[]{:S(2)}) collective-permute-start(bf16[240,384]{1,0:T(8,128)(2,1)} %get-tuple-element.139), channel_id=1, source_target_pairs={{0,2},{1,3},{2,0},{3,1},{4,6},{5,7},{6,4},{7,5},{8,10},{9,11},{10,... | collective-permute-start | bytes 552968 | tf_op jit(solution)/shard_map/ppermute | solution.py:1129
  199.3 19.4 %collective-permute-start.36 = (bf16[48,384]{1,0:T(8,128)(2,1)S(1)}, bf16[48,384]{1,0:T(8,128)(2,1)S(1)}, u32[]{:S(2)}, u32[]{:S(2)}) collective-permute-start(bf16[48,384]{1,0:T(8,128)(2,1)S(1)} %add_convert_fusion.1.refs_1_), channel_id=1, source_target_pairs={{0,2},{1,3},{2,0},{3,1},{4,6},{5,7},{6,4},{7,5},{8,10},{9,11},{10,... | collective-permute-start | bytes 110600 | tf_op jit(solution)/shard_map/ppermute | solution.py:1031
  204.1 14.6 %collective-permute-start.35 = (bf16[48,384]{1,0:T(8,128)(2,1)S(1)}, bf16[48,384]{1,0:T(8,128)(2,1)S(1)}, u32[]{:S(2)}, u32[]{:S(2)}) collective-permute-start(bf16[48,384]{1,0:T(8,128)(2,1)S(1)} %add_convert_fusion.1.refs_1_), channel_id=1, source_target_pairs={{0,3},{1,2},{2,1},{3,0},{4,7},{5,6},{6,5},{7,4},{8,11},{9,10},{10,... | collective-permute-start | bytes 110600 | tf_op jit(solution)/shard_map/ppermute | solution.py:1031
  205.4 13.3 %collective-permute-start.34 = (bf16[48,384]{1,0:T(8,128)(2,1)S(1)}, bf16[48,384]{1,0:T(8,128)(2,1)S(1)}, u32[]{:S(2)}, u32[]{:S(2)}) collective-permute-start(bf16[48,384]{1,0:T(8,128)(2,1)S(1)} %add_convert_fusion.1.refs_1_), channel_id=1, source_target_pairs={{0,1},{1,0},{2,3},{3,2},{4,5},{5,4},{6,7},{7,6},{8,9},{9,8},{10,11... | collective-permute-start | bytes 110600 | tf_op jit(solution)/shard_map/ppermute | solution.py:1031
  208.5 10.0 %collective-permute-start.39 = (bf16[240,384]{1,0:T(8,128)(2,1)S(1)}, bf16[240,384]{1,0:T(8,128)(2,1)S(1)}, u32[]{:S(2)}, u32[]{:S(2)}) collective-permute-start(bf16[240,384]{1,0:T(8,128)(2,1)S(1)} %add_convert_fusion), channel_id=1, source_target_pairs={{0,2},{1,3},{2,0},{3,1},{4,6},{5,7},{6,4},{7,5},{8,10},{9,11},{10,... | collective-permute-start | bytes 552968 | tf_op jit(solution)/shard_map/ppermute | solution.py:1129
  218.6 10.1 %collective-permute-start.40 = (bf16[480,384]{1,0:T(8,128)(2,1)S(1)}, bf16[480,384]{1,0:T(8,128)(2,1)S(1)}, u32[]{:S(2)}, u32[]{:S(2)}) collective-permute-start(bf16[480,384]{1,0:T(8,128)(2,1)S(1)} %maximum_select_fusion.4), channel_id=1, source_target_pairs={{0,1},{1,0},{2,3},{3,2},{4,5},{5,4},{6,7},{7,6},{8,9},{9,8},{10,11... | collective-permute-start | bytes 1105928 | tf_op jit(solution)/shard_map/ppermute | solution.py:1129
  (55 other events, 391.3 us)

commit v7 on v6

--- a/solution.py
+++ b/solution.py
@@ -173,15 +173,15 @@
         q_pair = qkv[rows, j * pair : (j + 1) * pair] * BF16((pair // 2) ** (-0.5))
         k_pair = qkv[rows, model + j * pair : model + (j + 1) * pair]
         v_pair = qkv[rows, 2 * model + j * pair : 2 * model + (j + 1) * pair]
-        total = None
+        v_turned = v_pair.T
+        parts = []
         for e in range(2):
-            scores = dot_rows(q_pair * masks[e], k_pair) + bias[2 * j + e].astype(F32)
-            raised = jnp.exp(scores - jnp.max(scores, axis=-1, keepdims=True))
-            p = (raised * (1.0 / jnp.sum(raised, axis=-1, keepdims=True))).astype(BF16)
+            scores = dot_rows(k_pair * masks[e], q_pair) + bias[2 * j + e].astype(F32)
+            raised = jnp.exp(scores - jnp.max(scores, axis=0, keepdims=True))
+            p = (raised * (1.0 / jnp.sum(raised, axis=0, keepdims=True))).astype(BF16)
             probs[b, 2 * j + e] = p
-            part = dot(p, v_pair * masks[e])
-            total = part if total is None else total + part
-        att[rows, j * pair : (j + 1) * pair] = total.astype(BF16)
+            parts.append(dot(v_turned[e * (pair // 2) : (e + 1) * (pair // 2), :], p))
+        att[rows, j * pair : (j + 1) * pair] = jnp.concatenate(parts, axis=0).astype(BF16).T
     out = dot(att[rows, :], w_proj[...]) + b_proj[...]
     branch[rows, :] = out
     middle[rows, :] = x + mod[b, 2:3, :] * out
@@ -262,21 +262,22 @@
         k_pair = qkv[rows, model + j * pair : model + (j + 1) * pair]
         v_pair = qkv[rows, 2 * model + j * pair : 2 * model + (j + 1) * pair]
         d_pair = d_att[:, j * pair : (j + 1) * pair]
-        d_q = d_k = d_v = None
+        k_turned = k_pair.T
+        d_k = d_v = None
+        q_parts = []
         for e in range(2):
             p_low = probs[b, 2 * j + e]
             p = p_low.astype(F32)
-            d_here = d_pair * masks[e]
-            d_p = dot_rows(d_here, v_pair)
-            d_s = (p * (d_p - jnp.sum(d_p * p, axis=-1, keepdims=True))).astype(BF16)
+            d_p = dot_rows(v_pair * masks[e], d_pair)
+            d_s = (p * (d_p - jnp.sum(d_p * p, axis=0, keepdims=True))).astype(BF16)
             score_sum[2 * j + e] += d_s.astype(F32)
-            v_part = dot_cols(p_low, d_here)
-            q_part = dot(d_s, k_pair * masks[e])
-            k_part = dot_cols(d_s, q_pair * masks[e])
+            v_part = dot(p_low, d_pair * masks[e])
+            k_part = dot(d_s, q_pair * masks[e])
+            q_parts.append(dot(k_turned[e * (pair // 2) : (e + 1) * (pair // 2), :], d_s))
             d_v = v_part if d_v is None else d_v + v_part
-            d_q = q_part if d_q is None else d_q + q_part
             d_k = k_part if d_k is None else d_k + k_part
-        d_qkv[rows, j * pair : (j + 1) * pair] = (d_q * scale).astype(BF16)
+        d_q = jnp.concatenate(q_parts, axis=0) * scale
+        d_qkv[rows, j * pair : (j + 1) * pair] = d_q.astype(BF16).T
         d_qkv[rows, model + j * pair : model + (j + 1) * pair] = (d_k * scale).astype(BF16)
         d_qkv[rows, 2 * model + j * pair : 2 * model + (j + 1) * pair] = d_v.astype(BF16)
     small[b, 3:4, :] = col_sum(d_qkv[rows, :model].astype(F32))
@@ -520,7 +521,7 @@
         out_specs=[pl.BlockSpec(memory_space=pltpu.VMEM) for _ in outs],
         scratch_shapes=shapes,
         cost_estimate=cost(work),
-        compiler_params=pltpu.CompilerParams(vmem_limit_bytes=VMEM_BYTES),
+        compiler_params=pltpu.CompilerParams(vmem_limit_bytes=VMEM_BYTES, fuse_transposed_lhs_in_matmul=True),
     )(pos, *operands, *in_hbm)
 
 
@@ -586,7 +587,8 @@
 
 
 def partial_kernel(pos, w_ada, cond_a, cond_b, cond_c, cond_d, b_ada, b_qv, b_proj, b_fc1, b_fc2, *rest):
-    outs, whole = rest[-5:-1], rest[-1]
+    copied, outs, whole = rest[-6], rest[-5:-1], rest[-1]
+    copied[...] = w_ada[...]
     shard = pos[1]
     q, wide = w_ada.shape
     samples, model = cond_a.shape
@@ -613,12 +615,13 @@
     q, wide = w_ada.shape
     samples, model = conds[0].shape
     return call(
-        partial_kernel, pos, (w_ada, *conds, *biases), earlier, [((samples, wide + 2 * model), F32)] * 4,
+        partial_kernel, pos, (w_ada, *conds, *biases), earlier, [(w_ada.shape, BF16)] + [((samples, wide + 2 * model), F32)] * 4,
         [((4 * q, wide), BF16)],
     )
 
 
-def line_kernel(pos, own, got_a, got_b, got_c, keep, send, total):
+def line_kernel(pos, own, got_a, got_b, got_c, *rest):
+    keep, send, total = rest[-3:]
     section = pos[0]
     samples = own.shape[0]
     each = samples // 2
@@ -632,10 +635,10 @@
             out[:, at : at + 2 * model] = total[row : row + 1, 6 * model :]
 
 
-def line_step(pos, own, got):
+def line_step(pos, own, got, earlier):
     samples, model = own.shape[0], own.shape[1] // 8
     shape = (1, (3 * samples + 8) * model)
-    return call(line_kernel, pos, (own, *got), (), [(shape, F32)] * 2, [(own.shape, F32)])
+    return call(line_kernel, pos, (own, *got), earlier, [(shape, F32)] * 2, [(own.shape, F32)])
 
 
 def first_kernel(keep1, other1, keep_m, other_m, own, *messages):
@@ -1063,6 +1066,7 @@
     live = (jnp.arange(half)[:, None, None] < lax.dynamic_index_in_dim(micro_sizes[0], section, 0)).astype(BF16)
     h0 = own_samples(inputs).reshape(half * length, model)
     grad1 = (own_samples(cotangent) * live).reshape(half * length, model)
+    index = relative_bias_index.T
     own_raw = [w_qkv[0], w_proj[0], w_fc1[0], w_fc2[0]]
     width = model // shards
     if direct:
@@ -1071,14 +1075,13 @@
         middle_row = own_pack.shape[0] // 2
         got_x = lax.ppermute(own_pack, "fsdp", pairs_of(shards, 1))
         got_y = lax.ppermute(own_pack, "fsdp", pairs_of(shards, 2))
-        partial = partial_step(pos, w_ada[0], conds, (b_ada, b_qv, b_proj, b_fc1, b_fc2), [own_pack])
-        table = after([bias_table[0]], [own_pack])[0]
-        bias_own = lookup(table, relative_bias_index, [h0, grad1, *partial])
+        bias_own = lookup(bias_table[0], index, [own_pack, *conds[1:]])
+        w_ada_copy, *partial = partial_step(pos, w_ada[0], conds, (b_ada, b_qv, b_proj, b_fc1, b_fc2), [bias_own])
         got_first = lax.ppermute(got_x[:middle_row], "fsdp", pairs_of(shards, 2))
         got_second = lax.ppermute(got_y[middle_row:], "fsdp", pairs_of(shards, 1))
         own_weights = [own_pack, got_x, got_y, got_first, got_second]
         weights = own_weights + [swap_section(w) for w in own_weights]
-        own_line, send_line = line_step(pos, partial[0], after(to_peers(partial[1:], "fsdp"), [got_x, got_y]))
+        own_line, send_line = line_step(pos, partial[0], after(to_peers(partial[1:], "fsdp"), [got_x, got_y]), [h0, grad1])
     else:
         row = jnp.concatenate([b_ada, b_qv, b_proj, b_fc1, b_fc2], axis=1)
         bias_rows = lax.all_gather(row[0], "fsdp", axis=0)
@@ -1087,7 +1090,7 @@
         weights = [own_whole, swap_section(own_whole)]
         acts = jax.nn.silu(conditioning.astype(F32)).astype(BF16)
         modulation = dot(acts, lax.all_gather(w_ada[0], "fsdp", axis=0, tiled=True))
-        bias_own = lookup(bias_table[0], relative_bias_index, [])
+        bias_own = lookup(bias_table[0], index, [])
         cuts = [b_ada.shape[1], b_qv.shape[1], b_proj.shape[1], b_fc1.shape[1], b_fc2.shape[1]]
         biases, at = [], 0
         for cut in cuts:
@@ -1101,7 +1104,7 @@
     bias_heads = (bias_own, swap_section(bias_own))
 
     if direct:
-        w_ada_later = after([w_ada[0]], weights[3:5])[0]
+        w_ada_later = after([w_ada_copy], weights[3:5])[0]
         w_ada_pieces = [w_ada_later] + from_peers(w_ada_later, "fsdp")
     else:
         w_ada_pieces = [lax.all_gather(w_ada[0], "fsdp", axis=0, tiled=True)]
@@ -1132,7 +1135,7 @@
         return jnp.where(bit == 0, jnp.concatenate([own, other]), jnp.concatenate([other, own]))
 
     if direct:
-        kept_small, send_small = small_step(pos, scores0, scores1, relative_bias_index, smalls, [])
+        kept_small, send_small = small_step(pos, scores0, scores1, index, smalls, [])
         other_small = swap_section(send_small)
         other_a0 = after([swap_section(send_a0)], [kept_small])[0]
         own_a0, own_small, *messages = plane_step(pos, keep_a0, other_a0, kept_small, other_small, conditioning)
@@ -1162,7 +1165,7 @@
         )
     else:
         other_a0 = swap_section(send_a0)
-        kept_small, send_small = small_step(pos, scores0, scores1, relative_bias_index, smalls, [])
+        kept_small, send_small = small_step(pos, scores0, scores1, index, smalls, [])
         theirs = swap_section(send_small).astype(F32)
         both = kept_small + theirs
         cut = half * 8

time: 235 us -> 236 us (level)
  Pallas kernels: 119 us -> 126 us
  waiting for transfers between devices: 48.3 us -> 44.5 us
    pallas_call x14, Pallas kernels: 100 us -> 108 us  [call(): pl.pallas_call(kernel, out_shape=[jax.ShapeDtypeStruct(shape, dtype) for...]
    unnamed x91 -> x82, local copies, waits for them, and re-layouts: 12 us -> 9.53 us
    ppermute x9, waiting for transfers between devices: 4.96 us -> 2.6 us  [from_peers(): lax.ppermute(value, axis, pairs_of(lax.axis_size(axis), p))]
  transfers between devices with their start and end apart: 42 -> 42, of which waited for: 15 -> 12; matrix products, arithmetic and copies ran while one was open for 5% -> 7% of each run, Pallas kernels for 36% -> 38%
where the time goes in v7:
time: 236 us
  Pallas kernels  126 us (53%)
  waiting for transfers between devices  44.5 us (19%)
  starting transfers between devices  40.9 us (17%)
  local copies, waits for them, and re-layouts  13.8 us (6%)
  other arithmetic  9.52 us (4%)
    pallas_call x14, Pallas kernels, call(): pl.pallas_call(kernel, out_shape=[jax.ShapeDtypeStruct(shape, dtype) for...  108 us
    ppermute x4, waiting for transfers between devices, replica(): return lax.ppermute(value, 'rep', pairs_of(replicas, step))  15.1 us
    ppermute x12, starting transfers between devices, to_peers(): lax.ppermute(messages[p - 1], axis, pairs_of(count, p))  14.9 us
    ppermute x9, starting transfers between devices, from_peers(): lax.ppermute(value, axis, pairs_of(lax.axis_size(axis), p))  14.2 us
    ppermute x12, waiting for transfers between devices, to_peers(): lax.ppermute(messages[p - 1], axis, pairs_of(count, p))  12 us
    pallas_call x1, Pallas kernels, lookup(): pl.pallas_call(lookup_kernel, out_shape=jax.ShapeDtypeStruct((heads, leng...  11.2 us
    ppermute x1, waiting for transfers between devices, per_device(): got_first = lax.ppermute(got_x[:middle_row], 'fsdp', pairs_of(shards, 2))  9.89 us
    unnamed x82, local copies, waits for them, and re-layouts  9.53 us
  transfers between devices with their start and end apart: 42, of which 12 were waited for; matrix products, arithmetic and copies ran while one was open for 7% of the time, Pallas kernels for 38%

profile of v7, /device:TPU:0, one launch (start us, length us, event | category | flops | bytes accessed | tf_op | source)
XLA Modules:
  0.0 235.6 jit_solution(12436924354943566225)
XLA Ops:
  0.7 3.0 %collective-permute-start = (bf16[4,384]{1,0:T(4,128)(2,1)}, bf16[4,384]{1,0:T(4,128)(2,1)S(1)}, u32[]{:S(2)}, u32[]{:S(2)}) collective-permute-start(bf16[4,384]{1,0:T(4,128)(2,1)} %cond.3), channel_id=1, source_target_pairs={{0,4},{4,0},{8,12},{12,8},{1,5},{5,1},{9,13},{13,9},{2,6},{6,2},{1... | collective-permute-start | bytes 9224 | tf_op jit(solution)/shard_map/ppermute | solution.py:1034
  5.2 2.2 shard_map.263.rest_0_
  7.4 1.9 collective-permute-start.6
  13.1 11.2 %shard_map.264.rest_0_.own_bias = bf16[6,256,256]{2,1,0:T(8,128)(2,1)} custom-call(bf16[128,64]{1,0:T(8,128)(2,1)} %bitcast.76, s32[256,256]{1,0:T(8,128)} %bitcast.65, bf16[1152,384]{1,0:T(8,128)(2,1)} %shard_map.263.rest_0_, bf16[4,384]{1,0:T(4,128)(2,1)} %copy-done.37, bf16[4,384]{1,0:T(4,128)(2,1)} %copy-done.38, bf16[4,384]{1,0:T(4,128)(2,1)} %copy-done.39), custom_call_target="tpu_custom_call" | custom-call | flops 11000000512 | tf_op jit(solution)/shard_map/pallas_call | solution.py:957
  24.9 3.6 %shard_map.265 = (bf16[96,2304]{1,0:T(8,128)(2,1)}, f32[4,3072]{1,0:T(4,128)}, f32[4,3072]{1,0:T(4,128)}, f32[4,3072]{1,0:T(4,128)}, f32[4,3072]{1,0:T(4,128)}) custom-call(s32[3]{0:T(128)} %pad_add_fusion.pos, bf16[96,2304]{1,0:T(8,128)(2,1)} %bitcast.78, bf16[4,384]{1,0:T(4,128)(2,1)} %cond.3, bf16[4,384]{1,0:T(4,128)(2,1)} %copy-done.37, ...), custom_call_target="tpu_custom_call" | custom-call | flops 2000000000 | tf_op jit(solution)/shard_map/pallas_call | solution.py:517
  29.5 2.6 %collective-permute-start.5 = (f32[4,3072]{1,0:T(4,128)}, f32[4,3072]{1,0:T(4,128)S(1)}, u32[]{:S(2)}, u32[]{:S(2)}) collective-permute-start(f32[4,3072]{1,0:T(4,128)} %get-tuple-element.86), channel_id=1, source_target_pairs={{0,12},{4,8},{8,4},{12,0},{1,13},{5,9},{9,5},{13,1},{2,14},{6,10},... | collective-permute-start | bytes 147464 | tf_op jit(solution)/shard_map/ppermute | solution.py:1001
  36.7 9.9 %collective-permute-done.10.refs_1_.rest_3_ = bf16[576,384]{1,0:T(8,128)(2,1)S(1)} collective-permute-done((bf16[576,384]{1,0:T(8,128)(2,1)}, bf16[576,384]{1,0:T(8,128)(2,1)S(1)}, u32[]{:S(2)}, u32[]{:S(2)}) %collective-permute-start.10) | collective-permute-done | bytes 442400 | tf_op jit(solution)/shard_map/ppermute | solution.py:1080
  47.2 2.1 dynamic-slice_multiply_fusion
  56.0 16.6 %shard_map.269 = (bf16[512,1152]{1,0:T(8,128)(2,1)}, bf16[2,6,256,256]{3,2,1,0:T(8,128)(2,1)}, bf16[512,384]{1,0:T(8,128)(2,1)}, f32[512,384]{1,0:T(8,128)}, f32...) custom-call(s32[3]{0:T(128)} %pad_add_fusion.pos, ...), custom_call_target="tpu_custom_call" | custom-call | flops 15000000512 | tf_op jit(solution)/shard_map/pallas_call | solution.py:517
  76.0 29.5 %shard_map.270 = (bf16[512,384]{1,0:T(8,128)(2,1)}, bf16[512,384]{1,0:T(8,128)(2,1)}, f32[2,8,384]{2,1,0:T(8,128)}, f32[2,8,384]{2,1,0:T(8,128)}, bf16[6,256,256...) custom-call(s32[3]{0:T(128)} %pad_add_fusion.pos, bf16[512,384]{1,0:T(8,128)(2,1)} %get-tuple-element.93.h, ...), custom_call_target="tpu_custom_call" | custom-call | flops 24999999488 | tf_op jit(solution)/shard_map/pallas_call | solution.py:517
  105.6 13.4 %shard_map.271 = (f32[512,384]{1,0:T(8,128)}, f32[2,8,384]{2,1,0:T(8,128)}, bf16[1536,384]{1,0:T(8,128)(2,1)}, bf16[1536,384]{1,0:T(8,128)(2,1)}) custom-call(s32[3]{0:T(128)} %pad_add_fusion.pos, bf16[512,384]{1,0:T(8,128)(2,1)} %get-tuple-element.100.grad.d_h1, f32[512,384]{1,0:T(8,128)} %get-tuple-element.101.middle, ...), custom_call_target="tpu_custom_call" | custom-call | flops 12000000000 | tf_op jit(solution)/shard_map/pallas_call | solution.py:517
  119.6 2.8 %collective-permute-done.21.other_m = bf16[1536,384]{1,0:T(8,128)(2,1)} collective-permute-done((bf16[1536,384]{1,0:T(8,128)(2,1)}, bf16[1536,384]{1,0:T(8,128)(2,1)}, u32[]{:S(2)}, u32[]{:S(2)}) %collective-permute-start.21) | collective-permute-done | bytes 1179680 | tf_op jit(solution)/shard_map/ppermute | solution.py:969
  123.7 4.8 %shard_map.272 = (f32[960,384]{1,0:T(8,128)}, bf16[960,384]{1,0:T(8,128)(2,1)}, bf16[960,384]{1,0:T(8,128)(2,1)}, bf16[960,384]{1,0:T(8,128)(2,1)}) custom-call(bf16[2304,384]{1,0:T(8,128)(2,1)} %get-tuple-element.106.keep1, bf16[2816,384]{1,0:T(8,128)(2,1)} %copy-done.1, bf16[1536,384]{1,0:T(8,128)(2,1)} %get-tuple-element.107.keep_m, ...), custom_call_target="tpu_custom_call" | custom-call | tf_op jit(solution)/shard_map/pallas_call | solution.py:663
  132.0 13.2 %shard_map.273 = (f32[512,384]{1,0:T(8,128)}, f32[2,8,384]{2,1,0:T(8,128)}, bf16[6,256,256]{2,1,0:T(8,128)(2,1)}, bf16[768,384]{1,0:T(8,128)(2,1)}, bf16[1280,384]{1,0:T(8,128)(2,1)}) custom-call(s32[3]{0:T(128)} %pad_add_fusion.pos, bf16[512,384]{1,0:T(8,128)(2,1)} %bitcast.59, f32[1,7680]{1,0:T(1,128)} %get-tuple-element.90.own_line, ...), custom_call_target="tpu_custom_call" | custom-call | flops 12999999488 | tf_op jit(solution)/shard_map/pallas_call | solution.py:517
  145.3 11.6 %shard_map.274 = (f32[48,384]{1,0:T(8,128)}, bf16[48,384]{1,0:T(8,128)(2,1)}) custom-call(s32[3]{0:T(128)} %pad_add_fusion.pos, bf16[6,256,256]{2,1,0:T(8,128)(2,1)} %get-tuple-element.114.scores0, bf16[6,256,256]{2,1,0:T(8,128)(2,1)} %get-tuple-element.115.scores1, s32[256,256]{1,0:T(8,128)} %bitcast.66, f32[2,8,384]{2,1,0:T(8,128)} %get-tuple-element.116.small_a0, ...), custom_call_target="tpu_custom_call" | custom-call | flops 12000000000 | tf_op jit(solution)/shard_map/pallas_call | solution.py:517
  159.1 2.4 %shard_map.276 = (f32[192,384]{1,0:T(8,128)}, bf16[64,384]{1,0:T(8,128)(2,1)}, bf16[256,384]{1,0:T(8,128)(2,1)}, bf16[256,384]{1,0:T(8,128)(2,1)}, bf16[256,384]{1,0:T(8,128)(2,1)}) custom-call(s32[3]{0:T(128)} %pad_add_fusion.pos, bf16[768,384]{1,0:T(8,128)(2,1)} %get-tuple-element.121.keep, bf16[1280,384]{1,0:T(8,128)(2,1)} %shard_map.275.other, ...), custom_call_target="tpu_custom_call" | custom-call | flops 2000000000 | tf_op jit(solution)/shard_map/pallas_call | solution.py:517
  167.2 3.3 %shard_map.278 = (f32[480,384]{1,0:T(8,128)}, bf16[480,384]{1,0:T(8,128)(2,1)}) custom-call(s32[3]{0:T(128)} %pad_add_fusion.pos, f32[960,384]{1,0:T(8,128)} %get-tuple-element.124.own, bf16[960,384]{1,0:T(8,128)(2,1)} %get-tuple-element.125.got_a, bf16[960,384]{1,0:T(8,128)(2,1)} %get-tuple-element.126.got_b, bf16[960,384]{1,0:T(8,128)(2,1)} %get-tuple-element.127.got_c), custom_call_target="tpu_custom_call" | custom-call | flops 2000000000 | tf_op jit(solution)/shard_map/pallas_call | solution.py:517
  170.5 1.6 collective-permute-start.37
  172.1 2.1 collective-permute-done.29.got_b
  174.9 2.1 shard_map.281
  177.0 2.8 %shard_map.280 = f32[4,384]{1,0:T(4,128)} custom-call(s32[3]{0:T(128)} %pad_add_fusion.pos, bf16[64,384]{1,0:T(8,128)(2,1)} %shard_map.279.small, bf16[4,384]{1,0:T(4,128)(2,1)} %cond.3, bf16[96,2304]{1,0:T(8,128)(2,1)} %shard_map.268.rest_10_.rest_0_, bf16[96,2304]{1,0:T(8,128)(2,1)} %copy-done.25, bf16[96,2304]{1,0:T(8,128)(2,1)} %copy-done.26, ...), custom_call_target="tpu_custom_call" | custom-call | flops 2000000000 | tf_op jit(solution)/shard_map/pallas_call | solution.py:517
  181.1 1.6 collective-permute-start.31
  182.6 2.6 %collective-permute-start.32 = (bf16[192,384]{1,0:T(8,128)(2,1)S(1)}, bf16[192,384]{1,0:T(8,128)(2,1)S(1)}, u32[]{:S(2)}, u32[]{:S(2)}) collective-permute-start(bf16[192,384]{1,0:T(8,128)(2,1)S(1)} %copy-done.33), channel_id=1, source_target_pairs={{0,2},{1,3},{2,0},{3,1},{4,6},{5,7},{6,4},{7,5},{8,10},{9,11},{10,... | collective-permute-start | bytes 442376 | tf_op jit(solution)/shard_map/ppermute | solution.py:1001
  186.8 2.1 shard_map.284
  188.9 1.7 collective-permute-start.38
  190.6 9.9 %collective-permute-done.32.got_b = bf16[192,384]{1,0:T(8,128)(2,1)S(1)} collective-permute-done((bf16[192,384]{1,0:T(8,128)(2,1)S(1)}, bf16[192,384]{1,0:T(8,128)(2,1)S(1)}, u32[]{:S(2)}, u32[]{:S(2)}) %collective-permute-start.32) | collective-permute-done | bytes 147488 | tf_op jit(solution)/shard_map/ppermute | solution.py:1001
  200.6 4.8 %collective-permute-start.36 = (bf16[48,384]{1,0:T(8,128)(2,1)S(1)}, bf16[48,384]{1,0:T(8,128)(2,1)S(1)}, u32[]{:S(2)}, u32[]{:S(2)}) collective-permute-start(bf16[48,384]{1,0:T(8,128)(2,1)S(1)} %add_convert_fusion.1.refs_1_), channel_id=1, source_target_pairs={{0,2},{1,3},{2,0},{3,1},{4,6},{5,7},{6,4},{7,5},{8,10},{9,11},{10,... | collective-permute-start | bytes 110600 | tf_op jit(solution)/shard_map/ppermute | solution.py:1034
  209.8 1.8 collective-permute-start.39
  211.6 2.8 %shard_map.282 = (f32[96,2304]{1,0:T(8,128)}, f32[1,576]{1,0:T(1,128)}, f32[1,192]{1,0:T(1,128)}, f32[1,96]{1,0:T(1,128)}, f32[1,384]{1,0:T(1,128)}, /*index=5*/f32[1,96]{1,0:T(1,128)}, f32[6,961]{1,0:T(8,128)}) custom-call(s32[3]{0:T(128)} %pad_add_fusion.pos, bf16[144,384]{1,0:T(8,128)(2,1)} %get-tuple-element.133.own_small.refs_1_, ...), custom_call_target="tpu_custom_call" | custom-call | flops 2000000000 | tf_op jit(solution)/shard_map/pallas_call | solution.py:517
  215.8 3.9 %collective-permute-done.39 = bf16[240,384]{1,0:T(8,128)(2,1)S(1)} collective-permute-done((bf16[240,384]{1,0:T(8,128)(2,1)S(1)}, bf16[240,384]{1,0:T(8,128)(2,1)S(1)}, u32[]{:S(2)}, u32[]{:S(2)}) %collective-permute-start.39) | collective-permute-done | bytes 184352 | tf_op jit(solution)/shard_map/ppermute | solution.py:1132
  220.1 9.9 %collective-permute-done.40 = bf16[480,384]{1,0:T(8,128)(2,1)S(1)} collective-permute-done((bf16[480,384]{1,0:T(8,128)(2,1)S(1)}, bf16[480,384]{1,0:T(8,128)(2,1)S(1)}, u32[]{:S(2)}, u32[]{:S(2)}) %collective-permute-start.40) | collective-permute-done | bytes 368672 | tf_op jit(solution)/shard_map/ppermute | solution.py:1132
  233.1 2.5 %shard_map.286 = (f32[96,1152]{1,0:T(8,128)}, f32[96,384]{1,0:T(8,128)}, f32[96,1536]{1,0:T(8,128)}, f32[384,384]{1,0:T(8,128)}) custom-call(s32[3]{0:T(128)} %pad_add_fusion.pos, bf16[192,384]{1,0:T(8,128)(2,1)} %slice_select_fusion.1.own_a, bf16[384,384]{1,0:T(8,128)(2,1)} %slice_select_fusion.own_m, bf16[576,384]{1,0:T(8,128)(2,1)} %copy-done.28), custom_call_target="tpu_custom_call" | custom-call | flops 2000000000 | tf_op jit(solution)/shard_map/pallas_call | solution.py:517
  (189 shorter events, 48.1 us)
Async XLA Ops:
  0.7 11.8 %collective-permute-start = (bf16[4,384]{1,0:T(4,128)(2,1)}, bf16[4,384]{1,0:T(4,128)(2,1)S(1)}, u32[]{:S(2)}, u32[]{:S(2)}) collective-permute-start(bf16[4,384]{1,0:T(4,128)(2,1)} %cond.3), channel_id=1, source_target_pairs={{0,4},{4,0},{8,12},{12,8},{1,5},{5,1},{9,13},{13,9},{2,6},{6,2},{1... | collective-permute-start | bytes 9224 | tf_op jit(solution)/shard_map/ppermute | solution.py:1034
  3.7 8.8 %collective-permute-start.1 = (bf16[4,384]{1,0:T(4,128)(2,1)}, bf16[4,384]{1,0:T(4,128)(2,1)S(1)}, u32[]{:S(2)}, u32[]{:S(2)}) collective-permute-start(bf16[4,384]{1,0:T(4,128)(2,1)} %cond.3), channel_id=1, source_target_pairs={{0,8},{4,12},{8,0},{12,4},{1,9},{5,13},{9,1},{13,5},{2,10},{6,14},... | collective-permute-start | bytes 9224 | tf_op jit(solution)/shard_map/ppermute | solution.py:1034
  7.4 22.1 %collective-permute-start.6 = (bf16[1152,384]{1,0:T(8,128)(2,1)}, bf16[1152,384]{1,0:T(8,128)(2,1)S(1)}, u32[]{:S(2)}, u32[]{:S(2)}) collective-permute-start(bf16[1152,384]{1,0:T(8,128)(2,1)} %shard_map.263.rest_0_), channel_id=1, source_target_pairs={{0,4},{4,0},{8,12},{12,8},{1,5},{5,1},{9,13},{13,9},{2,6},{6,2},{1... | collective-permute-start | bytes 2654216 | tf_op jit(solution)/shard_map/ppermute | solution.py:1076
  9.4 22.7 %collective-permute-start.7 = (bf16[1152,384]{1,0:T(8,128)(2,1)}, bf16[1152,384]{1,0:T(8,128)(2,1)S(1)}, u32[]{:S(2)}, u32[]{:S(2)}) collective-permute-start(bf16[1152,384]{1,0:T(8,128)(2,1)} %shard_map.263.rest_0_), channel_id=1, source_target_pairs={{0,8},{4,12},{8,0},{12,4},{1,9},{5,13},{9,1},{13,5},{2,10},{6,14},... | collective-permute-start | bytes 2654216 | tf_op jit(solution)/shard_map/ppermute | solution.py:1077
  24.3 10.6 %collective-permute-start.9 = (bf16[6,256,256]{2,1,0:T(8,128)(2,1)}, bf16[6,256,256]{2,1,0:T(8,128)(2,1)}, u32[]{:S(2)}, u32[]{:S(2)}) collective-permute-start(bf16[6,256,256]{2,1,0:T(8,128)(2,1)} %shard_map.264.rest_0_.own_bias), channel_id=1, source_target_pairs={{0,16},{16,0},{1,17},{17,1},{2,18},{18,2},{3,19},{19,3},{4,20},{20... | collective-permute-start | bytes 2359304 | tf_op jit(solution)/shard_map/ppermute | solution.py:969
  32.1 18.8 %collective-permute-start.12 = (bf16[1152,384]{1,0:T(8,128)(2,1)S(1)}, bf16[1152,384]{1,0:T(8,128)(2,1)}, u32[]{:S(2)}, u32[]{:S(2)}) collective-permute-start(bf16[1152,384]{1,0:T(8,128)(2,1)S(1)} %copy-done.5), channel_id=1, source_target_pairs={{0,16},{16,0},{1,17},{17,1},{2,18},{18,2},{3,19},{19,3},{4,20},{20... | collective-permute-start | bytes 2654216 | tf_op jit(solution)/shard_map/ppermute | solution.py:969
  33.9 12.6 %collective-permute-start.10 = (bf16[576,384]{1,0:T(8,128)(2,1)}, bf16[576,384]{1,0:T(8,128)(2,1)S(1)}, u32[]{:S(2)}, u32[]{:S(2)}) collective-permute-start(bf16[576,384]{1,0:T(8,128)(2,1)} %slice.57), channel_id=1, source_target_pairs={{0,8},{4,12},{8,0},{12,4},{1,9},{5,13},{9,1},{13,5},{2,10},{6,14},... | collective-permute-start | bytes 1327112 | tf_op jit(solution)/shard_map/ppermute | solution.py:1080
  34.8 12.4 %collective-permute-start.11 = (bf16[576,384]{1,0:T(8,128)(2,1)}, bf16[576,384]{1,0:T(8,128)(2,1)}, u32[]{:S(2)}, u32[]{:S(2)}) collective-permute-start(bf16[576,384]{1,0:T(8,128)(2,1)} %slice.58), channel_id=1, source_target_pairs={{0,4},{4,0},{8,12},{12,8},{1,5},{5,1},{9,13},{13,9},{2,6},{6,2},{1... | collective-permute-start | bytes 1327112 | tf_op jit(solution)/shard_map/ppermute | solution.py:1081
  34.9 18.1 %collective-permute-start.13 = (bf16[1152,384]{1,0:T(8,128)(2,1)S(1)}, bf16[1152,384]{1,0:T(8,128)(2,1)}, u32[]{:S(2)}, u32[]{:S(2)}) collective-permute-start(bf16[1152,384]{1,0:T(8,128)(2,1)S(1)} %collective-permute-done.6.refs_3_.rest_1_), channel_id=1, source_target_pairs={{0,16},{16,0},{1,17},{17,1},{2,18},{18,2},{3,19},{19,3},{4,20},{20... | collective-permute-start | bytes 2654216 | tf_op jit(solution)/shard_map/ppermute | solution.py:969
  34.9 19.6 %collective-permute-start.14 = (bf16[1152,384]{1,0:T(8,128)(2,1)S(1)}, bf16[1152,384]{1,0:T(8,128)(2,1)}, u32[]{:S(2)}, u32[]{:S(2)}) collective-permute-start(bf16[1152,384]{1,0:T(8,128)(2,1)S(1)} %collective-permute-done.7.refs_4_.rest_2_), channel_id=1, source_target_pairs={{0,16},{16,0},{1,17},{17,1},{2,18},{18,2},{3,19},{19,3},{4,20},{20... | collective-permute-start | bytes 2654216 | tf_op jit(solution)/shard_map/ppermute | solution.py:969
  46.5 9.4 %collective-permute-start.15 = (bf16[576,384]{1,0:T(8,128)(2,1)S(1)}, bf16[576,384]{1,0:T(8,128)(2,1)}, u32[]{:S(2)}, u32[]{:S(2)}) collective-permute-start(bf16[576,384]{1,0:T(8,128)(2,1)S(1)} %collective-permute-done.10.refs_1_.rest_3_), channel_id=1, source_target_pairs={{0,16},{16,0},{1,17},{17,1},{2,18},{18,2},{3,19},{19,3},{4,20},{20... | collective-permute-start | bytes 1327112 | tf_op jit(solution)/shard_map/ppermute | solution.py:969
  52.5 20.2 %collective-permute-start.17 = (bf16[96,2304]{1,0:T(8,128)(2,1)}, bf16[96,2304]{1,0:T(8,128)(2,1)S(1)}, u32[]{:S(2)}, u32[]{:S(2)}) collective-permute-start(bf16[96,2304]{1,0:T(8,128)(2,1)} %shard_map.268.rest_10_.rest_0_), channel_id=1, source_target_pairs={{0,4},{4,0},{8,12},{12,8},{1,5},{5,1},{9,13},{13,9},{2,6},{6,2},{1... | collective-permute-start | bytes 1327112 | tf_op jit(solution)/shard_map/ppermute | solution.py:1034
  53.0 21.0 %collective-permute-start.18 = (bf16[96,2304]{1,0:T(8,128)(2,1)}, bf16[96,2304]{1,0:T(8,128)(2,1)S(1)}, u32[]{:S(2)}, u32[]{:S(2)}) collective-permute-start(bf16[96,2304]{1,0:T(8,128)(2,1)} %shard_map.268.rest_10_.rest_0_), channel_id=1, source_target_pairs={{0,8},{4,12},{8,0},{12,4},{1,9},{5,13},{9,1},{13,5},{2,10},{6,14},... | collective-permute-start | bytes 1327112 | tf_op jit(solution)/shard_map/ppermute | solution.py:1034
  54.5 20.7 %collective-permute-start.19 = (bf16[96,2304]{1,0:T(8,128)(2,1)}, bf16[96,2304]{1,0:T(8,128)(2,1)S(1)}, u32[]{:S(2)}, u32[]{:S(2)}) collective-permute-start(bf16[96,2304]{1,0:T(8,128)(2,1)} %shard_map.268.rest_10_.rest_0_), channel_id=1, source_target_pairs={{0,12},{4,8},{8,4},{12,0},{1,13},{5,9},{9,5},{13,1},{2,14},{6,10},... | collective-permute-start | bytes 1327112 | tf_op jit(solution)/shard_map/ppermute | solution.py:1034
  105.5 16.8 %collective-permute-start.20 = (bf16[2816,384]{1,0:T(8,128)(2,1)}, bf16[2816,384]{1,0:T(8,128)(2,1)S(1)}, u32[]{:S(2)}, u32[]{:S(2)}) collective-permute-start(bf16[2816,384]{1,0:T(8,128)(2,1)} %get-tuple-element.95), channel_id=1, source_target_pairs={{0,16},{16,0},{1,17},{17,1},{2,18},{18,2},{3,19},{19,3},{4,20},{20... | collective-permute-start | bytes 6488072 | tf_op jit(solution)/shard_map/ppermute | solution.py:969
  128.5 35.5 %collective-permute-start.24 = (bf16[960,384]{1,0:T(8,128)(2,1)}, bf16[960,384]{1,0:T(8,128)(2,1)}, u32[]{:S(2)}, u32[]{:S(2)}) collective-permute-start(bf16[960,384]{1,0:T(8,128)(2,1)} %get-tuple-element.109.rest_10_), channel_id=1, source_target_pairs={{0,4},{4,0},{8,12},{12,8},{1,5},{5,1},{9,13},{13,9},{2,6},{6,2},{1... | collective-permute-start | bytes 2211848 | tf_op jit(solution)/shard_map/ppermute | solution.py:1001
  129.8 37.4 %collective-permute-start.25 = (bf16[960,384]{1,0:T(8,128)(2,1)}, bf16[960,384]{1,0:T(8,128)(2,1)}, u32[]{:S(2)}, u32[]{:S(2)}) collective-permute-start(bf16[960,384]{1,0:T(8,128)(2,1)} %get-tuple-element.110.rest_11_), channel_id=1, source_target_pairs={{0,8},{4,12},{8,0},{12,4},{1,9},{5,13},{9,1},{13,5},{2,10},{6,14},... | collective-permute-start | bytes 2211848 | tf_op jit(solution)/shard_map/ppermute | solution.py:1001
  131.0 36.2 %collective-permute-start.26 = (bf16[960,384]{1,0:T(8,128)(2,1)}, bf16[960,384]{1,0:T(8,128)(2,1)}, u32[]{:S(2)}, u32[]{:S(2)}) collective-permute-start(bf16[960,384]{1,0:T(8,128)(2,1)} %get-tuple-element.111.rest_12_), channel_id=1, source_target_pairs={{0,12},{4,8},{8,4},{12,0},{1,13},{5,9},{9,5},{13,1},{2,14},{6,10},... | collective-permute-start | bytes 2211848 | tf_op jit(solution)/shard_map/ppermute | solution.py:1001
  145.2 12.3 %collective-permute-start.22 = (bf16[1280,384]{1,0:T(8,128)(2,1)}, bf16[1280,384]{1,0:T(8,128)(2,1)S(1)}, u32[]{:S(2)}, u32[]{:S(2)}) collective-permute-start(bf16[1280,384]{1,0:T(8,128)(2,1)} %get-tuple-element.113), channel_id=1, source_target_pairs={{0,16},{16,0},{1,17},{17,1},{2,18},{18,2},{3,19},{19,3},{4,20},{20... | collective-permute-start | bytes 2949128 | tf_op jit(solution)/shard_map/ppermute | solution.py:969
  161.6 10.5 %collective-permute-start.28 = (bf16[256,384]{1,0:T(8,128)(2,1)}, bf16[256,384]{1,0:T(8,128)(2,1)S(1)}, u32[]{:S(2)}, u32[]{:S(2)}) collective-permute-start(bf16[256,384]{1,0:T(8,128)(2,1)} %get-tuple-element.130), channel_id=1, source_target_pairs={{0,4},{4,0},{8,12},{12,8},{1,5},{5,1},{9,13},{13,9},{2,6},{6,2},{1... | collective-permute-start | bytes 589832 | tf_op jit(solution)/shard_map/ppermute | solution.py:1001
  162.8 11.3 %collective-permute-start.29 = (bf16[256,384]{1,0:T(8,128)(2,1)}, bf16[256,384]{1,0:T(8,128)(2,1)S(1)}, u32[]{:S(2)}, u32[]{:S(2)}) collective-permute-start(bf16[256,384]{1,0:T(8,128)(2,1)} %get-tuple-element.131), channel_id=1, source_target_pairs={{0,8},{4,12},{8,0},{12,4},{1,9},{5,13},{9,1},{13,5},{2,10},{6,14},... | collective-permute-start | bytes 589832 | tf_op jit(solution)/shard_map/ppermute | solution.py:1001
  164.1 10.1 %collective-permute-start.30 = (bf16[256,384]{1,0:T(8,128)(2,1)}, bf16[256,384]{1,0:T(8,128)(2,1)S(1)}, u32[]{:S(2)}, u32[]{:S(2)}) collective-permute-start(bf16[256,384]{1,0:T(8,128)(2,1)} %get-tuple-element.132), channel_id=1, source_target_pairs={{0,12},{4,8},{8,4},{12,0},{1,13},{5,9},{9,5},{13,1},{2,14},{6,10},... | collective-permute-start | bytes 589832 | tf_op jit(solution)/shard_map/ppermute | solution.py:1001
  170.5 15.6 %collective-permute-start.37 = (bf16[480,384]{1,0:T(8,128)(2,1)}, bf16[480,384]{1,0:T(8,128)(2,1)S(1)}, u32[]{:S(2)}, u32[]{:S(2)}) collective-permute-start(bf16[480,384]{1,0:T(8,128)(2,1)} %get-tuple-element.128.refs_1_), channel_id=1, source_target_pairs={{0,1},{1,0},{2,3},{3,2},{4,5},{5,4},{6,7},{7,6},{8,9},{9,8},{10,11... | collective-permute-start | bytes 1105928 | tf_op jit(solution)/shard_map/ppermute | solution.py:1132
  181.1 9.5 %collective-permute-start.31 = (bf16[192,384]{1,0:T(8,128)(2,1)S(1)}, bf16[192,384]{1,0:T(8,128)(2,1)S(1)}, u32[]{:S(2)}, u32[]{:S(2)}) collective-permute-start(bf16[192,384]{1,0:T(8,128)(2,1)S(1)} %copy-done.34), channel_id=1, source_target_pairs={{0,1},{1,0},{2,3},{3,2},{4,5},{5,4},{6,7},{7,6},{8,9},{9,8},{10,11... | collective-permute-start | bytes 442376 | tf_op jit(solution)/shard_map/ppermute | solution.py:1001
  182.6 17.9 %collective-permute-start.32 = (bf16[192,384]{1,0:T(8,128)(2,1)S(1)}, bf16[192,384]{1,0:T(8,128)(2,1)S(1)}, u32[]{:S(2)}, u32[]{:S(2)}) collective-permute-start(bf16[192,384]{1,0:T(8,128)(2,1)S(1)} %copy-done.33), channel_id=1, source_target_pairs={{0,2},{1,3},{2,0},{3,1},{4,6},{5,7},{6,4},{7,5},{8,10},{9,11},{10,... | collective-permute-start | bytes 442376 | tf_op jit(solution)/shard_map/ppermute | solution.py:1001
  185.2 15.3 %collective-permute-start.33 = (bf16[192,384]{1,0:T(8,128)(2,1)S(1)}, bf16[192,384]{1,0:T(8,128)(2,1)S(1)}, u32[]{:S(2)}, u32[]{:S(2)}) collective-permute-start(bf16[192,384]{1,0:T(8,128)(2,1)S(1)} %copy-done.32), channel_id=1, source_target_pairs={{0,3},{1,2},{2,1},{3,0},{4,7},{5,6},{6,5},{7,4},{8,11},{9,10},{10,... | collective-permute-start | bytes 442376 | tf_op jit(solution)/shard_map/ppermute | solution.py:1001
  188.9 19.1 %collective-permute-start.38 = (bf16[240,384]{1,0:T(8,128)(2,1)}, bf16[240,384]{1,0:T(8,128)(2,1)S(1)}, u32[]{:S(2)}, u32[]{:S(2)}) collective-permute-start(bf16[240,384]{1,0:T(8,128)(2,1)} %get-tuple-element.141), channel_id=1, source_target_pairs={{0,2},{1,3},{2,0},{3,1},{4,6},{5,7},{6,4},{7,5},{8,10},{9,11},{10,... | collective-permute-start | bytes 552968 | tf_op jit(solution)/shard_map/ppermute | solution.py:1132
  200.6 19.4 %collective-permute-start.36 = (bf16[48,384]{1,0:T(8,128)(2,1)S(1)}, bf16[48,384]{1,0:T(8,128)(2,1)S(1)}, u32[]{:S(2)}, u32[]{:S(2)}) collective-permute-start(bf16[48,384]{1,0:T(8,128)(2,1)S(1)} %add_convert_fusion.1.refs_1_), channel_id=1, source_target_pairs={{0,2},{1,3},{2,0},{3,1},{4,6},{5,7},{6,4},{7,5},{8,10},{9,11},{10,... | collective-permute-start | bytes 110600 | tf_op jit(solution)/shard_map/ppermute | solution.py:1034
  205.4 14.6 %collective-permute-start.35 = (bf16[48,384]{1,0:T(8,128)(2,1)S(1)}, bf16[48,384]{1,0:T(8,128)(2,1)S(1)}, u32[]{:S(2)}, u32[]{:S(2)}) collective-permute-start(bf16[48,384]{1,0:T(8,128)(2,1)S(1)} %add_convert_fusion.1.refs_1_), channel_id=1, source_target_pairs={{0,3},{1,2},{2,1},{3,0},{4,7},{5,6},{6,5},{7,4},{8,11},{9,10},{10,... | collective-permute-start | bytes 110600 | tf_op jit(solution)/shard_map/ppermute | solution.py:1034
  206.7 13.3 %collective-permute-start.34 = (bf16[48,384]{1,0:T(8,128)(2,1)S(1)}, bf16[48,384]{1,0:T(8,128)(2,1)S(1)}, u32[]{:S(2)}, u32[]{:S(2)}) collective-permute-start(bf16[48,384]{1,0:T(8,128)(2,1)S(1)} %add_convert_fusion.1.refs_1_), channel_id=1, source_target_pairs={{0,1},{1,0},{2,3},{3,2},{4,5},{5,4},{6,7},{7,6},{8,9},{9,8},{10,11... | collective-permute-start | bytes 110600 | tf_op jit(solution)/shard_map/ppermute | solution.py:1034
  209.8 10.0 %collective-permute-start.39 = (bf16[240,384]{1,0:T(8,128)(2,1)S(1)}, bf16[240,384]{1,0:T(8,128)(2,1)S(1)}, u32[]{:S(2)}, u32[]{:S(2)}) collective-permute-start(bf16[240,384]{1,0:T(8,128)(2,1)S(1)} %add_convert_fusion), channel_id=1, source_target_pairs={{0,2},{1,3},{2,0},{3,1},{4,6},{5,7},{6,4},{7,5},{8,10},{9,11},{10,... | collective-permute-start | bytes 552968 | tf_op jit(solution)/shard_map/ppermute | solution.py:1132
  219.9 10.1 %collective-permute-start.40 = (bf16[480,384]{1,0:T(8,128)(2,1)S(1)}, bf16[480,384]{1,0:T(8,128)(2,1)S(1)}, u32[]{:S(2)}, u32[]{:S(2)}) collective-permute-start(bf16[480,384]{1,0:T(8,128)(2,1)S(1)} %maximum_select_fusion.4), channel_id=1, source_target_pairs={{0,1},{1,0},{2,3},{3,2},{4,5},{5,4},{6,7},{7,6},{8,9},{9,8},{10,11... | collective-permute-start | bytes 1105928 | tf_op jit(solution)/shard_map/ppermute | solution.py:1132
  (51 other events, 359.8 us)

commit v8 on v6

--- a/solution.py
+++ b/solution.py
@@ -331,10 +331,23 @@
         out[...] = jnp.concatenate(parts[layer * heads : (layer + 1) * heads], axis=1)
 
 
-def small_kernel(pos, scores0, scores1, index, small_a0, small_m0, small_a1, small_m1, *rest):
-    keep, send, table0, table1 = rest[-4:]
+def table_kernel(scores, index, out):
+    add_tables((scores,), index, (out,))
+
+
+def table_step(scores, index):
+    return pl.pallas_call(
+        table_kernel,
+        out_shape=jax.ShapeDtypeStruct((HIGH, scores.shape[0] * LOW), F32),
+        cost_estimate=cost(8),
+        compiler_params=pltpu.CompilerParams(vmem_limit_bytes=VMEM_BYTES),
+    )(scores, index)
+
+
+def small_kernel(pos, scores, index, small_a0, small_m0, small_a1, small_m1, table1, *rest):
+    keep, send, table0 = rest[-3:]
     size = small_a0.shape[0] * small_a0.shape[1]
-    add_tables((scores0, scores1), index, (table0, table1))
+    add_tables((scores,), index, (table0,))
     parts = (
         (small_a0[...], small_m0[...], table0[...]),
         (small_a1[...], small_m1[...], table1[...]),
@@ -354,12 +367,12 @@
         send[...] = rows[0].astype(BF16)
 
 
-def small_step(pos, scores0, scores1, index, smalls, earlier):
+def small_step(pos, scores, index, smalls, table1, earlier):
     samples, _, model = smalls[0].shape
     shape = (16 * samples + HIGH, model)
     return call(
-        small_kernel, pos, (scores0, scores1, index, *smalls), earlier, [(shape, F32), (shape, BF16)],
-        [((HIGH, model), F32)] * 2, work=12,
+        small_kernel, pos, (scores, index, *smalls, table1), earlier, [(shape, F32), (shape, BF16)],
+        [((HIGH, model), F32)], work=8,
     )
 
 
@@ -586,7 +599,8 @@
 
 
 def partial_kernel(pos, w_ada, cond_a, cond_b, cond_c, cond_d, b_ada, b_qv, b_proj, b_fc1, b_fc2, *rest):
-    outs, whole = rest[-5:-1], rest[-1]
+    copied, outs, whole = rest[-6], rest[-5:-1], rest[-1]
+    copied[...] = w_ada[...]
     shard = pos[1]
     q, wide = w_ada.shape
     samples, model = cond_a.shape
@@ -613,12 +627,13 @@
     q, wide = w_ada.shape
     samples, model = conds[0].shape
     return call(
-        partial_kernel, pos, (w_ada, *conds, *biases), earlier, [((samples, wide + 2 * model), F32)] * 4,
+        partial_kernel, pos, (w_ada, *conds, *biases), earlier, [(w_ada.shape, BF16)] + [((samples, wide + 2 * model), F32)] * 4,
         [((4 * q, wide), BF16)],
     )
 
 
-def line_kernel(pos, own, got_a, got_b, got_c, keep, send, total):
+def line_kernel(pos, own, got_a, got_b, got_c, *rest):
+    keep, send, total = rest[-3:]
     section = pos[0]
     samples = own.shape[0]
     each = samples // 2
@@ -632,36 +647,136 @@
             out[:, at : at + 2 * model] = total[row : row + 1, 6 * model :]
 
 
-def line_step(pos, own, got):
+def line_step(pos, own, got, earlier):
     samples, model = own.shape[0], own.shape[1] // 8
     shape = (1, (3 * samples + 8) * model)
-    return call(line_kernel, pos, (own, *got), (), [(shape, F32)] * 2, [(own.shape, F32)])
-
-
-def first_kernel(keep1, other1, keep_m, other_m, own, *messages):
-    pieces = 4
-    size1, size_m = keep1.shape[0] // pieces, keep_m.shape[0] // pieces
-    n1, nm = size1 // 4, size_m // 4
-    for p in range(pieces):
-        for k in range(4):
-            at = k * (n1 + nm)
-            for keep, other, first, n, to in (
-                (keep1, other1, p * size1 + k * n1, n1, at), (keep_m, other_m, p * size_m + k * nm, nm, at + n1)
-            ):
-                total = keep[first : first + n, :].astype(F32) + other[first : first + n, :].astype(F32)
-                if p == 0:
-                    own[to : to + n, :] = total
-                else:
-                    messages[p - 1][to : to + n, :] = total.astype(BF16)
-
-
-def first_step(keep1, other1, keep_m, other_m):
-    shape = ((keep1.shape[0] + keep_m.shape[0]) // 4, keep1.shape[1])
+    return call(line_kernel, pos, (own, *got), earlier, [(shape, F32)] * 2, [(own.shape, F32)])
+
+
+def sum_kernel(keep, other, own, *messages):
+    size = own.shape[0]
+    for p in range(4):
+        total = keep[p * size : (p + 1) * size, :].astype(F32) + other[p * size : (p + 1) * size, :].astype(F32)
+        if p == 0:
+            own[...] = total
+        else:
+            messages[p - 1][...] = total.astype(BF16)
+
+
+def sum_step(keep, other):
+    shape = (keep.shape[0] // 4, keep.shape[1])
     return pl.pallas_call(
-        first_kernel,
+        sum_kernel,
         out_shape=[jax.ShapeDtypeStruct(shape, F32)] + [jax.ShapeDtypeStruct(shape, BF16)] * 3,
         compiler_params=pltpu.CompilerParams(vmem_limit_bytes=VMEM_BYTES),
-    )(keep1, other1, keep_m, other_m)
+    )(keep, other)
+
+
+def halve(bit, own, got, keep, send):
+    n = own.shape[0] // 4
+    for high in range(2):
+        for out, low in ((keep, bit), (send, 1 - bit)):
+            rows = pl.ds(pl.multiple_of((2 * high + low) * n, 16), n)
+            total = own[rows, :]
+            for piece in got:
+                total = total + piece[rows, :].astype(F32)
+            out[high * n : (high + 1) * n, :] = total.astype(out.dtype)
+
+
+def quarter(bit, kept, got, keep, send):
+    n = kept.shape[0] // 2
+    for out, high in ((keep, bit), (send, 1 - bit)):
+        rows = pl.ds(pl.multiple_of(high * n, 16), n)
+        out[...] = (kept[rows, :] + got[rows, :].astype(F32)).astype(out.dtype)
+
+
+def pair_up(bit, own, got, out):
+    n = own.shape[0]
+    out[pl.ds(pl.multiple_of(bit * n, 16), n), :] = own[...]
+    out[pl.ds(pl.multiple_of((1 - bit) * n, 16), n), :] = got[...]
+
+
+def whole_from(bit, pair, got, out, at=0):
+    n = pair.shape[0] // 2
+    for high in range(2):
+        rows = slice(high * n, (high + 1) * n)
+        out[pl.ds(pl.multiple_of(at + (2 * high + bit) * n, 16), n), :] = pair[rows, :]
+        out[pl.ds(pl.multiple_of(at + (2 * high + 1 - bit) * n, 16), n), :] = got[rows, :]
+
+
+def a_kernel(pos, own1, got_a, got_b, got_c, keep_m, other_m, keep1, send1, own_m, *messages):
+    halve(pos[2] & 1, own1, (got_a, got_b, got_c), keep1, send1)
+    sum_kernel(keep_m, other_m, own_m, *messages)
+
+
+def a_step(pos, own1, got1, keep_m, other_m):
+    two = (own1.shape[0] // 2, own1.shape[1])
+    one = (keep_m.shape[0] // 4, keep_m.shape[1])
+    return call(a_kernel, pos, (own1, *got1, keep_m, other_m), (), [(two, F32), (two, BF16), (one, F32)] + [(one, BF16)] * 3, [])
+
+
+def b_kernel(pos, kept1, got1, own_m, got_a, got_b, got_c, keep1, send1, keep_m, send_m):
+    quarter(pos[2] >> 1, kept1, got1, keep1, send1)
+    halve(pos[2] & 1, own_m, (got_a, got_b, got_c), keep_m, send_m)
+
+
+def b_step(pos, kept1, got1, own_m, got_m):
+    one, two = (kept1.shape[0] // 2, kept1.shape[1]), (own_m.shape[0] // 2, own_m.shape[1])
+    return call(b_kernel, pos, (kept1, got1, own_m, *got_m), (), [(one, F32), (one, BF16), (two, F32), (two, BF16)], [])
+
+
+def c_kernel(pos, kept1, got1, kept_m, got_m, quarter1, keep_m, send_m):
+    quarter1[...] = (kept1[...] + got1[...].astype(F32)).astype(BF16)
+    quarter(pos[2] >> 1, kept_m, got_m, keep_m, send_m)
+
+
+def c_step(pos, kept1, got1, kept_m, got_m):
+    one = (kept_m.shape[0] // 2, kept_m.shape[1])
+    return call(c_kernel, pos, (kept1, got1, kept_m, got_m), (), [(kept1.shape, BF16), (one, F32), (one, BF16)], [])
+
+
+def d_kernel(pos, quarter1, got1, kept_m, got_m, pair1, quarter_m):
+    pair_up(pos[2] >> 1, quarter1, got1, pair1)
+    quarter_m[...] = (kept_m[...] + got_m[...].astype(F32)).astype(BF16)
+
+
+def d_step(pos, quarter1, got1, kept_m, got_m):
+    two = (2 * quarter1.shape[0], quarter1.shape[1])
+    return call(d_kernel, pos, (quarter1, got1, kept_m, got_m), (), [(two, BF16), (kept_m.shape, BF16)], [])
+
+
+def e_kernel(pos, pair1, got1, quarter_m, got_m, half1, pair_m):
+    whole_from(pos[2] & 1, pair1, got1, half1)
+    pair_up(pos[2] >> 1, quarter_m, got_m, pair_m)
+
+
+def e_step(pos, pair1, got1, quarter_m, got_m):
+    two = (2 * quarter_m.shape[0], quarter_m.shape[1])
+    return call(e_kernel, pos, (pair1, got1, quarter_m, got_m), (), [((2 * pair1.shape[0], pair1.shape[1]), BF16), (two, BF16)], [])
+
+
+def g_kernel(pos, quarter_a, got_a, got_b, got_c, pair_m, got_m, half1, *rest):
+    own, send = rest[-2:]
+    n = quarter_a.shape[0]
+
+    def layer0(out):
+        for j, piece in enumerate((quarter_a, got_a, got_b, got_c)):
+            out[pl.ds(pl.multiple_of((pos[2] ^ j) * n, 16), n), :] = piece[...]
+        whole_from(pos[2] & 1, pair_m, got_m, out, 4 * n)
+
+    @pl.when(pos[0] == 0)
+    def _():
+        layer0(own)
+        send[...] = half1[...]
+
+    @pl.when(pos[0] == 1)
+    def _():
+        layer0(send)
+        own[...] = half1[...]
+
+
+def g_step(pos, quarter_a, got_a, pair_m, got_m, half1, earlier):
+    return call(g_kernel, pos, (quarter_a, *got_a, pair_m, got_m, half1), earlier, [(half1.shape, BF16)] * 2, [])
 
 
 def plane_kernel(samples, pos, keep, other, kept_small, other_small, cond, own, own_small, *rest):
@@ -826,67 +941,33 @@
     )[0]
 
 
-def final_kernel(pos, own_a, own_m, other, g_qkv, g_proj, g_fc1, g_fc2):
-    section = pos[0]
+def final_kernel(pos, own, other, g_qkv, g_proj, g_fc1, g_fc2):
     q, model = g_proj.shape
-    cut = own_a.shape[0]
-
-    def write(first_a, first_m, second_a, second_m):
+
+    def write(first, second):
         for c in range(2):
-            g_qkv[:, c * model : (c + 1) * model] = first_a[c * q : (c + 1) * q, :].astype(F32)
-        g_qkv[:, 2 * model : 3 * model] = second_a[:q, :].astype(F32)
-        g_proj[...] = second_a[q : 2 * q, :].astype(F32)
+            g_qkv[:, c * model : (c + 1) * model] = first[c * q : (c + 1) * q, :].astype(F32)
+        g_qkv[:, 2 * model : 3 * model] = second[:q, :].astype(F32)
+        g_proj[...] = second[q : 2 * q, :].astype(F32)
         for c in range(4):
-            g_fc1[:, c * model : (c + 1) * model] = first_m[c * q : (c + 1) * q, :].astype(F32)
-        g_fc2[...] = second_m[...].astype(F32)
-
-    other_a, other_m = other.at[:cut, :], other.at[cut:, :]
-
-    @pl.when(section == 0)
+            g_fc1[:, c * model : (c + 1) * model] = first[(2 + c) * q : (3 + c) * q, :].astype(F32)
+        g_fc2[...] = second[2 * q : 6 * q, :].astype(F32)
+
+    @pl.when(pos[0] == 0)
     def _():
-        write(own_a, own_m, other_a, other_m)
-
-    @pl.when(section == 1)
+        write(own, other)
+
+    @pl.when(pos[0] == 1)
     def _():
-        write(other_a, other_m, own_a, own_m)
-
-
-def final_step(pos, own_a, own_m, other):
-    q, model = own_a.shape[0] // 2, own_a.shape[1]
+        write(other, own)
+
+
+def final_step(pos, own, other):
+    q, model = own.shape[0] // 6, own.shape[1]
     return call(
-        final_kernel, pos, (own_a, own_m, other), (),
+        final_kernel, pos, (own, other), (),
         [((q, 3 * model), F32), ((q, model), F32), ((q, 4 * model), F32), ((4 * q, model), F32)], [],
     )
-
-
-def halve_kernel(pos, own, got_a, got_b, got_c, keep, send):
-    bit = pos[2] & 1
-    n = own.shape[0] // 4
-    for high in range(2):
-        for out, low in ((keep, bit), (send, 1 - bit)):
-            rows = pl.ds(pl.multiple_of((2 * high + low) * n, 16), n)
-            total = own[rows, :]
-            for piece in (got_a, got_b, got_c):
-                total = total + piece[rows, :].astype(F32)
-            out[high * n : (high + 1) * n, :] = total.astype(out.dtype)
-
-
-def halve_step(pos, own, got):
-    shape = (own.shape[0] // 2, own.shape[1])
-    return call(halve_kernel, pos, (own, *got), (), [(shape, F32), (shape, BF16)], [])
-
-
-def quarter_kernel(pos, kept, got, keep, send):
-    bit = pos[2] >> 1
-    n = kept.shape[0] // 2
-    for out, high in ((keep, bit), (send, 1 - bit)):
-        rows = pl.ds(pl.multiple_of(high * n, 16), n)
-        out[...] = (kept[rows, :] + got[rows, :].astype(F32)).astype(out.dtype)
-
-
-def quarter_step(pos, kept, got):
-    shape = (kept.shape[0] // 2, kept.shape[1])
-    return call(quarter_kernel, pos, (kept, got), (), [(shape, F32), (shape, BF16)], [])
 
 
 def pack_kernel(qkv, proj, fc1, fc2, out):
@@ -1063,6 +1144,7 @@
     live = (jnp.arange(half)[:, None, None] < lax.dynamic_index_in_dim(micro_sizes[0], section, 0)).astype(BF16)
     h0 = own_samples(inputs).reshape(half * length, model)
     grad1 = (own_samples(cotangent) * live).reshape(half * length, model)
+    index = relative_bias_index
     own_raw = [w_qkv[0], w_proj[0], w_fc1[0], w_fc2[0]]
     width = model // shards
     if direct:
@@ -1071,14 +1153,13 @@
         middle_row = own_pack.shape[0] // 2
         got_x = lax.ppermute(own_pack, "fsdp", pairs_of(shards, 1))
         got_y = lax.ppermute(own_pack, "fsdp", pairs_of(shards, 2))
-        partial = partial_step(pos, w_ada[0], conds, (b_ada, b_qv, b_proj, b_fc1, b_fc2), [own_pack])
-        table = after([bias_table[0]], [own_pack])[0]
-        bias_own = lookup(table, relative_bias_index, [h0, grad1, *partial])
+        bias_own = lookup(bias_table[0], index, [own_pack, *conds[1:]])
+        w_ada_copy, *partial = partial_step(pos, w_ada[0], conds, (b_ada, b_qv, b_proj, b_fc1, b_fc2), [bias_own])
         got_first = lax.ppermute(got_x[:middle_row], "fsdp", pairs_of(shards, 2))
         got_second = lax.ppermute(got_y[middle_row:], "fsdp", pairs_of(shards, 1))
         own_weights = [own_pack, got_x, got_y, got_first, got_second]
         weights = own_weights + [swap_section(w) for w in own_weights]
-        own_line, send_line = line_step(pos, partial[0], after(to_peers(partial[1:], "fsdp"), [got_x, got_y]))
+        own_line, send_line = line_step(pos, partial[0], after(to_peers(partial[1:], "fsdp"), [got_x, got_y]), [h0, grad1])
     else:
         row = jnp.concatenate([b_ada, b_qv, b_proj, b_fc1, b_fc2], axis=1)
         bias_rows = lax.all_gather(row[0], "fsdp", axis=0)
@@ -1087,7 +1168,7 @@
         weights = [own_whole, swap_section(own_whole)]
         acts = jax.nn.silu(conditioning.astype(F32)).astype(BF16)
         modulation = dot(acts, lax.all_gather(w_ada[0], "fsdp", axis=0, tiled=True))
-        bias_own = lookup(bias_table[0], relative_bias_index, [])
+        bias_own = lookup(bias_table[0], index, [])
         cuts = [b_ada.shape[1], b_qv.shape[1], b_proj.shape[1], b_fc1.shape[1], b_fc2.shape[1]]
         biases, at = [], 0
         for cut in cuts:
@@ -1101,24 +1182,31 @@
     bias_heads = (bias_own, swap_section(bias_own))
 
     if direct:
-        w_ada_later = after([w_ada[0]], weights[3:5])[0]
+        w_ada_later = after([w_ada_copy], weights[3:5])[0]
         w_ada_pieces = [w_ada_later] + from_peers(w_ada_later, "fsdp")
     else:
         w_ada_pieces = [lax.all_gather(w_ada[0], "fsdp", axis=0, tiled=True)]
     qkv, probs, att, branch, middle, act, slope, out_branch, h1 = forward_layer(0, z, pos, h0, lines, bias_heads, weights, w_ada_pieces[:1] if direct else [])
     out1, d_h1, small_a1, small_m1, scores1, keep1, send1 = both_ways(1, z, pos, h1, grad1, lines, bias_heads, weights, w_ada_pieces[1:])
-    d_middle, small_m0, keep_m0, send_m0 = backward_mlp(0, z, pos, d_h1, middle, lines, act, slope, out_branch, weights, [])
-    pieces = z.pieces
     rows = half * length
-    other1 = swap_section(send1)
+    table1 = table_step(scores1, index)
+    other1 = after([swap_section(send1)], [table1])[0]
+    if direct:
+        own1, *messages = sum_step(keep1, other1)
+        earlier = messages
+    else:
+        earlier = []
+    d_middle, small_m0, keep_m0, send_m0 = backward_mlp(0, z, pos, d_h1, middle, lines, act, slope, out_branch, weights, earlier)
+    if direct:
+        got1 = after(to_peers(messages, "fsdp"), [d_middle])
+        send_m0 = after([send_m0], got1)[0]
     other_m0 = swap_section(send_m0)
     if direct:
-        own_first, *first_messages = first_step(keep1, other1, keep_m0, other_m0)
-        earlier = first_messages
+        keep_z1, send_z1, own_m, *messages = a_step(pos, own1, got1, keep_m0, other_m0)
+        earlier = [send_z1, *messages]
     else:
-        sums1 = section_sums(keep1, other1[: keep1.shape[0]], pieces)
-        sums_m0 = section_sums(keep_m0, other_m0, pieces)
-        earlier = []
+        sums1 = section_sums(keep1, other1[: keep1.shape[0]], z.pieces)
+        sums_m0 = section_sums(keep_m0, other_m0, z.pieces)
     d_h0, small_a0, scores0, keep_a0, send_a0 = backward_attention(
         0, z, pos, h0, lines, qkv, probs, att, branch, d_middle, d_h1, weights, earlier
     )
@@ -1128,41 +1216,36 @@
     def replica(value, step):
         return lax.ppermute(value, "rep", pairs_of(replicas, step))
 
-    def ordered(own, other, bit):
-        return jnp.where(bit == 0, jnp.concatenate([own, other]), jnp.concatenate([other, own]))
-
     if direct:
-        kept_small, send_small = small_step(pos, scores0, scores1, relative_bias_index, smalls, [])
+        got_z1, *got_m = after([replica(send_z1, 1), *to_peers(messages, "fsdp")], [d_h0])
+        other_a0 = swap_section(after([send_a0], [got_z1, *got_m])[0])
+        keep_z1, send_z1, keep_zm, send_zm = b_step(pos, keep_z1, got_z1, own_m, got_m)
+        kept_small, send_small = small_step(pos, scores0, index, smalls, table1, [send_z1, send_zm])
         other_small = swap_section(send_small)
-        other_a0 = after([swap_section(send_a0)], [kept_small])[0]
+        other_a0, got_z1, got_zm = after([other_a0, replica(send_z1, 2), replica(send_zm, 1)], [kept_small])
         own_a0, own_small, *messages = plane_step(pos, keep_a0, other_a0, kept_small, other_small, conditioning)
         got = to_peers(messages, "fsdp")
-        got_first = after(to_peers(first_messages, "fsdp"), [own_small])
-        keep_z, send_z = halve_step(pos, own_first, got_first)
-        cond_part = cond_step(pos, after([own_small], [send_z])[0], w_ada_pieces, conditioning)
+        got_z1, got_zm = after([got_z1, got_zm], [own_small])
+        quarter1, keep_zm, send_zm = c_step(pos, keep_z1, got_z1, keep_zm, got_zm)
         part0, plane_small, *messages = column_step(pos, own_a0, own_small, got, samples)
-        got_z = after([replica(send_z, 1)], [plane_small])[0]
-        keep_z, send_z = quarter_step(pos, keep_z, got_z)
+        got_z1, got_zm = after([replica(quarter1, 2), replica(send_zm, 2)], [plane_small])
         got = to_peers(messages, "rep")
+        pair1, quarter_m = d_step(pos, quarter1, got_z1, keep_zm, got_zm)
+        cond_part = cond_step(pos, after([own_small], [pair1])[0], w_ada_pieces, conditioning)
         size = part0.shape[0]
-        high, low = rank >> 1, rank & 1
         quarter0 = add_pieces(part0, [x[:size] for x in got]).astype(BF16)
-        got_z = after([replica(send_z, 2)], [quarter0])[0]
-        quarter = (keep_z + got_z.astype(F32)).astype(BF16)
-        pair = ordered(quarter, replica(quarter, 2), high)
-        half_a0 = by_rank([quarter0] + from_peers(quarter0, "rep"), rank).reshape(-1, model)
-        n = pair.shape[0] // 2
-        quarters = ordered(pair.reshape(1, 2, n, model), replica(pair, 1).reshape(1, 2, n, model), low)
-        quarters = jnp.transpose(quarters, (1, 0, 2, 3)).reshape(4, n, model)
-        n = 3 * n // 5
-        half1 = quarters[:, :n].reshape(-1, model)
-        half_m0 = quarters[:, n:].reshape(-1, model)
+        got_z1, got_zm, cond_part = after([replica(pair1, 1), replica(quarter_m, 2), cond_part], [quarter0])
+        half1, pair_m = e_step(pos, pair1, got_z1, quarter_m, got_zm)
         g_ada, g_b_ada, g_b_qv, g_b_proj, g_b_fc1, g_b_fc2, g_table = finish_step(
             pos, plane_small, got, samples, width, heads, entries
         )
+        cond_grad = cond_part + swap_section(cond_part)
+        own_half, send_half = g_step(
+            pos, quarter0, from_peers(quarter0, "rep"), pair_m, replica(pair_m, 1), half1, [g_ada, cond_grad]
+        )
     else:
         other_a0 = swap_section(send_a0)
-        kept_small, send_small = small_step(pos, scores0, scores1, relative_bias_index, smalls, [])
+        kept_small, send_small = small_step(pos, scores0, index, smalls, table1, [])
         theirs = swap_section(send_small).astype(F32)
         both = kept_small + theirs
         cut = half * 8
@@ -1187,15 +1270,12 @@
             lax.dynamic_slice_in_dim(v, shard * (v.shape[0] // shards), v.shape[0] // shards, 0)[None] for v in vectors
         ]
         g_table = jnp.transpose(summed[8:].reshape(HIGH, heads, LOW), (1, 0, 2)).reshape(heads, HIGH * LOW)[:, :entries]
-        sums_a0 = section_sums(keep_a0, other_a0[:size_a], pieces)
-        half_a0, half_m0, half1 = sums_a0[0].astype(BF16), sums_m0[0].astype(BF16), sums1[0].astype(BF16)
-    cond_grad = cond_part + swap_section(cond_part)
-    cut = half_a0.shape[0]
-    half_a1, half_m1 = half1[:cut], half1[cut:]
-    grads = final_step(
-        pos, mine(half_a0, half_a1), mine(half_m0, half_m1),
-        swap_section(mine(jnp.concatenate([half_a1, half_m1]), jnp.concatenate([half_a0, half_m0]))),
-    )
+        sums_a0 = section_sums(keep_a0, other_a0[:size_a], z.pieces)
+        cond_grad = cond_part + swap_section(cond_part)
+        half0 = jnp.concatenate([sums_a0[0], sums_m0[0]]).astype(BF16)
+        half1 = sums1[0].astype(BF16)
+        own_half, send_half = mine(half0, half1), mine(half1, half0)
+    grads = final_step(pos, own_half, swap_section(send_half))
     if not direct:
         grads = [lax.psum_scatter(g.astype(BF16), "fsdp", scatter_dimension=0, tiled=True) for g in grads]
         grads = [g.astype(F32) for g in lax.psum(tuple(grads), "rep")]

time: 235 us -> 246 us (1.047)
  Pallas kernels: 119 us -> 131 us
  waiting for transfers between devices: 48.3 us -> 42.2 us
  starting transfers between devices: 42.3 us -> 47.4 us
    ppermute x4 -> x8, waiting for transfers between devices: 15.1 us -> 3.98 us  [replica(): return lax.ppermute(value, 'rep', pairs_of(replicas, step))]
    ppermute x1, waiting for transfers between devices: 8.41 us -> 0.67 us  [per_device(): got_first = lax.ppermute(got_x[:middle_row], 'fsdp', pairs_of(shards, 2))]
    ppermute x1, waiting for transfers between devices: 2.45 us -> 9.91 us  [per_device(): got_second = lax.ppermute(got_y[middle_row:], 'fsdp', pairs_of(shards, 1))]
    pallas_call x1 -> x2, Pallas kernels: 4.8 us -> 11.3 us  [the longest x1 7.65 us: table_step(): pl.pallas_call(table_kernel, out_shape=jax.ShapeDtypeStruct((HIGH, scores...]
    ppermute x4 -> x8, starting transfers between devices: 5.13 us -> 10.9 us  [replica(): return lax.ppermute(value, 'rep', pairs_of(replicas, step))]
    pallas_call x14 -> x18, Pallas kernels: 100 us -> 106 us  [call(): pl.pallas_call(kernel, out_shape=[jax.ShapeDtypeStruct(shape, dtype) for...]
    ppermute x12 -> x15, waiting for transfers between devices: 13.2 us -> 18.8 us  [to_peers(): lax.ppermute(messages[p - 1], axis, pairs_of(count, p))]
    ppermute x12 -> x15, starting transfers between devices: 14.9 us -> 18.3 us  [to_peers(): lax.ppermute(messages[p - 1], axis, pairs_of(count, p))]
  transfers between devices with their start and end apart: 42 -> 49, of which waited for: 15 -> 14; matrix products, arithmetic and copies ran while one was open for 5% -> 5% of each run, Pallas kernels for 36% -> 36%
where the time goes in v8:
time: 246 us
  Pallas kernels  131 us (53%)
  starting transfers between devices  47.4 us (19%)
  waiting for transfers between devices  42.2 us (17%)
  local copies, waits for them, and re-layouts  17.6 us (7%)
  other arithmetic  6.47 us (3%)
    pallas_call x18, Pallas kernels, call(): pl.pallas_call(kernel, out_shape=[jax.ShapeDtypeStruct(shape, dtype) for...  106 us
    ppermute x15, waiting for transfers between devices, to_peers(): lax.ppermute(messages[p - 1], axis, pairs_of(count, p))  18.8 us
    ppermute x15, starting transfers between devices, to_peers(): lax.ppermute(messages[p - 1], axis, pairs_of(count, p))  18.3 us
    ppermute x9, starting transfers between devices, from_peers(): lax.ppermute(value, axis, pairs_of(lax.axis_size(axis), p))  12.5 us
    unnamed x111, local copies, waits for them, and re-layouts  12.5 us
    pallas_call x1, Pallas kernels, lookup(): pl.pallas_call(lookup_kernel, out_shape=jax.ShapeDtypeStruct((heads, leng...  11.2 us
    ppermute x8, starting transfers between devices, replica(): return lax.ppermute(value, 'rep', pairs_of(replicas, step))  10.9 us
    ppermute x1, waiting for transfers between devices, per_device(): got_second = lax.ppermute(got_y[middle_row:], 'fsdp', pairs_of(shards, 1))  9.91 us
  transfers between devices with their start and end apart: 49, of which 14 were waited for; matrix products, arithmetic and copies ran while one was open for 5% of the time, Pallas kernels for 36%

profile of v8, /device:TPU:0, one launch (start us, length us, event | category | flops | bytes accessed | tf_op | source)
XLA Modules:
  0.0 245.5 jit_solution(11781098382767558324)
XLA Ops:
  0.7 4.0 %collective-permute-start.2 = (bf16[4,384]{1,0:T(4,128)(2,1)}, bf16[4,384]{1,0:T(4,128)(2,1)S(1)}, u32[]{:S(2)}, u32[]{:S(2)}) collective-permute-start(bf16[4,384]{1,0:T(4,128)(2,1)} %cond.3), channel_id=1, source_target_pairs={{0,12},{4,8},{8,4},{12,0},{1,13},{5,9},{9,5},{13,1},{2,14},{6,10},... | collective-permute-start | bytes 9224 | tf_op jit(solution)/shard_map/ppermute | solution.py:1112
  5.3 2.2 shard_map.263.rest_0_
  12.2 11.2 %shard_map.264.rest_0_.own_bias = bf16[6,256,256]{2,1,0:T(8,128)(2,1)} custom-call(bf16[128,64]{1,0:T(8,128)(2,1)} %bitcast.42, s32[256,256]{1,0:T(8,128)} %index.5, bf16[1152,384]{1,0:T(8,128)(2,1)} %shard_map.263.rest_0_, bf16[4,384]{1,0:T(4,128)(2,1)} %copy-done.54, bf16[4,384]{1,0:T(4,128)(2,1)} %copy-done.53, bf16[4,384]{1,0:T(4,128)(2,1)} %copy-done.52), custom_call_target="tpu_custom_call" | custom-call | flops 11000000512 | tf_op jit(solution)/shard_map/pallas_call | solution.py:1035
  24.1 3.6 %shard_map.265 = (bf16[96,2304]{1,0:T(8,128)(2,1)}, f32[4,3072]{1,0:T(4,128)}, f32[4,3072]{1,0:T(4,128)}, f32[4,3072]{1,0:T(4,128)}, f32[4,3072]{1,0:T(4,128)}) custom-call(s32[3]{0:T(128)} %pad_add_fusion.pos, bf16[96,2304]{1,0:T(8,128)(2,1)} %bitcast.44, bf16[4,384]{1,0:T(4,128)(2,1)} %cond.3, bf16[4,384]{1,0:T(4,128)(2,1)} %copy-done.54, ...), custom_call_target="tpu_custom_call" | custom-call | flops 2000000000 | tf_op jit(solution)/shard_map/pallas_call | solution.py:529
  28.7 2.5 %collective-permute-start.5 = (f32[4,3072]{1,0:T(4,128)}, f32[4,3072]{1,0:T(4,128)S(1)}, u32[]{:S(2)}, u32[]{:S(2)}) collective-permute-start(f32[4,3072]{1,0:T(4,128)} %get-tuple-element.115), channel_id=1, source_target_pairs={{0,12},{4,8},{8,4},{12,0},{1,13},{5,9},{9,5},{13,1},{2,14},{6,10},... | collective-permute-start | bytes 147464 | tf_op jit(solution)/shard_map/ppermute | solution.py:1079
  35.8 9.9 %collective-permute-done.11.refs_2_.rest_4_ = bf16[576,384]{1,0:T(8,128)(2,1)S(1)} collective-permute-done((bf16[576,384]{1,0:T(8,128)(2,1)}, bf16[576,384]{1,0:T(8,128)(2,1)S(1)}, u32[]{:S(2)}, u32[]{:S(2)}) %collective-permute-start.11) | collective-permute-done | bytes 442400 | tf_op jit(solution)/shard_map/ppermute | solution.py:1159
  46.4 2.1 dynamic-slice_multiply_fusion
  55.2 15.2 %shard_map.269 = (bf16[512,1152]{1,0:T(8,128)(2,1)}, bf16[2,6,256,256]{3,2,1,0:T(8,128)(2,1)}, bf16[512,384]{1,0:T(8,128)(2,1)}, f32[512,384]{1,0:T(8,128)}, f32...) custom-call(s32[3]{0:T(128)} %pad_add_fusion.pos, ...), custom_call_target="tpu_custom_call" | custom-call | flops 15000000512 | tf_op jit(solution)/shard_map/pallas_call | solution.py:529
  70.4 4.3 %collective-permute-done.18.rest_11_.rest_2_ = bf16[96,2304]{1,0:T(8,128)(2,1)S(1)} collective-permute-done((bf16[96,2304]{1,0:T(8,128)(2,1)}, bf16[96,2304]{1,0:T(8,128)(2,1)S(1)}, u32[]{:S(2)}, u32[]{:S(2)}) %collective-permute-start.18) | collective-permute-done | bytes 442400 | tf_op jit(solution)/shard_map/ppermute | solution.py:1112
  75.6 26.1 %shard_map.270 = (bf16[512,384]{1,0:T(8,128)(2,1)}, bf16[512,384]{1,0:T(8,128)(2,1)}, f32[2,8,384]{2,1,0:T(8,128)}, f32[2,8,384]{2,1,0:T(8,128)}, bf16[6,256,256...) custom-call(s32[3]{0:T(128)} %pad_add_fusion.pos, bf16[512,384]{1,0:T(8,128)(2,1)} %get-tuple-element.122.h, ...), custom_call_target="tpu_custom_call" | custom-call | flops 24999999488 | tf_op jit(solution)/shard_map/pallas_call | solution.py:529
  101.8 7.7 %shard_map.271.refs_1_.table1 = f32[16,384]{1,0:T(8,128)} custom-call(bf16[6,256,256]{2,1,0:T(8,128)(2,1)} %get-tuple-element.125.scores, s32[256,256]{1,0:T(8,128)} %index.5), custom_call_target="tpu_custom_call" | custom-call | flops 8000000000 | tf_op jit(solution)/shard_map/pallas_call | solution.py:339
  110.8 3.6 %shard_map.273 = (f32[576,384]{1,0:T(8,128)}, bf16[576,384]{1,0:T(8,128)(2,1)}, bf16[576,384]{1,0:T(8,128)(2,1)}, bf16[576,384]{1,0:T(8,128)(2,1)}) custom-call(bf16[2304,384]{1,0:T(8,128)(2,1)} %get-tuple-element.135.keep, bf16[2816,384]{1,0:T(8,128)(2,1)} %shard_map.272.other), custom_call_target="tpu_custom_call" | custom-call | tf_op jit(solution)/shard_map/pallas_call | solution.py:668
  117.9 11.9 %shard_map.274 = (f32[512,384]{1,0:T(8,128)}, f32[2,8,384]{2,1,0:T(8,128)}, bf16[1536,384]{1,0:T(8,128)(2,1)}, bf16[1536,384]{1,0:T(8,128)(2,1)}) custom-call(s32[3]{0:T(128)} %pad_add_fusion.pos, bf16[512,384]{1,0:T(8,128)(2,1)} %get-tuple-element.130.grad.d_h1, f32[512,384]{1,0:T(8,128)} %get-tuple-element.131.middle, ...), custom_call_target="tpu_custom_call" | custom-call | flops 12000000000 | tf_op jit(solution)/shard_map/pallas_call | solution.py:529
  129.9 7.2 %collective-permute-done.22.refs_1_ = bf16[576,384]{1,0:T(8,128)(2,1)S(1)} collective-permute-done((bf16[576,384]{1,0:T(8,128)(2,1)}, bf16[576,384]{1,0:T(8,128)(2,1)S(1)}, u32[]{:S(2)}, u32[]{:S(2)}) %collective-permute-start.22) | collective-permute-done | bytes 442400 | tf_op jit(solution)/shard_map/ppermute | solution.py:1079
  138.0 3.1 %collective-permute-done.24.other_m = bf16[1536,384]{1,0:T(8,128)(2,1)S(1)} collective-permute-done((bf16[1536,384]{1,0:T(8,128)(2,1)}, bf16[1536,384]{1,0:T(8,128)(2,1)S(1)}, u32[]{:S(2)}, u32[]{:S(2)}) %collective-permute-start.24) | collective-permute-done | bytes 1179680 | tf_op jit(solution)/shard_map/ppermute | solution.py:1047
  142.1 3.8 %shard_map.277 = (f32[288,384]{1,0:T(8,128)}, bf16[288,384]{1,0:T(8,128)(2,1)}, f32[384,384]{1,0:T(8,128)}, bf16[384,384]{1,0:T(8,128)(2,1)}, bf16[384,384]{1,0:T(8,128)(2,1)}, /*index=5*/bf16[384,384]{1,0:T(8,128)(2,1)}) custom-call(s32[3]{0:T(128)} %pad_add_fusion.pos, f32[576,384]{1,0:T(8,128)} %get-tuple-element.140.own1, ...), custom_call_target="tpu_custom_call" | custom-call | flops 2000000000 | tf_op jit(solution)/shard_map/pallas_call | solution.py:529
  151.2 12.6 %shard_map.278 = (f32[512,384]{1,0:T(8,128)}, f32[2,8,384]{2,1,0:T(8,128)}, bf16[6,256,256]{2,1,0:T(8,128)(2,1)}, bf16[768,384]{1,0:T(8,128)(2,1)}, bf16[1280,384]{1,0:T(8,128)(2,1)}) custom-call(s32[3]{0:T(128)} %pad_add_fusion.pos, bf16[512,384]{1,0:T(8,128)(2,1)} %bitcast.34, f32[1,7680]{1,0:T(1,128)} %get-tuple-element.119.own_line, ...), custom_call_target="tpu_custom_call" | custom-call | flops 12999999488 | tf_op jit(solution)/shard_map/pallas_call | solution.py:529
  164.7 2.5 %shard_map.281 = (f32[144,384]{1,0:T(8,128)}, bf16[144,384]{1,0:T(8,128)(2,1)}, f32[192,384]{1,0:T(8,128)}, bf16[192,384]{1,0:T(8,128)(2,1)}) custom-call(s32[3]{0:T(128)} %pad_add_fusion.pos, f32[288,384]{1,0:T(8,128)} %get-tuple-element.156.kept1, bf16[288,384]{1,0:T(8,128)(2,1)} %get-tuple-element.152.refs_1_.got1, f32[384,384]{1,0:T(8,128)} %get-tuple-element.157.own_m, ...), custom_call_target="tpu_custom_call" | custom-call | flops 2000000000 | tf_op jit(solution)/shard_map/pallas_call | solution.py:529
  167.3 2.6 %collective-permute-start.30 = (bf16[144,384]{1,0:T(8,128)(2,1)}, bf16[144,384]{1,0:T(8,128)(2,1)S(1)}, u32[]{:S(2)}, u32[]{:S(2)}) collective-permute-start(bf16[144,384]{1,0:T(8,128)(2,1)} %get-tuple-element.158.rest_0_), channel_id=1, source_target_pairs={{0,2},{1,3},{2,0},{3,1},{4,6},{5,7},{6,4},{7,5},{8,10},{9,11},{10,... | collective-permute-start | bytes 331784 | tf_op jit(solution)/shard_map/ppermute | solution.py:1217
  170.3 8.0 %shard_map.282 = (f32[48,384]{1,0:T(8,128)}, bf16[48,384]{1,0:T(8,128)(2,1)}) custom-call(s32[3]{0:T(128)} %pad_add_fusion.pos, bf16[6,256,256]{2,1,0:T(8,128)(2,1)} %get-tuple-element.160.scores, s32[256,256]{1,0:T(8,128)} %index.5, f32[2,8,384]{2,1,0:T(8,128)} %get-tuple-element.161.small_a0, f32[2,8,384]{2,1,0:T(8,128)} %get-tuple-element.162.small_m0, ...), custom_call_target="tpu_custom_call" | custom-call | flops 8000000000 | tf_op jit(solution)/shard_map/pallas_call | solution.py:529
  180.4 2.5 %shard_map.284 = (f32[192,384]{1,0:T(8,128)}, bf16[64,384]{1,0:T(8,128)(2,1)}, bf16[256,384]{1,0:T(8,128)(2,1)}, bf16[256,384]{1,0:T(8,128)(2,1)}, bf16[256,384]{1,0:T(8,128)(2,1)}) custom-call(s32[3]{0:T(128)} %pad_add_fusion.pos, bf16[768,384]{1,0:T(8,128)(2,1)} %get-tuple-element.170.keep, bf16[1280,384]{1,0:T(8,128)(2,1)} %get-tuple-element.166.other, ...), custom_call_target="tpu_custom_call" | custom-call | flops 2000000000 | tf_op jit(solution)/shard_map/pallas_call | solution.py:529
  189.7 2.6 %collective-permute-start.33 = (bf16[144,384]{1,0:T(8,128)(2,1)}, bf16[144,384]{1,0:T(8,128)(2,1)S(1)}, u32[]{:S(2)}, u32[]{:S(2)}) collective-permute-start(bf16[144,384]{1,0:T(8,128)(2,1)} %get-tuple-element.176.quarter1), channel_id=1, source_target_pairs={{0,2},{1,3},{2,0},{3,1},{4,6},{5,7},{6,4},{7,5},{8,10},{9,11},{10,... | collective-permute-start | bytes 331784 | tf_op jit(solution)/shard_map/ppermute | solution.py:1217
  192.3 2.9 %collective-permute-done.36.got_b = bf16[256,384]{1,0:T(8,128)(2,1)S(1)} collective-permute-done((bf16[256,384]{1,0:T(8,128)(2,1)}, bf16[256,384]{1,0:T(8,128)(2,1)S(1)}, u32[]{:S(2)}, u32[]{:S(2)}) %collective-permute-start.36) | collective-permute-done | bytes 196640 | tf_op jit(solution)/shard_map/ppermute | solution.py:1079
  195.9 2.1 shard_map.287
  204.8 2.9 %collective-permute-start.41 = (bf16[192,384]{1,0:T(8,128)(2,1)S(1)}, bf16[192,384]{1,0:T(8,128)(2,1)S(1)}, u32[]{:S(2)}, u32[]{:S(2)}) collective-permute-start(bf16[192,384]{1,0:T(8,128)(2,1)S(1)} %copy-done.44), channel_id=1, source_target_pairs={{0,2},{1,3},{2,0},{3,1},{4,6},{5,7},{6,4},{7,5},{8,10},{9,11},{10,... | collective-permute-start | bytes 442376 | tf_op jit(solution)/shard_map/ppermute | solution.py:1079
  209.1 2.8 %shard_map.291.refs_2_ = f32[4,384]{1,0:T(4,128)} custom-call(s32[3]{0:T(128)} %pad_add_fusion.pos, bf16[64,384]{1,0:T(8,128)(2,1)} %shard_map.290.small, bf16[4,384]{1,0:T(4,128)(2,1)} %cond.3, bf16[96,2304]{1,0:T(8,128)(2,1)} %shard_map.268.rest_10_.rest_0_, bf16[96,2304]{1,0:T(8,128)(2,1)} %copy-done.38, bf16[96,2304]{1,0:T(8,128)(2,1)} %copy-done.37, ...), custom_call_target="tpu_custom_call" | custom-call | flops 2000000000 | tf_op jit(solution)/shard_map/pallas_call | solution.py:529
  211.9 6.5 %collective-permute-done.40.got_a = bf16[192,384]{1,0:T(8,128)(2,1)S(1)} collective-permute-done((bf16[192,384]{1,0:T(8,128)(2,1)S(1)}, bf16[192,384]{1,0:T(8,128)(2,1)S(1)}, u32[]{:S(2)}, u32[]{:S(2)}) %collective-permute-start.40) | collective-permute-done | bytes 147488 | tf_op jit(solution)/shard_map/ppermute | solution.py:1079
  218.4 2.0 collective-permute-done.42.got_c
  220.5 2.1 collective-permute-start.46
  229.6 2.8 %shard_map.293 = (f32[96,2304]{1,0:T(8,128)}, f32[1,576]{1,0:T(1,128)}, f32[1,192]{1,0:T(1,128)}, f32[1,96]{1,0:T(1,128)}, f32[1,384]{1,0:T(1,128)}, /*index=5*/f32[1,96]{1,0:T(1,128)}, f32[6,961]{1,0:T(8,128)}) custom-call(s32[3]{0:T(128)} %pad_add_fusion.pos, bf16[144,384]{1,0:T(8,128)(2,1)} %get-tuple-element.182.refs_2_.own_small, ...), custom_call_target="tpu_custom_call" | custom-call | flops 2000000000 | tf_op jit(solution)/shard_map/pallas_call | solution.py:529
  235.4 2.3 shard_map.295
  243.0 2.5 %shard_map.296 = (f32[96,1152]{1,0:T(8,128)}, f32[96,384]{1,0:T(8,128)}, f32[96,1536]{1,0:T(8,128)}, f32[384,384]{1,0:T(8,128)}) custom-call(s32[3]{0:T(128)} %pad_add_fusion.pos, bf16[576,384]{1,0:T(8,128)(2,1)} %get-tuple-element.198.own, bf16[576,384]{1,0:T(8,128)(2,1)} %copy-done.39), custom_call_target="tpu_custom_call" | custom-call | flops 2000000000 | tf_op jit(solution)/shard_map/pallas_call | solution.py:529
  (229 shorter events, 66.3 us)
Async XLA Ops:
  0.7 10.9 %collective-permute-start.2 = (bf16[4,384]{1,0:T(4,128)(2,1)}, bf16[4,384]{1,0:T(4,128)(2,1)S(1)}, u32[]{:S(2)}, u32[]{:S(2)}) collective-permute-start(bf16[4,384]{1,0:T(4,128)(2,1)} %cond.3), channel_id=1, source_target_pairs={{0,12},{4,8},{8,4},{12,0},{1,13},{5,9},{9,5},{13,1},{2,14},{6,10},... | collective-permute-start | bytes 9224 | tf_op jit(solution)/shard_map/ppermute | solution.py:1112
  7.5 21.3 %collective-permute-start.7 = (bf16[1152,384]{1,0:T(8,128)(2,1)}, bf16[1152,384]{1,0:T(8,128)(2,1)S(1)}, u32[]{:S(2)}, u32[]{:S(2)}) collective-permute-start(bf16[1152,384]{1,0:T(8,128)(2,1)} %shard_map.263.rest_0_), channel_id=1, source_target_pairs={{0,8},{4,12},{8,0},{12,4},{1,9},{5,13},{9,1},{13,5},{2,10},{6,14},... | collective-permute-start | bytes 2654216 | tf_op jit(solution)/shard_map/ppermute | solution.py:1155
  9.4 21.9 %collective-permute-start.6 = (bf16[1152,384]{1,0:T(8,128)(2,1)}, bf16[1152,384]{1,0:T(8,128)(2,1)S(1)}, u32[]{:S(2)}, u32[]{:S(2)}) collective-permute-start(bf16[1152,384]{1,0:T(8,128)(2,1)} %shard_map.263.rest_0_), channel_id=1, source_target_pairs={{0,4},{4,0},{8,12},{12,8},{1,5},{5,1},{9,13},{13,9},{2,6},{6,2},{1... | collective-permute-start | bytes 2654216 | tf_op jit(solution)/shard_map/ppermute | solution.py:1154
  23.5 10.7 %collective-permute-start.9 = (bf16[6,256,256]{2,1,0:T(8,128)(2,1)}, bf16[6,256,256]{2,1,0:T(8,128)(2,1)}, u32[]{:S(2)}, u32[]{:S(2)}) collective-permute-start(bf16[6,256,256]{2,1,0:T(8,128)(2,1)} %shard_map.264.rest_0_.own_bias), channel_id=1, source_target_pairs={{0,16},{16,0},{1,17},{17,1},{2,18},{18,2},{3,19},{19,3},{4,20},{20... | collective-permute-start | bytes 2359304 | tf_op jit(solution)/shard_map/ppermute | solution.py:1047
  31.3 18.8 %collective-permute-start.12 = (bf16[1152,384]{1,0:T(8,128)(2,1)S(1)}, bf16[1152,384]{1,0:T(8,128)(2,1)}, u32[]{:S(2)}, u32[]{:S(2)}) collective-permute-start(bf16[1152,384]{1,0:T(8,128)(2,1)S(1)} %copy-done.12), channel_id=1, source_target_pairs={{0,16},{16,0},{1,17},{17,1},{2,18},{18,2},{3,19},{19,3},{4,20},{20... | collective-permute-start | bytes 2654216 | tf_op jit(solution)/shard_map/ppermute | solution.py:1047
  33.1 12.7 %collective-permute-start.11 = (bf16[576,384]{1,0:T(8,128)(2,1)}, bf16[576,384]{1,0:T(8,128)(2,1)S(1)}, u32[]{:S(2)}, u32[]{:S(2)}) collective-permute-start(bf16[576,384]{1,0:T(8,128)(2,1)} %slice.29), channel_id=1, source_target_pairs={{0,4},{4,0},{8,12},{12,8},{1,5},{5,1},{9,13},{13,9},{2,6},{6,2},{1... | collective-permute-start | bytes 1327112 | tf_op jit(solution)/shard_map/ppermute | solution.py:1159
  33.9 12.5 %collective-permute-start.10 = (bf16[576,384]{1,0:T(8,128)(2,1)}, bf16[576,384]{1,0:T(8,128)(2,1)}, u32[]{:S(2)}, u32[]{:S(2)}) collective-permute-start(bf16[576,384]{1,0:T(8,128)(2,1)} %slice.28), channel_id=1, source_target_pairs={{0,8},{4,12},{8,0},{12,4},{1,9},{5,13},{9,1},{13,5},{2,10},{6,14},... | collective-permute-start | bytes 1327112 | tf_op jit(solution)/shard_map/ppermute | solution.py:1158
  34.1 20.3 %collective-permute-start.14 = (bf16[1152,384]{1,0:T(8,128)(2,1)S(1)}, bf16[1152,384]{1,0:T(8,128)(2,1)}, u32[]{:S(2)}, u32[]{:S(2)}) collective-permute-start(bf16[1152,384]{1,0:T(8,128)(2,1)S(1)} %collective-permute-done.7.refs_4_.rest_2_), channel_id=1, source_target_pairs={{0,16},{16,0},{1,17},{17,1},{2,18},{18,2},{3,19},{19,3},{4,20},{20... | collective-permute-start | bytes 2654216 | tf_op jit(solution)/shard_map/ppermute | solution.py:1047
  34.1 21.1 %collective-permute-start.13 = (bf16[1152,384]{1,0:T(8,128)(2,1)S(1)}, bf16[1152,384]{1,0:T(8,128)(2,1)}, u32[]{:S(2)}, u32[]{:S(2)}) collective-permute-start(bf16[1152,384]{1,0:T(8,128)(2,1)S(1)} %collective-permute-done.6.refs_3_.rest_1_), channel_id=1, source_target_pairs={{0,16},{16,0},{1,17},{17,1},{2,18},{18,2},{3,19},{19,3},{4,20},{20... | collective-permute-start | bytes 2654216 | tf_op jit(solution)/shard_map/ppermute | solution.py:1047
  51.7 18.7 %collective-permute-start.19 = (bf16[96,2304]{1,0:T(8,128)(2,1)}, bf16[96,2304]{1,0:T(8,128)(2,1)S(1)}, u32[]{:S(2)}, u32[]{:S(2)}) collective-permute-start(bf16[96,2304]{1,0:T(8,128)(2,1)} %shard_map.268.rest_10_.rest_0_), channel_id=1, source_target_pairs={{0,12},{4,8},{8,4},{12,0},{1,13},{5,9},{9,5},{13,1},{2,14},{6,10},... | collective-permute-start | bytes 1327112 | tf_op jit(solution)/shard_map/ppermute | solution.py:1112
  53.1 21.6 %collective-permute-start.18 = (bf16[96,2304]{1,0:T(8,128)(2,1)}, bf16[96,2304]{1,0:T(8,128)(2,1)S(1)}, u32[]{:S(2)}, u32[]{:S(2)}) collective-permute-start(bf16[96,2304]{1,0:T(8,128)(2,1)} %shard_map.268.rest_10_.rest_0_), channel_id=1, source_target_pairs={{0,8},{4,12},{8,0},{12,4},{1,9},{5,13},{9,1},{13,5},{2,10},{6,14},... | collective-permute-start | bytes 1327112 | tf_op jit(solution)/shard_map/ppermute | solution.py:1112
  54.3 20.4 %collective-permute-start.17 = (bf16[96,2304]{1,0:T(8,128)(2,1)}, bf16[96,2304]{1,0:T(8,128)(2,1)S(1)}, u32[]{:S(2)}, u32[]{:S(2)}) collective-permute-start(bf16[96,2304]{1,0:T(8,128)(2,1)} %shard_map.268.rest_10_.rest_0_), channel_id=1, source_target_pairs={{0,4},{4,0},{8,12},{12,8},{1,5},{5,1},{9,13},{13,9},{2,6},{6,2},{1... | collective-permute-start | bytes 1327112 | tf_op jit(solution)/shard_map/ppermute | solution.py:1112
  114.4 15.4 %collective-permute-start.21 = (bf16[576,384]{1,0:T(8,128)(2,1)}, bf16[576,384]{1,0:T(8,128)(2,1)S(1)}, u32[]{:S(2)}, u32[]{:S(2)}) collective-permute-start(bf16[576,384]{1,0:T(8,128)(2,1)} %get-tuple-element.136.rest_10_), channel_id=1, source_target_pairs={{0,4},{4,0},{8,12},{12,8},{1,5},{5,1},{9,13},{13,9},{2,6},{6,2},{1... | collective-permute-start | bytes 1327112 | tf_op jit(solution)/shard_map/ppermute | solution.py:1079
  115.1 22.0 %collective-permute-start.22 = (bf16[576,384]{1,0:T(8,128)(2,1)}, bf16[576,384]{1,0:T(8,128)(2,1)S(1)}, u32[]{:S(2)}, u32[]{:S(2)}) collective-permute-start(bf16[576,384]{1,0:T(8,128)(2,1)} %get-tuple-element.137.rest_11_), channel_id=1, source_target_pairs={{0,8},{4,12},{8,0},{12,4},{1,9},{5,13},{9,1},{13,5},{2,10},{6,14},... | collective-permute-start | bytes 1327112 | tf_op jit(solution)/shard_map/ppermute | solution.py:1079
  116.4 20.6 %collective-permute-start.23 = (bf16[576,384]{1,0:T(8,128)(2,1)}, bf16[576,384]{1,0:T(8,128)(2,1)S(1)}, u32[]{:S(2)}, u32[]{:S(2)}) collective-permute-start(bf16[576,384]{1,0:T(8,128)(2,1)} %get-tuple-element.138.rest_12_), channel_id=1, source_target_pairs={{0,12},{4,8},{8,4},{12,0},{1,13},{5,9},{9,5},{13,1},{2,14},{6,10},... | collective-permute-start | bytes 1327112 | tf_op jit(solution)/shard_map/ppermute | solution.py:1079
  145.9 17.8 %collective-permute-start.25 = (bf16[288,384]{1,0:T(8,128)(2,1)}, bf16[288,384]{1,0:T(8,128)(2,1)S(1)}, u32[]{:S(2)}, u32[]{:S(2)}) collective-permute-start(bf16[288,384]{1,0:T(8,128)(2,1)} %get-tuple-element.146.rest_10_), channel_id=1, source_target_pairs={{0,1},{1,0},{2,3},{3,2},{4,5},{5,4},{6,7},{7,6},{8,9},{9,8},{10,11... | collective-permute-start | bytes 663560 | tf_op jit(solution)/shard_map/ppermute | solution.py:1217
  147.7 16.1 %collective-permute-start.26 = (bf16[384,384]{1,0:T(8,128)(2,1)}, bf16[384,384]{1,0:T(8,128)(2,1)S(1)}, u32[]{:S(2)}, u32[]{:S(2)}) collective-permute-start(bf16[384,384]{1,0:T(8,128)(2,1)} %get-tuple-element.147.rest_11_), channel_id=1, source_target_pairs={{0,4},{4,0},{8,12},{12,8},{1,5},{5,1},{9,13},{13,9},{2,6},{6,2},{1... | collective-permute-start | bytes 884744 | tf_op jit(solution)/shard_map/ppermute | solution.py:1079
  148.9 15.0 %collective-permute-start.27 = (bf16[384,384]{1,0:T(8,128)(2,1)}, bf16[384,384]{1,0:T(8,128)(2,1)S(1)}, u32[]{:S(2)}, u32[]{:S(2)}) collective-permute-start(bf16[384,384]{1,0:T(8,128)(2,1)} %get-tuple-element.148.rest_12_), channel_id=1, source_target_pairs={{0,8},{4,12},{8,0},{12,4},{1,9},{5,13},{9,1},{13,5},{2,10},{6,14},... | collective-permute-start | bytes 884744 | tf_op jit(solution)/shard_map/ppermute | solution.py:1079
  149.3 14.7 %collective-permute-start.28 = (bf16[384,384]{1,0:T(8,128)(2,1)}, bf16[384,384]{1,0:T(8,128)(2,1)S(1)}, u32[]{:S(2)}, u32[]{:S(2)}) collective-permute-start(bf16[384,384]{1,0:T(8,128)(2,1)} %get-tuple-element.149.rest_13_), channel_id=1, source_target_pairs={{0,12},{4,8},{8,4},{12,0},{1,13},{5,9},{9,5},{13,1},{2,14},{6,10},... | collective-permute-start | bytes 884744 | tf_op jit(solution)/shard_map/ppermute | solution.py:1079
  164.7 13.6 %collective-permute-start.29 = (bf16[1280,384]{1,0:T(8,128)(2,1)}, bf16[1280,384]{1,0:T(8,128)(2,1)S(1)}, u32[]{:S(2)}, u32[]{:S(2)}) collective-permute-start(bf16[1280,384]{1,0:T(8,128)(2,1)} %shard_map.280), channel_id=1, source_target_pairs={{0,16},{16,0},{1,17},{17,1},{2,18},{18,2},{3,19},{19,3},{4,20},{20... | collective-permute-start | bytes 2949128 | tf_op jit(solution)/shard_map/ppermute | solution.py:1047
  167.3 11.1 %collective-permute-start.30 = (bf16[144,384]{1,0:T(8,128)(2,1)}, bf16[144,384]{1,0:T(8,128)(2,1)S(1)}, u32[]{:S(2)}, u32[]{:S(2)}) collective-permute-start(bf16[144,384]{1,0:T(8,128)(2,1)} %get-tuple-element.158.rest_0_), channel_id=1, source_target_pairs={{0,2},{1,3},{2,0},{3,1},{4,6},{5,7},{6,4},{7,5},{8,10},{9,11},{10,... | collective-permute-start | bytes 331784 | tf_op jit(solution)/shard_map/ppermute | solution.py:1217
  184.0 11.1 %collective-permute-start.36 = (bf16[256,384]{1,0:T(8,128)(2,1)}, bf16[256,384]{1,0:T(8,128)(2,1)S(1)}, u32[]{:S(2)}, u32[]{:S(2)}) collective-permute-start(bf16[256,384]{1,0:T(8,128)(2,1)} %get-tuple-element.180), channel_id=1, source_target_pairs={{0,8},{4,12},{8,0},{12,4},{1,9},{5,13},{9,1},{13,5},{2,10},{6,14},... | collective-permute-start | bytes 589832 | tf_op jit(solution)/shard_map/ppermute | solution.py:1079
  184.8 10.3 %collective-permute-start.37 = (bf16[256,384]{1,0:T(8,128)(2,1)}, bf16[256,384]{1,0:T(8,128)(2,1)S(1)}, u32[]{:S(2)}, u32[]{:S(2)}) collective-permute-start(bf16[256,384]{1,0:T(8,128)(2,1)} %get-tuple-element.181), channel_id=1, source_target_pairs={{0,12},{4,8},{8,4},{12,0},{1,13},{5,9},{9,5},{13,1},{2,14},{6,10},... | collective-permute-start | bytes 589832 | tf_op jit(solution)/shard_map/ppermute | solution.py:1079
  189.4 9.7 %collective-permute-start.34 = (bf16[96,384]{1,0:T(8,128)(2,1)}, bf16[96,384]{1,0:T(8,128)(2,1)S(1)}, u32[]{:S(2)}, u32[]{:S(2)}) collective-permute-start(bf16[96,384]{1,0:T(8,128)(2,1)} %get-tuple-element.177), channel_id=1, source_target_pairs={{0,2},{1,3},{2,0},{3,1},{4,6},{5,7},{6,4},{7,5},{8,10},{9,11},{10,... | collective-permute-start | bytes 221192 | tf_op jit(solution)/shard_map/ppermute | solution.py:1217
  189.7 10.6 %collective-permute-start.33 = (bf16[144,384]{1,0:T(8,128)(2,1)}, bf16[144,384]{1,0:T(8,128)(2,1)S(1)}, u32[]{:S(2)}, u32[]{:S(2)}) collective-permute-start(bf16[144,384]{1,0:T(8,128)(2,1)} %get-tuple-element.176.quarter1), channel_id=1, source_target_pairs={{0,2},{1,3},{2,0},{3,1},{4,6},{5,7},{6,4},{7,5},{8,10},{9,11},{10,... | collective-permute-start | bytes 331784 | tf_op jit(solution)/shard_map/ppermute | solution.py:1217
  202.8 22.2 %collective-permute-start.38 = (bf16[288,384]{1,0:T(8,128)(2,1)}, bf16[288,384]{1,0:T(8,128)(2,1)S(1)}, u32[]{:S(2)}, u32[]{:S(2)}) collective-permute-start(bf16[288,384]{1,0:T(8,128)(2,1)} %get-tuple-element.186.refs_1_.pair1), channel_id=1, source_target_pairs={{0,1},{1,0},{2,3},{3,2},{4,5},{5,4},{6,7},{7,6},{8,9},{9,8},{10,11... | collective-permute-start | bytes 663560 | tf_op jit(solution)/shard_map/ppermute | solution.py:1217
  202.8 22.1 %collective-permute-start.39 = (bf16[96,384]{1,0:T(8,128)(2,1)}, bf16[96,384]{1,0:T(8,128)(2,1)S(1)}, u32[]{:S(2)}, u32[]{:S(2)}) collective-permute-start(bf16[96,384]{1,0:T(8,128)(2,1)} %get-tuple-element.187.quarter_m), channel_id=1, source_target_pairs={{0,2},{1,3},{2,0},{3,1},{4,6},{5,7},{6,4},{7,5},{8,10},{9,11},{10,... | collective-permute-start | bytes 221192 | tf_op jit(solution)/shard_map/ppermute | solution.py:1217
  204.7 13.7 %collective-permute-start.40 = (bf16[192,384]{1,0:T(8,128)(2,1)S(1)}, bf16[192,384]{1,0:T(8,128)(2,1)S(1)}, u32[]{:S(2)}, u32[]{:S(2)}) collective-permute-start(bf16[192,384]{1,0:T(8,128)(2,1)S(1)} %copy-done.45), channel_id=1, source_target_pairs={{0,1},{1,0},{2,3},{3,2},{4,5},{5,4},{6,7},{7,6},{8,9},{9,8},{10,11... | collective-permute-start | bytes 442376 | tf_op jit(solution)/shard_map/ppermute | solution.py:1079
  204.8 13.6 %collective-permute-start.41 = (bf16[192,384]{1,0:T(8,128)(2,1)S(1)}, bf16[192,384]{1,0:T(8,128)(2,1)S(1)}, u32[]{:S(2)}, u32[]{:S(2)}) collective-permute-start(bf16[192,384]{1,0:T(8,128)(2,1)S(1)} %copy-done.44), channel_id=1, source_target_pairs={{0,2},{1,3},{2,0},{3,1},{4,6},{5,7},{6,4},{7,5},{8,10},{9,11},{10,... | collective-permute-start | bytes 442376 | tf_op jit(solution)/shard_map/ppermute | solution.py:1079
  207.7 12.7 %collective-permute-start.42 = (bf16[192,384]{1,0:T(8,128)(2,1)S(1)}, bf16[192,384]{1,0:T(8,128)(2,1)S(1)}, u32[]{:S(2)}, u32[]{:S(2)}) collective-permute-start(bf16[192,384]{1,0:T(8,128)(2,1)S(1)} %copy-done.43), channel_id=1, source_target_pairs={{0,3},{1,2},{2,1},{3,0},{4,7},{5,6},{6,5},{7,4},{8,11},{9,10},{10,... | collective-permute-start | bytes 442376 | tf_op jit(solution)/shard_map/ppermute | solution.py:1079
  220.5 12.6 %collective-permute-start.46 = (bf16[48,384]{1,0:T(8,128)(2,1)S(1)}, bf16[48,384]{1,0:T(8,128)(2,1)S(1)}, u32[]{:S(2)}, u32[]{:S(2)}) collective-permute-start(bf16[48,384]{1,0:T(8,128)(2,1)S(1)} %add_convert_fusion.refs_3_.quarter_a), channel_id=1, source_target_pairs={{0,3},{1,2},{2,1},{3,0},{4,7},{5,6},{6,5},{7,4},{8,11},{9,10},{10,... | collective-permute-start | bytes 110600 | tf_op jit(solution)/shard_map/ppermute | solution.py:1112
  222.6 10.5 %collective-permute-start.45 = (bf16[48,384]{1,0:T(8,128)(2,1)S(1)}, bf16[48,384]{1,0:T(8,128)(2,1)S(1)}, u32[]{:S(2)}, u32[]{:S(2)}) collective-permute-start(bf16[48,384]{1,0:T(8,128)(2,1)S(1)} %add_convert_fusion.refs_3_.quarter_a), channel_id=1, source_target_pairs={{0,2},{1,3},{2,0},{3,1},{4,6},{5,7},{6,4},{7,5},{8,10},{9,11},{10,... | collective-permute-start | bytes 110600 | tf_op jit(solution)/shard_map/ppermute | solution.py:1112
  (72 other events, 363.6 us)

commit v9 on v8

--- a/solution.py
+++ b/solution.py
@@ -331,23 +331,10 @@
         out[...] = jnp.concatenate(parts[layer * heads : (layer + 1) * heads], axis=1)
 
 
-def table_kernel(scores, index, out):
-    add_tables((scores,), index, (out,))
-
-
-def table_step(scores, index):
-    return pl.pallas_call(
-        table_kernel,
-        out_shape=jax.ShapeDtypeStruct((HIGH, scores.shape[0] * LOW), F32),
-        cost_estimate=cost(8),
-        compiler_params=pltpu.CompilerParams(vmem_limit_bytes=VMEM_BYTES),
-    )(scores, index)
-
-
-def small_kernel(pos, scores, index, small_a0, small_m0, small_a1, small_m1, table1, *rest):
-    keep, send, table0 = rest[-3:]
+def small_kernel(pos, scores0, scores1, index, small_a0, small_m0, small_a1, small_m1, *rest):
+    keep, send, table0, table1 = rest[-4:]
     size = small_a0.shape[0] * small_a0.shape[1]
-    add_tables((scores,), index, (table0,))
+    add_tables((scores0, scores1), index, (table0, table1))
     parts = (
         (small_a0[...], small_m0[...], table0[...]),
         (small_a1[...], small_m1[...], table1[...]),
@@ -367,12 +354,12 @@
         send[...] = rows[0].astype(BF16)
 
 
-def small_step(pos, scores, index, smalls, table1, earlier):
+def small_step(pos, scores0, scores1, index, smalls, earlier):
     samples, _, model = smalls[0].shape
     shape = (16 * samples + HIGH, model)
     return call(
-        small_kernel, pos, (scores, index, *smalls, table1), earlier, [(shape, F32), (shape, BF16)],
-        [((HIGH, model), F32)], work=8,
+        small_kernel, pos, (scores0, scores1, index, *smalls), earlier, [(shape, F32), (shape, BF16)],
+        [((HIGH, model), F32)] * 2, work=12,
     )
 
 
@@ -653,23 +640,28 @@
     return call(line_kernel, pos, (own, *got), earlier, [(shape, F32)] * 2, [(own.shape, F32)])
 
 
-def sum_kernel(keep, other, own, *messages):
-    size = own.shape[0]
-    for p in range(4):
-        total = keep[p * size : (p + 1) * size, :].astype(F32) + other[p * size : (p + 1) * size, :].astype(F32)
-        if p == 0:
-            own[...] = total
-        else:
-            messages[p - 1][...] = total.astype(BF16)
-
-
-def sum_step(keep, other):
-    shape = (keep.shape[0] // 4, keep.shape[1])
+def first_kernel(keep1, other1, keep_m, other_m, own1, own_m, *messages):
+    at = 0
+    for keep, other, own in ((keep1, other1, own1), (keep_m, other_m, own_m)):
+        size = own.shape[0]
+        for p in range(4):
+            total = keep[p * size : (p + 1) * size, :].astype(F32) + other[p * size : (p + 1) * size, :].astype(F32)
+            if p == 0:
+                own[...] = total
+            else:
+                messages[p - 1][at : at + size, :] = total.astype(BF16)
+        at += size
+
+
+def first_step(keep1, other1, keep_m, other_m):
+    model = keep1.shape[1]
+    one, two = keep1.shape[0] // 4, keep_m.shape[0] // 4
     return pl.pallas_call(
-        sum_kernel,
-        out_shape=[jax.ShapeDtypeStruct(shape, F32)] + [jax.ShapeDtypeStruct(shape, BF16)] * 3,
+        first_kernel,
+        out_shape=[jax.ShapeDtypeStruct((one, model), F32), jax.ShapeDtypeStruct((two, model), F32)]
+        + [jax.ShapeDtypeStruct((one + two, model), BF16)] * 3,
         compiler_params=pltpu.CompilerParams(vmem_limit_bytes=VMEM_BYTES),
-    )(keep, other)
+    )(keep1, other1, keep_m, other_m)
 
 
 def halve(bit, own, got, keep, send):
@@ -704,79 +696,55 @@
         out[pl.ds(pl.multiple_of(at + (2 * high + 1 - bit) * n, 16), n), :] = got[rows, :]
 
 
-def a_kernel(pos, own1, got_a, got_b, got_c, keep_m, other_m, keep1, send1, own_m, *messages):
-    halve(pos[2] & 1, own1, (got_a, got_b, got_c), keep1, send1)
-    sum_kernel(keep_m, other_m, own_m, *messages)
-
-
-def a_step(pos, own1, got1, keep_m, other_m):
-    two = (own1.shape[0] // 2, own1.shape[1])
-    one = (keep_m.shape[0] // 4, keep_m.shape[1])
-    return call(a_kernel, pos, (own1, *got1, keep_m, other_m), (), [(two, F32), (two, BF16), (one, F32)] + [(one, BF16)] * 3, [])
-
-
-def b_kernel(pos, kept1, got1, own_m, got_a, got_b, got_c, keep1, send1, keep_m, send_m):
-    quarter(pos[2] >> 1, kept1, got1, keep1, send1)
-    halve(pos[2] & 1, own_m, (got_a, got_b, got_c), keep_m, send_m)
-
-
-def b_step(pos, kept1, got1, own_m, got_m):
-    one, two = (kept1.shape[0] // 2, kept1.shape[1]), (own_m.shape[0] // 2, own_m.shape[1])
-    return call(b_kernel, pos, (kept1, got1, own_m, *got_m), (), [(one, F32), (one, BF16), (two, F32), (two, BF16)], [])
-
-
-def c_kernel(pos, kept1, got1, kept_m, got_m, quarter1, keep_m, send_m):
-    quarter1[...] = (kept1[...] + got1[...].astype(F32)).astype(BF16)
-    quarter(pos[2] >> 1, kept_m, got_m, keep_m, send_m)
-
-
-def c_step(pos, kept1, got1, kept_m, got_m):
-    one = (kept_m.shape[0] // 2, kept_m.shape[1])
-    return call(c_kernel, pos, (kept1, got1, kept_m, got_m), (), [(kept1.shape, BF16), (one, F32), (one, BF16)], [])
-
-
-def d_kernel(pos, quarter1, got1, kept_m, got_m, pair1, quarter_m):
-    pair_up(pos[2] >> 1, quarter1, got1, pair1)
-    quarter_m[...] = (kept_m[...] + got_m[...].astype(F32)).astype(BF16)
-
-
-def d_step(pos, quarter1, got1, kept_m, got_m):
-    two = (2 * quarter1.shape[0], quarter1.shape[1])
-    return call(d_kernel, pos, (quarter1, got1, kept_m, got_m), (), [(two, BF16), (kept_m.shape, BF16)], [])
-
-
-def e_kernel(pos, pair1, got1, quarter_m, got_m, half1, pair_m):
-    whole_from(pos[2] & 1, pair1, got1, half1)
-    pair_up(pos[2] >> 1, quarter_m, got_m, pair_m)
-
-
-def e_step(pos, pair1, got1, quarter_m, got_m):
-    two = (2 * quarter_m.shape[0], quarter_m.shape[1])
-    return call(e_kernel, pos, (pair1, got1, quarter_m, got_m), (), [((2 * pair1.shape[0], pair1.shape[1]), BF16), (two, BF16)], [])
-
-
-def g_kernel(pos, quarter_a, got_a, got_b, got_c, pair_m, got_m, half1, *rest):
+def halve_kernel(pos, own, got_a, got_b, got_c, keep, send):
+    halve(pos[2] & 1, own, (got_a, got_b, got_c), keep, send)
+
+
+def halve_step(pos, own, got):
+    shape = (own.shape[0] // 2, own.shape[1])
+    return call(halve_kernel, pos, (own, *got), (), [(shape, F32), (shape, BF16)], [])
+
+
+def quarter_kernel(pos, kept, got, keep, send):
+    quarter(pos[2] >> 1, kept, got, keep, send)
+
+
+def quarter_step(pos, kept, got):
+    shape = (kept.shape[0] // 2, kept.shape[1])
+    return call(quarter_kernel, pos, (kept, got), (), [(shape, F32), (shape, BF16)], [])
+
+
+def pair_kernel(pos, own, got, out):
+    pair_up(pos[2] >> 1, own, got, out)
+
+
+def pair_step(pos, own, got):
+    return call(pair_kernel, pos, (own, got), (), [((2 * own.shape[0], own.shape[1]), BF16)], [])[0]
+
+
+def g_kernel(cut, pos, quarter_a, got_a, got_b, got_c, pair1, got1, *rest):
     own, send = rest[-2:]
     n = quarter_a.shape[0]
 
     def layer0(out):
         for j, piece in enumerate((quarter_a, got_a, got_b, got_c)):
-            out[pl.ds(pl.multiple_of((pos[2] ^ j) * n, 16), n), :] = piece[...]
-        whole_from(pos[2] & 1, pair_m, got_m, out, 4 * n)
+            out[pl.ds(pl.multiple_of((pos[2] ^ j) * cut, 16), cut), :] = piece[:cut, :]
+            out[pl.ds(pl.multiple_of(4 * cut + (pos[2] ^ j) * (n - cut), 16), n - cut), :] = piece[cut:, :]
 
     @pl.when(pos[0] == 0)
     def _():
         layer0(own)
-        send[...] = half1[...]
+        whole_from(pos[2] & 1, pair1, got1, send)
 
     @pl.when(pos[0] == 1)
     def _():
         layer0(send)
-        own[...] = half1[...]
-
-
-def g_step(pos, quarter_a, got_a, pair_m, got_m, half1, earlier):
-    return call(g_kernel, pos, (quarter_a, *got_a, pair_m, got_m, half1), earlier, [(half1.shape, BF16)] * 2, [])
+        whole_from(pos[2] & 1, pair1, got1, own)
+
+
+def g_step(pos, cut, quarter_a, got_a, pair1, got1, earlier):
+    shape = (2 * pair1.shape[0], pair1.shape[1])
+    return call(functools.partial(g_kernel, cut), pos, (quarter_a, *got_a, pair1, got1), earlier, [(shape, BF16)] * 2, [])
 
 
 def plane_kernel(samples, pos, keep, other, kept_small, other_small, cond, own, own_small, *rest):
@@ -824,21 +792,25 @@
     )
 
 
-def column_kernel(samples, pos, own, own_small, got_a, got_b, got_c, part, own_out, *rest):
+def column_kernel(samples, pos, own, own_small, got_a, got_b, got_c, own_m, first_a, first_b, first_c, part, own_out, *rest):
     messages, work = rest[:3], rest[3]
     rank = pos[2]
-    size, model = own.shape
-    n = size // 4
+    size, size_m = own.shape[0], own_m.shape[0]
+    n, nm = size // 4, size_m // 4
+    skip = first_a.shape[0] - size_m
     got = (got_a, got_b, got_c)
     for j in range(4):
         at = pl.multiple_of((rank ^ j) * n, 16)
         total = own[pl.ds(at, n), :]
         for piece in got:
             total = total + piece[pl.ds(at, n), :].astype(F32)
-        if j == 0:
-            part[...] = total
-        else:
-            messages[j - 1][:n, :] = total.astype(BF16)
+        at = pl.multiple_of((rank ^ j) * nm, 16)
+        total_m = own_m[pl.ds(at, nm), :]
+        for piece in (first_a, first_b, first_c):
+            total_m = total_m + piece[pl.ds(skip + at, nm), :].astype(F32)
+        out = part if j == 0 else messages[j - 1]
+        out[:n, :] = total.astype(out.dtype)
+        out[n : n + nm, :] = total_m.astype(out.dtype)
     smalls = [own_small[...].astype(F32)] + [piece[size:, :].astype(F32) for piece in got]
     work[...] = jnp.zeros_like(work)
     for p in range(4):
@@ -851,15 +823,16 @@
     small = work[...].astype(BF16)
     own_out[...] = small
     for message in messages:
-        message[n:, :] = small
-
-
-def column_step(pos, own, own_small, got, samples):
-    size, model = own.shape
+        message[n + nm :, :] = small
+
+
+def column_step(pos, own, own_small, got, own_m, first, samples):
+    model = own.shape[1]
+    n = (own.shape[0] + own_m.shape[0]) // 4
     small = -(-(28 * samples + 8 + HIGH) // 16) * 16
-    outs = [((size // 4, model), F32), ((small, model), BF16)] + [((size // 4 + small, model), BF16)] * 3
+    outs = [((n, model), F32), ((small, model), BF16)] + [((n + small, model), BF16)] * 3
     return call(
-        functools.partial(column_kernel, samples), pos, (own, own_small, *got), (), outs, [((small, model), F32)]
+        functools.partial(column_kernel, samples), pos, (own, own_small, *got, own_m, *first), (), outs, [((small, model), F32)]
     )
 
 
@@ -916,6 +889,51 @@
     )
 
 
+def plane_kernel(samples, pos, keep, other, kept_small, other_small, cond, own, own_small, *rest):
+    messages, work = rest[:3], rest[3]
+    section = pos[0]
+    size, model = own.shape
+    for p in range(4):
+        rows = slice(p * size, (p + 1) * size)
+        total = keep[rows, :].astype(F32) + other[rows, :].astype(F32)
+        if p == 0:
+            own[...] = total
+        else:
+            messages[p - 1][:size, :] = total.astype(BF16)
+    theirs = other_small[...].astype(F32)
+    mine = kept_small[...]
+    each = samples // 2
+    work[...] = jnp.zeros_like(work)
+    for b in range(each):
+        for kind in range(6):
+            row = b * 8 + kind if kind < 3 else (each + b) * 8 + kind - 3
+            work[pl.ds(kind * samples + section * each + b, 1), :] = mine[row : row + 1, :]
+            work[pl.ds(kind * samples + (1 - section) * each + b, 1), :] = theirs[row : row + 1, :]
+    work[6 * samples : 7 * samples, :] = cond[...].astype(F32)
+    both = mine + theirs
+    bias_rows = sum(both[(each + b) * 8 + 3 : (each + b) * 8 + 8, :] for b in range(each))
+    more_rows = sum(both[b * 8 + 3 : b * 8 + 6, :] for b in range(each))
+    at = 7 * samples
+    work[at : at + 5, :] = bias_rows
+    work[at + 5 : at + 8, :] = more_rows
+    work[at + 8 : at + 8 + HIGH, :] = both[2 * each * 8 :, :]
+    small = work[...].astype(BF16)
+    own_small[...] = small
+    for message in messages:
+        message[size:, :] = small
+
+
+def plane_step(pos, keep, other, kept_small, other_small, cond):
+    samples, model = cond.shape
+    size = keep.shape[0] // 4
+    small = -(-(7 * samples + 8 + HIGH) // 16) * 16
+    outs = [((size, model), F32), ((small, model), BF16)] + [((size + small, model), BF16)] * 3
+    return call(
+        functools.partial(plane_kernel, samples), pos, (keep, other, kept_small, other_small, cond), (), outs,
+        [((small, model), F32)],
+    )
+
+
 def cond_kernel(samples, pos, small, cond, *rest):
     out, w_ada = rest[-2:]
     model = cond.shape[1]
@@ -1188,25 +1206,18 @@
         w_ada_pieces = [lax.all_gather(w_ada[0], "fsdp", axis=0, tiled=True)]
     qkv, probs, att, branch, middle, act, slope, out_branch, h1 = forward_layer(0, z, pos, h0, lines, bias_heads, weights, w_ada_pieces[:1] if direct else [])
     out1, d_h1, small_a1, small_m1, scores1, keep1, send1 = both_ways(1, z, pos, h1, grad1, lines, bias_heads, weights, w_ada_pieces[1:])
+    d_middle, small_m0, keep_m0, send_m0 = backward_mlp(0, z, pos, d_h1, middle, lines, act, slope, out_branch, weights, [])
+    pieces = z.pieces
     rows = half * length
-    table1 = table_step(scores1, index)
-    other1 = after([swap_section(send1)], [table1])[0]
-    if direct:
-        own1, *messages = sum_step(keep1, other1)
-        earlier = messages
-    else:
-        earlier = []
-    d_middle, small_m0, keep_m0, send_m0 = backward_mlp(0, z, pos, d_h1, middle, lines, act, slope, out_branch, weights, earlier)
-    if direct:
-        got1 = after(to_peers(messages, "fsdp"), [d_middle])
-        send_m0 = after([send_m0], got1)[0]
+    other1 = swap_section(send1)
     other_m0 = swap_section(send_m0)
     if direct:
-        keep_z1, send_z1, own_m, *messages = a_step(pos, own1, got1, keep_m0, other_m0)
-        earlier = [send_z1, *messages]
+        own1, own_m, *first_messages = first_step(keep1, other1, keep_m0, other_m0)
+        earlier = first_messages
     else:
-        sums1 = section_sums(keep1, other1[: keep1.shape[0]], z.pieces)
-        sums_m0 = section_sums(keep_m0, other_m0, z.pieces)
+        sums1 = section_sums(keep1, other1[: keep1.shape[0]], pieces)
+        sums_m0 = section_sums(keep_m0, other_m0, pieces)
+        earlier = []
     d_h0, small_a0, scores0, keep_a0, send_a0 = backward_attention(
         0, z, pos, h0, lines, qkv, probs, att, branch, d_middle, d_h1, weights, earlier
     )
@@ -1217,35 +1228,34 @@
         return lax.ppermute(value, "rep", pairs_of(replicas, step))
 
     if direct:
-        got_z1, *got_m = after([replica(send_z1, 1), *to_peers(messages, "fsdp")], [d_h0])
-        other_a0 = swap_section(after([send_a0], [got_z1, *got_m])[0])
-        keep_z1, send_z1, keep_zm, send_zm = b_step(pos, keep_z1, got_z1, own_m, got_m)
-        kept_small, send_small = small_step(pos, scores0, index, smalls, table1, [send_z1, send_zm])
+        kept_small, send_small = small_step(pos, scores0, scores1, index, smalls, [])
         other_small = swap_section(send_small)
-        other_a0, got_z1, got_zm = after([other_a0, replica(send_z1, 2), replica(send_zm, 1)], [kept_small])
+        other_a0 = after([swap_section(send_a0)], [kept_small])[0]
         own_a0, own_small, *messages = plane_step(pos, keep_a0, other_a0, kept_small, other_small, conditioning)
         got = to_peers(messages, "fsdp")
-        got_z1, got_zm = after([got_z1, got_zm], [own_small])
-        quarter1, keep_zm, send_zm = c_step(pos, keep_z1, got_z1, keep_zm, got_zm)
-        part0, plane_small, *messages = column_step(pos, own_a0, own_small, got, samples)
-        got_z1, got_zm = after([replica(quarter1, 2), replica(send_zm, 2)], [plane_small])
-        got = to_peers(messages, "rep")
-        pair1, quarter_m = d_step(pos, quarter1, got_z1, keep_zm, got_zm)
-        cond_part = cond_step(pos, after([own_small], [pair1])[0], w_ada_pieces, conditioning)
+        got_first = after(to_peers(first_messages, "fsdp"), [own_small])
+        keep_z, send_z = halve_step(pos, own1, got_first)
+        part0, plane_small, *messages = column_step(pos, own_a0, own_small, got, own_m, got_first, samples)
+        got_z = after([replica(send_z, 1)], [plane_small])[0]
+        keep_z, send_z = quarter_step(pos, keep_z, got_z)
+        cond_part = cond_step(pos, after([own_small], [send_z])[0], w_ada_pieces, conditioning)
+        got_z = after([replica(send_z, 2)], [cond_part])[0]
+        quarter1 = (keep_z + got_z.astype(F32)).astype(BF16)
+        got = after(to_peers(messages, "rep"), [quarter1])
         size = part0.shape[0]
         quarter0 = add_pieces(part0, [x[:size] for x in got]).astype(BF16)
-        got_z1, got_zm, cond_part = after([replica(pair1, 1), replica(quarter_m, 2), cond_part], [quarter0])
-        half1, pair_m = e_step(pos, pair1, got_z1, quarter_m, got_zm)
         g_ada, g_b_ada, g_b_qv, g_b_proj, g_b_fc1, g_b_fc2, g_table = finish_step(
             pos, plane_small, got, samples, width, heads, entries
         )
+        got_z, cond_part = after([replica(quarter1, 2), cond_part], [quarter0, g_ada])
+        pair1 = pair_step(pos, quarter1, got_z)
         cond_grad = cond_part + swap_section(cond_part)
         own_half, send_half = g_step(
-            pos, quarter0, from_peers(quarter0, "rep"), pair_m, replica(pair_m, 1), half1, [g_ada, cond_grad]
+            pos, own_a0.shape[0] // 4, quarter0, from_peers(quarter0, "rep"), pair1, replica(pair1, 1), [g_ada, cond_grad]
         )
     else:
         other_a0 = swap_section(send_a0)
-        kept_small, send_small = small_step(pos, scores0, index, smalls, table1, [])
+        kept_small, send_small = small_step(pos, scores0, scores1, index, smalls, [])
         theirs = swap_section(send_small).astype(F32)
         both = kept_small + theirs
         cut = half * 8

time: 246 us -> 235 us (0.955)
  starting transfers between devices: 47.4 us -> 37.7 us
  Pallas kernels: 131 us -> 123 us
  waiting for transfers between devices: 42.2 us -> 47.5 us
    ppermute x8 -> x4, waiting for transfers between devices: 3.98 us -> 24.7 us  [replica(): return lax.ppermute(value, 'rep', pairs_of(replicas, step))]
    ppermute x15 -> x12, waiting for transfers between devices: 18.8 us -> 2.93 us  [to_peers(): lax.ppermute(messages[p - 1], axis, pairs_of(count, p))]
    ppermute x8 -> x4, starting transfers between devices: 10.9 us -> 3.5 us  [replica(): return lax.ppermute(value, 'rep', pairs_of(replicas, step))]
    pallas_call x2 -> x1, Pallas kernels: 11.3 us -> 4.81 us  [first_step(): pl.pallas_call(first_kernel, out_shape=[jax.ShapeDtypeStruct((one, model)...]
    ppermute x15 -> x12, starting transfers between devices: 18.3 us -> 14.9 us  [to_peers(): lax.ppermute(messages[p - 1], axis, pairs_of(count, p))]
    pallas_call x18 -> x16, Pallas kernels: 106 us -> 105 us  [call(): pl.pallas_call(kernel, out_shape=[jax.ShapeDtypeStruct(shape, dtype) for...]
    unnamed x111 -> x95, local copies, waits for them, and re-layouts: 12.5 us -> 12.5 us
  transfers between devices with their start and end apart: 49 -> 42, of which waited for: 14 -> 11; matrix products, arithmetic and copies ran while one was open for 5% -> 6% of each run, Pallas kernels for 36% -> 37%
where the time goes in v9:
time: 235 us
  Pallas kernels  123 us (52%)
  waiting for transfers between devices  47.5 us (20%)
  starting transfers between devices  37.7 us (16%)
  local copies, waits for them, and re-layouts  16.7 us (7%)
  other arithmetic  8.38 us (4%)
    pallas_call x16, Pallas kernels, call(): pl.pallas_call(kernel, out_shape=[jax.ShapeDtypeStruct(shape, dtype) for...  105 us
    ppermute x4, waiting for transfers between devices, replica(): return lax.ppermute(value, 'rep', pairs_of(replicas, step))  24.7 us
    ppermute x12, starting transfers between devices, to_peers(): lax.ppermute(messages[p - 1], axis, pairs_of(count, p))  14.9 us
    ppermute x9, starting transfers between devices, from_peers(): lax.ppermute(value, axis, pairs_of(lax.axis_size(axis), p))  12.6 us
    unnamed x95, local copies, waits for them, and re-layouts  12.5 us
    pallas_call x1, Pallas kernels, lookup(): pl.pallas_call(lookup_kernel, out_shape=jax.ShapeDtypeStruct((heads, leng...  11.2 us
    ppermute x1, waiting for transfers between devices, per_device(): got_second = lax.ppermute(got_y[middle_row:], 'fsdp', pairs_of(shards, 1))  9.88 us
    ppermute x13, waiting for transfers between devices, swap_section(): return lax.ppermute(value, 'section', [(0, 1), (1, 0)])  4.98 us
  transfers between devices with their start and end apart: 42, of which 11 were waited for; matrix products, arithmetic and copies ran while one was open for 6% of the time, Pallas kernels for 37%

profile of v9, /device:TPU:0, one launch (start us, length us, event | category | flops | bytes accessed | tf_op | source)
XLA Modules:
  0.0 234.6 jit_solution(8586595360080227530)
XLA Ops:
  0.7 4.0 %collective-permute-start.2 = (bf16[4,384]{1,0:T(4,128)(2,1)}, bf16[4,384]{1,0:T(4,128)(2,1)S(1)}, u32[]{:S(2)}, u32[]{:S(2)}) collective-permute-start(bf16[4,384]{1,0:T(4,128)(2,1)} %cond.3), channel_id=1, source_target_pairs={{0,12},{4,8},{8,4},{12,0},{1,13},{5,9},{9,5},{13,1},{2,14},{6,10},... | collective-permute-start | bytes 9224 | tf_op jit(solution)/shard_map/ppermute | solution.py:1130
  5.3 2.2 shard_map.263.rest_0_
  7.5 1.9 collective-permute-start.7
  12.2 11.2 %shard_map.264.rest_0_.own_bias = bf16[6,256,256]{2,1,0:T(8,128)(2,1)} custom-call(bf16[128,64]{1,0:T(8,128)(2,1)} %bitcast.43, s32[256,256]{1,0:T(8,128)} %index.3, bf16[1152,384]{1,0:T(8,128)(2,1)} %shard_map.263.rest_0_, bf16[4,384]{1,0:T(4,128)(2,1)} %copy-done.46, bf16[4,384]{1,0:T(4,128)(2,1)} %copy-done.45, bf16[4,384]{1,0:T(4,128)(2,1)} %copy-done.44), custom_call_target="tpu_custom_call" | custom-call | flops 11000000512 | tf_op jit(solution)/shard_map/pallas_call | solution.py:1053
  24.1 3.6 %shard_map.265 = (bf16[96,2304]{1,0:T(8,128)(2,1)}, f32[4,3072]{1,0:T(4,128)}, f32[4,3072]{1,0:T(4,128)}, f32[4,3072]{1,0:T(4,128)}, f32[4,3072]{1,0:T(4,128)}) custom-call(s32[3]{0:T(128)} %pad_add_fusion.pos, bf16[96,2304]{1,0:T(8,128)(2,1)} %bitcast.45, bf16[4,384]{1,0:T(4,128)(2,1)} %cond.3, bf16[4,384]{1,0:T(4,128)(2,1)} %copy-done.46, ...), custom_call_target="tpu_custom_call" | custom-call | flops 2000000000 | tf_op jit(solution)/shard_map/pallas_call | solution.py:516
  28.7 2.5 %collective-permute-start.5 = (f32[4,3072]{1,0:T(4,128)}, f32[4,3072]{1,0:T(4,128)S(1)}, u32[]{:S(2)}, u32[]{:S(2)}) collective-permute-start(f32[4,3072]{1,0:T(4,128)} %get-tuple-element.94), channel_id=1, source_target_pairs={{0,12},{4,8},{8,4},{12,0},{1,13},{5,9},{9,5},{13,1},{2,14},{6,10},... | collective-permute-start | bytes 147464 | tf_op jit(solution)/shard_map/ppermute | solution.py:1097
  35.8 9.9 %collective-permute-done.11.refs_2_.rest_4_ = bf16[576,384]{1,0:T(8,128)(2,1)S(1)} collective-permute-done((bf16[576,384]{1,0:T(8,128)(2,1)}, bf16[576,384]{1,0:T(8,128)(2,1)S(1)}, u32[]{:S(2)}, u32[]{:S(2)}) %collective-permute-start.11) | collective-permute-done | bytes 442400 | tf_op jit(solution)/shard_map/ppermute | solution.py:1177
  46.4 2.1 dynamic-slice_multiply_fusion
  55.1 15.1 %shard_map.269 = (bf16[512,1152]{1,0:T(8,128)(2,1)}, bf16[2,6,256,256]{3,2,1,0:T(8,128)(2,1)}, bf16[512,384]{1,0:T(8,128)(2,1)}, f32[512,384]{1,0:T(8,128)}, f32...) custom-call(s32[3]{0:T(128)} %pad_add_fusion.pos, ...), custom_call_target="tpu_custom_call" | custom-call | flops 15000000512 | tf_op jit(solution)/shard_map/pallas_call | solution.py:516
  70.3 4.3 %collective-permute-done.18.rest_11_.rest_2_ = bf16[96,2304]{1,0:T(8,128)(2,1)S(1)} collective-permute-done((bf16[96,2304]{1,0:T(8,128)(2,1)}, bf16[96,2304]{1,0:T(8,128)(2,1)S(1)}, u32[]{:S(2)}, u32[]{:S(2)}) %collective-permute-start.18) | collective-permute-done | bytes 442400 | tf_op jit(solution)/shard_map/ppermute | solution.py:1130
  75.6 26.1 %shard_map.270 = (bf16[512,384]{1,0:T(8,128)(2,1)}, bf16[512,384]{1,0:T(8,128)(2,1)}, f32[2,8,384]{2,1,0:T(8,128)}, f32[2,8,384]{2,1,0:T(8,128)}, bf16[6,256,256...) custom-call(s32[3]{0:T(128)} %pad_add_fusion.pos, bf16[512,384]{1,0:T(8,128)(2,1)} %get-tuple-element.101.h, ...), custom_call_target="tpu_custom_call" | custom-call | flops 24999999488 | tf_op jit(solution)/shard_map/pallas_call | solution.py:516
  101.7 12.0 %shard_map.271 = (f32[512,384]{1,0:T(8,128)}, f32[2,8,384]{2,1,0:T(8,128)}, bf16[1536,384]{1,0:T(8,128)(2,1)}, bf16[1536,384]{1,0:T(8,128)(2,1)}) custom-call(s32[3]{0:T(128)} %pad_add_fusion.pos, bf16[512,384]{1,0:T(8,128)(2,1)} %get-tuple-element.108.grad.d_h1, f32[512,384]{1,0:T(8,128)} %get-tuple-element.109.middle, ...), custom_call_target="tpu_custom_call" | custom-call | flops 12000000000 | tf_op jit(solution)/shard_map/pallas_call | solution.py:516
  114.2 2.7 %collective-permute-done.21.other_m = bf16[1536,384]{1,0:T(8,128)(2,1)S(1)} collective-permute-done((bf16[1536,384]{1,0:T(8,128)(2,1)}, bf16[1536,384]{1,0:T(8,128)(2,1)S(1)}, u32[]{:S(2)}, u32[]{:S(2)}) %collective-permute-start.21) | collective-permute-done | bytes 1179680 | tf_op jit(solution)/shard_map/ppermute | solution.py:1065
  118.6 4.8 %shard_map.272 = (f32[576,384]{1,0:T(8,128)}, f32[384,384]{1,0:T(8,128)}, bf16[960,384]{1,0:T(8,128)(2,1)}, bf16[960,384]{1,0:T(8,128)(2,1)}, bf16[960,384]{1,0:T(8,128)(2,1)}) custom-call(bf16[2304,384]{1,0:T(8,128)(2,1)} %get-tuple-element.114.keep1, bf16[2816,384]{1,0:T(8,128)(2,1)} %copy-done.1, bf16[1536,384]{1,0:T(8,128)(2,1)} %get-tuple-element.115.keep_m, ...), custom_call_target="tpu_custom_call" | custom-call | tf_op jit(solution)/shard_map/pallas_call | solution.py:659
  126.9 12.7 %shard_map.273 = (f32[512,384]{1,0:T(8,128)}, f32[2,8,384]{2,1,0:T(8,128)}, bf16[6,256,256]{2,1,0:T(8,128)(2,1)}, bf16[768,384]{1,0:T(8,128)(2,1)}, bf16[1280,384]{1,0:T(8,128)(2,1)}) custom-call(s32[3]{0:T(128)} %pad_add_fusion.pos, bf16[512,384]{1,0:T(8,128)(2,1)} %bitcast.35, f32[1,7680]{1,0:T(1,128)} %get-tuple-element.98.own_line, ...), custom_call_target="tpu_custom_call" | custom-call | flops 12999999488 | tf_op jit(solution)/shard_map/pallas_call | solution.py:516
  139.7 11.5 %shard_map.274 = (f32[48,384]{1,0:T(8,128)}, bf16[48,384]{1,0:T(8,128)(2,1)}) custom-call(s32[3]{0:T(128)} %pad_add_fusion.pos, bf16[6,256,256]{2,1,0:T(8,128)(2,1)} %get-tuple-element.122.scores0, bf16[6,256,256]{2,1,0:T(8,128)(2,1)} %get-tuple-element.123.scores1, s32[256,256]{1,0:T(8,128)} %index.3, f32[2,8,384]{2,1,0:T(8,128)} %get-tuple-element.124.small_a0, ...), custom_call_target="tpu_custom_call" | custom-call | flops 12000000000 | tf_op jit(solution)/shard_map/pallas_call | solution.py:516
  153.4 2.4 %shard_map.276 = (f32[192,384]{1,0:T(8,128)}, bf16[64,384]{1,0:T(8,128)(2,1)}, bf16[256,384]{1,0:T(8,128)(2,1)}, bf16[256,384]{1,0:T(8,128)(2,1)}, bf16[256,384]{1,0:T(8,128)(2,1)}) custom-call(s32[3]{0:T(128)} %pad_add_fusion.pos, bf16[768,384]{1,0:T(8,128)(2,1)} %get-tuple-element.130.keep, bf16[1280,384]{1,0:T(8,128)(2,1)} %shard_map.275.other, ...), custom_call_target="tpu_custom_call" | custom-call | flops 2000000000 | tf_op jit(solution)/shard_map/pallas_call | solution.py:516
  160.4 2.8 %shard_map.278 = (f32[288,384]{1,0:T(8,128)}, bf16[288,384]{1,0:T(8,128)(2,1)}) custom-call(s32[3]{0:T(128)} %pad_add_fusion.pos, f32[576,384]{1,0:T(8,128)} %get-tuple-element.129.own, bf16[960,384]{1,0:T(8,128)(2,1)} %get-tuple-element.133.got_a.first_a, bf16[960,384]{1,0:T(8,128)(2,1)} %get-tuple-element.134.got_b.first_b, ...), custom_call_target="tpu_custom_call" | custom-call | flops 2000000000 | tf_op jit(solution)/shard_map/pallas_call | solution.py:516
  164.8 2.9 %collective-permute-done.29.got_b = bf16[256,384]{1,0:T(8,128)(2,1)S(1)} collective-permute-done((bf16[256,384]{1,0:T(8,128)(2,1)}, bf16[256,384]{1,0:T(8,128)(2,1)S(1)}, u32[]{:S(2)}, u32[]{:S(2)}) %collective-permute-start.29) | collective-permute-done | bytes 196640 | tf_op jit(solution)/shard_map/ppermute | solution.py:1097
  168.5 3.1 %shard_map.279 = (f32[144,384]{1,0:T(8,128)}, bf16[144,384]{1,0:T(8,128)(2,1)}, bf16[288,384]{1,0:T(8,128)(2,1)}, bf16[288,384]{1,0:T(8,128)(2,1)}, bf16[288,384]{1,0:T(8,128)(2,1)}) custom-call(s32[3]{0:T(128)} %pad_add_fusion.pos, f32[192,384]{1,0:T(8,128)} %get-tuple-element.138.own, bf16[64,384]{1,0:T(8,128)(2,1)} %get-tuple-element.132.refs_3_.own_small.refs_0_, ...), custom_call_target="tpu_custom_call" | custom-call | flops 2000000000 | tf_op jit(solution)/shard_map/pallas_call | solution.py:516
  173.3 2.6 %collective-permute-start.34 = (bf16[288,384]{1,0:T(8,128)(2,1)}, bf16[288,384]{1,0:T(8,128)(2,1)S(1)}, u32[]{:S(2)}, u32[]{:S(2)}) collective-permute-start(bf16[288,384]{1,0:T(8,128)(2,1)} %get-tuple-element.148), channel_id=1, source_target_pairs={{0,2},{1,3},{2,0},{3,1},{4,6},{5,7},{6,4},{7,5},{8,10},{9,11},{10,... | collective-permute-start | bytes 663560 | tf_op jit(solution)/shard_map/ppermute | solution.py:1097
  176.7 1.8 shard_map.281
  178.5 1.9 collective-permute-start.31
  180.4 2.8 %shard_map.283.refs_1_ = f32[4,384]{1,0:T(4,128)} custom-call(s32[3]{0:T(128)} %pad_add_fusion.pos, bf16[64,384]{1,0:T(8,128)(2,1)} %shard_map.282.small, bf16[4,384]{1,0:T(4,128)(2,1)} %cond.3, bf16[96,2304]{1,0:T(8,128)(2,1)} %shard_map.268.rest_10_.rest_0_, bf16[96,2304]{1,0:T(8,128)(2,1)} %copy-done.33, bf16[96,2304]{1,0:T(8,128)(2,1)} %copy-done.32, ...), custom_call_target="tpu_custom_call" | custom-call | flops 2000000000 | tf_op jit(solution)/shard_map/pallas_call | solution.py:516
  183.2 16.3 %collective-permute-done.31.refs_0_ = bf16[144,384]{1,0:T(8,128)(2,1)S(1)} collective-permute-done((bf16[144,384]{1,0:T(8,128)(2,1)}, bf16[144,384]{1,0:T(8,128)(2,1)S(1)}, u32[]{:S(2)}, u32[]{:S(2)}) %collective-permute-start.31) | collective-permute-done | bytes 110624 | tf_op jit(solution)/shard_map/ppermute | solution.py:1228
  203.7 2.5 %collective-permute-start.39 = (bf16[144,384]{1,0:T(8,128)(2,1)S(1)}, bf16[144,384]{1,0:T(8,128)(2,1)S(1)}, u32[]{:S(2)}, u32[]{:S(2)}) collective-permute-start(bf16[144,384]{1,0:T(8,128)(2,1)S(1)} %add_convert_fusion.refs_2_.quarter_a), channel_id=1, source_target_pairs={{0,3},{1,2},{2,1},{3,0},{4,7},{5,6},{6,5},{7,4},{8,11},{9,10},{10,... | collective-permute-start | bytes 331784 | tf_op jit(solution)/shard_map/ppermute | solution.py:1130
  206.2 2.0 collective-permute-start.38
  208.2 2.9 %shard_map.286 = (f32[96,2304]{1,0:T(8,128)}, f32[1,576]{1,0:T(1,128)}, f32[1,192]{1,0:T(1,128)}, f32[1,96]{1,0:T(1,128)}, f32[1,384]{1,0:T(1,128)}, /*index=5*/f32[1,96]{1,0:T(1,128)}, f32[6,961]{1,0:T(8,128)}) custom-call(s32[3]{0:T(128)} %pad_add_fusion.pos, bf16[144,384]{1,0:T(8,128)(2,1)} %get-tuple-element.143.refs_1_.own_small, ...), custom_call_target="tpu_custom_call" | custom-call | flops 2000000000 | tf_op jit(solution)/shard_map/pallas_call | solution.py:516
  211.1 2.2 collective-permute-done.32.refs_0_
  217.5 6.2 %collective-permute-done.40.got1 = bf16[288,384]{1,0:T(8,128)(2,1)S(1)} collective-permute-done((bf16[288,384]{1,0:T(8,128)(2,1)}, bf16[288,384]{1,0:T(8,128)(2,1)S(1)}, u32[]{:S(2)}, u32[]{:S(2)}) %collective-permute-start.40) | collective-permute-done | bytes 221216 | tf_op jit(solution)/shard_map/ppermute | solution.py:1228
  224.5 2.3 shard_map.289
  232.1 2.5 %shard_map.290 = (f32[96,1152]{1,0:T(8,128)}, f32[96,384]{1,0:T(8,128)}, f32[96,1536]{1,0:T(8,128)}, f32[384,384]{1,0:T(8,128)}) custom-call(s32[3]{0:T(128)} %pad_add_fusion.pos, bf16[576,384]{1,0:T(8,128)(2,1)} %get-tuple-element.156.own, bf16[576,384]{1,0:T(8,128)(2,1)} %copy-done.34), custom_call_target="tpu_custom_call" | custom-call | flops 2000000000 | tf_op jit(solution)/shard_map/pallas_call | solution.py:516
  (195 shorter events, 49.6 us)
Async XLA Ops:
  0.7 10.9 %collective-permute-start.2 = (bf16[4,384]{1,0:T(4,128)(2,1)}, bf16[4,384]{1,0:T(4,128)(2,1)S(1)}, u32[]{:S(2)}, u32[]{:S(2)}) collective-permute-start(bf16[4,384]{1,0:T(4,128)(2,1)} %cond.3), channel_id=1, source_target_pairs={{0,12},{4,8},{8,4},{12,0},{1,13},{5,9},{9,5},{13,1},{2,14},{6,10},... | collective-permute-start | bytes 9224 | tf_op jit(solution)/shard_map/ppermute | solution.py:1130
  7.5 21.2 %collective-permute-start.7 = (bf16[1152,384]{1,0:T(8,128)(2,1)}, bf16[1152,384]{1,0:T(8,128)(2,1)S(1)}, u32[]{:S(2)}, u32[]{:S(2)}) collective-permute-start(bf16[1152,384]{1,0:T(8,128)(2,1)} %shard_map.263.rest_0_), channel_id=1, source_target_pairs={{0,8},{4,12},{8,0},{12,4},{1,9},{5,13},{9,1},{13,5},{2,10},{6,14},... | collective-permute-start | bytes 2654216 | tf_op jit(solution)/shard_map/ppermute | solution.py:1173
  9.4 21.8 %collective-permute-start.6 = (bf16[1152,384]{1,0:T(8,128)(2,1)}, bf16[1152,384]{1,0:T(8,128)(2,1)S(1)}, u32[]{:S(2)}, u32[]{:S(2)}) collective-permute-start(bf16[1152,384]{1,0:T(8,128)(2,1)} %shard_map.263.rest_0_), channel_id=1, source_target_pairs={{0,4},{4,0},{8,12},{12,8},{1,5},{5,1},{9,13},{13,9},{2,6},{6,2},{1... | collective-permute-start | bytes 2654216 | tf_op jit(solution)/shard_map/ppermute | solution.py:1172
  23.5 10.6 %collective-permute-start.9 = (bf16[6,256,256]{2,1,0:T(8,128)(2,1)}, bf16[6,256,256]{2,1,0:T(8,128)(2,1)}, u32[]{:S(2)}, u32[]{:S(2)}) collective-permute-start(bf16[6,256,256]{2,1,0:T(8,128)(2,1)} %shard_map.264.rest_0_.own_bias), channel_id=1, source_target_pairs={{0,16},{16,0},{1,17},{17,1},{2,18},{18,2},{3,19},{19,3},{4,20},{20... | collective-permute-start | bytes 2359304 | tf_op jit(solution)/shard_map/ppermute | solution.py:1065
  31.2 18.8 %collective-permute-start.12 = (bf16[1152,384]{1,0:T(8,128)(2,1)S(1)}, bf16[1152,384]{1,0:T(8,128)(2,1)}, u32[]{:S(2)}, u32[]{:S(2)}) collective-permute-start(bf16[1152,384]{1,0:T(8,128)(2,1)S(1)} %copy-done.6), channel_id=1, source_target_pairs={{0,16},{16,0},{1,17},{17,1},{2,18},{18,2},{3,19},{19,3},{4,20},{20... | collective-permute-start | bytes 2654216 | tf_op jit(solution)/shard_map/ppermute | solution.py:1065
  33.1 12.6 %collective-permute-start.11 = (bf16[576,384]{1,0:T(8,128)(2,1)}, bf16[576,384]{1,0:T(8,128)(2,1)S(1)}, u32[]{:S(2)}, u32[]{:S(2)}) collective-permute-start(bf16[576,384]{1,0:T(8,128)(2,1)} %slice.29), channel_id=1, source_target_pairs={{0,4},{4,0},{8,12},{12,8},{1,5},{5,1},{9,13},{13,9},{2,6},{6,2},{1... | collective-permute-start | bytes 1327112 | tf_op jit(solution)/shard_map/ppermute | solution.py:1177
  33.9 12.4 %collective-permute-start.10 = (bf16[576,384]{1,0:T(8,128)(2,1)}, bf16[576,384]{1,0:T(8,128)(2,1)}, u32[]{:S(2)}, u32[]{:S(2)}) collective-permute-start(bf16[576,384]{1,0:T(8,128)(2,1)} %slice.28), channel_id=1, source_target_pairs={{0,8},{4,12},{8,0},{12,4},{1,9},{5,13},{9,1},{13,5},{2,10},{6,14},... | collective-permute-start | bytes 1327112 | tf_op jit(solution)/shard_map/ppermute | solution.py:1176
  34.1 20.2 %collective-permute-start.14 = (bf16[1152,384]{1,0:T(8,128)(2,1)S(1)}, bf16[1152,384]{1,0:T(8,128)(2,1)}, u32[]{:S(2)}, u32[]{:S(2)}) collective-permute-start(bf16[1152,384]{1,0:T(8,128)(2,1)S(1)} %collective-permute-done.7.refs_4_.rest_2_), channel_id=1, source_target_pairs={{0,16},{16,0},{1,17},{17,1},{2,18},{18,2},{3,19},{19,3},{4,20},{20... | collective-permute-start | bytes 2654216 | tf_op jit(solution)/shard_map/ppermute | solution.py:1065
  34.1 21.1 %collective-permute-start.13 = (bf16[1152,384]{1,0:T(8,128)(2,1)S(1)}, bf16[1152,384]{1,0:T(8,128)(2,1)}, u32[]{:S(2)}, u32[]{:S(2)}) collective-permute-start(bf16[1152,384]{1,0:T(8,128)(2,1)S(1)} %collective-permute-done.6.refs_3_.rest_1_), channel_id=1, source_target_pairs={{0,16},{16,0},{1,17},{17,1},{2,18},{18,2},{3,19},{19,3},{4,20},{20... | collective-permute-start | bytes 2654216 | tf_op jit(solution)/shard_map/ppermute | solution.py:1065
  45.7 7.4 %collective-permute-start.16 = (bf16[576,384]{1,0:T(8,128)(2,1)S(1)}, bf16[576,384]{1,0:T(8,128)(2,1)}, u32[]{:S(2)}, u32[]{:S(2)}) collective-permute-start(bf16[576,384]{1,0:T(8,128)(2,1)S(1)} %collective-permute-done.11.refs_2_.rest_4_), channel_id=1, source_target_pairs={{0,16},{16,0},{1,17},{17,1},{2,18},{18,2},{3,19},{19,3},{4,20},{20... | collective-permute-start | bytes 1327112 | tf_op jit(solution)/shard_map/ppermute | solution.py:1065
  46.4 8.8 %collective-permute-start.15 = (bf16[576,384]{1,0:T(8,128)(2,1)}, bf16[576,384]{1,0:T(8,128)(2,1)}, u32[]{:S(2)}, u32[]{:S(2)}) collective-permute-start(bf16[576,384]{1,0:T(8,128)(2,1)} %collective-permute-done.10.refs_1_.rest_3_), channel_id=1, source_target_pairs={{0,16},{16,0},{1,17},{17,1},{2,18},{18,2},{3,19},{19,3},{4,20},{20... | collective-permute-start | bytes 1327112 | tf_op jit(solution)/shard_map/ppermute | solution.py:1065
  51.6 18.7 %collective-permute-start.19 = (bf16[96,2304]{1,0:T(8,128)(2,1)}, bf16[96,2304]{1,0:T(8,128)(2,1)S(1)}, u32[]{:S(2)}, u32[]{:S(2)}) collective-permute-start(bf16[96,2304]{1,0:T(8,128)(2,1)} %shard_map.268.rest_10_.rest_0_), channel_id=1, source_target_pairs={{0,12},{4,8},{8,4},{12,0},{1,13},{5,9},{9,5},{13,1},{2,14},{6,10},... | collective-permute-start | bytes 1327112 | tf_op jit(solution)/shard_map/ppermute | solution.py:1130
  53.1 21.6 %collective-permute-start.18 = (bf16[96,2304]{1,0:T(8,128)(2,1)}, bf16[96,2304]{1,0:T(8,128)(2,1)S(1)}, u32[]{:S(2)}, u32[]{:S(2)}) collective-permute-start(bf16[96,2304]{1,0:T(8,128)(2,1)} %shard_map.268.rest_10_.rest_0_), channel_id=1, source_target_pairs={{0,8},{4,12},{8,0},{12,4},{1,9},{5,13},{9,1},{13,5},{2,10},{6,14},... | collective-permute-start | bytes 1327112 | tf_op jit(solution)/shard_map/ppermute | solution.py:1130
  54.3 20.4 %collective-permute-start.17 = (bf16[96,2304]{1,0:T(8,128)(2,1)}, bf16[96,2304]{1,0:T(8,128)(2,1)S(1)}, u32[]{:S(2)}, u32[]{:S(2)}) collective-permute-start(bf16[96,2304]{1,0:T(8,128)(2,1)} %shard_map.268.rest_10_.rest_0_), channel_id=1, source_target_pairs={{0,4},{4,0},{8,12},{12,8},{1,5},{5,1},{9,13},{13,9},{2,6},{6,2},{1... | collective-permute-start | bytes 1327112 | tf_op jit(solution)/shard_map/ppermute | solution.py:1130
  101.7 15.3 %collective-permute-start.20 = (bf16[2816,384]{1,0:T(8,128)(2,1)}, bf16[2816,384]{1,0:T(8,128)(2,1)S(1)}, u32[]{:S(2)}, u32[]{:S(2)}) collective-permute-start(bf16[2816,384]{1,0:T(8,128)(2,1)} %get-tuple-element.103), channel_id=1, source_target_pairs={{0,16},{16,0},{1,17},{17,1},{2,18},{18,2},{3,19},{19,3},{4,20},{20... | collective-permute-start | bytes 6488072 | tf_op jit(solution)/shard_map/ppermute | solution.py:1065
  123.4 34.3 %collective-permute-start.23 = (bf16[960,384]{1,0:T(8,128)(2,1)}, bf16[960,384]{1,0:T(8,128)(2,1)S(1)}, u32[]{:S(2)}, u32[]{:S(2)}) collective-permute-start(bf16[960,384]{1,0:T(8,128)(2,1)} %get-tuple-element.117.rest_10_), channel_id=1, source_target_pairs={{0,4},{4,0},{8,12},{12,8},{1,5},{5,1},{9,13},{13,9},{2,6},{6,2},{1... | collective-permute-start | bytes 2211848 | tf_op jit(solution)/shard_map/ppermute | solution.py:1097
  124.1 35.2 %collective-permute-start.24 = (bf16[960,384]{1,0:T(8,128)(2,1)}, bf16[960,384]{1,0:T(8,128)(2,1)S(1)}, u32[]{:S(2)}, u32[]{:S(2)}) collective-permute-start(bf16[960,384]{1,0:T(8,128)(2,1)} %get-tuple-element.118.rest_11_), channel_id=1, source_target_pairs={{0,8},{4,12},{8,0},{12,4},{1,9},{5,13},{9,1},{13,5},{2,10},{6,14},... | collective-permute-start | bytes 2211848 | tf_op jit(solution)/shard_map/ppermute | solution.py:1097
  125.4 33.9 %collective-permute-start.25 = (bf16[960,384]{1,0:T(8,128)(2,1)}, bf16[960,384]{1,0:T(8,128)(2,1)S(1)}, u32[]{:S(2)}, u32[]{:S(2)}) collective-permute-start(bf16[960,384]{1,0:T(8,128)(2,1)} %get-tuple-element.119.rest_12_), channel_id=1, source_target_pairs={{0,12},{4,8},{8,4},{12,0},{1,13},{5,9},{9,5},{13,1},{2,14},{6,10},... | collective-permute-start | bytes 2211848 | tf_op jit(solution)/shard_map/ppermute | solution.py:1097
  139.6 12.1 %collective-permute-start.22 = (bf16[1280,384]{1,0:T(8,128)(2,1)}, bf16[1280,384]{1,0:T(8,128)(2,1)S(1)}, u32[]{:S(2)}, u32[]{:S(2)}) collective-permute-start(bf16[1280,384]{1,0:T(8,128)(2,1)} %get-tuple-element.121), channel_id=1, source_target_pairs={{0,16},{16,0},{1,17},{17,1},{2,18},{18,2},{3,19},{19,3},{4,20},{20... | collective-permute-start | bytes 2949128 | tf_op jit(solution)/shard_map/ppermute | solution.py:1065
  155.8 9.0 %collective-permute-start.28 = (bf16[256,384]{1,0:T(8,128)(2,1)}, bf16[256,384]{1,0:T(8,128)(2,1)S(1)}, u32[]{:S(2)}, u32[]{:S(2)}) collective-permute-start(bf16[256,384]{1,0:T(8,128)(2,1)} %get-tuple-element.139), channel_id=1, source_target_pairs={{0,4},{4,0},{8,12},{12,8},{1,5},{5,1},{9,13},{13,9},{2,6},{6,2},{1... | collective-permute-start | bytes 589832 | tf_op jit(solution)/shard_map/ppermute | solution.py:1097
  156.4 11.3 %collective-permute-start.29 = (bf16[256,384]{1,0:T(8,128)(2,1)}, bf16[256,384]{1,0:T(8,128)(2,1)S(1)}, u32[]{:S(2)}, u32[]{:S(2)}) collective-permute-start(bf16[256,384]{1,0:T(8,128)(2,1)} %get-tuple-element.140), channel_id=1, source_target_pairs={{0,8},{4,12},{8,0},{12,4},{1,9},{5,13},{9,1},{13,5},{2,10},{6,14},... | collective-permute-start | bytes 589832 | tf_op jit(solution)/shard_map/ppermute | solution.py:1097
  157.7 10.0 %collective-permute-start.30 = (bf16[256,384]{1,0:T(8,128)(2,1)}, bf16[256,384]{1,0:T(8,128)(2,1)S(1)}, u32[]{:S(2)}, u32[]{:S(2)}) collective-permute-start(bf16[256,384]{1,0:T(8,128)(2,1)} %get-tuple-element.141), channel_id=1, source_target_pairs={{0,12},{4,8},{8,4},{12,0},{1,13},{5,9},{9,5},{13,1},{2,14},{6,10},... | collective-permute-start | bytes 589832 | tf_op jit(solution)/shard_map/ppermute | solution.py:1097
  163.2 12.8 %collective-permute-start.27 = (bf16[288,384]{1,0:T(8,128)(2,1)}, bf16[288,384]{1,0:T(8,128)(2,1)S(1)}, u32[]{:S(2)}, u32[]{:S(2)}) collective-permute-start(bf16[288,384]{1,0:T(8,128)(2,1)} %get-tuple-element.137), channel_id=1, source_target_pairs={{0,1},{1,0},{2,3},{3,2},{4,5},{5,4},{6,7},{7,6},{8,9},{9,8},{10,11... | collective-permute-start | bytes 663560 | tf_op jit(solution)/shard_map/ppermute | solution.py:1228
  171.6 29.5 %collective-permute-start.33 = (bf16[288,384]{1,0:T(8,128)(2,1)}, bf16[288,384]{1,0:T(8,128)(2,1)S(1)}, u32[]{:S(2)}, u32[]{:S(2)}) collective-permute-start(bf16[288,384]{1,0:T(8,128)(2,1)} %get-tuple-element.147), channel_id=1, source_target_pairs={{0,1},{1,0},{2,3},{3,2},{4,5},{5,4},{6,7},{7,6},{8,9},{9,8},{10,11... | collective-permute-start | bytes 663560 | tf_op jit(solution)/shard_map/ppermute | solution.py:1097
  173.3 27.8 %collective-permute-start.34 = (bf16[288,384]{1,0:T(8,128)(2,1)}, bf16[288,384]{1,0:T(8,128)(2,1)S(1)}, u32[]{:S(2)}, u32[]{:S(2)}) collective-permute-start(bf16[288,384]{1,0:T(8,128)(2,1)} %get-tuple-element.148), channel_id=1, source_target_pairs={{0,2},{1,3},{2,0},{3,1},{4,6},{5,7},{6,4},{7,5},{8,10},{9,11},{10,... | collective-permute-start | bytes 663560 | tf_op jit(solution)/shard_map/ppermute | solution.py:1097
  175.9 25.2 %collective-permute-start.35 = (bf16[288,384]{1,0:T(8,128)(2,1)}, bf16[288,384]{1,0:T(8,128)(2,1)S(1)}, u32[]{:S(2)}, u32[]{:S(2)}) collective-permute-start(bf16[288,384]{1,0:T(8,128)(2,1)} %get-tuple-element.149), channel_id=1, source_target_pairs={{0,3},{1,2},{2,1},{3,0},{4,7},{5,6},{6,5},{7,4},{8,11},{9,10},{10,... | collective-permute-start | bytes 663560 | tf_op jit(solution)/shard_map/ppermute | solution.py:1097
  178.5 20.9 %collective-permute-start.31 = (bf16[144,384]{1,0:T(8,128)(2,1)}, bf16[144,384]{1,0:T(8,128)(2,1)S(1)}, u32[]{:S(2)}, u32[]{:S(2)}) collective-permute-start(bf16[144,384]{1,0:T(8,128)(2,1)} %get-tuple-element.145.refs_1_), channel_id=1, source_target_pairs={{0,2},{1,3},{2,0},{3,1},{4,6},{5,7},{6,4},{7,5},{8,10},{9,11},{10,... | collective-permute-start | bytes 331784 | tf_op jit(solution)/shard_map/ppermute | solution.py:1228
  201.0 12.3 %collective-permute-start.32 = (bf16[144,384]{1,0:T(8,128)(2,1)S(1)}, bf16[144,384]{1,0:T(8,128)(2,1)S(1)}, u32[]{:S(2)}, u32[]{:S(2)}) collective-permute-start(bf16[144,384]{1,0:T(8,128)(2,1)S(1)} %add_convert_fusion.1.refs_3_.own), channel_id=1, source_target_pairs={{0,2},{1,3},{2,0},{3,1},{4,6},{5,7},{6,4},{7,5},{8,10},{9,11},{10,... | collective-permute-start | bytes 331784 | tf_op jit(solution)/shard_map/ppermute | solution.py:1228
  203.7 13.8 %collective-permute-start.39 = (bf16[144,384]{1,0:T(8,128)(2,1)S(1)}, bf16[144,384]{1,0:T(8,128)(2,1)S(1)}, u32[]{:S(2)}, u32[]{:S(2)}) collective-permute-start(bf16[144,384]{1,0:T(8,128)(2,1)S(1)} %add_convert_fusion.refs_2_.quarter_a), channel_id=1, source_target_pairs={{0,3},{1,2},{2,1},{3,0},{4,7},{5,6},{6,5},{7,4},{8,11},{9,10},{10,... | collective-permute-start | bytes 331784 | tf_op jit(solution)/shard_map/ppermute | solution.py:1130
  206.2 11.3 %collective-permute-start.38 = (bf16[144,384]{1,0:T(8,128)(2,1)S(1)}, bf16[144,384]{1,0:T(8,128)(2,1)S(1)}, u32[]{:S(2)}, u32[]{:S(2)}) collective-permute-start(bf16[144,384]{1,0:T(8,128)(2,1)S(1)} %add_convert_fusion.refs_2_.quarter_a), channel_id=1, source_target_pairs={{0,2},{1,3},{2,0},{3,1},{4,6},{5,7},{6,4},{7,5},{8,10},{9,11},{10,... | collective-permute-start | bytes 331784 | tf_op jit(solution)/shard_map/ppermute | solution.py:1130
  208.2 9.3 %collective-permute-start.37 = (bf16[144,384]{1,0:T(8,128)(2,1)S(1)}, bf16[144,384]{1,0:T(8,128)(2,1)S(1)}, u32[]{:S(2)}, u32[]{:S(2)}) collective-permute-start(bf16[144,384]{1,0:T(8,128)(2,1)S(1)} %add_convert_fusion.refs_2_.quarter_a), channel_id=1, source_target_pairs={{0,1},{1,0},{2,3},{3,2},{4,5},{5,4},{6,7},{7,6},{8,9},{9,8},{10,11... | collective-permute-start | bytes 331784 | tf_op jit(solution)/shard_map/ppermute | solution.py:1130
  215.7 8.1 %collective-permute-start.40 = (bf16[288,384]{1,0:T(8,128)(2,1)}, bf16[288,384]{1,0:T(8,128)(2,1)S(1)}, u32[]{:S(2)}, u32[]{:S(2)}) collective-permute-start(bf16[288,384]{1,0:T(8,128)(2,1)} %shard_map.288.pair1), channel_id=1, source_target_pairs={{0,1},{1,0},{2,3},{3,2},{4,5},{5,4},{6,7},{7,6},{8,9},{9,8},{10,11... | collective-permute-start | bytes 663560 | tf_op jit(solution)/shard_map/ppermute | solution.py:1228
  (58 other events, 292.8 us)

commit v10 on v6

--- a/solution.py
+++ b/solution.py
@@ -586,7 +586,8 @@
 
 
 def partial_kernel(pos, w_ada, cond_a, cond_b, cond_c, cond_d, b_ada, b_qv, b_proj, b_fc1, b_fc2, *rest):
-    outs, whole = rest[-5:-1], rest[-1]
+    copied, outs, whole = rest[-6], rest[-5:-1], rest[-1]
+    copied[...] = w_ada[...]
     shard = pos[1]
     q, wide = w_ada.shape
     samples, model = cond_a.shape
@@ -613,12 +614,13 @@
     q, wide = w_ada.shape
     samples, model = conds[0].shape
     return call(
-        partial_kernel, pos, (w_ada, *conds, *biases), earlier, [((samples, wide + 2 * model), F32)] * 4,
+        partial_kernel, pos, (w_ada, *conds, *biases), earlier, [(w_ada.shape, BF16)] + [((samples, wide + 2 * model), F32)] * 4,
         [((4 * q, wide), BF16)],
     )
 
 
-def line_kernel(pos, own, got_a, got_b, got_c, keep, send, total):
+def line_kernel(pos, own, got_a, got_b, got_c, *rest):
+    keep, send, total = rest[-3:]
     section = pos[0]
     samples = own.shape[0]
     each = samples // 2
@@ -632,10 +634,10 @@
             out[:, at : at + 2 * model] = total[row : row + 1, 6 * model :]
 
 
-def line_step(pos, own, got):
+def line_step(pos, own, got, earlier):
     samples, model = own.shape[0], own.shape[1] // 8
     shape = (1, (3 * samples + 8) * model)
-    return call(line_kernel, pos, (own, *got), (), [(shape, F32)] * 2, [(own.shape, F32)])
+    return call(line_kernel, pos, (own, *got), earlier, [(shape, F32)] * 2, [(own.shape, F32)])
 
 
 def first_kernel(keep1, other1, keep_m, other_m, own, *messages):
@@ -1063,6 +1065,7 @@
     live = (jnp.arange(half)[:, None, None] < lax.dynamic_index_in_dim(micro_sizes[0], section, 0)).astype(BF16)
     h0 = own_samples(inputs).reshape(half * length, model)
     grad1 = (own_samples(cotangent) * live).reshape(half * length, model)
+    index = relative_bias_index
     own_raw = [w_qkv[0], w_proj[0], w_fc1[0], w_fc2[0]]
     width = model // shards
     if direct:
@@ -1071,14 +1074,18 @@
         middle_row = own_pack.shape[0] // 2
         got_x = lax.ppermute(own_pack, "fsdp", pairs_of(shards, 1))
         got_y = lax.ppermute(own_pack, "fsdp", pairs_of(shards, 2))
-        partial = partial_step(pos, w_ada[0], conds, (b_ada, b_qv, b_proj, b_fc1, b_fc2), [own_pack])
-        table = after([bias_table[0]], [own_pack])[0]
-        bias_own = lookup(table, relative_bias_index, [h0, grad1, *partial])
-        got_first = lax.ppermute(got_x[:middle_row], "fsdp", pairs_of(shards, 2))
-        got_second = lax.ppermute(got_y[middle_row:], "fsdp", pairs_of(shards, 1))
+        bias_own = lookup(bias_table[0], index, [own_pack, *conds[1:]])
+        got_x, got_y = after([got_x, got_y], [bias_own])
+        forward_x, forward_y = got_x[:middle_row], got_y[middle_row:]
+        w_ada_copy, *partial = partial_step(
+            pos, w_ada[0], conds, (b_ada, b_qv, b_proj, b_fc1, b_fc2), [bias_own]
+        )
+        got_first = lax.ppermute(forward_x, "fsdp", pairs_of(shards, 2))
+        got_second = lax.ppermute(forward_y, "fsdp", pairs_of(shards, 1))
+        got_first, got_second = after([got_first, got_second], [partial[0]])
         own_weights = [own_pack, got_x, got_y, got_first, got_second]
         weights = own_weights + [swap_section(w) for w in own_weights]
-        own_line, send_line = line_step(pos, partial[0], after(to_peers(partial[1:], "fsdp"), [got_x, got_y]))
+        own_line, send_line = line_step(pos, partial[0], to_peers(after(partial[1:], [got_first, got_second]), "fsdp"), [h0, grad1])
     else:
         row = jnp.concatenate([b_ada, b_qv, b_proj, b_fc1, b_fc2], axis=1)
         bias_rows = lax.all_gather(row[0], "fsdp", axis=0)
@@ -1087,7 +1094,7 @@
         weights = [own_whole, swap_section(own_whole)]
         acts = jax.nn.silu(conditioning.astype(F32)).astype(BF16)
         modulation = dot(acts, lax.all_gather(w_ada[0], "fsdp", axis=0, tiled=True))
-        bias_own = lookup(bias_table[0], relative_bias_index, [])
+        bias_own = lookup(bias_table[0], index, [])
         cuts = [b_ada.shape[1], b_qv.shape[1], b_proj.shape[1], b_fc1.shape[1], b_fc2.shape[1]]
         biases, at = [], 0
         for cut in cuts:
@@ -1101,7 +1108,7 @@
     bias_heads = (bias_own, swap_section(bias_own))
 
     if direct:
-        w_ada_later = after([w_ada[0]], weights[3:5])[0]
+        w_ada_later = after([w_ada_copy], weights[3:5])[0]
         w_ada_pieces = [w_ada_later] + from_peers(w_ada_later, "fsdp")
     else:
         w_ada_pieces = [lax.all_gather(w_ada[0], "fsdp", axis=0, tiled=True)]
@@ -1132,22 +1139,22 @@
         return jnp.where(bit == 0, jnp.concatenate([own, other]), jnp.concatenate([other, own]))
 
     if direct:
-        kept_small, send_small = small_step(pos, scores0, scores1, relative_bias_index, smalls, [])
+        kept_small, send_small = small_step(pos, scores0, scores1, index, smalls, [])
         other_small = swap_section(send_small)
         other_a0 = after([swap_section(send_a0)], [kept_small])[0]
         own_a0, own_small, *messages = plane_step(pos, keep_a0, other_a0, kept_small, other_small, conditioning)
         got = to_peers(messages, "fsdp")
         got_first = after(to_peers(first_messages, "fsdp"), [own_small])
         keep_z, send_z = halve_step(pos, own_first, got_first)
-        cond_part = cond_step(pos, after([own_small], [send_z])[0], w_ada_pieces, conditioning)
         part0, plane_small, *messages = column_step(pos, own_a0, own_small, got, samples)
         got_z = after([replica(send_z, 1)], [plane_small])[0]
         keep_z, send_z = quarter_step(pos, keep_z, got_z)
-        got = to_peers(messages, "rep")
+        cond_part = cond_step(pos, after([own_small], [send_z])[0], w_ada_pieces, conditioning)
+        got = after(to_peers(messages, "rep"), [cond_part])
         size = part0.shape[0]
         high, low = rank >> 1, rank & 1
         quarter0 = add_pieces(part0, [x[:size] for x in got]).astype(BF16)
-        got_z = after([replica(send_z, 2)], [quarter0])[0]
+        got_z, cond_part = after([replica(send_z, 2), cond_part], [quarter0])
         quarter = (keep_z + got_z.astype(F32)).astype(BF16)
         pair = ordered(quarter, replica(quarter, 2), high)
         half_a0 = by_rank([quarter0] + from_peers(quarter0, "rep"), rank).reshape(-1, model)
@@ -1162,7 +1169,7 @@
         )
     else:
         other_a0 = swap_section(send_a0)
-        kept_small, send_small = small_step(pos, scores0, scores1, relative_bias_index, smalls, [])
+        kept_small, send_small = small_step(pos, scores0, scores1, index, smalls, [])
         theirs = swap_section(send_small).astype(F32)
         both = kept_small + theirs
         cut = half * 8
@@ -1187,7 +1194,7 @@
             lax.dynamic_slice_in_dim(v, shard * (v.shape[0] // shards), v.shape[0] // shards, 0)[None] for v in vectors
         ]
         g_table = jnp.transpose(summed[8:].reshape(HIGH, heads, LOW), (1, 0, 2)).reshape(heads, HIGH * LOW)[:, :entries]
-        sums_a0 = section_sums(keep_a0, other_a0[:size_a], pieces)
+        sums_a0 = section_sums(keep_a0, other_a0[:size_a], z.pieces)
         half_a0, half_m0, half1 = sums_a0[0].astype(BF16), sums_m0[0].astype(BF16), sums1[0].astype(BF16)
     cond_grad = cond_part + swap_section(cond_part)
     cut = half_a0.shape[0]

time: 235 us -> 240 us (1.021)
  local copies, waits for them, and re-layouts: 15.4 us -> 18.1 us
    ppermute x4, waiting for transfers between devices: 15.1 us -> 7.09 us  [replica(): return lax.ppermute(value, 'rep', pairs_of(replicas, step))]
    ppermute x12, waiting for transfers between devices: 13.2 us -> 18.4 us  [to_peers(): lax.ppermute(messages[p - 1], axis, pairs_of(count, p))]
    ppermute x1, waiting for transfers between devices: 0.01 us -> 4.99 us  [per_device(): got_x = lax.ppermute(own_pack, 'fsdp', pairs_of(shards, 1))]
    ppermute x2, waiting for transfers between devices: 10.9 us -> 6.8 us  [the longest x1 5.11 us: per_device(): got_first = lax.ppermute(forward_x, 'fsdp', pairs_of(shards, 2))]
    slice x2, local copies, waits for them, and re-layouts: 0.09 us -> 3.77 us  [per_device(): forward_x, forward_y = (got_x[:middle_row], got_y[middle_row:])]
    unnamed x91 -> x87, local copies, waits for them, and re-layouts: 12 us -> 11.8 us
  transfers between devices with their start and end apart: 42 -> 42, of which waited for: 15 -> 17; matrix products, arithmetic and copies ran while one was open for 5% -> 7% of each run, Pallas kernels for 36% -> 34%
where the time goes in v10:
time: 240 us; the launch traced here: 239 us
  Pallas kernels  119 us (50%)
  waiting for transfers between devices  48.3 us (20%)
  starting transfers between devices  42.6 us (18%)
  local copies, waits for them, and re-layouts  18.1 us (8%)
  other arithmetic  10.4 us (4%)
    pallas_call x14, Pallas kernels, call(): pl.pallas_call(kernel, out_shape=[jax.ShapeDtypeStruct(shape, dtype) for...  101 us
    ppermute x12, waiting for transfers between devices, to_peers(): lax.ppermute(messages[p - 1], axis, pairs_of(count, p))  18.4 us
    ppermute x12, starting transfers between devices, to_peers(): lax.ppermute(messages[p - 1], axis, pairs_of(count, p))  14.2 us
    ppermute x9, starting transfers between devices, from_peers(): lax.ppermute(value, axis, pairs_of(lax.axis_size(axis), p))  13.5 us
    unnamed x87, local copies, waits for them, and re-layouts  11.8 us
    pallas_call x1, Pallas kernels, lookup(): pl.pallas_call(lookup_kernel, out_shape=jax.ShapeDtypeStruct((heads, leng...  11.2 us
    ppermute x4, waiting for transfers between devices, replica(): return lax.ppermute(value, 'rep', pairs_of(replicas, step))  7.09 us
    ppermute x4, starting transfers between devices, replica(): return lax.ppermute(value, 'rep', pairs_of(replicas, step))  6.28 us
  transfers between devices with their start and end apart: 42, of which 17 were waited for; matrix products, arithmetic and copies ran while one was open for 7% of the time, Pallas kernels for 34%

profile of v10, /device:TPU:0, one launch (start us, length us, event | category | flops | bytes accessed | tf_op | source)
XLA Modules:
  0.0 239.5 jit_solution(399786735446767788)
XLA Ops:
  0.7 3.0 %collective-permute-start = (bf16[4,384]{1,0:T(4,128)(2,1)}, bf16[4,384]{1,0:T(4,128)(2,1)S(1)}, u32[]{:S(2)}, u32[]{:S(2)}) collective-permute-start(bf16[4,384]{1,0:T(4,128)(2,1)} %cond.3), channel_id=1, source_target_pairs={{0,4},{4,0},{8,12},{12,8},{1,5},{5,1},{9,13},{13,9},{2,6},{6,2},{1... | collective-permute-start | bytes 9224 | tf_op jit(solution)/shard_map/ppermute | solution.py:1033
  5.2 2.2 shard_map.263.rest_0_
  12.2 11.2 %shard_map.264.rest_0_.refs_2_.own_bias = bf16[6,256,256]{2,1,0:T(8,128)(2,1)} custom-call(bf16[128,64]{1,0:T(8,128)(2,1)} %bitcast.73, s32[256,256]{1,0:T(8,128)} %index.3, bf16[1152,384]{1,0:T(8,128)(2,1)} %shard_map.263.rest_0_, bf16[4,384]{1,0:T(4,128)(2,1)} %copy-done.40, bf16[4,384]{1,0:T(4,128)(2,1)} %copy-done.41, bf16[4,384]{1,0:T(4,128)(2,1)} %copy-done.42), custom_call_target="tpu_custom_call" | custom-call | flops 11000000512 | tf_op jit(solution)/shard_map/pallas_call | solution.py:956
  23.5 5.0 %collective-permute-done.3.refs_0_ = bf16[1152,384]{1,0:T(8,128)(2,1)S(1)} collective-permute-done((bf16[1152,384]{1,0:T(8,128)(2,1)}, bf16[1152,384]{1,0:T(8,128)(2,1)S(1)}, u32[]{:S(2)}, u32[]{:S(2)}) %collective-permute-start.3) | collective-permute-done | bytes 884768 | tf_op jit(solution)/shard_map/ppermute | solution.py:1075
  30.8 1.9 slice.44
  37.8 5.1 %collective-permute-done.5.refs_0_ = bf16[576,384]{1,0:T(8,128)(2,1)S(1)} collective-permute-done((bf16[576,384]{1,0:T(8,128)(2,1)}, bf16[576,384]{1,0:T(8,128)(2,1)S(1)}, u32[]{:S(2)}, u32[]{:S(2)}) %collective-permute-start.5) | collective-permute-done | bytes 442400 | tf_op jit(solution)/shard_map/ppermute | solution.py:1083
  43.6 3.6 %shard_map.265 = (bf16[96,2304]{1,0:T(8,128)(2,1)}, f32[4,3072]{1,0:T(4,128)}, f32[4,3072]{1,0:T(4,128)}, f32[4,3072]{1,0:T(4,128)}, f32[4,3072]{1,0:T(4,128)}) custom-call(s32[3]{0:T(128)} %pad_add_fusion.pos, bf16[96,2304]{1,0:T(8,128)(2,1)} %bitcast.75, bf16[4,384]{1,0:T(4,128)(2,1)} %cond.3, bf16[4,384]{1,0:T(4,128)(2,1)} %copy-done.40, ...), custom_call_target="tpu_custom_call" | custom-call | flops 2000000000 | tf_op jit(solution)/shard_map/pallas_call | solution.py:516
  51.9 2.0 collective-permute-done.7.got_a
  55.8 3.3 %collective-permute-done.9.got_c = f32[4,3072]{1,0:T(4,128)S(1)} collective-permute-done((f32[4,3072]{1,0:T(4,128)}, f32[4,3072]{1,0:T(4,128)S(1)}, u32[]{:S(2)}, u32[]{:S(2)}) %collective-permute-start.9) | collective-permute-done | bytes 49184 | tf_op jit(solution)/shard_map/ppermute | solution.py:1000
  59.1 2.1 dynamic-slice_multiply_fusion
  67.9 15.2 %shard_map.271 = (bf16[512,1152]{1,0:T(8,128)(2,1)}, bf16[2,6,256,256]{3,2,1,0:T(8,128)(2,1)}, bf16[512,384]{1,0:T(8,128)(2,1)}, f32[512,384]{1,0:T(8,128)}, f32...) custom-call(s32[3]{0:T(128)} %pad_add_fusion.pos, ...), custom_call_target="tpu_custom_call" | custom-call | flops 15000000512 | tf_op jit(solution)/shard_map/pallas_call | solution.py:516
  83.1 4.3 %collective-permute-done.18.rest_11_.rest_2_ = bf16[96,2304]{1,0:T(8,128)(2,1)S(1)} collective-permute-done((bf16[96,2304]{1,0:T(8,128)(2,1)}, bf16[96,2304]{1,0:T(8,128)(2,1)S(1)}, u32[]{:S(2)}, u32[]{:S(2)}) %collective-permute-start.18) | collective-permute-done | bytes 442400 | tf_op jit(solution)/shard_map/ppermute | solution.py:1033
  88.4 26.1 %shard_map.272 = (bf16[512,384]{1,0:T(8,128)(2,1)}, bf16[512,384]{1,0:T(8,128)(2,1)}, f32[2,8,384]{2,1,0:T(8,128)}, f32[2,8,384]{2,1,0:T(8,128)}, bf16[6,256,256...) custom-call(s32[3]{0:T(128)} %pad_add_fusion.pos, bf16[512,384]{1,0:T(8,128)(2,1)} %get-tuple-element.106.h, ...), custom_call_target="tpu_custom_call" | custom-call | flops 24999999488 | tf_op jit(solution)/shard_map/pallas_call | solution.py:516
  114.6 12.0 %shard_map.273 = (f32[512,384]{1,0:T(8,128)}, f32[2,8,384]{2,1,0:T(8,128)}, bf16[1536,384]{1,0:T(8,128)(2,1)}, bf16[1536,384]{1,0:T(8,128)(2,1)}) custom-call(s32[3]{0:T(128)} %pad_add_fusion.pos, bf16[512,384]{1,0:T(8,128)(2,1)} %get-tuple-element.113.grad.d_h1, f32[512,384]{1,0:T(8,128)} %get-tuple-element.114.middle, ...), custom_call_target="tpu_custom_call" | custom-call | flops 12000000000 | tf_op jit(solution)/shard_map/pallas_call | solution.py:516
  127.2 2.8 %collective-permute-done.21.other_m = bf16[1536,384]{1,0:T(8,128)(2,1)} collective-permute-done((bf16[1536,384]{1,0:T(8,128)(2,1)}, bf16[1536,384]{1,0:T(8,128)(2,1)}, u32[]{:S(2)}, u32[]{:S(2)}) %collective-permute-start.21) | collective-permute-done | bytes 1179680 | tf_op jit(solution)/shard_map/ppermute | solution.py:968
  131.3 4.8 %shard_map.274 = (f32[960,384]{1,0:T(8,128)}, bf16[960,384]{1,0:T(8,128)(2,1)}, bf16[960,384]{1,0:T(8,128)(2,1)}, bf16[960,384]{1,0:T(8,128)(2,1)}) custom-call(bf16[2304,384]{1,0:T(8,128)(2,1)} %get-tuple-element.119.keep1, bf16[2816,384]{1,0:T(8,128)(2,1)} %copy-done.3, bf16[1536,384]{1,0:T(8,128)(2,1)} %get-tuple-element.120.keep_m, ...), custom_call_target="tpu_custom_call" | custom-call | tf_op jit(solution)/shard_map/pallas_call | solution.py:662
  139.5 12.7 %shard_map.275 = (f32[512,384]{1,0:T(8,128)}, f32[2,8,384]{2,1,0:T(8,128)}, bf16[6,256,256]{2,1,0:T(8,128)(2,1)}, bf16[768,384]{1,0:T(8,128)(2,1)}, bf16[1280,384]{1,0:T(8,128)(2,1)}) custom-call(s32[3]{0:T(128)} %pad_add_fusion.pos, bf16[512,384]{1,0:T(8,128)(2,1)} %bitcast.58, f32[1,7680]{1,0:T(1,128)} %get-tuple-element.103.own_line, ...), custom_call_target="tpu_custom_call" | custom-call | flops 12999999488 | tf_op jit(solution)/shard_map/pallas_call | solution.py:516
  152.3 11.6 %shard_map.276 = (f32[48,384]{1,0:T(8,128)}, bf16[48,384]{1,0:T(8,128)(2,1)}) custom-call(s32[3]{0:T(128)} %pad_add_fusion.pos, bf16[6,256,256]{2,1,0:T(8,128)(2,1)} %get-tuple-element.127.scores0, bf16[6,256,256]{2,1,0:T(8,128)(2,1)} %get-tuple-element.128.scores1, s32[256,256]{1,0:T(8,128)} %index.3, f32[2,8,384]{2,1,0:T(8,128)} %get-tuple-element.129.small_a0, ...), custom_call_target="tpu_custom_call" | custom-call | flops 12000000000 | tf_op jit(solution)/shard_map/pallas_call | solution.py:516
  166.1 2.4 %shard_map.278 = (f32[192,384]{1,0:T(8,128)}, bf16[64,384]{1,0:T(8,128)(2,1)}, bf16[256,384]{1,0:T(8,128)(2,1)}, bf16[256,384]{1,0:T(8,128)(2,1)}, bf16[256,384]{1,0:T(8,128)(2,1)}) custom-call(s32[3]{0:T(128)} %pad_add_fusion.pos, bf16[768,384]{1,0:T(8,128)(2,1)} %get-tuple-element.135.keep, bf16[1280,384]{1,0:T(8,128)(2,1)} %shard_map.277.other, ...), custom_call_target="tpu_custom_call" | custom-call | flops 2000000000 | tf_op jit(solution)/shard_map/pallas_call | solution.py:516
  168.5 3.0 %collective-permute-done.24.refs_1_ = bf16[960,384]{1,0:T(8,128)(2,1)} collective-permute-done((bf16[960,384]{1,0:T(8,128)(2,1)}, bf16[960,384]{1,0:T(8,128)(2,1)}, u32[]{:S(2)}, u32[]{:S(2)}) %collective-permute-start.24) | collective-permute-done | bytes 737312 | tf_op jit(solution)/shard_map/ppermute | solution.py:1000
  171.5 3.3 %shard_map.280 = (f32[480,384]{1,0:T(8,128)}, bf16[480,384]{1,0:T(8,128)(2,1)}) custom-call(s32[3]{0:T(128)} %pad_add_fusion.pos, f32[960,384]{1,0:T(8,128)} %get-tuple-element.134.own, bf16[960,384]{1,0:T(8,128)(2,1)} %get-tuple-element.138.got_a, bf16[960,384]{1,0:T(8,128)(2,1)} %get-tuple-element.139.got_b, bf16[960,384]{1,0:T(8,128)(2,1)} %get-tuple-element.140.got_c), custom_call_target="tpu_custom_call" | custom-call | flops 2000000000 | tf_op jit(solution)/shard_map/pallas_call | solution.py:516
  183.9 3.5 %collective-permute-done.29.got_b = bf16[256,384]{1,0:T(8,128)(2,1)S(1)} collective-permute-done((bf16[256,384]{1,0:T(8,128)(2,1)S(1)}, bf16[256,384]{1,0:T(8,128)(2,1)S(1)}, u32[]{:S(2)}, u32[]{:S(2)}) %collective-permute-start.29) | collective-permute-done | bytes 196640 | tf_op jit(solution)/shard_map/ppermute | solution.py:1000
  188.2 2.1 shard_map.281
  190.8 2.6 %collective-permute-start.33 = (bf16[192,384]{1,0:T(8,128)(2,1)}, bf16[192,384]{1,0:T(8,128)(2,1)S(1)}, u32[]{:S(2)}, u32[]{:S(2)}) collective-permute-start(bf16[192,384]{1,0:T(8,128)(2,1)} %get-tuple-element.151), channel_id=1, source_target_pairs={{0,2},{1,3},{2,0},{3,1},{4,6},{5,7},{6,4},{7,5},{8,10},{9,11},{10,... | collective-permute-start | bytes 442376 | tf_op jit(solution)/shard_map/ppermute | solution.py:1000
  195.5 2.1 shard_map.283
  199.2 2.9 %shard_map.285.refs_3_.refs_1_ = f32[4,384]{1,0:T(4,128)} custom-call(s32[3]{0:T(128)} %pad_add_fusion.pos, bf16[64,384]{1,0:T(8,128)(2,1)} %shard_map.284.small, bf16[4,384]{1,0:T(4,128)(2,1)} %cond.3, bf16[96,2304]{1,0:T(8,128)(2,1)} %shard_map.270.rest_10_.rest_0_, bf16[96,2304]{1,0:T(8,128)(2,1)} %copy-done.25, bf16[96,2304]{1,0:T(8,128)(2,1)} %copy-done.26, ...), custom_call_target="tpu_custom_call" | custom-call | flops 2000000000 | tf_op jit(solution)/shard_map/pallas_call | solution.py:516
  202.1 6.0 %collective-permute-done.33.refs_1_ = bf16[192,384]{1,0:T(8,128)(2,1)S(1)} collective-permute-done((bf16[192,384]{1,0:T(8,128)(2,1)}, bf16[192,384]{1,0:T(8,128)(2,1)S(1)}, u32[]{:S(2)}, u32[]{:S(2)}) %collective-permute-start.33) | collective-permute-done | bytes 147488 | tf_op jit(solution)/shard_map/ppermute | solution.py:1000
  210.3 4.0 %collective-permute-start.38 = (bf16[48,384]{1,0:T(8,128)(2,1)S(1)}, bf16[48,384]{1,0:T(8,128)(2,1)S(1)}, u32[]{:S(2)}, u32[]{:S(2)}) collective-permute-start(bf16[48,384]{1,0:T(8,128)(2,1)S(1)} %add_convert_fusion.1.refs_2_), channel_id=1, source_target_pairs={{0,2},{1,3},{2,0},{3,1},{4,6},{5,7},{6,4},{7,5},{8,10},{9,11},{10,... | collective-permute-start | bytes 110600 | tf_op jit(solution)/shard_map/ppermute | solution.py:1033
  217.5 2.9 %collective-permute-start.39 = (bf16[240,384]{1,0:T(8,128)(2,1)S(1)}, bf16[240,384]{1,0:T(8,128)(2,1)S(1)}, u32[]{:S(2)}, u32[]{:S(2)}) collective-permute-start(bf16[240,384]{1,0:T(8,128)(2,1)S(1)} %add_convert_fusion), channel_id=1, source_target_pairs={{0,2},{1,3},{2,0},{3,1},{4,6},{5,7},{6,4},{7,5},{8,10},{9,11},{10,... | collective-permute-start | bytes 552968 | tf_op jit(solution)/shard_map/ppermute | solution.py:1136
  220.4 2.8 %shard_map.288 = (f32[96,2304]{1,0:T(8,128)}, f32[1,576]{1,0:T(1,128)}, f32[1,192]{1,0:T(1,128)}, f32[1,96]{1,0:T(1,128)}, f32[1,384]{1,0:T(1,128)}, /*index=5*/f32[1,96]{1,0:T(1,128)}, f32[6,961]{1,0:T(8,128)}) custom-call(s32[3]{0:T(128)} %pad_add_fusion.pos, bf16[144,384]{1,0:T(8,128)(2,1)} %get-tuple-element.147.refs_1_.own_small, ...), custom_call_target="tpu_custom_call" | custom-call | flops 2000000000 | tf_op jit(solution)/shard_map/pallas_call | solution.py:516
  228.3 5.5 %collective-permute-done.40 = bf16[480,384]{1,0:T(8,128)(2,1)S(1)} collective-permute-done((bf16[480,384]{1,0:T(8,128)(2,1)S(1)}, bf16[480,384]{1,0:T(8,128)(2,1)S(1)}, u32[]{:S(2)}, u32[]{:S(2)}) %collective-permute-start.40) | collective-permute-done | bytes 368672 | tf_op jit(solution)/shard_map/ppermute | solution.py:1136
  237.0 2.5 %shard_map.289 = (f32[96,1152]{1,0:T(8,128)}, f32[96,384]{1,0:T(8,128)}, f32[96,1536]{1,0:T(8,128)}, f32[384,384]{1,0:T(8,128)}) custom-call(s32[3]{0:T(128)} %pad_add_fusion.pos, bf16[192,384]{1,0:T(8,128)(2,1)} %slice_select_fusion.1.own_a, bf16[384,384]{1,0:T(8,128)(2,1)} %slice_select_fusion.own_m, bf16[576,384]{1,0:T(8,128)(2,1)} %copy-done.28), custom_call_target="tpu_custom_call" | custom-call | flops 2000000000 | tf_op jit(solution)/shard_map/pallas_call | solution.py:516
  (197 shorter events, 63.8 us)
Async XLA Ops:
  0.7 10.9 %collective-permute-start = (bf16[4,384]{1,0:T(4,128)(2,1)}, bf16[4,384]{1,0:T(4,128)(2,1)S(1)}, u32[]{:S(2)}, u32[]{:S(2)}) collective-permute-start(bf16[4,384]{1,0:T(4,128)(2,1)} %cond.3), channel_id=1, source_target_pairs={{0,4},{4,0},{8,12},{12,8},{1,5},{5,1},{9,13},{13,9},{2,6},{6,2},{1... | collective-permute-start | bytes 9224 | tf_op jit(solution)/shard_map/ppermute | solution.py:1033
  3.7 7.9 %collective-permute-start.1 = (bf16[4,384]{1,0:T(4,128)(2,1)}, bf16[4,384]{1,0:T(4,128)(2,1)S(1)}, u32[]{:S(2)}, u32[]{:S(2)}) collective-permute-start(bf16[4,384]{1,0:T(4,128)(2,1)} %cond.3), channel_id=1, source_target_pairs={{0,8},{4,12},{8,0},{12,4},{1,9},{5,13},{9,1},{13,5},{2,10},{6,14},... | collective-permute-start | bytes 9224 | tf_op jit(solution)/shard_map/ppermute | solution.py:1033
  7.4 21.0 %collective-permute-start.3 = (bf16[1152,384]{1,0:T(8,128)(2,1)}, bf16[1152,384]{1,0:T(8,128)(2,1)S(1)}, u32[]{:S(2)}, u32[]{:S(2)}) collective-permute-start(bf16[1152,384]{1,0:T(8,128)(2,1)} %shard_map.263.rest_0_), channel_id=1, source_target_pairs={{0,4},{4,0},{8,12},{12,8},{1,5},{5,1},{9,13},{13,9},{2,6},{6,2},{1... | collective-permute-start | bytes 2654216 | tf_op jit(solution)/shard_map/ppermute | solution.py:1075
  9.4 20.5 %collective-permute-start.4 = (bf16[1152,384]{1,0:T(8,128)(2,1)}, bf16[1152,384]{1,0:T(8,128)(2,1)S(1)}, u32[]{:S(2)}, u32[]{:S(2)}) collective-permute-start(bf16[1152,384]{1,0:T(8,128)(2,1)} %shard_map.263.rest_0_), channel_id=1, source_target_pairs={{0,8},{4,12},{8,0},{12,4},{1,9},{5,13},{9,1},{13,5},{2,10},{6,14},... | collective-permute-start | bytes 2654216 | tf_op jit(solution)/shard_map/ppermute | solution.py:1076
  32.7 10.2 %collective-permute-start.5 = (bf16[576,384]{1,0:T(8,128)(2,1)}, bf16[576,384]{1,0:T(8,128)(2,1)S(1)}, u32[]{:S(2)}, u32[]{:S(2)}) collective-permute-start(bf16[576,384]{1,0:T(8,128)(2,1)} %slice.44), channel_id=1, source_target_pairs={{0,8},{4,12},{8,0},{12,4},{1,9},{5,13},{9,1},{13,5},{2,10},{6,14},... | collective-permute-start | bytes 1327112 | tf_op jit(solution)/shard_map/ppermute | solution.py:1083
  34.2 17.2 %collective-permute-start.11 = (bf16[6,256,256]{2,1,0:T(8,128)(2,1)}, bf16[6,256,256]{2,1,0:T(8,128)(2,1)}, u32[]{:S(2)}, u32[]{:S(2)}) collective-permute-start(bf16[6,256,256]{2,1,0:T(8,128)(2,1)} %shard_map.264.rest_0_.refs_2_.own_bias), channel_id=1, source_target_pairs={{0,16},{16,0},{1,17},{17,1},{2,18},{18,2},{3,19},{19,3},{4,20},{20... | collective-permute-start | bytes 2359304 | tf_op jit(solution)/shard_map/ppermute | solution.py:968
  36.1 12.8 %collective-permute-start.6 = (bf16[576,384]{1,0:T(8,128)(2,1)}, bf16[576,384]{1,0:T(8,128)(2,1)S(1)}, u32[]{:S(2)}, u32[]{:S(2)}) collective-permute-start(bf16[576,384]{1,0:T(8,128)(2,1)} %slice.45), channel_id=1, source_target_pairs={{0,4},{4,0},{8,12},{12,8},{1,5},{5,1},{9,13},{13,9},{2,6},{6,2},{1... | collective-permute-start | bytes 1327112 | tf_op jit(solution)/shard_map/ppermute | solution.py:1084
  37.3 25.6 %collective-permute-start.12 = (bf16[1152,384]{1,0:T(8,128)(2,1)S(1)}, bf16[1152,384]{1,0:T(8,128)(2,1)}, u32[]{:S(2)}, u32[]{:S(2)}) collective-permute-start(bf16[1152,384]{1,0:T(8,128)(2,1)S(1)} %copy-done.9), channel_id=1, source_target_pairs={{0,16},{16,0},{1,17},{17,1},{2,18},{18,2},{3,19},{19,3},{4,20},{20... | collective-permute-start | bytes 2654216 | tf_op jit(solution)/shard_map/ppermute | solution.py:968
  37.5 28.1 %collective-permute-start.13 = (bf16[1152,384]{1,0:T(8,128)(2,1)S(1)}, bf16[1152,384]{1,0:T(8,128)(2,1)}, u32[]{:S(2)}, u32[]{:S(2)}) collective-permute-start(bf16[1152,384]{1,0:T(8,128)(2,1)S(1)} %copy-done.5), channel_id=1, source_target_pairs={{0,16},{16,0},{1,17},{17,1},{2,18},{18,2},{3,19},{19,3},{4,20},{20... | collective-permute-start | bytes 2654216 | tf_op jit(solution)/shard_map/ppermute | solution.py:968
  42.9 23.2 %collective-permute-start.14 = (bf16[1152,384]{1,0:T(8,128)(2,1)S(1)}, bf16[1152,384]{1,0:T(8,128)(2,1)}, u32[]{:S(2)}, u32[]{:S(2)}) collective-permute-start(bf16[1152,384]{1,0:T(8,128)(2,1)S(1)} %copy-done.7), channel_id=1, source_target_pairs={{0,16},{16,0},{1,17},{17,1},{2,18},{18,2},{3,19},{19,3},{4,20},{20... | collective-permute-start | bytes 2654216 | tf_op jit(solution)/shard_map/ppermute | solution.py:968
  55.8 12.1 %collective-permute-start.15 = (bf16[576,384]{1,0:T(8,128)(2,1)}, bf16[576,384]{1,0:T(8,128)(2,1)}, u32[]{:S(2)}, u32[]{:S(2)}) collective-permute-start(bf16[576,384]{1,0:T(8,128)(2,1)} %get-tuple-element.98.refs_3_.refs_1_.rest_3_), channel_id=1, source_target_pairs={{0,16},{16,0},{1,17},{17,1},{2,18},{18,2},{3,19},{19,3},{4,20},{20... | collective-permute-start | bytes 1327112 | tf_op jit(solution)/shard_map/ppermute | solution.py:968
  59.1 8.7 %collective-permute-start.16 = (bf16[576,384]{1,0:T(8,128)(2,1)}, bf16[576,384]{1,0:T(8,128)(2,1)}, u32[]{:S(2)}, u32[]{:S(2)}) collective-permute-start(bf16[576,384]{1,0:T(8,128)(2,1)} %get-tuple-element.99.refs_4_.refs_2_.rest_4_), channel_id=1, source_target_pairs={{0,16},{16,0},{1,17},{17,1},{2,18},{18,2},{3,19},{19,3},{4,20},{20... | collective-permute-start | bytes 1327112 | tf_op jit(solution)/shard_map/ppermute | solution.py:968
  64.4 18.7 %collective-permute-start.17 = (bf16[96,2304]{1,0:T(8,128)(2,1)}, bf16[96,2304]{1,0:T(8,128)(2,1)S(1)}, u32[]{:S(2)}, u32[]{:S(2)}) collective-permute-start(bf16[96,2304]{1,0:T(8,128)(2,1)} %shard_map.270.rest_10_.rest_0_), channel_id=1, source_target_pairs={{0,4},{4,0},{8,12},{12,8},{1,5},{5,1},{9,13},{13,9},{2,6},{6,2},{1... | collective-permute-start | bytes 1327112 | tf_op jit(solution)/shard_map/ppermute | solution.py:1033
  65.6 21.8 %collective-permute-start.18 = (bf16[96,2304]{1,0:T(8,128)(2,1)}, bf16[96,2304]{1,0:T(8,128)(2,1)S(1)}, u32[]{:S(2)}, u32[]{:S(2)}) collective-permute-start(bf16[96,2304]{1,0:T(8,128)(2,1)} %shard_map.270.rest_10_.rest_0_), channel_id=1, source_target_pairs={{0,8},{4,12},{8,0},{12,4},{1,9},{5,13},{9,1},{13,5},{2,10},{6,14},... | collective-permute-start | bytes 1327112 | tf_op jit(solution)/shard_map/ppermute | solution.py:1033
  66.1 21.3 %collective-permute-start.19 = (bf16[96,2304]{1,0:T(8,128)(2,1)}, bf16[96,2304]{1,0:T(8,128)(2,1)S(1)}, u32[]{:S(2)}, u32[]{:S(2)}) collective-permute-start(bf16[96,2304]{1,0:T(8,128)(2,1)} %shard_map.270.rest_10_.rest_0_), channel_id=1, source_target_pairs={{0,12},{4,8},{8,4},{12,0},{1,13},{5,9},{9,5},{13,1},{2,14},{6,10},... | collective-permute-start | bytes 1327112 | tf_op jit(solution)/shard_map/ppermute | solution.py:1033
  114.5 15.5 %collective-permute-start.20 = (bf16[2816,384]{1,0:T(8,128)(2,1)}, bf16[2816,384]{1,0:T(8,128)(2,1)S(1)}, u32[]{:S(2)}, u32[]{:S(2)}) collective-permute-start(bf16[2816,384]{1,0:T(8,128)(2,1)} %get-tuple-element.108), channel_id=1, source_target_pairs={{0,16},{16,0},{1,17},{17,1},{2,18},{18,2},{3,19},{19,3},{4,20},{20... | collective-permute-start | bytes 6488072 | tf_op jit(solution)/shard_map/ppermute | solution.py:968
  136.0 32.5 %collective-permute-start.23 = (bf16[960,384]{1,0:T(8,128)(2,1)}, bf16[960,384]{1,0:T(8,128)(2,1)}, u32[]{:S(2)}, u32[]{:S(2)}) collective-permute-start(bf16[960,384]{1,0:T(8,128)(2,1)} %get-tuple-element.122.rest_10_), channel_id=1, source_target_pairs={{0,4},{4,0},{8,12},{12,8},{1,5},{5,1},{9,13},{13,9},{2,6},{6,2},{1... | collective-permute-start | bytes 2211848 | tf_op jit(solution)/shard_map/ppermute | solution.py:1000
  136.9 34.6 %collective-permute-start.24 = (bf16[960,384]{1,0:T(8,128)(2,1)}, bf16[960,384]{1,0:T(8,128)(2,1)}, u32[]{:S(2)}, u32[]{:S(2)}) collective-permute-start(bf16[960,384]{1,0:T(8,128)(2,1)} %get-tuple-element.123.rest_11_), channel_id=1, source_target_pairs={{0,8},{4,12},{8,0},{12,4},{1,9},{5,13},{9,1},{13,5},{2,10},{6,14},... | collective-permute-start | bytes 2211848 | tf_op jit(solution)/shard_map/ppermute | solution.py:1000
  137.7 33.8 %collective-permute-start.25 = (bf16[960,384]{1,0:T(8,128)(2,1)}, bf16[960,384]{1,0:T(8,128)(2,1)}, u32[]{:S(2)}, u32[]{:S(2)}) collective-permute-start(bf16[960,384]{1,0:T(8,128)(2,1)} %get-tuple-element.124.rest_12_), channel_id=1, source_target_pairs={{0,12},{4,8},{8,4},{12,0},{1,13},{5,9},{9,5},{13,1},{2,14},{6,10},... | collective-permute-start | bytes 2211848 | tf_op jit(solution)/shard_map/ppermute | solution.py:1000
  152.2 12.3 %collective-permute-start.22 = (bf16[1280,384]{1,0:T(8,128)(2,1)}, bf16[1280,384]{1,0:T(8,128)(2,1)S(1)}, u32[]{:S(2)}, u32[]{:S(2)}) collective-permute-start(bf16[1280,384]{1,0:T(8,128)(2,1)} %get-tuple-element.126), channel_id=1, source_target_pairs={{0,16},{16,0},{1,17},{17,1},{2,18},{18,2},{3,19},{19,3},{4,20},{20... | collective-permute-start | bytes 2949128 | tf_op jit(solution)/shard_map/ppermute | solution.py:968
  174.8 19.9 %collective-permute-start.27 = (bf16[480,384]{1,0:T(8,128)(2,1)}, bf16[480,384]{1,0:T(8,128)(2,1)S(1)}, u32[]{:S(2)}, u32[]{:S(2)}) collective-permute-start(bf16[480,384]{1,0:T(8,128)(2,1)} %get-tuple-element.142), channel_id=1, source_target_pairs={{0,1},{1,0},{2,3},{3,2},{4,5},{5,4},{6,7},{7,6},{8,9},{9,8},{10,11... | collective-permute-start | bytes 1105928 | tf_op jit(solution)/shard_map/ppermute | solution.py:1136
  177.6 9.8 %collective-permute-start.29 = (bf16[256,384]{1,0:T(8,128)(2,1)S(1)}, bf16[256,384]{1,0:T(8,128)(2,1)S(1)}, u32[]{:S(2)}, u32[]{:S(2)}) collective-permute-start(bf16[256,384]{1,0:T(8,128)(2,1)S(1)} %copy-done.30), channel_id=1, source_target_pairs={{0,8},{4,12},{8,0},{12,4},{1,9},{5,13},{9,1},{13,5},{2,10},{6,14},... | collective-permute-start | bytes 589832 | tf_op jit(solution)/shard_map/ppermute | solution.py:1000
  178.1 9.3 %collective-permute-start.30 = (bf16[256,384]{1,0:T(8,128)(2,1)S(1)}, bf16[256,384]{1,0:T(8,128)(2,1)S(1)}, u32[]{:S(2)}, u32[]{:S(2)}) collective-permute-start(bf16[256,384]{1,0:T(8,128)(2,1)S(1)} %copy-done.29), channel_id=1, source_target_pairs={{0,12},{4,8},{8,4},{12,0},{1,13},{5,9},{9,5},{13,1},{2,14},{6,10},... | collective-permute-start | bytes 589832 | tf_op jit(solution)/shard_map/ppermute | solution.py:1000
  190.3 11.8 %collective-permute-start.32 = (bf16[192,384]{1,0:T(8,128)(2,1)}, bf16[192,384]{1,0:T(8,128)(2,1)S(1)}, u32[]{:S(2)}, u32[]{:S(2)}) collective-permute-start(bf16[192,384]{1,0:T(8,128)(2,1)} %get-tuple-element.150), channel_id=1, source_target_pairs={{0,1},{1,0},{2,3},{3,2},{4,5},{5,4},{6,7},{7,6},{8,9},{9,8},{10,11... | collective-permute-start | bytes 442376 | tf_op jit(solution)/shard_map/ppermute | solution.py:1000
  190.8 17.3 %collective-permute-start.33 = (bf16[192,384]{1,0:T(8,128)(2,1)}, bf16[192,384]{1,0:T(8,128)(2,1)S(1)}, u32[]{:S(2)}, u32[]{:S(2)}) collective-permute-start(bf16[192,384]{1,0:T(8,128)(2,1)} %get-tuple-element.151), channel_id=1, source_target_pairs={{0,2},{1,3},{2,0},{3,1},{4,6},{5,7},{6,4},{7,5},{8,10},{9,11},{10,... | collective-permute-start | bytes 442376 | tf_op jit(solution)/shard_map/ppermute | solution.py:1000
  193.4 14.7 %collective-permute-start.34 = (bf16[192,384]{1,0:T(8,128)(2,1)}, bf16[192,384]{1,0:T(8,128)(2,1)S(1)}, u32[]{:S(2)}, u32[]{:S(2)}) collective-permute-start(bf16[192,384]{1,0:T(8,128)(2,1)} %get-tuple-element.152), channel_id=1, source_target_pairs={{0,3},{1,2},{2,1},{3,0},{4,7},{5,6},{6,5},{7,4},{8,11},{9,10},{10,... | collective-permute-start | bytes 442376 | tf_op jit(solution)/shard_map/ppermute | solution.py:1000
  197.5 18.3 %collective-permute-start.31 = (bf16[240,384]{1,0:T(8,128)(2,1)}, bf16[240,384]{1,0:T(8,128)(2,1)S(1)}, u32[]{:S(2)}, u32[]{:S(2)}) collective-permute-start(bf16[240,384]{1,0:T(8,128)(2,1)} %get-tuple-element.148.refs_1_), channel_id=1, source_target_pairs={{0,2},{1,3},{2,0},{3,1},{4,6},{5,7},{6,4},{7,5},{8,10},{9,11},{10,... | collective-permute-start | bytes 552968 | tf_op jit(solution)/shard_map/ppermute | solution.py:1136
  210.3 16.1 %collective-permute-start.38 = (bf16[48,384]{1,0:T(8,128)(2,1)S(1)}, bf16[48,384]{1,0:T(8,128)(2,1)S(1)}, u32[]{:S(2)}, u32[]{:S(2)}) collective-permute-start(bf16[48,384]{1,0:T(8,128)(2,1)S(1)} %add_convert_fusion.1.refs_2_), channel_id=1, source_target_pairs={{0,2},{1,3},{2,0},{3,1},{4,6},{5,7},{6,4},{7,5},{8,10},{9,11},{10,... | collective-permute-start | bytes 110600 | tf_op jit(solution)/shard_map/ppermute | solution.py:1033
  214.3 12.1 %collective-permute-start.37 = (bf16[48,384]{1,0:T(8,128)(2,1)S(1)}, bf16[48,384]{1,0:T(8,128)(2,1)S(1)}, u32[]{:S(2)}, u32[]{:S(2)}) collective-permute-start(bf16[48,384]{1,0:T(8,128)(2,1)S(1)} %add_convert_fusion.1.refs_2_), channel_id=1, source_target_pairs={{0,3},{1,2},{2,1},{3,0},{4,7},{5,6},{6,5},{7,4},{8,11},{9,10},{10,... | collective-permute-start | bytes 110600 | tf_op jit(solution)/shard_map/ppermute | solution.py:1033
  215.8 10.6 %collective-permute-start.36 = (bf16[48,384]{1,0:T(8,128)(2,1)S(1)}, bf16[48,384]{1,0:T(8,128)(2,1)S(1)}, u32[]{:S(2)}, u32[]{:S(2)}) collective-permute-start(bf16[48,384]{1,0:T(8,128)(2,1)S(1)} %add_convert_fusion.1.refs_2_), channel_id=1, source_target_pairs={{0,1},{1,0},{2,3},{3,2},{4,5},{5,4},{6,7},{7,6},{8,9},{9,8},{10,11... | collective-permute-start | bytes 110600 | tf_op jit(solution)/shard_map/ppermute | solution.py:1033
  217.5 8.7 %collective-permute-start.39 = (bf16[240,384]{1,0:T(8,128)(2,1)S(1)}, bf16[240,384]{1,0:T(8,128)(2,1)S(1)}, u32[]{:S(2)}, u32[]{:S(2)}) collective-permute-start(bf16[240,384]{1,0:T(8,128)(2,1)S(1)} %add_convert_fusion), channel_id=1, source_target_pairs={{0,2},{1,3},{2,0},{3,1},{4,6},{5,7},{6,4},{7,5},{8,10},{9,11},{10,... | collective-permute-start | bytes 552968 | tf_op jit(solution)/shard_map/ppermute | solution.py:1136
  226.3 7.6 %collective-permute-start.40 = (bf16[480,384]{1,0:T(8,128)(2,1)S(1)}, bf16[480,384]{1,0:T(8,128)(2,1)S(1)}, u32[]{:S(2)}, u32[]{:S(2)}) collective-permute-start(bf16[480,384]{1,0:T(8,128)(2,1)S(1)} %maximum_select_fusion.4), channel_id=1, source_target_pairs={{0,1},{1,0},{2,3},{3,2},{4,5},{5,4},{6,7},{7,6},{8,9},{9,8},{10,11... | collective-permute-start | bytes 1105928 | tf_op jit(solution)/shard_map/ppermute | solution.py:1136
  (54 other events, 307.9 us)

commit v11 on v10

--- a/solution.py
+++ b/solution.py
@@ -1075,17 +1075,12 @@
         got_x = lax.ppermute(own_pack, "fsdp", pairs_of(shards, 1))
         got_y = lax.ppermute(own_pack, "fsdp", pairs_of(shards, 2))
         bias_own = lookup(bias_table[0], index, [own_pack, *conds[1:]])
-        got_x, got_y = after([got_x, got_y], [bias_own])
-        forward_x, forward_y = got_x[:middle_row], got_y[middle_row:]
-        w_ada_copy, *partial = partial_step(
-            pos, w_ada[0], conds, (b_ada, b_qv, b_proj, b_fc1, b_fc2), [bias_own]
-        )
-        got_first = lax.ppermute(forward_x, "fsdp", pairs_of(shards, 2))
-        got_second = lax.ppermute(forward_y, "fsdp", pairs_of(shards, 1))
-        got_first, got_second = after([got_first, got_second], [partial[0]])
+        w_ada_copy, *partial = partial_step(pos, w_ada[0], conds, (b_ada, b_qv, b_proj, b_fc1, b_fc2), [bias_own])
+        got_first = lax.ppermute(got_x[:middle_row], "fsdp", pairs_of(shards, 2))
+        got_second = lax.ppermute(got_y[middle_row:], "fsdp", pairs_of(shards, 1))
         own_weights = [own_pack, got_x, got_y, got_first, got_second]
         weights = own_weights + [swap_section(w) for w in own_weights]
-        own_line, send_line = line_step(pos, partial[0], to_peers(after(partial[1:], [got_first, got_second]), "fsdp"), [h0, grad1])
+        own_line, send_line = line_step(pos, partial[0], after(to_peers(partial[1:], "fsdp"), [got_x, got_y]), [h0, grad1])
     else:
         row = jnp.concatenate([b_ada, b_qv, b_proj, b_fc1, b_fc2], axis=1)
         bias_rows = lax.all_gather(row[0], "fsdp", axis=0)

time: 240 us -> 226 us (0.942)
  waiting for transfers between devices: 48.3 us -> 39.5 us
  local copies, waits for them, and re-layouts: 18.1 us -> 14.3 us
    ppermute x12, waiting for transfers between devices: 18.4 us -> 12.5 us  [to_peers(): lax.ppermute(messages[p - 1], axis, pairs_of(count, p))]
    ppermute x1, waiting for transfers between devices: 4.99 us -> 0.01 us  [per_device(): got_x = lax.ppermute(own_pack, 'fsdp', pairs_of(shards, 1))]
    ppermute x2, waiting for transfers between devices: 6.8 us -> 10.5 us  [the longest x1 9.89 us: per_device(): got_first = lax.ppermute(got_x[:middle_row], 'fsdp', pairs_of(shards, 2))]
    unnamed x87 -> x81, local copies, waits for them, and re-layouts: 11.8 us -> 9.99 us
  transfers between devices with their start and end apart: 42 -> 42, of which waited for: 17 -> 15; matrix products, arithmetic and copies ran while one was open for 7% -> 7% of each run, Pallas kernels for 34% -> 36%
where the time goes in v11:
time: 226 us
  Pallas kernels  119 us (53%)
  starting transfers between devices  41.5 us (18%)
  waiting for transfers between devices  39.5 us (17%)
  local copies, waits for them, and re-layouts  14.3 us (6%)
  other arithmetic  10.3 us (5%)
    pallas_call x14, Pallas kernels, call(): pl.pallas_call(kernel, out_shape=[jax.ShapeDtypeStruct(shape, dtype) for...  101 us
    ppermute x12, starting transfers between devices, to_peers(): lax.ppermute(messages[p - 1], axis, pairs_of(count, p))  14.9 us
    ppermute x9, starting transfers between devices, from_peers(): lax.ppermute(value, axis, pairs_of(lax.axis_size(axis), p))  13.5 us
    ppermute x12, waiting for transfers between devices, to_peers(): lax.ppermute(messages[p - 1], axis, pairs_of(count, p))  12.5 us
    pallas_call x1, Pallas kernels, lookup(): pl.pallas_call(lookup_kernel, out_shape=jax.ShapeDtypeStruct((heads, leng...  11.2 us
    unnamed x81, local copies, waits for them, and re-layouts  9.99 us
    ppermute x1, waiting for transfers between devices, per_device(): got_first = lax.ppermute(got_x[:middle_row], 'fsdp', pairs_of(shards, 2))  9.89 us
    ppermute x4, waiting for transfers between devices, replica(): return lax.ppermute(value, 'rep', pairs_of(replicas, step))  7.07 us
  transfers between devices with their start and end apart: 42, of which 15 were waited for; matrix products, arithmetic and copies ran while one was open for 7% of the time, Pallas kernels for 36%

profile of v11, /device:TPU:0, one launch (start us, length us, event | category | flops | bytes accessed | tf_op | source)
XLA Modules:
  0.0 225.6 jit_solution(13149371683460274277)
XLA Ops:
  0.7 3.0 %collective-permute-start = (bf16[4,384]{1,0:T(4,128)(2,1)}, bf16[4,384]{1,0:T(4,128)(2,1)S(1)}, u32[]{:S(2)}, u32[]{:S(2)}) collective-permute-start(bf16[4,384]{1,0:T(4,128)(2,1)} %cond.3), channel_id=1, source_target_pairs={{0,4},{4,0},{8,12},{12,8},{1,5},{5,1},{9,13},{13,9},{2,6},{6,2},{1... | collective-permute-start | bytes 9224 | tf_op jit(solution)/shard_map/ppermute | solution.py:1033
  5.2 2.2 shard_map.263.rest_0_
  7.4 1.9 collective-permute-start.6
  12.2 11.2 %shard_map.264.rest_0_.own_bias = bf16[6,256,256]{2,1,0:T(8,128)(2,1)} custom-call(bf16[128,64]{1,0:T(8,128)(2,1)} %bitcast.73, s32[256,256]{1,0:T(8,128)} %index.3, bf16[1152,384]{1,0:T(8,128)(2,1)} %shard_map.263.rest_0_, bf16[4,384]{1,0:T(4,128)(2,1)} %copy-done.37, bf16[4,384]{1,0:T(4,128)(2,1)} %copy-done.38, bf16[4,384]{1,0:T(4,128)(2,1)} %copy-done.39), custom_call_target="tpu_custom_call" | custom-call | flops 11000000512 | tf_op jit(solution)/shard_map/pallas_call | solution.py:956
  24.1 3.6 %shard_map.265 = (bf16[96,2304]{1,0:T(8,128)(2,1)}, f32[4,3072]{1,0:T(4,128)}, f32[4,3072]{1,0:T(4,128)}, f32[4,3072]{1,0:T(4,128)}, f32[4,3072]{1,0:T(4,128)}) custom-call(s32[3]{0:T(128)} %pad_add_fusion.pos, bf16[96,2304]{1,0:T(8,128)(2,1)} %bitcast.75, bf16[4,384]{1,0:T(4,128)(2,1)} %cond.3, bf16[4,384]{1,0:T(4,128)(2,1)} %copy-done.37, ...), custom_call_target="tpu_custom_call" | custom-call | flops 2000000000 | tf_op jit(solution)/shard_map/pallas_call | solution.py:516
  28.6 2.6 %collective-permute-start.5 = (f32[4,3072]{1,0:T(4,128)}, f32[4,3072]{1,0:T(4,128)S(1)}, u32[]{:S(2)}, u32[]{:S(2)}) collective-permute-start(f32[4,3072]{1,0:T(4,128)} %get-tuple-element.91), channel_id=1, source_target_pairs={{0,12},{4,8},{8,4},{12,0},{1,13},{5,9},{9,5},{13,1},{2,14},{6,10},... | collective-permute-start | bytes 147464 | tf_op jit(solution)/shard_map/ppermute | solution.py:1000
  35.8 9.9 %collective-permute-done.10.refs_1_.rest_3_ = bf16[576,384]{1,0:T(8,128)(2,1)S(1)} collective-permute-done((bf16[576,384]{1,0:T(8,128)(2,1)}, bf16[576,384]{1,0:T(8,128)(2,1)S(1)}, u32[]{:S(2)}, u32[]{:S(2)}) %collective-permute-start.10) | collective-permute-done | bytes 442400 | tf_op jit(solution)/shard_map/ppermute | solution.py:1079
  46.3 2.1 dynamic-slice_multiply_fusion
  55.1 15.1 %shard_map.269 = (bf16[512,1152]{1,0:T(8,128)(2,1)}, bf16[2,6,256,256]{3,2,1,0:T(8,128)(2,1)}, bf16[512,384]{1,0:T(8,128)(2,1)}, f32[512,384]{1,0:T(8,128)}, f32...) custom-call(s32[3]{0:T(128)} %pad_add_fusion.pos, ...), custom_call_target="tpu_custom_call" | custom-call | flops 15000000512 | tf_op jit(solution)/shard_map/pallas_call | solution.py:516
  70.3 2.9 %collective-permute-done.18.rest_11_.rest_2_ = bf16[96,2304]{1,0:T(8,128)(2,1)S(1)} collective-permute-done((bf16[96,2304]{1,0:T(8,128)(2,1)}, bf16[96,2304]{1,0:T(8,128)(2,1)S(1)}, u32[]{:S(2)}, u32[]{:S(2)}) %collective-permute-start.18) | collective-permute-done | bytes 442400 | tf_op jit(solution)/shard_map/ppermute | solution.py:1033
  75.2 26.1 %shard_map.270 = (bf16[512,384]{1,0:T(8,128)(2,1)}, bf16[512,384]{1,0:T(8,128)(2,1)}, f32[2,8,384]{2,1,0:T(8,128)}, f32[2,8,384]{2,1,0:T(8,128)}, bf16[6,256,256...) custom-call(s32[3]{0:T(128)} %pad_add_fusion.pos, bf16[512,384]{1,0:T(8,128)(2,1)} %get-tuple-element.98.h, ...), custom_call_target="tpu_custom_call" | custom-call | flops 24999999488 | tf_op jit(solution)/shard_map/pallas_call | solution.py:516
  101.4 12.0 %shard_map.271 = (f32[512,384]{1,0:T(8,128)}, f32[2,8,384]{2,1,0:T(8,128)}, bf16[1536,384]{1,0:T(8,128)(2,1)}, bf16[1536,384]{1,0:T(8,128)(2,1)}) custom-call(s32[3]{0:T(128)} %pad_add_fusion.pos, bf16[512,384]{1,0:T(8,128)(2,1)} %get-tuple-element.105.grad.d_h1, f32[512,384]{1,0:T(8,128)} %get-tuple-element.106.middle, ...), custom_call_target="tpu_custom_call" | custom-call | flops 12000000000 | tf_op jit(solution)/shard_map/pallas_call | solution.py:516
  114.0 2.8 %collective-permute-done.21.other_m = bf16[1536,384]{1,0:T(8,128)(2,1)} collective-permute-done((bf16[1536,384]{1,0:T(8,128)(2,1)}, bf16[1536,384]{1,0:T(8,128)(2,1)}, u32[]{:S(2)}, u32[]{:S(2)}) %collective-permute-start.21) | collective-permute-done | bytes 1179680 | tf_op jit(solution)/shard_map/ppermute | solution.py:968
  118.1 4.7 %shard_map.272 = (f32[960,384]{1,0:T(8,128)}, bf16[960,384]{1,0:T(8,128)(2,1)}, bf16[960,384]{1,0:T(8,128)(2,1)}, bf16[960,384]{1,0:T(8,128)(2,1)}) custom-call(bf16[2304,384]{1,0:T(8,128)(2,1)} %get-tuple-element.111.keep1, bf16[2816,384]{1,0:T(8,128)(2,1)} %copy-done.1, bf16[1536,384]{1,0:T(8,128)(2,1)} %get-tuple-element.112.keep_m, ...), custom_call_target="tpu_custom_call" | custom-call | tf_op jit(solution)/shard_map/pallas_call | solution.py:662
  126.4 12.6 %shard_map.273 = (f32[512,384]{1,0:T(8,128)}, f32[2,8,384]{2,1,0:T(8,128)}, bf16[6,256,256]{2,1,0:T(8,128)(2,1)}, bf16[768,384]{1,0:T(8,128)(2,1)}, bf16[1280,384]{1,0:T(8,128)(2,1)}) custom-call(s32[3]{0:T(128)} %pad_add_fusion.pos, bf16[512,384]{1,0:T(8,128)(2,1)} %bitcast.58, f32[1,7680]{1,0:T(1,128)} %get-tuple-element.95.own_line, ...), custom_call_target="tpu_custom_call" | custom-call | flops 12999999488 | tf_op jit(solution)/shard_map/pallas_call | solution.py:516
  139.1 11.6 %shard_map.274 = (f32[48,384]{1,0:T(8,128)}, bf16[48,384]{1,0:T(8,128)(2,1)}) custom-call(s32[3]{0:T(128)} %pad_add_fusion.pos, bf16[6,256,256]{2,1,0:T(8,128)(2,1)} %get-tuple-element.119.scores0, bf16[6,256,256]{2,1,0:T(8,128)(2,1)} %get-tuple-element.120.scores1, s32[256,256]{1,0:T(8,128)} %index.3, f32[2,8,384]{2,1,0:T(8,128)} %get-tuple-element.121.small_a0, ...), custom_call_target="tpu_custom_call" | custom-call | flops 12000000000 | tf_op jit(solution)/shard_map/pallas_call | solution.py:516
  152.9 2.4 %shard_map.276 = (f32[192,384]{1,0:T(8,128)}, bf16[64,384]{1,0:T(8,128)(2,1)}, bf16[256,384]{1,0:T(8,128)(2,1)}, bf16[256,384]{1,0:T(8,128)(2,1)}, bf16[256,384]{1,0:T(8,128)(2,1)}) custom-call(s32[3]{0:T(128)} %pad_add_fusion.pos, bf16[768,384]{1,0:T(8,128)(2,1)} %get-tuple-element.127.keep, bf16[1280,384]{1,0:T(8,128)(2,1)} %shard_map.275.other, ...), custom_call_target="tpu_custom_call" | custom-call | flops 2000000000 | tf_op jit(solution)/shard_map/pallas_call | solution.py:516
  155.3 3.4 %collective-permute-done.24.refs_1_ = bf16[960,384]{1,0:T(8,128)(2,1)} collective-permute-done((bf16[960,384]{1,0:T(8,128)(2,1)}, bf16[960,384]{1,0:T(8,128)(2,1)}, u32[]{:S(2)}, u32[]{:S(2)}) %collective-permute-start.24) | collective-permute-done | bytes 737312 | tf_op jit(solution)/shard_map/ppermute | solution.py:1000
  158.8 3.3 %shard_map.278 = (f32[480,384]{1,0:T(8,128)}, bf16[480,384]{1,0:T(8,128)(2,1)}) custom-call(s32[3]{0:T(128)} %pad_add_fusion.pos, f32[960,384]{1,0:T(8,128)} %get-tuple-element.126.own, bf16[960,384]{1,0:T(8,128)(2,1)} %get-tuple-element.130.got_a, bf16[960,384]{1,0:T(8,128)(2,1)} %get-tuple-element.131.got_b, bf16[960,384]{1,0:T(8,128)(2,1)} %get-tuple-element.132.got_c), custom_call_target="tpu_custom_call" | custom-call | flops 2000000000 | tf_op jit(solution)/shard_map/pallas_call | solution.py:516
  162.1 1.6 collective-permute-start.27
  171.5 3.1 %collective-permute-done.29.got_b = bf16[256,384]{1,0:T(8,128)(2,1)S(1)} collective-permute-done((bf16[256,384]{1,0:T(8,128)(2,1)S(1)}, bf16[256,384]{1,0:T(8,128)(2,1)S(1)}, u32[]{:S(2)}, u32[]{:S(2)}) %collective-permute-start.29) | collective-permute-done | bytes 196640 | tf_op jit(solution)/shard_map/ppermute | solution.py:1000
  175.4 2.1 shard_map.279
  177.9 2.6 %collective-permute-start.33 = (bf16[192,384]{1,0:T(8,128)(2,1)}, bf16[192,384]{1,0:T(8,128)(2,1)S(1)}, u32[]{:S(2)}, u32[]{:S(2)}) collective-permute-start(bf16[192,384]{1,0:T(8,128)(2,1)} %get-tuple-element.143), channel_id=1, source_target_pairs={{0,2},{1,3},{2,0},{3,1},{4,6},{5,7},{6,4},{7,5},{8,10},{9,11},{10,... | collective-permute-start | bytes 442376 | tf_op jit(solution)/shard_map/ppermute | solution.py:1000
  182.6 2.1 shard_map.281
  184.7 1.7 collective-permute-start.31
  186.4 2.9 %shard_map.283.refs_3_.refs_1_ = f32[4,384]{1,0:T(4,128)} custom-call(s32[3]{0:T(128)} %pad_add_fusion.pos, bf16[64,384]{1,0:T(8,128)(2,1)} %shard_map.282.small, bf16[4,384]{1,0:T(4,128)(2,1)} %cond.3, bf16[96,2304]{1,0:T(8,128)(2,1)} %shard_map.268.rest_10_.rest_0_, bf16[96,2304]{1,0:T(8,128)(2,1)} %copy-done.25, bf16[96,2304]{1,0:T(8,128)(2,1)} %copy-done.26, ...), custom_call_target="tpu_custom_call" | custom-call | flops 2000000000 | tf_op jit(solution)/shard_map/pallas_call | solution.py:516
  189.2 5.0 %collective-permute-done.33.refs_1_ = bf16[192,384]{1,0:T(8,128)(2,1)S(1)} collective-permute-done((bf16[192,384]{1,0:T(8,128)(2,1)}, bf16[192,384]{1,0:T(8,128)(2,1)S(1)}, u32[]{:S(2)}, u32[]{:S(2)}) %collective-permute-start.33) | collective-permute-done | bytes 147488 | tf_op jit(solution)/shard_map/ppermute | solution.py:1000
  196.4 4.0 %collective-permute-start.38 = (bf16[48,384]{1,0:T(8,128)(2,1)S(1)}, bf16[48,384]{1,0:T(8,128)(2,1)S(1)}, u32[]{:S(2)}, u32[]{:S(2)}) collective-permute-start(bf16[48,384]{1,0:T(8,128)(2,1)S(1)} %add_convert_fusion.1.refs_2_), channel_id=1, source_target_pairs={{0,2},{1,3},{2,0},{3,1},{4,6},{5,7},{6,4},{7,5},{8,10},{9,11},{10,... | collective-permute-start | bytes 110600 | tf_op jit(solution)/shard_map/ppermute | solution.py:1033
  203.6 2.9 %collective-permute-start.39 = (bf16[240,384]{1,0:T(8,128)(2,1)S(1)}, bf16[240,384]{1,0:T(8,128)(2,1)S(1)}, u32[]{:S(2)}, u32[]{:S(2)}) collective-permute-start(bf16[240,384]{1,0:T(8,128)(2,1)S(1)} %add_convert_fusion), channel_id=1, source_target_pairs={{0,2},{1,3},{2,0},{3,1},{4,6},{5,7},{6,4},{7,5},{8,10},{9,11},{10,... | collective-permute-start | bytes 552968 | tf_op jit(solution)/shard_map/ppermute | solution.py:1131
  206.5 2.8 %shard_map.286 = (f32[96,2304]{1,0:T(8,128)}, f32[1,576]{1,0:T(1,128)}, f32[1,192]{1,0:T(1,128)}, f32[1,96]{1,0:T(1,128)}, f32[1,384]{1,0:T(1,128)}, /*index=5*/f32[1,96]{1,0:T(1,128)}, f32[6,961]{1,0:T(8,128)}) custom-call(s32[3]{0:T(128)} %pad_add_fusion.pos, bf16[144,384]{1,0:T(8,128)(2,1)} %get-tuple-element.139.refs_1_.own_small, ...), custom_call_target="tpu_custom_call" | custom-call | flops 2000000000 | tf_op jit(solution)/shard_map/pallas_call | solution.py:516
  214.4 5.5 %collective-permute-done.40 = bf16[480,384]{1,0:T(8,128)(2,1)S(1)} collective-permute-done((bf16[480,384]{1,0:T(8,128)(2,1)S(1)}, bf16[480,384]{1,0:T(8,128)(2,1)S(1)}, u32[]{:S(2)}, u32[]{:S(2)}) %collective-permute-start.40) | collective-permute-done | bytes 368672 | tf_op jit(solution)/shard_map/ppermute | solution.py:1131
  223.1 2.5 %shard_map.287 = (f32[96,1152]{1,0:T(8,128)}, f32[96,384]{1,0:T(8,128)}, f32[96,1536]{1,0:T(8,128)}, f32[384,384]{1,0:T(8,128)}) custom-call(s32[3]{0:T(128)} %pad_add_fusion.pos, bf16[192,384]{1,0:T(8,128)(2,1)} %slice_select_fusion.1.own_a, bf16[384,384]{1,0:T(8,128)(2,1)} %slice_select_fusion.own_m, bf16[576,384]{1,0:T(8,128)(2,1)} %copy-done.28), custom_call_target="tpu_custom_call" | custom-call | flops 2000000000 | tf_op jit(solution)/shard_map/pallas_call | solution.py:516
  (189 shorter events, 52.0 us)
Async XLA Ops:
  0.7 10.9 %collective-permute-start = (bf16[4,384]{1,0:T(4,128)(2,1)}, bf16[4,384]{1,0:T(4,128)(2,1)S(1)}, u32[]{:S(2)}, u32[]{:S(2)}) collective-permute-start(bf16[4,384]{1,0:T(4,128)(2,1)} %cond.3), channel_id=1, source_target_pairs={{0,4},{4,0},{8,12},{12,8},{1,5},{5,1},{9,13},{13,9},{2,6},{6,2},{1... | collective-permute-start | bytes 9224 | tf_op jit(solution)/shard_map/ppermute | solution.py:1033
  3.7 7.9 %collective-permute-start.1 = (bf16[4,384]{1,0:T(4,128)(2,1)}, bf16[4,384]{1,0:T(4,128)(2,1)S(1)}, u32[]{:S(2)}, u32[]{:S(2)}) collective-permute-start(bf16[4,384]{1,0:T(4,128)(2,1)} %cond.3), channel_id=1, source_target_pairs={{0,8},{4,12},{8,0},{12,4},{1,9},{5,13},{9,1},{13,5},{2,10},{6,14},... | collective-permute-start | bytes 9224 | tf_op jit(solution)/shard_map/ppermute | solution.py:1033
  7.4 21.2 %collective-permute-start.6 = (bf16[1152,384]{1,0:T(8,128)(2,1)}, bf16[1152,384]{1,0:T(8,128)(2,1)S(1)}, u32[]{:S(2)}, u32[]{:S(2)}) collective-permute-start(bf16[1152,384]{1,0:T(8,128)(2,1)} %shard_map.263.rest_0_), channel_id=1, source_target_pairs={{0,4},{4,0},{8,12},{12,8},{1,5},{5,1},{9,13},{13,9},{2,6},{6,2},{1... | collective-permute-start | bytes 2654216 | tf_op jit(solution)/shard_map/ppermute | solution.py:1075
  9.4 21.9 %collective-permute-start.7 = (bf16[1152,384]{1,0:T(8,128)(2,1)}, bf16[1152,384]{1,0:T(8,128)(2,1)S(1)}, u32[]{:S(2)}, u32[]{:S(2)}) collective-permute-start(bf16[1152,384]{1,0:T(8,128)(2,1)} %shard_map.263.rest_0_), channel_id=1, source_target_pairs={{0,8},{4,12},{8,0},{12,4},{1,9},{5,13},{9,1},{13,5},{2,10},{6,14},... | collective-permute-start | bytes 2654216 | tf_op jit(solution)/shard_map/ppermute | solution.py:1076
  23.5 10.6 %collective-permute-start.9 = (bf16[6,256,256]{2,1,0:T(8,128)(2,1)}, bf16[6,256,256]{2,1,0:T(8,128)(2,1)}, u32[]{:S(2)}, u32[]{:S(2)}) collective-permute-start(bf16[6,256,256]{2,1,0:T(8,128)(2,1)} %shard_map.264.rest_0_.own_bias), channel_id=1, source_target_pairs={{0,16},{16,0},{1,17},{17,1},{2,18},{18,2},{3,19},{19,3},{4,20},{20... | collective-permute-start | bytes 2359304 | tf_op jit(solution)/shard_map/ppermute | solution.py:968
  31.2 18.8 %collective-permute-start.12 = (bf16[1152,384]{1,0:T(8,128)(2,1)S(1)}, bf16[1152,384]{1,0:T(8,128)(2,1)}, u32[]{:S(2)}, u32[]{:S(2)}) collective-permute-start(bf16[1152,384]{1,0:T(8,128)(2,1)S(1)} %copy-done.5), channel_id=1, source_target_pairs={{0,16},{16,0},{1,17},{17,1},{2,18},{18,2},{3,19},{19,3},{4,20},{20... | collective-permute-start | bytes 2654216 | tf_op jit(solution)/shard_map/ppermute | solution.py:968
  33.0 12.7 %collective-permute-start.10 = (bf16[576,384]{1,0:T(8,128)(2,1)}, bf16[576,384]{1,0:T(8,128)(2,1)S(1)}, u32[]{:S(2)}, u32[]{:S(2)}) collective-permute-start(bf16[576,384]{1,0:T(8,128)(2,1)} %slice.57), channel_id=1, source_target_pairs={{0,8},{4,12},{8,0},{12,4},{1,9},{5,13},{9,1},{13,5},{2,10},{6,14},... | collective-permute-start | bytes 1327112 | tf_op jit(solution)/shard_map/ppermute | solution.py:1079
  33.9 12.4 %collective-permute-start.11 = (bf16[576,384]{1,0:T(8,128)(2,1)}, bf16[576,384]{1,0:T(8,128)(2,1)}, u32[]{:S(2)}, u32[]{:S(2)}) collective-permute-start(bf16[576,384]{1,0:T(8,128)(2,1)} %slice.58), channel_id=1, source_target_pairs={{0,4},{4,0},{8,12},{12,8},{1,5},{5,1},{9,13},{13,9},{2,6},{6,2},{1... | collective-permute-start | bytes 1327112 | tf_op jit(solution)/shard_map/ppermute | solution.py:1080
  34.1 18.1 %collective-permute-start.13 = (bf16[1152,384]{1,0:T(8,128)(2,1)S(1)}, bf16[1152,384]{1,0:T(8,128)(2,1)}, u32[]{:S(2)}, u32[]{:S(2)}) collective-permute-start(bf16[1152,384]{1,0:T(8,128)(2,1)S(1)} %collective-permute-done.6.refs_3_.rest_1_), channel_id=1, source_target_pairs={{0,16},{16,0},{1,17},{17,1},{2,18},{18,2},{3,19},{19,3},{4,20},{20... | collective-permute-start | bytes 2654216 | tf_op jit(solution)/shard_map/ppermute | solution.py:968
  34.1 19.6 %collective-permute-start.14 = (bf16[1152,384]{1,0:T(8,128)(2,1)S(1)}, bf16[1152,384]{1,0:T(8,128)(2,1)}, u32[]{:S(2)}, u32[]{:S(2)}) collective-permute-start(bf16[1152,384]{1,0:T(8,128)(2,1)S(1)} %collective-permute-done.7.refs_4_.rest_2_), channel_id=1, source_target_pairs={{0,16},{16,0},{1,17},{17,1},{2,18},{18,2},{3,19},{19,3},{4,20},{20... | collective-permute-start | bytes 2654216 | tf_op jit(solution)/shard_map/ppermute | solution.py:968
  45.7 9.4 %collective-permute-start.15 = (bf16[576,384]{1,0:T(8,128)(2,1)S(1)}, bf16[576,384]{1,0:T(8,128)(2,1)}, u32[]{:S(2)}, u32[]{:S(2)}) collective-permute-start(bf16[576,384]{1,0:T(8,128)(2,1)S(1)} %collective-permute-done.10.refs_1_.rest_3_), channel_id=1, source_target_pairs={{0,16},{16,0},{1,17},{17,1},{2,18},{18,2},{3,19},{19,3},{4,20},{20... | collective-permute-start | bytes 1327112 | tf_op jit(solution)/shard_map/ppermute | solution.py:968
  46.3 8.8 %collective-permute-start.16 = (bf16[576,384]{1,0:T(8,128)(2,1)}, bf16[576,384]{1,0:T(8,128)(2,1)}, u32[]{:S(2)}, u32[]{:S(2)}) collective-permute-start(bf16[576,384]{1,0:T(8,128)(2,1)} %collective-permute-done.11.refs_2_.rest_4_), channel_id=1, source_target_pairs={{0,16},{16,0},{1,17},{17,1},{2,18},{18,2},{3,19},{19,3},{4,20},{20... | collective-permute-start | bytes 1327112 | tf_op jit(solution)/shard_map/ppermute | solution.py:968
  51.6 18.6 %collective-permute-start.17 = (bf16[96,2304]{1,0:T(8,128)(2,1)}, bf16[96,2304]{1,0:T(8,128)(2,1)S(1)}, u32[]{:S(2)}, u32[]{:S(2)}) collective-permute-start(bf16[96,2304]{1,0:T(8,128)(2,1)} %shard_map.268.rest_10_.rest_0_), channel_id=1, source_target_pairs={{0,4},{4,0},{8,12},{12,8},{1,5},{5,1},{9,13},{13,9},{2,6},{6,2},{1... | collective-permute-start | bytes 1327112 | tf_op jit(solution)/shard_map/ppermute | solution.py:1033
  52.2 21.0 %collective-permute-start.18 = (bf16[96,2304]{1,0:T(8,128)(2,1)}, bf16[96,2304]{1,0:T(8,128)(2,1)S(1)}, u32[]{:S(2)}, u32[]{:S(2)}) collective-permute-start(bf16[96,2304]{1,0:T(8,128)(2,1)} %shard_map.268.rest_10_.rest_0_), channel_id=1, source_target_pairs={{0,8},{4,12},{8,0},{12,4},{1,9},{5,13},{9,1},{13,5},{2,10},{6,14},... | collective-permute-start | bytes 1327112 | tf_op jit(solution)/shard_map/ppermute | solution.py:1033
  53.7 20.7 %collective-permute-start.19 = (bf16[96,2304]{1,0:T(8,128)(2,1)}, bf16[96,2304]{1,0:T(8,128)(2,1)S(1)}, u32[]{:S(2)}, u32[]{:S(2)}) collective-permute-start(bf16[96,2304]{1,0:T(8,128)(2,1)} %shard_map.268.rest_10_.rest_0_), channel_id=1, source_target_pairs={{0,12},{4,8},{8,4},{12,0},{1,13},{5,9},{9,5},{13,1},{2,14},{6,10},... | collective-permute-start | bytes 1327112 | tf_op jit(solution)/shard_map/ppermute | solution.py:1033
  101.3 15.5 %collective-permute-start.20 = (bf16[2816,384]{1,0:T(8,128)(2,1)}, bf16[2816,384]{1,0:T(8,128)(2,1)S(1)}, u32[]{:S(2)}, u32[]{:S(2)}) collective-permute-start(bf16[2816,384]{1,0:T(8,128)(2,1)} %get-tuple-element.100), channel_id=1, source_target_pairs={{0,16},{16,0},{1,17},{17,1},{2,18},{18,2},{3,19},{19,3},{4,20},{20... | collective-permute-start | bytes 6488072 | tf_op jit(solution)/shard_map/ppermute | solution.py:968
  122.9 32.4 %collective-permute-start.23 = (bf16[960,384]{1,0:T(8,128)(2,1)}, bf16[960,384]{1,0:T(8,128)(2,1)}, u32[]{:S(2)}, u32[]{:S(2)}) collective-permute-start(bf16[960,384]{1,0:T(8,128)(2,1)} %get-tuple-element.114.rest_10_), channel_id=1, source_target_pairs={{0,4},{4,0},{8,12},{12,8},{1,5},{5,1},{9,13},{13,9},{2,6},{6,2},{1... | collective-permute-start | bytes 2211848 | tf_op jit(solution)/shard_map/ppermute | solution.py:1000
  124.1 34.6 %collective-permute-start.24 = (bf16[960,384]{1,0:T(8,128)(2,1)}, bf16[960,384]{1,0:T(8,128)(2,1)}, u32[]{:S(2)}, u32[]{:S(2)}) collective-permute-start(bf16[960,384]{1,0:T(8,128)(2,1)} %get-tuple-element.115.rest_11_), channel_id=1, source_target_pairs={{0,8},{4,12},{8,0},{12,4},{1,9},{5,13},{9,1},{13,5},{2,10},{6,14},... | collective-permute-start | bytes 2211848 | tf_op jit(solution)/shard_map/ppermute | solution.py:1000
  125.4 33.4 %collective-permute-start.25 = (bf16[960,384]{1,0:T(8,128)(2,1)}, bf16[960,384]{1,0:T(8,128)(2,1)}, u32[]{:S(2)}, u32[]{:S(2)}) collective-permute-start(bf16[960,384]{1,0:T(8,128)(2,1)} %get-tuple-element.116.rest_12_), channel_id=1, source_target_pairs={{0,12},{4,8},{8,4},{12,0},{1,13},{5,9},{9,5},{13,1},{2,14},{6,10},... | collective-permute-start | bytes 2211848 | tf_op jit(solution)/shard_map/ppermute | solution.py:1000
  139.0 12.3 %collective-permute-start.22 = (bf16[1280,384]{1,0:T(8,128)(2,1)}, bf16[1280,384]{1,0:T(8,128)(2,1)S(1)}, u32[]{:S(2)}, u32[]{:S(2)}) collective-permute-start(bf16[1280,384]{1,0:T(8,128)(2,1)} %get-tuple-element.118), channel_id=1, source_target_pairs={{0,16},{16,0},{1,17},{17,1},{2,18},{18,2},{3,19},{19,3},{4,20},{20... | collective-permute-start | bytes 2949128 | tf_op jit(solution)/shard_map/ppermute | solution.py:968
  162.1 19.8 %collective-permute-start.27 = (bf16[480,384]{1,0:T(8,128)(2,1)}, bf16[480,384]{1,0:T(8,128)(2,1)S(1)}, u32[]{:S(2)}, u32[]{:S(2)}) collective-permute-start(bf16[480,384]{1,0:T(8,128)(2,1)} %get-tuple-element.134), channel_id=1, source_target_pairs={{0,1},{1,0},{2,3},{3,2},{4,5},{5,4},{6,7},{7,6},{8,9},{9,8},{10,11... | collective-permute-start | bytes 1105928 | tf_op jit(solution)/shard_map/ppermute | solution.py:1131
  163.7 7.8 %collective-permute-start.28 = (bf16[256,384]{1,0:T(8,128)(2,1)S(1)}, bf16[256,384]{1,0:T(8,128)(2,1)S(1)}, u32[]{:S(2)}, u32[]{:S(2)}) collective-permute-start(bf16[256,384]{1,0:T(8,128)(2,1)S(1)} %copy-done.31), channel_id=1, source_target_pairs={{0,4},{4,0},{8,12},{12,8},{1,5},{5,1},{9,13},{13,9},{2,6},{6,2},{1... | collective-permute-start | bytes 589832 | tf_op jit(solution)/shard_map/ppermute | solution.py:1000
  164.6 10.0 %collective-permute-start.29 = (bf16[256,384]{1,0:T(8,128)(2,1)S(1)}, bf16[256,384]{1,0:T(8,128)(2,1)S(1)}, u32[]{:S(2)}, u32[]{:S(2)}) collective-permute-start(bf16[256,384]{1,0:T(8,128)(2,1)S(1)} %copy-done.30), channel_id=1, source_target_pairs={{0,8},{4,12},{8,0},{12,4},{1,9},{5,13},{9,1},{13,5},{2,10},{6,14},... | collective-permute-start | bytes 589832 | tf_op jit(solution)/shard_map/ppermute | solution.py:1000
  165.8 8.9 %collective-permute-start.30 = (bf16[256,384]{1,0:T(8,128)(2,1)S(1)}, bf16[256,384]{1,0:T(8,128)(2,1)S(1)}, u32[]{:S(2)}, u32[]{:S(2)}) collective-permute-start(bf16[256,384]{1,0:T(8,128)(2,1)S(1)} %copy-done.29), channel_id=1, source_target_pairs={{0,12},{4,8},{8,4},{12,0},{1,13},{5,9},{9,5},{13,1},{2,14},{6,10},... | collective-permute-start | bytes 589832 | tf_op jit(solution)/shard_map/ppermute | solution.py:1000
  177.5 11.7 %collective-permute-start.32 = (bf16[192,384]{1,0:T(8,128)(2,1)}, bf16[192,384]{1,0:T(8,128)(2,1)S(1)}, u32[]{:S(2)}, u32[]{:S(2)}) collective-permute-start(bf16[192,384]{1,0:T(8,128)(2,1)} %get-tuple-element.142), channel_id=1, source_target_pairs={{0,1},{1,0},{2,3},{3,2},{4,5},{5,4},{6,7},{7,6},{8,9},{9,8},{10,11... | collective-permute-start | bytes 442376 | tf_op jit(solution)/shard_map/ppermute | solution.py:1000
  177.9 16.3 %collective-permute-start.33 = (bf16[192,384]{1,0:T(8,128)(2,1)}, bf16[192,384]{1,0:T(8,128)(2,1)S(1)}, u32[]{:S(2)}, u32[]{:S(2)}) collective-permute-start(bf16[192,384]{1,0:T(8,128)(2,1)} %get-tuple-element.143), channel_id=1, source_target_pairs={{0,2},{1,3},{2,0},{3,1},{4,6},{5,7},{6,4},{7,5},{8,10},{9,11},{10,... | collective-permute-start | bytes 442376 | tf_op jit(solution)/shard_map/ppermute | solution.py:1000
  180.5 13.7 %collective-permute-start.34 = (bf16[192,384]{1,0:T(8,128)(2,1)}, bf16[192,384]{1,0:T(8,128)(2,1)S(1)}, u32[]{:S(2)}, u32[]{:S(2)}) collective-permute-start(bf16[192,384]{1,0:T(8,128)(2,1)} %get-tuple-element.144), channel_id=1, source_target_pairs={{0,3},{1,2},{2,1},{3,0},{4,7},{5,6},{6,5},{7,4},{8,11},{9,10},{10,... | collective-permute-start | bytes 442376 | tf_op jit(solution)/shard_map/ppermute | solution.py:1000
  184.7 17.2 %collective-permute-start.31 = (bf16[240,384]{1,0:T(8,128)(2,1)}, bf16[240,384]{1,0:T(8,128)(2,1)S(1)}, u32[]{:S(2)}, u32[]{:S(2)}) collective-permute-start(bf16[240,384]{1,0:T(8,128)(2,1)} %get-tuple-element.140.refs_1_), channel_id=1, source_target_pairs={{0,2},{1,3},{2,0},{3,1},{4,6},{5,7},{6,4},{7,5},{8,10},{9,11},{10,... | collective-permute-start | bytes 552968 | tf_op jit(solution)/shard_map/ppermute | solution.py:1131
  196.4 16.0 %collective-permute-start.38 = (bf16[48,384]{1,0:T(8,128)(2,1)S(1)}, bf16[48,384]{1,0:T(8,128)(2,1)S(1)}, u32[]{:S(2)}, u32[]{:S(2)}) collective-permute-start(bf16[48,384]{1,0:T(8,128)(2,1)S(1)} %add_convert_fusion.1.refs_2_), channel_id=1, source_target_pairs={{0,2},{1,3},{2,0},{3,1},{4,6},{5,7},{6,4},{7,5},{8,10},{9,11},{10,... | collective-permute-start | bytes 110600 | tf_op jit(solution)/shard_map/ppermute | solution.py:1033
  200.4 12.1 %collective-permute-start.37 = (bf16[48,384]{1,0:T(8,128)(2,1)S(1)}, bf16[48,384]{1,0:T(8,128)(2,1)S(1)}, u32[]{:S(2)}, u32[]{:S(2)}) collective-permute-start(bf16[48,384]{1,0:T(8,128)(2,1)S(1)} %add_convert_fusion.1.refs_2_), channel_id=1, source_target_pairs={{0,3},{1,2},{2,1},{3,0},{4,7},{5,6},{6,5},{7,4},{8,11},{9,10},{10,... | collective-permute-start | bytes 110600 | tf_op jit(solution)/shard_map/ppermute | solution.py:1033
  201.9 10.6 %collective-permute-start.36 = (bf16[48,384]{1,0:T(8,128)(2,1)S(1)}, bf16[48,384]{1,0:T(8,128)(2,1)S(1)}, u32[]{:S(2)}, u32[]{:S(2)}) collective-permute-start(bf16[48,384]{1,0:T(8,128)(2,1)S(1)} %add_convert_fusion.1.refs_2_), channel_id=1, source_target_pairs={{0,1},{1,0},{2,3},{3,2},{4,5},{5,4},{6,7},{7,6},{8,9},{9,8},{10,11... | collective-permute-start | bytes 110600 | tf_op jit(solution)/shard_map/ppermute | solution.py:1033
  203.6 8.7 %collective-permute-start.39 = (bf16[240,384]{1,0:T(8,128)(2,1)S(1)}, bf16[240,384]{1,0:T(8,128)(2,1)S(1)}, u32[]{:S(2)}, u32[]{:S(2)}) collective-permute-start(bf16[240,384]{1,0:T(8,128)(2,1)S(1)} %add_convert_fusion), channel_id=1, source_target_pairs={{0,2},{1,3},{2,0},{3,1},{4,6},{5,7},{6,4},{7,5},{8,10},{9,11},{10,... | collective-permute-start | bytes 552968 | tf_op jit(solution)/shard_map/ppermute | solution.py:1131
  (51 other events, 327.1 us)
